TPU v7x, 32 devices: a whole 2x2x4 slice. The times are simulated.
32 devices in a mesh: group: 2 (over y), dev: 16 (over z, x, core).
Axes of the slice: x: 2, y: 2, z: 4, core: 2. Of those that a mesh axis runs over, the one named last changes fastest.
Arguments:
- source_emb: float32 [256, 128, 128], P(('group', 'dev')), may hold values from -6 to 6
- target_emb: float32 [1024, 128, 128], P(('group', 'dev')), may hold values from -6 to 6
- source_mass: float32 [256, 128], P(('group', 'dev')), may hold values from 0.5 to 2
- target_mass: float32 [1024, 128], P(('group', 'dev')), may hold values from 0.5 to 2
- cand_device: int32 [256, 7], P(('group', 'dev')), may hold values from 0 to 15, all different within a row; in each aligned block of 8 rows (0 to 7, 8 to 15, ...) at most 5 rows name the same one
- cand_block: int32 [256, 8], P(('group', 'dev')), may hold values from 0 to 31
Outputs:
- src_scale: float32 [256, 128], P(('group', 'dev'))
- tgt_scale: float32 [1024, 128], P(('group', 'dev'))
Inputs may be any that keep to these rules, and one draw needn't show every extreme that they name: `cand_device`: the seven devices named by one source block are distinct; among the 8 source blocks of one device, no device is named more than 5 times, and some device is named exactly 5 times.
All inputs are finite; a program needn't handle non-finite values.
Results may differ from a plain program's by a relative error of at most 0.0001.
Values sent between devices are 32-bit elements; how exact they have to be, the bound alone decides.
No kernel may reach another device: no remote copies, remote signals or barrier semaphores. Data moves between devices by JAX's collectives and lax.ppermute only.
A program may use at most 64 MiB of HBM per device.

v0:
```python
import jax
import jax.numpy as jnp
from jax import lax
from jax.sharding import PartitionSpec as P

NODE_GROUP_SIZE = 128
FEATURE_LENGTH = 128
ITERS = 2


entropic_regularizer = 0.1
dustbin = 0.5
epsilon = 1e-06


def from_behind(x, axis, by):
    count = lax.axis_size(axis)
    return lax.ppermute(x, axis, [(i, (i + by) % count) for i in range(count)])


def unit_rows(emb):
    return emb * lax.rsqrt(jnp.mean(emb * emb, axis=-1, keepdims=True) + epsilon)


def selected_rows(table, asked_rows, dev_count, slot_cap):
    picked = jnp.take(table, asked_rows, axis=0)
    return picked.reshape((dev_count, slot_cap) + table.shape[1:])


def assemble(nearby_flattened, far_part, slot_index, sb_dev, near_count):
    near_part = jnp.take(nearby_flattened, slot_index, axis=0).reshape(
        (sb_dev, near_count) + nearby_flattened.shape[1:]
    )
    return jnp.concatenate([near_part, far_part[:, None]], axis=1)


def build_kernel(src_unit, pair_emb):
    alignment_affinity = jnp.einsum(
        "ibd,ikjd->ikbj", src_unit, pair_emb, precision=lax.Precision.HIGHEST
    )
    return jnp.exp(alignment_affinity * (1.0 / (FEATURE_LENGTH * entropic_regularizer))) / (
        8.0 * NODE_GROUP_SIZE
    )


def local(source_emb, target_emb, source_mass, target_mass, cand_device, cand_block):
    dev_count = lax.axis_size("dev")
    sb_dev = source_emb.shape[0]
    tb_dev = target_emb.shape[0]
    near_count = cand_device.shape[1]
    slot_cap = (near_count * sb_dev + dev_count - 1) // dev_count + 1
    count_of_pairs = sb_dev * near_count
    src_unit = unit_rows(source_emb)
    tgt_unit = unit_rows(target_emb)
    target_dev = cand_device.reshape(count_of_pairs)
    onehot = (target_dev[:, None] == jnp.arange(dev_count, dtype=jnp.int32)[None, :]).astype(
        jnp.int32
    )
    before = jnp.cumsum(onehot, axis=0) - onehot
    position_rank = jnp.sum(before * onehot, axis=1)
    slot_index = target_dev * slot_cap + position_rank
    wanted = (
        jnp.zeros((dev_count * slot_cap,), jnp.int32)
        .at[slot_index]
        .set(cand_block[:, :near_count].reshape(count_of_pairs))
    )
    asked_rows = lax.all_to_all(
        wanted.reshape(dev_count, slot_cap), "dev", split_axis=0, concat_axis=0, tiled=True
    ).reshape(dev_count * slot_cap)
    owner_hot = (asked_rows[:, None] == jnp.arange(tb_dev, dtype=jnp.int32)[None, :]).astype(
        jnp.float32
    )
    remote_node_group = cand_block[:, near_count]
    twin_hot = (remote_node_group[:, None] == jnp.arange(tb_dev, dtype=jnp.int32)[None, :]).astype(
        jnp.float32
    )
    twin_emb = from_behind(tgt_unit, "group", -1)
    far_emb = jnp.take(twin_emb, remote_node_group, axis=0)
    tgt_scale = jnp.ones_like(target_mass)
    src_scale = jnp.ones_like(source_mass)
    kernel = None
    near_emb = None
    near_emb = lax.all_to_all(
        selected_rows(tgt_unit, asked_rows, dev_count, slot_cap),
        "dev",
        split_axis=0,
        concat_axis=0,
        tiled=True,
    )
    near_emb = near_emb.reshape((dev_count * slot_cap,) + tgt_unit.shape[1:])
    for sweep in range(ITERS):
        if sweep == 0:
            far_scale = jnp.ones((sb_dev, target_mass.shape[1]), jnp.float32)
        else:
            twin_scale = from_behind(tgt_scale, "group", -1)
            far_scale = jnp.take(twin_scale, remote_node_group, axis=0)
        if sweep == 0:
            kernel = build_kernel(
                src_unit, assemble(near_emb, far_emb, slot_index, sb_dev, near_count)
            )
            near_scale = jnp.ones((dev_count * slot_cap, target_mass.shape[1]), jnp.float32)
        else:
            near_scale = lax.all_to_all(
                selected_rows(tgt_scale, asked_rows, dev_count, slot_cap),
                "dev",
                split_axis=0,
                concat_axis=0,
                tiled=True,
            )
            near_scale = near_scale.reshape(dev_count * slot_cap, target_mass.shape[1])
        pair_scale = assemble(near_scale, far_scale, slot_index, sb_dev, near_count)
        row_sums = jnp.einsum("ikbj,ikj->ib", kernel, pair_scale, precision=lax.Precision.HIGHEST)
        src_scale = source_mass / (dustbin + row_sums)
        col_parts = jnp.einsum("ikbj,ib->ikj", kernel, src_scale, precision=lax.Precision.HIGHEST)
        departing_messages = jnp.zeros((dev_count * slot_cap, col_parts.shape[2]), jnp.float32)
        departing_messages = departing_messages.at[slot_index].set(
            col_parts[:, :near_count].reshape(count_of_pairs, col_parts.shape[2])
        )
        arrived = lax.all_to_all(
            departing_messages.reshape(dev_count, slot_cap, col_parts.shape[2]),
            "dev",
            split_axis=0,
            concat_axis=0,
            tiled=True,
        )
        arrived = arrived.reshape(dev_count * slot_cap, col_parts.shape[2])
        col_sums = jnp.einsum("sn,sb->nb", owner_hot, arrived, precision=lax.Precision.HIGHEST)
        twin_parts = jnp.einsum(
            "sn,sb->nb", twin_hot, col_parts[:, near_count], precision=lax.Precision.HIGHEST
        )
        col_sums = col_sums + from_behind(twin_parts, "group", 1)
        tgt_scale = target_mass / (dustbin + col_sums)
    return (src_scale, tgt_scale)


def solution(mesh):
    placed = (
        P(("group", "dev"), None, None),
        P(("group", "dev"), None, None),
        P(("group", "dev"), None),
        P(("group", "dev"), None),
        P(("group", "dev"), None),
        P(("group", "dev"), None),
    )
    return jax.shard_map(
        local,
        mesh=mesh,
        in_specs=placed,
        out_specs=(P(("group", "dev"), None), P(("group", "dev"), None)),
        check_vma=False,
    )
```

profile of v0, /device:TPU:0, one launch (start us, length us, event | category | flops | bytes accessed | tf_op | source)
XLA Modules:
  0.0 214.0 jit_solution(4052466473595310931)
XLA Ops:
  0.6 0.8 reshape.202
  1.4 0.7 broadcast_multiply_fusion.1
  2.1 0.1 fusion.21
  2.2 0.1 reduce_window_sum.11
  2.2 0.2 select_reduce_fusion
  2.4 0.1 mul.58
  2.5 0.8 reshape.277
  3.3 0.7 scatter_custom_fusion
  4.0 0.7 all_to_all.18
  4.7 7.4 %all-to-all-start = ((s32[16,1,5]{2,1,0:T(1,128)}), s32[16,1,5]{2,1,0:T(1,128)S(1)}, u32[]{:S(2)}, u32[]{:S(2)}) async-start(s32[16,1,5]{2,1,0:T(1,128)} %bitcast.2), calls=%async_computation | async-start | bytes 16384 | tf_op jit(solution)/shard_map/all_to_all | solution.py:67
  12.1 2.2 %multiply_reduce_fusion = f32[32,128]{1,0:T(8,128)S(1)} fusion(f32[32,128,128]{2,1,0:T(8,128)} %param.9), kind=kLoop, calls=%fused_computation.24 | loop fusion | flops 1044480 | bytes 2113536 | tf_op jit(solution)/shard_map/reduce_sum | solution.py:22
  14.3 2.2 %broadcast_multiply_fusion = f32[32,128,128]{2,1,0:T(8,128)S(1)} fusion(f32[32,128,128]{2,1,0:T(8,128)} %param.9, f32[32,128]{1,0:T(8,128)S(1)} %add_rsqrt_fusion), kind=kLoop, calls=%fused_computation.32 | loop fusion | flops 524288 | bytes 4210688 | tf_op jit(solution)/shard_map/mul | solution.py:22
  16.5 1.9 all-to-all-done
  18.4 0.5 broadcast.228
  18.9 0.7 reduce.11
  19.6 0.1 reshape.205
  19.7 0.1 copy.17
  19.8 0.1 copy.18
  19.9 3.2 %gather_fusion = f32[80,128,128]{2,1,0:T(8,128)} fusion(f32[32,128,128]{2,1,0:T(8,128)S(1)} %broadcast_multiply_fusion, s32[1024]{0:T(1024)S(1)} %pad_clamp_fusion.3), kind=kCustom, calls=%fused_computation.2 | custom fusion | bytes 10486080 | tf_op jit(solution)/shard_map/jit(_take)/gather | solution.py:26
  23.1 5.2 %broadcast_select_fusion = f32[16,5,128,128]{3,2,1,0:T(8,128)} fusion(f32[16,5,128,128]{3,2,1,0:T(8,128)} %bitcast.71, pred[16,5]{1,0:T(8,128)(4,1)S(1)} %copy.18), kind=kLoop, calls=%fused_computation.23 | loop fusion | flops 1310720 | bytes 10485840 | tf_op jit(solution)/shard_map/jit(_take)/select_n | solution.py:26
  28.4 4.9 %all-to-all-start.1 = ((f32[16,5,128,128]{3,2,1,0:T(8,128)}), f32[16,5,128,128]{3,2,1,0:T(8,128)}, u32[]{:S(2)}, u32[]{:S(2)}) async-start(f32[16,5,128,128]{3,2,1,0:T(8,128)} %broadcast_select_fusion), calls=%async_computation.1 | async-start | bytes 10485760 | tf_op jit(solution)/shard_map/all_to_all | solution.py:83
  33.3 1.6 collective-permute-start
  34.9 0.1 reduce_sum.32
  35.0 0.6 gather_fusion.5
  35.6 0.1 broadcast_select_fusion.4
  35.7 0.2 slice_reduce_fusion
  35.9 0.2 and_reduce_fusion
  36.1 0.2 multiply_reduce_fusion.1
  36.3 44.7 %collective-permute-done = f32[32,128,128]{2,1,0:T(8,128)} collective-permute-done((f32[32,128,128]{2,1,0:T(8,128)S(1)}, f32[32,128,128]{2,1,0:T(8,128)}, u32[]{:S(2)}, u32[]{:S(2)}) %collective-permute-start) | collective-permute-done | bytes 2097184 | tf_op jit(solution)/shard_map/ppermute | solution.py:18
  81.0 2.2 %gather_fusion.2 = f32[8,128,128]{2,1,0:T(8,128)S(1)} fusion(f32[32,128,128]{2,1,0:T(8,128)} %collective-permute-done, s32[1024]{0:T(1024)S(1)} %pad_clamp_fusion.1), kind=kCustom, calls=%fused_computation.4 | custom fusion | bytes 1048608 | tf_op jit(solution)/shard_map/jit(_take)/gather | solution.py:78
  83.2 0.1 bitcast_select_fusion
  83.3 45.6 %all-to-all-done.1 = f32[16,5,128,128]{3,2,1,0:T(8,128)} async-done(((f32[16,5,128,128]{3,2,1,0:T(8,128)}), f32[16,5,128,128]{3,2,1,0:T(8,128)}, u32[]{:S(2)}, u32[]{:S(2)}) %all-to-all-start.1) | async-done | bytes 5242912 | tf_op jit(solution)/shard_map/all_to_all | solution.py:83
  128.9 5.1 %gather_fusion.1 = f32[56,128,128]{2,1,0:T(8,128)} fusion(f32[80,128,128]{2,1,0:T(8,128)} %bitcast.6, s32[1024]{0:T(1024)S(1)} %pad_clamp_fusion.2), kind=kCustom, calls=%fused_computation.3 | custom fusion | bytes 7340256 | tf_op jit(solution)/shard_map/jit(_take)/gather | solution.py:31
  134.1 2.3 %broadcast_select_fusion.1 = f32[8,7,128,128]{3,2,1,0:T(8,128)S(1)} fusion(f32[8,7,128,128]{3,2,1,0:T(8,128)} %bitcast.72, pred[8,7]{1,0:T(8,128)(4,1)S(1)} %compare_and_fusion.1), kind=kLoop, calls=%fused_computation.25 | loop fusion | flops 917504 | bytes 7340088 | tf_op jit(solution)/shard_map/jit(_take)/select_n | solution.py:31
  136.4 4.7 %exponential_multiply_fusion = f32[8,8,128,128]{3,2,1,0:T(8,128)S(1)} fusion(f32[8,1,128,128]{3,2,1,0:T(8,128)S(1)} %bitcast_select_fusion, f32[8,7,128,128]{3,2,1,0:T(8,128)S(1)} %broadcast_select_fusion.1, f32[8,128,128]{2,1,0:T(8,128)S(1)} %copy-done.2, f32[8,128]{1,0:T(8,128)S(1)} %add_rsqrt_fusion.1), kind=kOutput, calls=%fused_computation.22 | convolution fusion | flops 1613889536 | bytes 8916992 | tf_op jit(solution)/shard_map/ibd,ikjd->ikbj/dot_general | solution.py:38
  141.1 0.0 copy-start.7
  141.1 2.3 %fusion.10 = f32[8,1,128,1]{2,1,3,0:T(1,128)S(1)} fusion(f32[8,8,128,1]{2,3,1,0:T(1,128)S(1)} %bitcast.77, f32[8,8,128,128]{3,2,1,0:T(8,128)S(1)} %exponential_multiply_fusion), kind=kOutput, calls=%fused_computation.20 | convolution fusion | flops 12582912 | bytes 4231168 | tf_op jit(solution)/shard_map/ikbj,ikj->ib/dot_general | solution.py:112
  143.5 3.6 %fusion.8 = f32[8,1,8,128]{3,1,2,0:T(1,128)S(1)} fusion(f32[8,128,1,1]{1,2,3,0:T(1,128)S(1)} %bitcast.83, f32[8,8,128,128]{3,2,1,0:T(8,128)S(1)} %exponential_multiply_fusion), kind=kOutput, calls=%fused_computation.18 | convolution fusion | flops 12582912 | bytes 4231168 | tf_op jit(solution)/shard_map/ikbj,ib->ikj/dot_general | solution.py:114
  147.1 0.7 scatter_custom_fusion.1
  147.8 0.6 reshape.210
  148.5 23.8 %all-to-all-start.2 = ((f32[16,5,128]{2,1,0:T(8,128)}), f32[16,5,128]{2,1,0:T(8,128)S(1)}, u32[]{:S(2)}, u32[]{:S(2)}) async-start(f32[16,5,128]{2,1,0:T(8,128)} %reshape.210), calls=%async_computation.2 | async-start | bytes 131072 | tf_op jit(solution)/shard_map/all_to_all | solution.py:119
  172.3 0.3 fusion.29
  172.6 1.6 collective-permute-start.1
  174.2 0.1 reshape.207
  174.2 5.0 %all-to-all-done.2 = f32[16,5,128]{2,1,0:T(8,128)S(1)} async-done(((f32[16,5,128]{2,1,0:T(8,128)}), f32[16,5,128]{2,1,0:T(8,128)S(1)}, u32[]{:S(2)}, u32[]{:S(2)}) %all-to-all-start.2) | async-done | bytes 40992 | tf_op jit(solution)/shard_map/all_to_all | solution.py:119
  179.2 0.3 fusion.17
  179.5 1.6 collective-permute-start.2
  181.1 0.6 gather_fusion.3
  181.7 0.7 broadcast_select_fusion.2
  182.4 3.7 %all-to-all-start.3 = ((f32[16,5,128]{2,1,0:T(8,128)}), f32[16,5,128]{2,1,0:T(8,128)S(1)}, u32[]{:S(2)}, u32[]{:S(2)}) async-start(f32[16,5,128]{2,1,0:T(8,128)} %broadcast_select_fusion.2), calls=%async_computation.3 | async-start | bytes 131072 | tf_op jit(solution)/shard_map/all_to_all | solution.py:103
  186.2 0.6 gather_fusion.4
  186.7 0.1 bitcast_select_fusion.1
  186.8 6.0 %all-to-all-done.3 = f32[16,5,128]{2,1,0:T(8,128)S(1)} async-done(((f32[16,5,128]{2,1,0:T(8,128)}), f32[16,5,128]{2,1,0:T(8,128)S(1)}, u32[]{:S(2)}, u32[]{:S(2)}) %all-to-all-start.3) | async-done | bytes 40992 | tf_op jit(solution)/shard_map/all_to_all | solution.py:103
  192.8 0.6 gather_fusion.6
  193.4 0.1 broadcast_select_fusion.3
  193.5 4.2 %fusion.6 = f32[8,1,128,1]{2,1,3,0:T(1,128)S(1)} fusion(f32[8,8,128,1]{2,3,1,0:T(1,128)S(1)} %bitcast.78, f32[8,8,128,128]{3,2,1,0:T(8,128)} %copy-done), kind=kOutput, calls=%fused_computation.16 | convolution fusion | flops 12582912 | bytes 4231168 | tf_op jit(solution)/shard_map/ikbj,ikj->ib/dot_general | solution.py:112
  197.8 3.6 %fusion.4 = f32[8,1,8,128]{3,1,2,0:T(1,128)S(1)} fusion(f32[8,128,1,1]{1,2,3,0:T(1,128)S(1)} %bitcast.81, f32[8,8,128,128]{3,2,1,0:T(8,128)S(1)} %copy-done.1), kind=kOutput, calls=%fused_computation.14 | convolution fusion | flops 12582912 | bytes 4231168 | tf_op jit(solution)/shard_map/ikbj,ib->ikj/dot_general | solution.py:114
  201.4 0.7 scatter_custom_fusion.2
  202.1 0.6 reshape.215
  202.8 3.5 %all-to-all-start.4 = ((f32[16,5,128]{2,1,0:T(8,128)}), f32[16,5,128]{2,1,0:T(8,128)S(1)}, u32[]{:S(2)}, u32[]{:S(2)}) async-start(f32[16,5,128]{2,1,0:T(8,128)} %reshape.215), calls=%async_computation.4 | async-start | bytes 131072 | tf_op jit(solution)/shard_map/all_to_all | solution.py:119
  206.3 0.3 fusion.28
  206.5 0.6 collective-permute-start.3
  207.1 6.0 %all-to-all-done.4 = f32[16,5,128]{2,1,0:T(8,128)S(1)} async-done(((f32[16,5,128]{2,1,0:T(8,128)}), f32[16,5,128]{2,1,0:T(8,128)S(1)}, u32[]{:S(2)}, u32[]{:S(2)}) %all-to-all-start.4) | async-done | bytes 40992 | tf_op jit(solution)/shard_map/all_to_all | solution.py:119
  213.1 0.9 fusion.15
  (44 shorter events, 0.2 us)
Async XLA Ops:
  4.7 13.7 %all-to-all-start = ((s32[16,1,5]{2,1,0:T(1,128)}), s32[16,1,5]{2,1,0:T(1,128)S(1)}, u32[]{:S(2)}, u32[]{:S(2)}) async-start(s32[16,1,5]{2,1,0:T(1,128)} %bitcast.2), calls=%async_computation | async-start | bytes 16384 | tf_op jit(solution)/shard_map/all_to_all | solution.py:67
  28.4 7.3 %copy-start.4 = (s32[8,8]{1,0:T(8,128)S(1)}, s32[8,8]{1,0:T(8,128)}, u32[]{:S(2)}) copy-start(s32[8,8]{1,0:T(8,128)} %param.13) | copy-start | bytes 772
  28.4 7.7 %copy-start.2 = (f32[8,128,128]{2,1,0:T(8,128)S(1)}, f32[8,128,128]{2,1,0:T(8,128)}, u32[]{:S(2)}) copy-start(f32[8,128,128]{2,1,0:T(8,128)} %param.8) | copy-start | bytes 1572868
  28.4 7.9 %copy-start.5 = (s32[8,7]{1,0:T(8,128)S(1)}, s32[8,7]{1,0:T(8,128)}, u32[]{:S(2)}) copy-start(s32[8,7]{1,0:T(8,128)} %param.12) | copy-start | bytes 676
  28.4 100.6 %all-to-all-start.1 = ((f32[16,5,128,128]{3,2,1,0:T(8,128)}), f32[16,5,128,128]{3,2,1,0:T(8,128)}, u32[]{:S(2)}, u32[]{:S(2)}) async-start(f32[16,5,128,128]{3,2,1,0:T(8,128)} %broadcast_select_fusion), calls=%async_computation.1 | async-start | bytes 10485760 | tf_op jit(solution)/shard_map/all_to_all | solution.py:83
  33.3 47.8 %collective-permute-start = (f32[32,128,128]{2,1,0:T(8,128)S(1)}, f32[32,128,128]{2,1,0:T(8,128)}, u32[]{:S(2)}, u32[]{:S(2)}) collective-permute-start(f32[32,128,128]{2,1,0:T(8,128)S(1)} %broadcast_multiply_fusion), channel_id=1, source_target_pairs={{0,16},{16,0},{1,17},{17,1},{2,18},{18,2},{3,19},{19,3},{4,20},{20... | collective-permute-start | bytes 6291464 | tf_op jit(solution)/shard_map/ppermute | solution.py:18
  141.1 6.0 %copy-start = (f32[8,8,128,128]{3,2,1,0:T(8,128)}, f32[8,8,128,128]{3,2,1,0:T(8,128)S(1)}, u32[]{:S(2)}) copy-start(f32[8,8,128,128]{3,2,1,0:T(8,128)S(1)} %exponential_multiply_fusion) | copy-start | bytes 12582916
  141.1 2.3 %copy-start.7 = (f32[8,128]{1,0:T(8,128)S(1)}, f32[8,128]{1,0:T(8,128)}, u32[]{:S(2)}) copy-start(f32[8,128]{1,0:T(8,128)} %param.10) | copy-start | bytes 12292
  141.1 38.1 %copy-start.3 = (f32[32,128]{1,0:T(8,128)S(1)}, f32[32,128]{1,0:T(8,128)}, u32[]{:S(2)}) copy-start(f32[32,128]{1,0:T(8,128)} %param.11) | copy-start | bytes 49156
  148.5 30.7 %all-to-all-start.2 = ((f32[16,5,128]{2,1,0:T(8,128)}), f32[16,5,128]{2,1,0:T(8,128)S(1)}, u32[]{:S(2)}, u32[]{:S(2)}) async-start(f32[16,5,128]{2,1,0:T(8,128)} %reshape.210), calls=%async_computation.2 | async-start | bytes 131072 | tf_op jit(solution)/shard_map/all_to_all | solution.py:119
  172.6 6.6 %collective-permute-start.1 = (f32[32,128]{1,0:T(8,128)S(1)}, f32[32,128]{1,0:T(8,128)S(1)}, u32[]{:S(2)}, u32[]{:S(2)}) collective-permute-start(f32[32,128]{1,0:T(8,128)S(1)} %fusion.29), channel_id=1, source_target_pairs={{0,16},{16,0},{1,17},{17,1},{2,18},{18,2},{3,19},{19,3},{4,20},{20... | collective-permute-start | bytes 49160 | tf_op jit(solution)/shard_map/ppermute | solution.py:18
  179.5 6.7 %collective-permute-start.2 = (f32[32,128]{1,0:T(8,128)S(1)}, f32[32,128]{1,0:T(8,128)S(1)}, u32[]{:S(2)}, u32[]{:S(2)}) collective-permute-start(f32[32,128]{1,0:T(8,128)S(1)} %fusion.17), channel_id=1, source_target_pairs={{0,16},{16,0},{1,17},{17,1},{2,18},{18,2},{3,19},{19,3},{4,20},{20... | collective-permute-start | bytes 49160 | tf_op jit(solution)/shard_map/ppermute | solution.py:18
  182.4 10.4 %all-to-all-start.3 = ((f32[16,5,128]{2,1,0:T(8,128)}), f32[16,5,128]{2,1,0:T(8,128)S(1)}, u32[]{:S(2)}, u32[]{:S(2)}) async-start(f32[16,5,128]{2,1,0:T(8,128)} %broadcast_select_fusion.2), calls=%async_computation.3 | async-start | bytes 131072 | tf_op jit(solution)/shard_map/all_to_all | solution.py:103
  193.5 4.3 %copy-start.1 = (f32[8,8,128,128]{3,2,1,0:T(8,128)S(1)}, f32[8,8,128,128]{3,2,1,0:T(8,128)}, u32[]{:S(2)}) copy-start(f32[8,8,128,128]{3,2,1,0:T(8,128)} %copy-done) | copy-start | bytes 12582916
  197.8 16.3 %copy-start.6 = (f32[8,128]{1,0:T(8,128)}, f32[8,128]{1,0:T(8,128)S(1)}, u32[]{:S(2)}) copy-start(f32[8,128]{1,0:T(8,128)S(1)} %add_divide_fusion) | copy-start | bytes 12292
  202.8 10.4 %all-to-all-start.4 = ((f32[16,5,128]{2,1,0:T(8,128)}), f32[16,5,128]{2,1,0:T(8,128)S(1)}, u32[]{:S(2)}, u32[]{:S(2)}) async-start(f32[16,5,128]{2,1,0:T(8,128)} %reshape.215), calls=%async_computation.4 | async-start | bytes 131072 | tf_op jit(solution)/shard_map/all_to_all | solution.py:119
  206.5 6.6 %collective-permute-start.3 = (f32[32,128]{1,0:T(8,128)S(1)}, f32[32,128]{1,0:T(8,128)S(1)}, u32[]{:S(2)}, u32[]{:S(2)}) collective-permute-start(f32[32,128]{1,0:T(8,128)S(1)} %fusion.28), channel_id=1, source_target_pairs={{0,16},{16,0},{1,17},{17,1},{2,18},{18,2},{3,19},{19,3},{4,20},{20... | collective-permute-start | bytes 49160 | tf_op jit(solution)/shard_map/ppermute | solution.py:18
where the time goes:
time: 215 us; the launch traced here: 214 us
  waiting for transfers between devices  109 us (51%)
  starting transfers between devices  48.6 us (23%)
  matrix products  20.1 us (9%)
  local copies, waits for them, and re-layouts  19.7 us (9%)
  other arithmetic  15.4 us (7%)
    all_to_all x1, waiting for transfers between devices, local(): lax.all_to_all(selected_rows(tgt_unit, asked_rows, dev_count, slot_cap),...  45.6 us
    ppermute x4, waiting for transfers between devices, from_behind(): return lax.ppermute(x, axis, [(i, (i + by) % count) for i in range(count)])  44.7 us
    all_to_all x2, starting transfers between devices, local(): lax.all_to_all(departing_messages.reshape(dev_count, slot_cap, col_parts....  27.3 us
    all_to_all x2, waiting for transfers between devices, local(): lax.all_to_all(departing_messages.reshape(dev_count, slot_cap, col_parts....  11 us
    all_to_all x1, starting transfers between devices, local(): lax.all_to_all(wanted.reshape(dev_count, slot_cap), 'dev', split_axis=0,...  7.36 us
    dot_general x2, matrix products, local(): jnp.einsum('ikbj,ib->ikj', kernel, src_scale, precision=lax.Precision.HIG...  7.21 us
    dot_general x2, matrix products, local(): jnp.einsum('ikbj,ikj->ib', kernel, pair_scale, precision=lax.Precision.HI...  6.53 us
    gather x3, local copies, waits for them, and re-layouts, assemble(): jnp.take(nearby_flattened, slot_index, axis=0)  6.31 us
  transfers between devices with their start and end apart: 9, of which 6 were waited for; matrix products, arithmetic and copies ran while one was open for 5% of the time, Pallas kernels for 0%

commit v1 on v0

v1 whole, which is shorter than its diff:
```python
import functools

import jax
import jax.numpy as jnp
from jax import lax
from jax.experimental import pallas as pl
from jax.experimental.pallas import tpu as pltpu
from jax.sharding import PartitionSpec as P

ITERS = 2

entropic_regularizer = 0.1
dustbin = 0.5
epsilon = 1e-06

VMEM = pl.BlockSpec(memory_space=pltpu.VMEM)
SMEM = pl.BlockSpec(memory_space=pltpu.SMEM)
NT = (((1,), (1,)), ((), ()))
NN = (((1,), (0,)), ((), ()))


def split2(x):
    high = x.astype(jnp.bfloat16)
    low = (x - high.astype(jnp.float32)).astype(jnp.bfloat16)
    return high, low


def unit(x):
    return x * lax.rsqrt(jnp.mean(x * x, axis=-1, keepdims=True) + epsilon)


def stacked_parts(row):
    x = jnp.broadcast_to(row, (8, row.shape[1]))
    high = x.astype(jnp.bfloat16).astype(jnp.float32)
    rest = x - high
    low = rest.astype(jnp.bfloat16).astype(jnp.float32)
    place = lax.broadcasted_iota(jnp.int32, x.shape, 0)
    parts = jnp.where(place == 0, high, jnp.where(place == 1, low, jnp.where(place == 2, rest - low, 0.0)))
    return parts.astype(jnp.bfloat16)


def column_product(parts, tile):
    both = lax.dot_general(parts, tile, NN, preferred_element_type=jnp.float32)
    width = tile.shape[1] // 2
    return both[:, :width] + both[:, width:]


def row_product(parts, tile):
    return lax.dot_general(
        jnp.concatenate([parts, parts], axis=1), tile, NT, preferred_element_type=jnp.float32
    )


def target_kernel(emb_ref, out_ref):
    def one(block, carry):
        high, low = split2(unit(emb_ref[block]).T)
        out_ref[block] = jnp.concatenate([high, low], axis=1)
        return carry

    lax.fori_loop(0, emb_ref.shape[0], one, 0, unroll=2)


def target_operand(emb):
    blocks, rows, width = emb.shape
    return pl.pallas_call(
        target_kernel,
        out_shape=jax.ShapeDtypeStruct((blocks, width, 2 * rows), jnp.bfloat16),
        in_specs=[VMEM],
        out_specs=VMEM,
        cost_estimate=pl.CostEstimate(flops=0, bytes_accessed=3 * emb.size * 4, transcendentals=0),
        compiler_params=pltpu.CompilerParams(vmem_limit_bytes=32 << 20),
        name="target_operand",
    )(emb)


def tile_kernel(chunks, sides, slots, sb, half, *refs):
    loc, tgt = refs[:2]
    source = refs[2 : 2 + 2 * chunks]
    weight = refs[2 + 2 * chunks : 2 + 2 * chunks + sides]
    tiles, sums, partial = refs[2 + 2 * chunks + sides :]
    width = source[0].shape[1]
    scale = 1.0 / (width * entropic_regularizer)
    partial[...] = jnp.zeros_like(partial)
    place = lax.broadcasted_iota(jnp.int32, (8, 2 * width), 0)
    ones = jnp.where(place == 0, 1.0, 0.0).astype(jnp.bfloat16)
    for chunk in range(chunks):
        upper, lower = source[2 * chunk], source[2 * chunk + 1]
        for side in range(sides):
            for j in range(slots):
                at = (chunk * sides + side) * slots + j
                block = loc[at]
                start = pl.multiple_of(lax.rem(block, sb) * half, half)
                left = jnp.concatenate([upper[pl.ds(start, half)], lower[pl.ds(start, half)]], axis=0)
                high, low = split2(unit(left))
                right = weight[side][tgt[at]]
                both = lax.dot_general(
                    jnp.concatenate([high, low], axis=1),
                    jnp.concatenate([right, right], axis=0),
                    NN,
                    preferred_element_type=jnp.float32,
                )
                nodes = both.shape[1] // 2
                affinity = both[:, :nodes] + both[:, nodes:]
                tile = jnp.exp(affinity * scale) * (1.0 / (8.0 * nodes))
                tile = jnp.concatenate(split2(tile), axis=1)
                tiles[at] = tile
                spot = chunk * (sb + 1) + block
                partial[spot] += lax.dot_general(ones, tile, NT, preferred_element_type=jnp.float32)
        for block in range(sb):
            sums[chunk, block : block + 1] = partial[chunk * (sb + 1) + block][0:1]


def build_tiles(source, weight, loc, tgt, slots, sb):
    chunks, sides = len(source) // 2, len(weight)
    half, width = source[0].shape[0] // sb - 1, source[0].shape[1]
    nodes = weight[0].shape[2] // 2
    count = chunks * sides * slots
    return pl.pallas_call(
        functools.partial(tile_kernel, chunks, sides, slots, sb, half),
        out_shape=(
            jax.ShapeDtypeStruct((count, 2 * half, 2 * nodes), jnp.bfloat16),
            jax.ShapeDtypeStruct((chunks, sb, 2 * half), jnp.float32),
        ),
        in_specs=[SMEM, SMEM] + [VMEM] * (len(source) + sides),
        out_specs=(VMEM, VMEM),
        scratch_shapes=[pltpu.VMEM((chunks * (sb + 1), 8, 2 * half), jnp.float32)],
        cost_estimate=pl.CostEstimate(
            flops=count * 2 * half * nodes * width * 8,
            bytes_accessed=count * 2 * half * nodes * 4 + sides * weight[0].size * 2,
            transcendentals=count * 2 * half * nodes,
        ),
        compiler_params=pltpu.CompilerParams(vmem_limit_bytes=40 << 20),
        name="build_tiles",
    )(loc, tgt, *source, *weight)


def column_kernel(near, far, rows_at, sums_at, far_at, rows, mass, far_rows, far_mass, *refs):
    tiles, out, scale, total = refs[: len(near) + 1], refs[-3], refs[-2], refs[-1]
    count = rows.shape[0]
    scale[...] = jnp.zeros_like(scale)
    scale[0:count] = mass[...] / (dustbin + rows[...])
    scale[count + 8 : count + 8 + far] = far_mass[...] / (dustbin + far_rows[...])
    total[...] = jnp.zeros_like(total)
    base = 0
    for part, slots in enumerate(near):

        def one(slot, carry, part=part, base=base):
            at = base + slot
            parts = stacked_parts(scale[pl.ds(rows_at[at], 1), :])
            total[sums_at[at]] += column_product(parts, tiles[part][slot])
            return carry

        lax.fori_loop(0, slots, one, 0, unroll=True)
        base += slots
    for slot in range(far):
        parts = stacked_parts(scale[count + 8 + slot : count + 9 + slot, :])
        total[far_at[slot]] += column_product(parts, tiles[len(near)][slot])
    for block in range(out.shape[0]):
        out[block : block + 1] = jnp.sum(total[block], axis=0, keepdims=True)


def column_sums(tables, rows, mass, far_rows, far_mass, tiles, targets):
    near = tuple(t.shape[0] for t in tiles[:-1])
    far, nodes = tiles[-1].shape[0], tiles[-1].shape[2] // 2
    width = rows.shape[1]
    return pl.pallas_call(
        functools.partial(column_kernel, near, far),
        out_shape=jax.ShapeDtypeStruct((targets, nodes), jnp.float32),
        in_specs=[SMEM] * 3 + [VMEM] * (4 + len(tiles)),
        out_specs=VMEM,
        scratch_shapes=[
            pltpu.VMEM((rows.shape[0] + 8 + (far + 7) // 8 * 8, width), jnp.float32),
            pltpu.VMEM((targets + 1, 8, nodes), jnp.float32),
        ],
        cost_estimate=pl.CostEstimate(
            flops=sum(t.size for t in tiles) * 16, bytes_accessed=sum(t.size for t in tiles) * 2, transcendentals=0
        ),
        compiler_params=pltpu.CompilerParams(vmem_limit_bytes=40 << 20),
        name="column_sums",
    )(*tables, rows, mass, far_rows, far_mass, *tiles)


def row_kernel(near, far, rows_at, sums_at, far_at, mine, theirs, mass, other_mass, *refs):
    tiles, out, far_out, scale, total = refs[: len(near) + 1], refs[-4], refs[-3], refs[-2], refs[-1]
    blocks = mass.shape[0]
    scale[...] = jnp.zeros_like(scale)
    scale[0:blocks] = mass[...] / (dustbin + mine[0:blocks] + theirs[blocks : 2 * blocks])
    scale[blocks : 2 * blocks] = other_mass[...] / (dustbin + mine[blocks : 2 * blocks] + theirs[0:blocks])
    total[...] = jnp.zeros_like(total)
    base = 0
    for part, slots in enumerate(near):

        def one(slot, carry, part=part, base=base):
            at = base + slot
            parts = stacked_parts(scale[pl.ds(sums_at[at], 1), :])
            total[rows_at[at]] += row_product(parts, tiles[part][slot])
            return carry

        lax.fori_loop(0, slots, one, 0, unroll=True)
        base += slots
    for slot in range(far):
        parts = stacked_parts(scale[pl.ds(far_at[slot], 1), :])
        far_out[slot : slot + 1] = jnp.sum(row_product(parts, tiles[len(near)][slot]), axis=0, keepdims=True)
    for block in range(out.shape[0]):
        out[block : block + 1] = jnp.sum(total[block], axis=0, keepdims=True)


def row_sums(tables, mine, theirs, mass, other_mass, tiles, sources):
    near = tuple(t.shape[0] for t in tiles[:-1])
    far, nodes = tiles[-1].shape[0], tiles[-1].shape[2] // 2
    width = tiles[-1].shape[1]
    return pl.pallas_call(
        functools.partial(row_kernel, near, far),
        out_shape=(
            jax.ShapeDtypeStruct((sources, width), jnp.float32),
            jax.ShapeDtypeStruct((far, width), jnp.float32),
        ),
        in_specs=[SMEM] * 3 + [VMEM] * (4 + len(tiles)),
        out_specs=(VMEM, VMEM),
        scratch_shapes=[
            pltpu.VMEM((mine.shape[0] + 8, nodes), jnp.float32),
            pltpu.VMEM((sources + 1, 8, width), jnp.float32),
        ],
        cost_estimate=pl.CostEstimate(
            flops=sum(t.size for t in tiles) * 16, bytes_accessed=sum(t.size for t in tiles) * 2, transcendentals=0
        ),
        compiler_params=pltpu.CompilerParams(vmem_limit_bytes=40 << 20),
        name="row_sums",
    )(*tables, mine, theirs, mass, other_mass, *tiles)


def local(source_emb, target_emb, source_mass, target_mass, cand_device, cand_block):
    dev_count = lax.axis_size("dev")
    group_count = lax.axis_size("group")
    chips = dev_count // 2
    sb, rows, width = source_emb.shape
    tb = target_emb.shape[0]
    near_count = cand_device.shape[1]
    slot_cap = (near_count * sb + dev_count - 1) // dev_count + 1
    half = rows // 2

    ring = list(range(0, chips, 2)) + list(range(chips - 1, 0, -2))
    spot_of = [ring.index(chip) for chip in range(chips)]
    steps = chips // 2

    def around(x, by):
        pairs = [
            (2 * ring[i] + core, 2 * ring[(i + by) % chips] + core) for i in range(chips) for core in range(2)
        ]
        return lax.ppermute(x, "dev", pairs)

    def across(x, bit):
        return lax.ppermute(x, "dev", [(i, i ^ bit) for i in range(dev_count)])

    def along_group(x, by):
        return lax.ppermute(x, "group", [(i, (i + by) % group_count) for i in range(group_count)])

    device = lax.axis_index("dev")
    chip = device // 2
    spot = jnp.asarray(spot_of, jnp.int32)[chip]

    def chip_at(offset):
        return jnp.asarray(ring, jnp.int32)[(spot + offset + chips) % chips]

    candidates = jnp.concatenate([cand_device, cand_block], axis=1).astype(jnp.float32)
    candidates = jnp.pad(candidates, ((0, 0), (0, width - candidates.shape[1])))
    upper = jnp.concatenate([source_emb[:, :half].reshape(sb * half, width), candidates], axis=0)
    lower = jnp.concatenate([source_emb[:, half:].reshape(sb * half, width), source_mass], axis=0)

    sibling_emb = across(target_emb, 1)
    sibling_mass = across(target_mass, 1)

    own_weight = target_operand(target_emb)
    sibling_weight = target_operand(sibling_emb)
    weights = (own_weight, sibling_weight)

    sides = jnp.stack([device, device ^ 1])

    def tables_of(upper_chunk, chip_index):
        meta = upper_chunk[sb * half :].astype(jnp.int32)
        named, block = meta[:, :near_count], meta[:, near_count : 2 * near_count]
        hit = (named[None] == sides[:, None, None]).astype(jnp.int32)
        valid = jnp.sum(hit, axis=2)
        picked = jnp.sum(hit * block[None], axis=2)
        order = jnp.arange(sb, dtype=jnp.int32)
        rank = jnp.sum(valid[:, None, :] * (order[None, :] < order[:, None])[None].astype(jnp.int32), axis=2)
        chosen = valid[:, None, :] * (
            rank[:, None, :] == jnp.arange(slot_cap, dtype=jnp.int32)[None, :, None]
        ).astype(jnp.int32)
        filled = jnp.sum(chosen, axis=2)
        loc = jnp.sum(chosen * order[None, None, :], axis=2)
        tgt = jnp.sum(chosen * picked[:, None, :], axis=2)
        rows_at = jnp.where(filled > 0, chip_index * sb + loc, chips * sb)
        sums_at = jnp.where(filled > 0, tgt + tb * jnp.arange(2, dtype=jnp.int32)[:, None], 2 * tb)
        loc = jnp.where(filled > 0, loc, sb)
        return [x.reshape(-1) for x in (loc, tgt, rows_at, sums_at)]

    tiles, sums, where, masses = [], {}, [], {}

    def add(chunks):
        made = [tables_of(up, chip_at(offset)) for up, _, offset in chunks]
        joined = [jnp.concatenate([t[k] for t in made]) for k in range(4)]
        source = [x for up, low, _ in chunks for x in (up, low)]
        tile, partial = build_tiles(source, weights, joined[0], joined[1], slot_cap, sb)
        tiles.append(tile)
        where.append(joined[2:])
        for k, (_, low, offset) in enumerate(chunks):
            sums[offset % chips] = partial[k]
            masses[offset % chips] = low[sb * half :]

    up_a, up_b, down_a, down_b = upper, lower, upper, lower
    add([(upper, lower, 0)])
    far_upper = along_group(upper, 1)
    far_lower = along_group(lower, 1)
    far_at = far_upper[sb * half :, 2 * near_count].astype(jnp.int32)
    far_tiles, far_sums = build_tiles(
        (far_upper, far_lower), (own_weight,), jnp.arange(sb, dtype=jnp.int32), far_at, sb, sb
    )
    far_mass = far_lower[sb * half :]
    from_far = along_group(far_sums[0], -1)
    for step in range(1, steps + 1):
        up_a, down_b = around(up_a, 1), around(down_b, -1)
        if step < steps:
            up_b, down_a = around(up_b, 1), around(down_a, -1)
            add([(up_a, up_b, -step), (down_a, down_b, step)])
        else:
            add([(up_a, down_b, step)])
    tables = (
        jnp.concatenate([w[0] for w in where]),
        jnp.concatenate([w[1] for w in where]),
        far_at,
    )
    tiles.append(far_tiles)

    turn = jnp.asarray(spot_of, jnp.int32) - spot
    turn = jnp.where(turn < 0, turn + chips, turn)

    def by_chip(parts):
        return jnp.take(jnp.stack([parts[k] for k in range(chips)]), turn, axis=0).reshape(chips * sb, rows)

    all_mass = by_chip(masses)

    def over_chips(x):
        bit = 2
        while bit < dev_count:
            x = x + across(x, bit)
            bit *= 2
        return x

    sums[0] = sums[0] + from_far
    near_rows = by_chip(sums)
    for sweep in range(ITERS):
        if sweep > 0:
            near_rows, far_rows = row_sums(
                tables, mine, theirs, target_mass, sibling_mass, tiles, chips * sb
            )
            back = along_group(far_rows, -1)
            own = lax.dynamic_slice_in_dim(near_rows, chip * sb, sb, 0) + back
            near_rows = lax.dynamic_update_slice_in_dim(near_rows, own, chip * sb, 0)
        near_rows = over_chips(near_rows)
        own = lax.dynamic_slice_in_dim(near_rows, chip * sb, sb, 0)
        far_rows = along_group(own, 1)
        mine = column_sums(tables, near_rows, all_mass, far_rows, far_mass, tiles, 2 * tb)
        theirs = across(mine, 1)
    src_scale = source_mass / (dustbin + own)
    tgt_scale = target_mass / (dustbin + mine[:tb] + theirs[tb:])
    return (src_scale, tgt_scale)


def solution(mesh):
    placed = (
        P(("group", "dev"), None, None),
        P(("group", "dev"), None, None),
        P(("group", "dev"), None),
        P(("group", "dev"), None),
        P(("group", "dev"), None),
        P(("group", "dev"), None),
    )
    return jax.shard_map(
        local,
        mesh=mesh,
        in_specs=placed,
        out_specs=(P(("group", "dev"), None), P(("group", "dev"), None)),
        check_vma=False,
    )
```

time: 215 us -> 181 us (0.84)
  waiting for transfers between devices: 109 us -> 56.5 us
  Pallas kernels: 0 us -> 25.7 us
  starting transfers between devices: 48.6 us -> 25.6 us
  local copies, waits for them, and re-layouts: 19.7 us -> 41.8 us
  matrix products: 20.1 us -> 0 us
  between operations: 1.04 us -> 10.7 us
  other arithmetic: 15.4 us -> 19.7 us
    all_to_all x5 -> x0, waiting for transfers between devices: 64.5 us -> none  [the longest x1 45.6 us: local(): lax.all_to_all(selected_rows(tgt_unit, asked_rows, dev_count, slot_cap),...]
    all_to_all x5 -> x0, starting transfers between devices: 43.3 us -> none  [the longest x2 27.3 us: local(): lax.all_to_all(departing_messages.reshape(dev_count, slot_cap, col_parts....]
    pallas_call x0 -> x11, Pallas kernels: none -> 25.7 us  [the longest x6 11.2 us: build_tiles(): pl.pallas_call(functools.partial(tile_kernel, chunks, sides, slots, sb, h...]
    ppermute x4 -> x30, starting transfers between devices: 5.33 us -> 25.6 us  [the longest x14 15.1 us: around(): return lax.ppermute(x, 'dev', pairs)]
    dot_general x9 -> x0, matrix products: 20.1 us -> none  [the longest x2 7.21 us: local(): jnp.einsum('ikbj,ib->ikj', kernel, src_scale, precision=lax.Precision.HIG...]
    unnamed x16 -> x69, local copies, waits for them, and re-layouts: 0.04 us -> 14.7 us
    ppermute x4 -> x30, waiting for transfers between devices: 44.7 us -> 56.5 us  [the longest x14 26 us: around(): return lax.ppermute(x, 'dev', pairs)]
    gather x8 -> x2, local copies, waits for them, and re-layouts: 12.8 us -> 1.11 us  [by_chip(): jnp.take(jnp.stack([parts[k] for k in range(chips)]), turn, axis=0)]
  transfers between devices with their start and end apart: 9 -> 30, of which waited for: 6 -> 17; matrix products, arithmetic and copies ran while one was open for 5% -> 26% of each run, Pallas kernels for 0% -> 7%
where the time goes in v1:
time: 181 us; the launch traced here: 180 us
  waiting for transfers between devices  56.5 us (31%)
  local copies, waits for them, and re-layouts  41.8 us (23%)
  Pallas kernels  25.7 us (14%)
  starting transfers between devices  25.6 us (14%)
  other arithmetic  19.7 us (11%)
  between operations  10.7 us (6%)
    ppermute x14, waiting for transfers between devices, around(): return lax.ppermute(x, 'dev', pairs)  26 us
    ppermute x10, waiting for transfers between devices, across(): return lax.ppermute(x, 'dev', [(i, i ^ bit) for i in range(dev_count)])  23.5 us
    ppermute x14, starting transfers between devices, around(): return lax.ppermute(x, 'dev', pairs)  15.1 us
    unnamed x69, local copies, waits for them, and re-layouts  14.7 us
    pallas_call x6, Pallas kernels, build_tiles(): pl.pallas_call(functools.partial(tile_kernel, chunks, sides, slots, sb, h...  11.2 us
    gt x16, local copies, waits for them, and re-layouts, tables_of(): rows_at = jnp.where(filled > 0, chip_index * sb + loc, chips * sb)  9.37 us
    pallas_call x2, Pallas kernels, target_operand(): pl.pallas_call(target_kernel, out_shape=jax.ShapeDtypeStruct((blocks, wid...  9.3 us
    ppermute x6, waiting for transfers between devices, along_group(): lax.ppermute(x, 'group', [(i, (i + by) % group_count) for i in range(grou...  6.94 us
  transfers between devices with their start and end apart: 30, of which 17 were waited for; matrix products, arithmetic and copies ran while one was open for 26% of the time, Pallas kernels for 7%

profile of v1, /device:TPU:0, one launch (start us, length us, event | category | flops | bytes accessed | tf_op | source)
XLA Modules:
  0.0 180.0 jit_solution(9199729878863417903)
XLA Ops:
  0.7 1.1 fusion.27
  2.4 3.0 %collective-permute-start.12 = (f32[520,128]{1,0:T(8,128)S(1)}, f32[520,128]{1,0:T(8,128)S(1)}, u32[]{:S(2)}, u32[]{:S(2)}) collective-permute-start(f32[520,128]{1,0:T(8,128)S(1)} %pad_maximum_fusion.1.refs_3_), channel_id=1, source_target_pairs={{0,2},{1,3},{4,0},{5,1},{8,4},{9,5},{12,8},{13,9},{14,12},{15,13},... | collective-permute-start | bytes 798728 | tf_op jit(solution)/shard_map/ppermute | solution.py:250
  5.6 1.9 %collective-permute-start.9 = (f32[520,128]{1,0:T(8,128)S(1)}, f32[520,128]{1,0:T(8,128)S(1)}, u32[]{:S(2)}, u32[]{:S(2)}) collective-permute-start(f32[520,128]{1,0:T(8,128)S(1)} %pad_maximum_fusion.1.refs_3_), channel_id=1, source_target_pairs={{0,16},{16,0},{1,17},{17,1},{2,18},{18,2},{3,19},{19,3},{4,20},{20... | collective-permute-start | bytes 798728 | tf_op jit(solution)/shard_map/ppermute | solution.py:256
  7.5 0.8 add_convert_fusion
  8.5 1.9 %collective-permute-start.1 = (f32[520,128]{1,0:T(8,128)S(1)}, f32[520,128]{1,0:T(8,128)}, u32[]{:S(2)}, u32[]{:S(2)}) collective-permute-start(f32[520,128]{1,0:T(8,128)S(1)} %pad_maximum_fusion.refs_2_), channel_id=1, source_target_pairs={{0,2},{1,3},{4,0},{5,1},{8,4},{9,5},{12,8},{13,9},{14,12},{15,13},... | collective-permute-start | bytes 798728 | tf_op jit(solution)/shard_map/ppermute | solution.py:250
  11.0 1.2 compare_and_fusion
  24.0 4.7 %target_operand.2.refs_4_.refs_6_ = bf16[32,128,256]{2,1,0:T(8,128)(2,1)S(1)} custom-call(f32[32,128,128]{2,1,0:T(8,128)} %emb_ref.1), custom_call_target="tpu_custom_call" | custom-call | bytes 6291456 | tf_op jit(solution)/shard_map/target_operand/pallas_call | solution.py:65
  29.7 5.8 %collective-permute-done.refs_2_ = f32[520,128]{1,0:T(8,128)S(1)} collective-permute-done((f32[520,128]{1,0:T(8,128)S(1)}, f32[520,128]{1,0:T(8,128)S(1)}, u32[]{:S(2)}, u32[]{:S(2)}) %collective-permute-start) | collective-permute-done | bytes 266272 | tf_op jit(solution)/shard_map/ppermute | solution.py:250
  36.2 1.6 collective-permute-start.3
  37.8 0.9 fusion.25.refs_1_.far_at
  39.0 1.7 build_tiles.7
  40.7 0.8 copy-done.8
  41.5 1.5 collective-permute-start.10
  43.0 1.6 collective-permute-start.14
  46.3 7.7 %collective-permute-done.2.refs_2_ = f32[520,128]{1,0:T(8,128)S(1)} collective-permute-done((f32[520,128]{1,0:T(8,128)S(1)}, f32[520,128]{1,0:T(8,128)S(1)}, u32[]{:S(2)}, u32[]{:S(2)}) %collective-permute-start.2) | collective-permute-done | bytes 266272 | tf_op jit(solution)/shard_map/ppermute | solution.py:250
  54.0 1.6 collective-permute-start.5
  57.8 0.9 collective-permute-start.4
  58.7 3.0 %collective-permute-done.5.refs_4_ = f32[520,128]{1,0:T(8,128)} collective-permute-done((f32[520,128]{1,0:T(8,128)}, f32[520,128]{1,0:T(8,128)}, u32[]{:S(2)}, u32[]{:S(2)}) %collective-permute-start.5) | collective-permute-done | bytes 266272 | tf_op jit(solution)/shard_map/ppermute | solution.py:250
  62.9 4.5 %collective-permute-done.4.refs_2_ = f32[520,128]{1,0:T(8,128)} collective-permute-done((f32[520,128]{1,0:T(8,128)}, f32[520,128]{1,0:T(8,128)}, u32[]{:S(2)}, u32[]{:S(2)}) %collective-permute-start.4) | collective-permute-done | bytes 266272 | tf_op jit(solution)/shard_map/ppermute | solution.py:250
  68.2 0.9 collective-permute-start.6
  69.5 1.3 collective-permute-start.17
  71.4 4.6 %collective-permute-done.6.refs_2_ = f32[520,128]{1,0:T(8,128)} collective-permute-done((f32[520,128]{1,0:T(8,128)}, f32[520,128]{1,0:T(8,128)}, u32[]{:S(2)}, u32[]{:S(2)}) %collective-permute-start.6) | collective-permute-done | bytes 266272 | tf_op jit(solution)/shard_map/ppermute | solution.py:250
  76.9 0.8 fusion.16
  86.3 1.3 reduce_sum.503
  87.6 0.8 copy.40
  89.9 0.8 copy.22
  92.2 0.8 copy.25
  94.4 0.7 copy.28
  96.2 0.8 copy.31
  100.2 0.7 copy.37
  106.4 1.3 broadcast_select_fusion
  107.9 1.3 broadcast_select_fusion.6
  109.3 4.6 %target_operand.3.refs_5_.refs_7_ = bf16[32,128,256]{2,1,0:T(8,128)(2,1)S(1)} custom-call(f32[32,128,128]{2,1,0:T(8,128)} %collective-permute-done.8.emb_ref), custom_call_target="tpu_custom_call" | custom-call | bytes 6291456 | tf_op jit(solution)/shard_map/target_operand/pallas_call | solution.py:65
  114.0 1.2 build_tiles.6
  115.2 0.8 copy-done.4
  116.1 2.1 %build_tiles.8 = (bf16[20,128,256]{2,1,0:T(8,128)(2,1)S(1)}, f32[2,8,128]{2,1,0:T(8,128)S(1)}) custom-call(s32[20]{0:T(128)S(1)} %get-tuple-element.161.refs_0_, s32[20]{0:T(128)S(1)} %get-tuple-element.162.refs_1_, f32[520,128]{1,0:T(8,128)S(1)} %copy-done.17, f32[520,128]{1,0:T(8,128)S(1)} %copy-done.14, f32[520,128]{1,0:T(8,128)} %collective-permute-done.1.refs_4_, ...), custom_call_target="tpu_custom_call" | custom-call | flops 335544320 | bytes 5505024 | tf_op jit(solution)/shard_map/build_tiles/pallas_call | solution.py:118
  118.2 2.2 %build_tiles.9 = (bf16[20,128,256]{2,1,0:T(8,128)(2,1)S(1)}, f32[2,8,128]{2,1,0:T(8,128)S(1)}) custom-call(s32[20]{0:T(128)S(1)} %get-tuple-element.163.refs_0_, s32[20]{0:T(128)S(1)} %get-tuple-element.164.refs_1_, f32[520,128]{1,0:T(8,128)S(1)} %copy-done.19, f32[520,128]{1,0:T(8,128)} %collective-permute-done.13.refs_3_, ...), custom_call_target="tpu_custom_call" | custom-call | flops 335544320 | bytes 5505024 | tf_op jit(solution)/shard_map/build_tiles/pallas_call | solution.py:118
  120.4 1.1 copy-done
  121.5 2.3 %build_tiles.10 = (bf16[20,128,256]{2,1,0:T(8,128)(2,1)S(1)}, f32[2,8,128]{2,1,0:T(8,128)S(1)}) custom-call(s32[20]{0:T(128)S(1)} %get-tuple-element.165.refs_0_, s32[20]{0:T(128)S(1)} %get-tuple-element.166.refs_1_, f32[520,128]{1,0:T(8,128)} %collective-permute-done.4.refs_2_, f32[520,128]{1,0:T(8,128)} %collective-permute-done.15.refs_3_, ...), custom_call_target="tpu_custom_call" | custom-call | flops 335544320 | bytes 5505024 | tf_op jit(solution)/shard_map/build_tiles/pallas_call | solution.py:118
  123.7 1.1 copy-done.2
  124.8 1.7 build_tiles.11
  126.6 0.9 copy-done.6
  128.1 1.6 collective-permute-start.18
  129.8 2.3 %collective-permute-done.18 = f32[64,128]{1,0:T(8,128)S(1)} collective-permute-done((f32[64,128]{1,0:T(8,128)S(1)}, f32[64,128]{1,0:T(8,128)S(1)}, u32[]{:S(2)}, u32[]{:S(2)}) %collective-permute-start.18) | collective-permute-done | bytes 32800 | tf_op jit(solution)/shard_map/ppermute | solution.py:253
  132.5 3.5 %collective-permute-done.19 = f32[64,128]{1,0:T(8,128)S(1)} collective-permute-done((f32[64,128]{1,0:T(8,128)S(1)}, f32[64,128]{1,0:T(8,128)S(1)}, u32[]{:S(2)}, u32[]{:S(2)}) %collective-permute-start.19) | collective-permute-done | bytes 32800 | tf_op jit(solution)/shard_map/ppermute | solution.py:253
  136.4 4.7 %collective-permute-done.20 = f32[64,128]{1,0:T(8,128)S(1)} collective-permute-done((f32[64,128]{1,0:T(8,128)S(1)}, f32[64,128]{1,0:T(8,128)S(1)}, u32[]{:S(2)}, u32[]{:S(2)}) %collective-permute-start.20) | collective-permute-done | bytes 32800 | tf_op jit(solution)/shard_map/ppermute | solution.py:253
  142.3 0.8 concatenate.36.sums_at
  143.8 0.9 collective-permute-done.21.far_rows
  144.8 1.3 copy-done.1
  146.1 1.3 copy-done.3
  147.4 1.1 copy-done.5
  148.5 1.1 copy-done.7
  149.6 1.0 copy-done.9
  150.6 1.5 column_sums.2.mine
  152.7 0.8 collective-permute-done.23.other_mass
  153.6 2.2 %row_sums.1 = (f32[64,128]{1,0:T(8,128)S(1)}, f32[8,128]{1,0:T(8,128)S(1)}) custom-call(s32[80]{0:T(128)S(1)} %concatenate.35.rows_at, s32[80]{0:T(128)S(1)} %concatenate.36.sums_at, s32[8]{0:T(128)S(1)} %fusion.25.refs_1_.far_at, f32[64,128]{1,0:T(8,128)S(1)} %column_sums.2.mine, f32[64,128]{1,0:T(8,128)S(1)} %collective-permute-done.22.theirs, ...), custom_call_target="tpu_custom_call" | custom-call | flops 46137344 | bytes 5767168 | tf_op jit(solution)/shard_map/row_sums/pallas_call | solution.py:212
  156.4 3.0 %collective-permute-done.24 = f32[8,128]{1,0:T(8,128)S(1)} collective-permute-done((f32[8,128]{1,0:T(8,128)S(1)}, f32[8,128]{1,0:T(8,128)S(1)}, u32[]{:S(2)}, u32[]{:S(2)}) %collective-permute-start.24) | collective-permute-done | bytes 4128 | tf_op jit(solution)/shard_map/ppermute | solution.py:256
  159.4 1.6 collective-permute-start.25
  161.0 2.3 %collective-permute-done.25 = f32[64,128]{1,0:T(8,128)S(1)} collective-permute-done((f32[64,128]{1,0:T(8,128)S(1)}, f32[64,128]{1,0:T(8,128)S(1)}, u32[]{:S(2)}, u32[]{:S(2)}) %collective-permute-start.25) | collective-permute-done | bytes 32800 | tf_op jit(solution)/shard_map/ppermute | solution.py:253
  163.5 3.7 %collective-permute-done.26 = f32[64,128]{1,0:T(8,128)S(1)} collective-permute-done((f32[64,128]{1,0:T(8,128)S(1)}, f32[64,128]{1,0:T(8,128)S(1)}, u32[]{:S(2)}, u32[]{:S(2)}) %collective-permute-start.26) | collective-permute-done | bytes 32800 | tf_op jit(solution)/shard_map/ppermute | solution.py:253
  167.3 5.0 %collective-permute-done.27 = f32[64,128]{1,0:T(8,128)S(1)} collective-permute-done((f32[64,128]{1,0:T(8,128)S(1)}, f32[64,128]{1,0:T(8,128)S(1)}, u32[]{:S(2)}, u32[]{:S(2)}) %collective-permute-start.27) | collective-permute-done | bytes 32800 | tf_op jit(solution)/shard_map/ppermute | solution.py:253
  173.6 3.0 %collective-permute-done.28.far_rows = f32[8,128]{1,0:T(8,128)S(1)} collective-permute-done((f32[8,128]{1,0:T(8,128)S(1)}, f32[8,128]{1,0:T(8,128)S(1)}, u32[]{:S(2)}, u32[]{:S(2)}) %collective-permute-start.28) | collective-permute-done | bytes 4128 | tf_op jit(solution)/shard_map/ppermute | solution.py:256
  176.6 1.5 column_sums.3
  178.2 1.2 collective-permute-done.29
  (214 shorter events, 43.7 us)
Async XLA Ops:
  0.6 9.7 %copy-start.27 = (s32[8]{0:T(128)S(1)}, s32[8]{0:T(128)}, u32[]{:S(2)}) copy-start(s32[8]{0:T(128)} %constant.129.clone) | copy-start | bytes 100
  0.6 16.8 %copy-start.22 = (s32[8]{0:T(128)S(1)}, s32[8]{0:T(128)}, u32[]{:S(2)}) copy-start(s32[8]{0:T(128)} %constant.130.clone) | copy-start | bytes 100
  2.4 40.6 %collective-permute-start.12 = (f32[520,128]{1,0:T(8,128)S(1)}, f32[520,128]{1,0:T(8,128)S(1)}, u32[]{:S(2)}, u32[]{:S(2)}) collective-permute-start(f32[520,128]{1,0:T(8,128)S(1)} %pad_maximum_fusion.1.refs_3_), channel_id=1, source_target_pairs={{0,2},{1,3},{4,0},{5,1},{8,4},{9,5},{12,8},{13,9},{14,12},{15,13},... | collective-permute-start | bytes 798728 | tf_op jit(solution)/shard_map/ppermute | solution.py:250
  5.4 39.2 %collective-permute-start.11 = (f32[520,128]{1,0:T(8,128)S(1)}, f32[520,128]{1,0:T(8,128)S(1)}, u32[]{:S(2)}, u32[]{:S(2)}) collective-permute-start(f32[520,128]{1,0:T(8,128)S(1)} %pad_maximum_fusion.1.refs_3_), channel_id=1, source_target_pairs={{0,4},{1,5},{4,8},{5,9},{8,12},{9,13},{12,14},{13,15},{14,10},{15,... | collective-permute-start | bytes 798728 | tf_op jit(solution)/shard_map/ppermute | solution.py:250
  5.6 33.4 %collective-permute-start.9 = (f32[520,128]{1,0:T(8,128)S(1)}, f32[520,128]{1,0:T(8,128)S(1)}, u32[]{:S(2)}, u32[]{:S(2)}) collective-permute-start(f32[520,128]{1,0:T(8,128)S(1)} %pad_maximum_fusion.1.refs_3_), channel_id=1, source_target_pairs={{0,16},{16,0},{1,17},{17,1},{2,18},{18,2},{3,19},{19,3},{4,20},{20... | collective-permute-start | bytes 798728 | tf_op jit(solution)/shard_map/ppermute | solution.py:256
  8.3 27.3 %collective-permute-start.7 = (f32[520,128]{1,0:T(8,128)S(1)}, f32[520,128]{1,0:T(8,128)}, u32[]{:S(2)}, u32[]{:S(2)}) collective-permute-start(f32[520,128]{1,0:T(8,128)S(1)} %pad_maximum_fusion.refs_2_), channel_id=1, source_target_pairs={{0,16},{16,0},{1,17},{17,1},{2,18},{18,2},{3,19},{19,3},{4,20},{20... | collective-permute-start | bytes 798728 | tf_op jit(solution)/shard_map/ppermute | solution.py:256
  8.5 20.2 %collective-permute-start.1 = (f32[520,128]{1,0:T(8,128)S(1)}, f32[520,128]{1,0:T(8,128)}, u32[]{:S(2)}, u32[]{:S(2)}) collective-permute-start(f32[520,128]{1,0:T(8,128)S(1)} %pad_maximum_fusion.refs_2_), channel_id=1, source_target_pairs={{0,2},{1,3},{4,0},{5,1},{8,4},{9,5},{12,8},{13,9},{14,12},{15,13},... | collective-permute-start | bytes 798728 | tf_op jit(solution)/shard_map/ppermute | solution.py:250
  24.0 4.7 %copy-start.21 = (f32[8,128]{1,0:T(8,128)S(1)}, f32[8,128]{1,0:T(8,128)}, u32[]{:S(2)}) copy-start(f32[8,128]{1,0:T(8,128)} %param.20) | copy-start | bytes 12292
  28.7 6.8 %collective-permute-start = (f32[520,128]{1,0:T(8,128)S(1)}, f32[520,128]{1,0:T(8,128)S(1)}, u32[]{:S(2)}, u32[]{:S(2)}) collective-permute-start(f32[520,128]{1,0:T(8,128)S(1)} %pad_maximum_fusion.refs_2_), channel_id=1, source_target_pairs={{0,4},{1,5},{4,8},{5,9},{8,12},{9,13},{12,14},{13,15},{14,10},{15,... | collective-permute-start | bytes 798728 | tf_op jit(solution)/shard_map/ppermute | solution.py:250
  35.5 0.7 copy-start.15
  35.5 73.7 %collective-permute-start.8 = (f32[32,128,128]{2,1,0:T(8,128)}, f32[32,128,128]{2,1,0:T(8,128)}, u32[]{:S(2)}, u32[]{:S(2)}) collective-permute-start(f32[32,128,128]{2,1,0:T(8,128)} %emb_ref.1), channel_id=1, source_target_pairs={{0,1},{1,0},{2,3},{3,2},{4,5},{5,4},{6,7},{7,6},{8,9},{9,8},{10,11... | collective-permute-start | bytes 6291464 | tf_op jit(solution)/shard_map/ppermute | solution.py:253
  36.2 8.9 %collective-permute-start.3 = (f32[520,128]{1,0:T(8,128)}, f32[520,128]{1,0:T(8,128)}, u32[]{:S(2)}, u32[]{:S(2)}) collective-permute-start(f32[520,128]{1,0:T(8,128)} %collective-permute-done.1.refs_4_), channel_id=1, source_target_pairs={{0,2},{1,3},{4,0},{5,1},{8,4},{9,5},{12,8},{13,9},{14,12},{15,13},... | collective-permute-start | bytes 798728 | tf_op jit(solution)/shard_map/ppermute | solution.py:250
  39.0 5.6 %copy-start.16 = (f32[520,128]{1,0:T(8,128)S(1)}, f32[520,128]{1,0:T(8,128)}, u32[]{:S(2)}) copy-start(f32[520,128]{1,0:T(8,128)} %copy-done.15) | copy-start | bytes 798724
  39.0 77.1 %copy-start.10 = (f32[520,128]{1,0:T(8,128)}, f32[520,128]{1,0:T(8,128)S(1)}, u32[]{:S(2)}) copy-start(f32[520,128]{1,0:T(8,128)S(1)} %collective-permute-done.9.refs_3_) | copy-start | bytes 798724
  40.7 0.8 copy-start.8
  41.5 74.6 %collective-permute-start.10 = (f32[8,128]{1,0:T(8,128)S(1)}, f32[8,128]{1,0:T(8,128)S(1)}, u32[]{:S(2)}, u32[]{:S(2)}) collective-permute-start(f32[8,128]{1,0:T(8,128)S(1)} %bitcast.54), channel_id=1, source_target_pairs={{0,16},{16,0},{1,17},{17,1},{2,18},{18,2},{3,19},{19,3},{4,20},{20... | collective-permute-start | bytes 12296 | tf_op jit(solution)/shard_map/ppermute | solution.py:256
  43.0 70.9 %copy-start.11 = (f32[520,128]{1,0:T(8,128)}, f32[520,128]{1,0:T(8,128)S(1)}, u32[]{:S(2)}) copy-start(f32[520,128]{1,0:T(8,128)S(1)} %collective-permute-done.12.refs_5_) | copy-start | bytes 798724
  43.0 13.0 %collective-permute-start.14 = (f32[520,128]{1,0:T(8,128)S(1)}, f32[520,128]{1,0:T(8,128)}, u32[]{:S(2)}, u32[]{:S(2)}) collective-permute-start(f32[520,128]{1,0:T(8,128)S(1)} %collective-permute-done.12.refs_5_), channel_id=1, source_target_pairs={{0,2},{1,3},{4,0},{5,1},{8,4},{9,5},{12,8},{13,9},{14,12},{15,13},... | collective-permute-start | bytes 798728 | tf_op jit(solution)/shard_map/ppermute | solution.py:250
  44.6 69.3 %copy-start.13 = (f32[520,128]{1,0:T(8,128)}, f32[520,128]{1,0:T(8,128)S(1)}, u32[]{:S(2)}) copy-start(f32[520,128]{1,0:T(8,128)S(1)} %collective-permute-done.11.refs_3_) | copy-start | bytes 798724
  44.6 9.4 %collective-permute-start.2 = (f32[520,128]{1,0:T(8,128)S(1)}, f32[520,128]{1,0:T(8,128)S(1)}, u32[]{:S(2)}, u32[]{:S(2)}) collective-permute-start(f32[520,128]{1,0:T(8,128)S(1)} %copy-done.16), channel_id=1, source_target_pairs={{0,4},{1,5},{4,8},{5,9},{8,12},{9,13},{12,14},{13,15},{14,10},{15,... | collective-permute-start | bytes 798728 | tf_op jit(solution)/shard_map/ppermute | solution.py:250
  45.1 12.7 %collective-permute-start.13 = (f32[520,128]{1,0:T(8,128)S(1)}, f32[520,128]{1,0:T(8,128)}, u32[]{:S(2)}, u32[]{:S(2)}) collective-permute-start(f32[520,128]{1,0:T(8,128)S(1)} %collective-permute-done.11.refs_3_), channel_id=1, source_target_pairs={{0,4},{1,5},{4,8},{5,9},{8,12},{9,13},{12,14},{13,15},{14,10},{15,... | collective-permute-start | bytes 798728 | tf_op jit(solution)/shard_map/ppermute | solution.py:250
  54.0 1.6 copy-start.18
  54.0 7.7 %collective-permute-start.5 = (f32[520,128]{1,0:T(8,128)}, f32[520,128]{1,0:T(8,128)}, u32[]{:S(2)}, u32[]{:S(2)}) collective-permute-start(f32[520,128]{1,0:T(8,128)} %collective-permute-done.3.refs_4_), channel_id=1, source_target_pairs={{0,2},{1,3},{4,0},{5,1},{8,4},{9,5},{12,8},{13,9},{14,12},{15,13},... | collective-permute-start | bytes 798728 | tf_op jit(solution)/shard_map/ppermute | solution.py:250
  56.0 13.5 %collective-permute-start.16 = (f32[520,128]{1,0:T(8,128)}, f32[520,128]{1,0:T(8,128)}, u32[]{:S(2)}, u32[]{:S(2)}) collective-permute-start(f32[520,128]{1,0:T(8,128)} %collective-permute-done.14.refs_5_), channel_id=1, source_target_pairs={{0,2},{1,3},{4,0},{5,1},{8,4},{9,5},{12,8},{13,9},{14,12},{15,13},... | collective-permute-start | bytes 798728 | tf_op jit(solution)/shard_map/ppermute | solution.py:250
  57.8 9.6 %collective-permute-start.4 = (f32[520,128]{1,0:T(8,128)}, f32[520,128]{1,0:T(8,128)}, u32[]{:S(2)}, u32[]{:S(2)}) collective-permute-start(f32[520,128]{1,0:T(8,128)} %copy-done.18), channel_id=1, source_target_pairs={{0,4},{1,5},{4,8},{5,9},{8,12},{9,13},{12,14},{13,15},{14,10},{15,... | collective-permute-start | bytes 798728 | tf_op jit(solution)/shard_map/ppermute | solution.py:250
  61.7 42.2 %collective-permute-start.15 = (f32[520,128]{1,0:T(8,128)}, f32[520,128]{1,0:T(8,128)}, u32[]{:S(2)}, u32[]{:S(2)}) collective-permute-start(f32[520,128]{1,0:T(8,128)} %collective-permute-done.13.refs_3_), channel_id=1, source_target_pairs={{0,4},{1,5},{4,8},{5,9},{8,12},{9,13},{12,14},{13,15},{14,10},{15,... | collective-permute-start | bytes 798728 | tf_op jit(solution)/shard_map/ppermute | solution.py:250
  68.2 7.8 %collective-permute-start.6 = (f32[520,128]{1,0:T(8,128)}, f32[520,128]{1,0:T(8,128)}, u32[]{:S(2)}, u32[]{:S(2)}) collective-permute-start(f32[520,128]{1,0:T(8,128)} %collective-permute-done.4.refs_2_), channel_id=1, source_target_pairs={{0,4},{1,5},{4,8},{5,9},{8,12},{9,13},{12,14},{13,15},{14,10},{15,... | collective-permute-start | bytes 798728 | tf_op jit(solution)/shard_map/ppermute | solution.py:250
  69.5 33.8 %collective-permute-start.17 = (f32[520,128]{1,0:T(8,128)}, f32[520,128]{1,0:T(8,128)}, u32[]{:S(2)}, u32[]{:S(2)}) collective-permute-start(f32[520,128]{1,0:T(8,128)} %collective-permute-done.16.refs_5_), channel_id=1, source_target_pairs={{0,2},{1,3},{4,0},{5,1},{8,4},{9,5},{12,8},{13,9},{14,12},{15,13},... | collective-permute-start | bytes 798728 | tf_op jit(solution)/shard_map/ppermute | solution.py:250
  113.9 2.1 %copy-start.12 = (f32[520,128]{1,0:T(8,128)S(1)}, f32[520,128]{1,0:T(8,128)}, u32[]{:S(2)}) copy-start(f32[520,128]{1,0:T(8,128)} %copy-done.11) | copy-start | bytes 798724
  113.9 2.1 %copy-start.14 = (f32[520,128]{1,0:T(8,128)S(1)}, f32[520,128]{1,0:T(8,128)}, u32[]{:S(2)}) copy-start(f32[520,128]{1,0:T(8,128)} %copy-done.13) | copy-start | bytes 798724
  114.0 2.1 %copy-start.17 = (f32[520,128]{1,0:T(8,128)S(1)}, f32[520,128]{1,0:T(8,128)}, u32[]{:S(2)}) copy-start(f32[520,128]{1,0:T(8,128)} %copy-done.15) | copy-start | bytes 798724
  115.2 0.8 copy-start.4
  116.1 2.1 %copy-start.19 = (f32[520,128]{1,0:T(8,128)S(1)}, f32[520,128]{1,0:T(8,128)}, u32[]{:S(2)}) copy-start(f32[520,128]{1,0:T(8,128)} %copy-done.18) | copy-start | bytes 798724
  120.4 1.1 copy-start
  123.7 1.1 copy-start.2
  124.8 3.2 %copy-start.23 = (pred[8]{0:T(512)(128)(4,1)S(1)}, pred[8]{0:T(512)(128)(4,1)}, u32[]{:S(2)}) copy-start(pred[8]{0:T(512)(128)(4,1)} %get-tuple-element.95) | copy-start | bytes 28
  124.8 18.3 %copy-start.24 = (s32[10]{0:T(128)S(1)}, s32[10]{0:T(128)}, u32[]{:S(2)}) copy-start(s32[10]{0:T(128)} %get-tuple-element.118) | copy-start | bytes 124
  124.8 18.3 %copy-start.25 = (s32[10]{0:T(128)S(1)}, s32[10]{0:T(128)}, u32[]{:S(2)}) copy-start(s32[10]{0:T(128)} %get-tuple-element.140) | copy-start | bytes 124
  124.8 18.3 %copy-start.26 = (s32[10]{0:T(128)S(1)}, s32[10]{0:T(128)}, u32[]{:S(2)}) copy-start(s32[10]{0:T(128)} %get-tuple-element.143) | copy-start | bytes 124
  126.6 0.9 copy-start.6
  128.1 4.0 %collective-permute-start.18 = (f32[64,128]{1,0:T(8,128)S(1)}, f32[64,128]{1,0:T(8,128)S(1)}, u32[]{:S(2)}, u32[]{:S(2)}) collective-permute-start(f32[64,128]{1,0:T(8,128)S(1)} %get-tuple-element.134), channel_id=1, source_target_pairs={{0,2},{1,3},{2,0},{3,1},{4,6},{5,7},{6,4},{7,5},{8,10},{9,11},{10,... | collective-permute-start | bytes 98312 | tf_op jit(solution)/shard_map/ppermute | solution.py:253
  132.1 3.9 %collective-permute-start.19 = (f32[64,128]{1,0:T(8,128)S(1)}, f32[64,128]{1,0:T(8,128)S(1)}, u32[]{:S(2)}, u32[]{:S(2)}) collective-permute-start(f32[64,128]{1,0:T(8,128)S(1)} %add.348), channel_id=1, source_target_pairs={{0,4},{1,5},{2,6},{3,7},{4,0},{5,1},{6,2},{7,3},{8,12},{9,13},{10,... | collective-permute-start | bytes 98312 | tf_op jit(solution)/shard_map/ppermute | solution.py:253
  136.0 5.1 %collective-permute-start.20 = (f32[64,128]{1,0:T(8,128)S(1)}, f32[64,128]{1,0:T(8,128)S(1)}, u32[]{:S(2)}, u32[]{:S(2)}) collective-permute-start(f32[64,128]{1,0:T(8,128)S(1)} %add.349), channel_id=1, source_target_pairs={{0,8},{1,9},{2,10},{3,11},{4,12},{5,13},{6,14},{7,15},{8,0},{9,1},... | collective-permute-start | bytes 98312 | tf_op jit(solution)/shard_map/ppermute | solution.py:253
  141.1 3.7 %collective-permute-start.21 = (f32[8,128]{1,0:T(8,128)S(1)}, f32[8,128]{1,0:T(8,128)S(1)}, u32[]{:S(2)}, u32[]{:S(2)}) collective-permute-start(f32[8,128]{1,0:T(8,128)S(1)} %constant_dynamic-slice_fusion.1), channel_id=1, source_target_pairs={{0,16},{16,0},{1,17},{17,1},{2,18},{18,2},{3,19},{19,3},{4,20},{20... | collective-permute-start | bytes 12296 | tf_op jit(solution)/shard_map/ppermute | solution.py:256
  144.8 1.3 copy-start.1
  146.1 1.3 copy-start.3
  147.4 1.1 copy-start.5
  148.5 1.1 copy-start.7
  149.6 1.0 copy-start.9
  150.6 1.6 copy-start.20
  152.1 1.4 collective-permute-start.22
  152.2 1.3 collective-permute-start.23
  155.7 3.7 %collective-permute-start.24 = (f32[8,128]{1,0:T(8,128)S(1)}, f32[8,128]{1,0:T(8,128)S(1)}, u32[]{:S(2)}, u32[]{:S(2)}) collective-permute-start(f32[8,128]{1,0:T(8,128)S(1)} %get-tuple-element.30), channel_id=1, source_target_pairs={{0,16},{16,0},{1,17},{17,1},{2,18},{18,2},{3,19},{19,3},{4,20},{20... | collective-permute-start | bytes 12296 | tf_op jit(solution)/shard_map/ppermute | solution.py:256
  159.4 3.9 %collective-permute-start.25 = (f32[64,128]{1,0:T(8,128)S(1)}, f32[64,128]{1,0:T(8,128)S(1)}, u32[]{:S(2)}, u32[]{:S(2)}) collective-permute-start(f32[64,128]{1,0:T(8,128)S(1)} %add_dynamic-update-slice_fusion), channel_id=1, source_target_pairs={{0,2},{1,3},{2,0},{3,1},{4,6},{5,7},{6,4},{7,5},{8,10},{9,11},{10,... | collective-permute-start | bytes 98312 | tf_op jit(solution)/shard_map/ppermute | solution.py:253
  163.3 3.9 %collective-permute-start.26 = (f32[64,128]{1,0:T(8,128)S(1)}, f32[64,128]{1,0:T(8,128)S(1)}, u32[]{:S(2)}, u32[]{:S(2)}) collective-permute-start(f32[64,128]{1,0:T(8,128)S(1)} %add.353), channel_id=1, source_target_pairs={{0,4},{1,5},{2,6},{3,7},{4,0},{5,1},{6,2},{7,3},{8,12},{9,13},{10,... | collective-permute-start | bytes 98312 | tf_op jit(solution)/shard_map/ppermute | solution.py:253
  167.3 5.1 %collective-permute-start.27 = (f32[64,128]{1,0:T(8,128)S(1)}, f32[64,128]{1,0:T(8,128)S(1)}, u32[]{:S(2)}, u32[]{:S(2)}) collective-permute-start(f32[64,128]{1,0:T(8,128)S(1)} %add.354), channel_id=1, source_target_pairs={{0,8},{1,9},{2,10},{3,11},{4,12},{5,13},{6,14},{7,15},{8,0},{9,1},... | collective-permute-start | bytes 98312 | tf_op jit(solution)/shard_map/ppermute | solution.py:253
  172.9 3.6 %collective-permute-start.28 = (f32[8,128]{1,0:T(8,128)S(1)}, f32[8,128]{1,0:T(8,128)S(1)}, u32[]{:S(2)}, u32[]{:S(2)}) collective-permute-start(f32[8,128]{1,0:T(8,128)S(1)} %get-tuple-element.94), channel_id=1, source_target_pairs={{0,16},{16,0},{1,17},{17,1},{2,18},{18,2},{3,19},{19,3},{4,20},{20... | collective-permute-start | bytes 12296 | tf_op jit(solution)/shard_map/ppermute | solution.py:256
  178.1 1.3 collective-permute-start.29

commit v2 on v1

v2 whole, which is shorter than its diff:
```python
import functools

import jax
import jax.numpy as jnp
from jax import lax
from jax.experimental import pallas as pl
from jax.experimental.pallas import tpu as pltpu
from jax.sharding import PartitionSpec as P

ITERS = 2

entropic_regularizer = 0.1
dustbin = 0.5
epsilon = 1e-06

VMEM = pl.BlockSpec(memory_space=pltpu.VMEM)
SMEM = pl.BlockSpec(memory_space=pltpu.SMEM)
NT = (((1,), (1,)), ((), ()))
NN = (((1,), (0,)), ((), ()))


def split2(x):
    high = x.astype(jnp.bfloat16)
    low = (x - high.astype(jnp.float32)).astype(jnp.bfloat16)
    return high, low


def unit(x):
    return x * lax.rsqrt(jnp.mean(x * x, axis=-1, keepdims=True) + epsilon)


def stacked_parts(row):
    x = jnp.broadcast_to(row, (8, row.shape[1]))
    high = x.astype(jnp.bfloat16).astype(jnp.float32)
    rest = x - high
    low = rest.astype(jnp.bfloat16).astype(jnp.float32)
    place = lax.broadcasted_iota(jnp.int32, x.shape, 0)
    parts = jnp.where(place == 0, high, jnp.where(place == 1, low, jnp.where(place == 2, rest - low, 0.0)))
    return parts.astype(jnp.bfloat16)


def column_product(parts, tile):
    both = lax.dot_general(parts, tile, NN, preferred_element_type=jnp.float32)
    width = tile.shape[1] // 2
    return both[:, :width] + both[:, width:]


def row_product(parts, tile):
    return lax.dot_general(
        jnp.concatenate([parts, parts], axis=1), tile, NT, preferred_element_type=jnp.float32
    )


def target_kernel(emb_ref, out_ref):
    def one(block, carry):
        high, low = split2(unit(emb_ref[block]).T)
        out_ref[block] = jnp.concatenate([high, low], axis=1)
        return carry

    lax.fori_loop(0, emb_ref.shape[0], one, 0, unroll=2)


def target_operand(emb):
    blocks, rows, width = emb.shape
    return pl.pallas_call(
        target_kernel,
        out_shape=jax.ShapeDtypeStruct((blocks, width, 2 * rows), jnp.bfloat16),
        in_specs=[VMEM],
        out_specs=VMEM,
        cost_estimate=pl.CostEstimate(flops=0, bytes_accessed=3 * emb.size * 4, transcendentals=0),
        compiler_params=pltpu.CompilerParams(vmem_limit_bytes=16 << 20),
        name="target_operand",
    )(emb)


def pack_kernel(emb, mass, cand_device, cand_block, upper, lower):
    sb, rows, _ = emb.shape
    half, near = rows // 2, cand_device.shape[1]
    for block in range(sb):
        upper[block * half : (block + 1) * half] = emb[block, 0:half]
        lower[block * half : (block + 1) * half] = emb[block, half:rows]
    upper[sb * half :] = jnp.zeros((sb, emb.shape[2]), jnp.float32)
    upper[sb * half :, 0:near] = cand_device[...].astype(jnp.float32)
    upper[sb * half :, near : near + cand_block.shape[1]] = cand_block[...].astype(jnp.float32)
    lower[sb * half :] = mass[...]


def pack(emb, mass, cand_device, cand_block):
    sb, rows, width = emb.shape
    shape = jax.ShapeDtypeStruct((sb * (rows // 2 + 1), width), jnp.float32)
    return pl.pallas_call(
        pack_kernel,
        out_shape=(shape, shape),
        in_specs=[VMEM] * 4,
        out_specs=(VMEM, VMEM),
        compiler_params=pltpu.CompilerParams(vmem_limit_bytes=16 << 20),
        name="pack",
    )(emb, mass, cand_device, cand_block)


def chip_at(chips, chip, offset):
    odd = lax.rem(chip, 2)
    spot = jnp.where(odd == 1, chips - 1 - chip // 2, chip // 2) + offset
    spot = jnp.where(spot < 0, spot + chips, jnp.where(spot >= chips, spot - chips, spot))
    return jnp.where(spot < chips // 2, 2 * spot, 2 * chips - 1 - 2 * spot)


def tile_kernel(plan, *refs):
    chunks, slots, sb, half, tb, near, offsets, far, chained, closing = plan
    sides = 1 if far else 2
    refs = list(refs)
    device = refs.pop(0)
    source = [refs.pop(0) for _ in range(2 * chunks)]
    weight = [refs.pop(0) for _ in range(sides)]
    rows_in, mass_in = (refs.pop(0), refs.pop(0)) if chained else (None, None)
    back = refs.pop(0) if closing else None
    tiles, table, rows_out, mass_out, partial, staged, named, listed, arrived = refs
    count = chunks * sides * slots
    width = source[0].shape[1]
    scale = 1.0 / (width * entropic_regularizer)
    me = device[0]
    chips = rows_out.shape[0] // sb

    for chunk in range(chunks):
        staged[chunk * sb : (chunk + 1) * sb] = source[2 * chunk][sb * half :].astype(jnp.int32)
    copy = pltpu.make_async_copy(staged, named, arrived)
    copy.start()
    if chained:
        rows_out[...] = rows_in[...]
        mass_out[...] = mass_in[...]
    partial[...] = jnp.zeros_like(partial)
    place = lax.broadcasted_iota(jnp.int32, (8, 2 * width), 0)
    ones = jnp.where(place == 0, 1.0, 0.0).astype(jnp.bfloat16)
    copy.wait()

    chip_of = []
    for chunk in range(chunks):
        at_chip = jnp.int32(0) if far else chip_at(chips, me // 2, offsets[chunk])
        chip_of.append(at_chip)
        for side in range(sides):
            base = (chunk * sides + side) * slots
            if far:
                for j in range(sb):
                    listed[base + j] = j
                    table[j] = named[j, 2 * near]
                continue
            wanted = me if side == 0 else me + 1 - 2 * lax.rem(me, 2)
            filled = jnp.int32(0)
            for block in range(sb):
                found, which = jnp.int32(0), jnp.int32(0)
                for k in range(near):
                    hit = named[chunk * sb + block, k] == wanted
                    found = jnp.where(hit, 1, found)
                    which = jnp.where(hit, named[chunk * sb + block, near + k], which)
                listed[base + filled] = block
                table[count + base + filled] = which
                filled = filled + found
            for j in range(slots):
                valid = j < filled
                block = jnp.where(valid, listed[base + j], sb)
                which = jnp.where(valid, table[count + base + j], 2 * tb)
                listed[base + j] = block
                table[base + j] = jnp.where(valid, at_chip * sb + block, chips * sb)
                table[count + base + j] = jnp.where(valid, which + side * tb, 2 * tb)

    for chunk in range(chunks):
        upper, lower = source[2 * chunk], source[2 * chunk + 1]
        for side in range(sides):
            for j in range(slots):
                at = (chunk * sides + side) * slots + j
                block = listed[at]
                start = pl.multiple_of(lax.rem(block, sb) * half, half)
                left = jnp.concatenate([upper[pl.ds(start, half)], lower[pl.ds(start, half)]], axis=0)
                high, low = split2(unit(left))
                right = weight[side][table[at] if far else lax.rem(table[count + at], tb)]
                both = lax.dot_general(
                    jnp.concatenate([high, low], axis=1),
                    jnp.concatenate([right, right], axis=0),
                    NN,
                    preferred_element_type=jnp.float32,
                )
                nodes = both.shape[1] // 2
                affinity = both[:, :nodes] + both[:, nodes:]
                tile = jnp.exp(affinity * scale) * (1.0 / (8.0 * nodes))
                tile = jnp.concatenate(split2(tile), axis=1)
                tiles[at] = tile
                spot = chunk * (sb + 1) + block
                partial[spot] += lax.dot_general(ones, tile, NT, preferred_element_type=jnp.float32)
        start = pl.multiple_of(chip_of[chunk] * sb, sb)
        for block in range(sb):
            rows_out[pl.ds(start + block, 1)] = partial[chunk * (sb + 1) + block][0:1]
        mass_out[pl.ds(start, sb)] = lower[sb * half :]
    if closing:
        start = pl.multiple_of(me // 2 * sb, sb)
        rows_out[pl.ds(start, sb)] += back[...]


def build_tiles(device, source, weight, slots, sb, near, chips, offsets=(), chain=(), back=None):
    chunks, sides, far = len(source) // 2, len(weight), not offsets
    half, width = source[0].shape[0] // sb - 1, source[0].shape[1]
    tb, nodes = weight[0].shape[0], weight[0].shape[2] // 2
    count = chunks * sides * slots
    plan = (chunks, slots, sb, half, tb, near, offsets, far, bool(chain), back is not None)
    operands = [device, *source, *weight, *chain] + ([] if back is None else [back])
    rows = jax.ShapeDtypeStruct(((1 if far else chips) * sb, 2 * half), jnp.float32)
    return pl.pallas_call(
        functools.partial(tile_kernel, plan),
        out_shape=(
            jax.ShapeDtypeStruct((count, 2 * half, 2 * nodes), jnp.bfloat16),
            jax.ShapeDtypeStruct((count if far else 2 * count + 1,), jnp.int32),
            rows,
            rows,
        ),
        in_specs=[SMEM] + [VMEM] * (len(operands) - 1),
        out_specs=(VMEM, SMEM, VMEM, VMEM),
        scratch_shapes=[
            pltpu.VMEM((chunks * (sb + 1), 8, 2 * half), jnp.float32),
            pltpu.VMEM((chunks * sb, width), jnp.int32),
            pltpu.SMEM((chunks * sb, width), jnp.int32),
            pltpu.SMEM((count + 1,), jnp.int32),
            pltpu.SemaphoreType.DMA,
        ],
        cost_estimate=pl.CostEstimate(
            flops=count * 2 * half * nodes * width * 8,
            bytes_accessed=count * 2 * half * nodes * 4 + sides * weight[0].size * 2,
            transcendentals=count * 2 * half * nodes,
        ),
        compiler_params=pltpu.CompilerParams(vmem_limit_bytes=16 << 20),
        name="build_tiles",
    )(*operands)


def column_kernel(near, far, *refs):
    refs = list(refs)
    device = refs.pop(0)
    tables = [refs.pop(0) for _ in near]
    far_at, rows, mass, far_rows, far_mass = [refs.pop(0) for _ in range(5)]
    tiles = [refs.pop(0) for _ in range(len(near) + 1)]
    out, src_out, scale, total = refs
    count, sb = rows.shape[0], src_out.shape[0]
    scale[...] = jnp.zeros_like(scale)
    scale[0:count] = mass[...] / (dustbin + rows[...])
    scale[count + 8 : count + 8 + far] = far_mass[...] / (dustbin + far_rows[...])
    total[...] = jnp.zeros_like(total)
    for part, slots in enumerate(near):
        for slot in range(slots):
            parts = stacked_parts(scale[pl.ds(tables[part][slot], 1), :])
            total[tables[part][slots + slot]] += column_product(parts, tiles[part][slot])
    for slot in range(far):
        parts = stacked_parts(scale[count + 8 + slot : count + 9 + slot, :])
        total[far_at[slot]] += column_product(parts, tiles[len(near)][slot])
    for block in range(out.shape[0]):
        out[block : block + 1] = jnp.sum(total[block], axis=0, keepdims=True)
    src_out[...] = scale[pl.ds(pl.multiple_of(device[0] // 2 * sb, sb), sb)]


def column_sums(device, tables, far_at, rows, mass, far_rows, far_mass, tiles, targets):
    near = tuple(t.shape[0] for t in tiles[:-1])
    far, nodes = tiles[-1].shape[0], tiles[-1].shape[2] // 2
    width = rows.shape[1]
    return pl.pallas_call(
        functools.partial(column_kernel, near, far),
        out_shape=(
            jax.ShapeDtypeStruct((targets, nodes), jnp.float32),
            jax.ShapeDtypeStruct(far_rows.shape, jnp.float32),
        ),
        in_specs=[SMEM] * (2 + len(tables)) + [VMEM] * (4 + len(tiles)),
        out_specs=(VMEM, VMEM),
        scratch_shapes=[
            pltpu.VMEM((rows.shape[0] + 8 + (far + 7) // 8 * 8, width), jnp.float32),
            pltpu.VMEM((targets + 1, 8, nodes), jnp.float32),
        ],
        cost_estimate=pl.CostEstimate(
            flops=sum(t.size for t in tiles) * 16, bytes_accessed=sum(t.size for t in tiles) * 2, transcendentals=0
        ),
        compiler_params=pltpu.CompilerParams(vmem_limit_bytes=16 << 20),
        name="column_sums",
    )(device, *tables, far_at, rows, mass, far_rows, far_mass, *tiles)


def row_kernel(near, far, *refs):
    refs = list(refs)
    tables = [refs.pop(0) for _ in near]
    far_at, mine, theirs, mass, other_mass = [refs.pop(0) for _ in range(5)]
    tiles = [refs.pop(0) for _ in range(len(near) + 1)]
    out, far_out, scale, total = refs
    blocks = mass.shape[0]
    scale[2 * blocks :] = jnp.zeros((8, scale.shape[1]), jnp.float32)
    scale[0:blocks] = mass[...] / (dustbin + mine[0:blocks] + theirs[blocks : 2 * blocks])
    scale[blocks : 2 * blocks] = other_mass[...] / (dustbin + mine[blocks : 2 * blocks] + theirs[0:blocks])
    total[...] = jnp.zeros_like(total)
    for part, slots in enumerate(near):
        for slot in range(slots):
            parts = stacked_parts(scale[pl.ds(tables[part][slots + slot], 1), :])
            total[tables[part][slot]] += row_product(parts, tiles[part][slot])
    for slot in range(far):
        parts = stacked_parts(scale[pl.ds(far_at[slot], 1), :])
        far_out[slot : slot + 1] = jnp.sum(row_product(parts, tiles[len(near)][slot]), axis=0, keepdims=True)
    for block in range(out.shape[0]):
        out[block : block + 1] = jnp.sum(total[block], axis=0, keepdims=True)


def row_sums(tables, far_at, mine, theirs, mass, other_mass, tiles, sources):
    near = tuple(t.shape[0] for t in tiles[:-1])
    far, nodes = tiles[-1].shape[0], tiles[-1].shape[2] // 2
    width = tiles[-1].shape[1]
    return pl.pallas_call(
        functools.partial(row_kernel, near, far),
        out_shape=(
            jax.ShapeDtypeStruct((sources, width), jnp.float32),
            jax.ShapeDtypeStruct((far, width), jnp.float32),
        ),
        in_specs=[SMEM] * (1 + len(tables)) + [VMEM] * (4 + len(tiles)),
        out_specs=(VMEM, VMEM),
        scratch_shapes=[
            pltpu.VMEM((mine.shape[0] + 8, nodes), jnp.float32),
            pltpu.VMEM((sources + 1, 8, width), jnp.float32),
        ],
        cost_estimate=pl.CostEstimate(
            flops=sum(t.size for t in tiles) * 16, bytes_accessed=sum(t.size for t in tiles) * 2, transcendentals=0
        ),
        compiler_params=pltpu.CompilerParams(vmem_limit_bytes=16 << 20),
        name="row_sums",
    )(*tables, far_at, mine, theirs, mass, other_mass, *tiles)


def after(x, *others):
    return lax.optimization_barrier((x, *others))[0]


def local(source_emb, target_emb, source_mass, target_mass, cand_device, cand_block):
    dev_count = lax.axis_size("dev")
    group_count = lax.axis_size("group")
    chips = dev_count // 2
    sb, tb = source_emb.shape[0], target_emb.shape[0]
    near = cand_device.shape[1]
    slot_cap = (near * sb + dev_count - 1) // dev_count + 1
    steps = chips // 2
    ring = list(range(0, chips, 2)) + list(range(chips - 1, 0, -2))

    def around(x, by):
        pairs = [
            (2 * ring[i] + core, 2 * ring[(i + by) % chips] + core) for i in range(chips) for core in range(2)
        ]
        return lax.ppermute(x, "dev", pairs)

    def across(x, bit):
        return lax.ppermute(x, "dev", [(i, i ^ bit) for i in range(dev_count)])

    def to_group(x, by, bit=0):
        pairs = [
            (g * dev_count + i, (g + by) % group_count * dev_count + (i ^ bit))
            for g in range(group_count)
            for i in range(dev_count)
        ]
        return lax.ppermute(x, ("group", "dev"), pairs)

    device = lax.axis_index("dev").astype(jnp.int32)
    me = device.reshape(1)
    chip = device // 2

    def own_rows(x, bit=0):
        return lax.dynamic_slice_in_dim(x, ((device ^ bit) // 2) * sb, sb, 0)

    def add_rows(x, part, bit=0):
        return lax.dynamic_update_slice_in_dim(x, own_rows(x, bit) + part, ((device ^ bit) // 2) * sb, 0)

    upper, lower = pack(source_emb, source_mass, cand_device, cand_block)
    up_a, up_b, down_a, down_b = upper, lower, upper, lower
    tiles, tables, chain = [], [], ()
    build = functools.partial(build_tiles, me, sb=sb, near=near, chips=chips)

    def add(chunks, chain, back=None):
        tile, table, *chain = build(
            [x for up, low, _ in chunks for x in (up, low)],
            weights,
            slots=slot_cap,
            offsets=tuple(offset for _, _, offset in chunks),
            chain=chain,
            back=back,
        )
        tiles.append(tile)
        tables.append(table)
        return chain

    waiting = []
    for step in range(1, steps + 1):
        if step == 2:
            own_weight = target_operand(target_emb)
            up_a, down_b, own_weight = lax.optimization_barrier((up_a, down_b, own_weight))
        if step == 3:
            sibling_weight = target_operand(sibling_emb)
            up_a, down_b, sibling_weight = lax.optimization_barrier((up_a, down_b, sibling_weight))
            weights = (own_weight, sibling_weight)
        if step > 3:
            chain = add(waiting.pop(0), chain)
            up_a, down_b, *chain = lax.optimization_barrier((up_a, down_b, *chain))
        up_a, down_b = around(up_a, 1), around(down_b, -1)
        if step == 1:
            sibling_emb = across(target_emb, 1)
            sibling_mass = across(target_mass, 1)
            far_upper = to_group(upper, 1)
            far_lower = to_group(lower, 1)
        if step == 3:
            chain = add([(upper, lower, 0)], chain)
            far_tiles, far_at, far_sums, far_mass = build((far_upper, far_lower), (own_weight,), slots=sb)
            up_b, down_a, *chain = lax.optimization_barrier((up_b, down_a, *chain, far_sums))
            far_sums = chain.pop()
            from_far = to_group(far_sums, -1)
        if step < steps:
            up_b, down_a = around(up_b, 1), around(down_a, -1)
            waiting.append([(up_a, up_b, -step), (down_a, down_b, step)])
    for chunks in waiting:
        chain = add(chunks, chain)
    near_rows, all_mass = add([(up_a, down_b, steps)], chain, from_far)
    tiles.append(far_tiles)

    last = dev_count // 2
    for sweep in range(ITERS):
        if sweep > 0:
            near_rows, far_rows = row_sums(
                tables, far_at, mine, theirs, target_mass, sibling_mass, tiles, chips * sb
            )
            to_own, to_next = to_group(far_rows, -1), to_group(far_rows, -1, 2)
        bit = 2
        while bit < dev_count:
            if bit == last:
                far_rows = to_group(own_rows(near_rows), 1)
                far_rows = far_rows + to_group(own_rows(near_rows, last), 1, last)
            near_rows = near_rows + across(near_rows, bit)
            if sweep > 0 and bit == 2:
                near_rows = add_rows(add_rows(near_rows, to_own), to_next, 2)
            bit *= 2
        mine, src_scale = column_sums(
            me, tables, far_at, near_rows, all_mass, far_rows, far_mass, tiles, 2 * tb
        )
        theirs = across(mine, 1)
    tgt_scale = target_mass / (dustbin + mine[:tb] + theirs[tb:])
    return (src_scale, tgt_scale)


def solution(mesh):
    placed = (
        P(("group", "dev"), None, None),
        P(("group", "dev"), None, None),
        P(("group", "dev"), None),
        P(("group", "dev"), None),
        P(("group", "dev"), None),
        P(("group", "dev"), None),
    )
    return jax.shard_map(
        local,
        mesh=mesh,
        in_specs=placed,
        out_specs=(P(("group", "dev"), None), P(("group", "dev"), None)),
        check_vma=False,
    )
```

time: 181 us -> 113 us (0.62)
  waiting for transfers between devices: 56.5 us -> 24 us
  local copies, waits for them, and re-layouts: 41.8 us -> 20.6 us
  other arithmetic: 19.7 us -> 0.66 us
  starting transfers between devices: 25.6 us -> 38.2 us
  between operations: 10.7 us -> 0.96 us
  Pallas kernels: 25.7 us -> 27.7 us
    ppermute x14, waiting for transfers between devices: 26 us -> 4.88 us  [around(): return lax.ppermute(x, 'dev', pairs)]
    ppermute x10, waiting for transfers between devices: 23.5 us -> 9.5 us  [across(): return lax.ppermute(x, 'dev', [(i, i ^ bit) for i in range(dev_count)])]
    reduce_sum x32 -> x0, local copies, waits for them, and re-layouts: 9.51 us -> none  [the longest x16 6.92 us: tables_of(): loc = jnp.sum(chosen * order[None, None, :], axis=2)]
    gt x16 -> x0, local copies, waits for them, and re-layouts: 9.37 us -> none  [tables_of(): rows_at = jnp.where(filled > 0, chip_index * sb + loc, chips * sb)]
    ppermute x6 -> x9, starting transfers between devices: 5.45 us -> 13.1 us  [to_group(): return lax.ppermute(x, ('group', 'dev'), pairs)]
    unnamed x69 -> x68, local copies, waits for them, and re-layouts: 14.7 us -> 20.6 us
    ppermute x10, starting transfers between devices: 4.97 us -> 10.3 us  [across(): return lax.ppermute(x, 'dev', [(i, i ^ bit) for i in range(dev_count)])]
    pallas_call x8 -> x9, Pallas kernels: 14.2 us -> 19.4 us  [the longest x6 15.2 us: build_tiles(): pl.pallas_call(functools.partial(tile_kernel, plan), out_shape=(jax.Shape...]
  transfers between devices with their start and end apart: 30 -> 33, of which waited for: 17 -> 16; matrix products, arithmetic and copies ran while one was open for 26% -> 0% of each run, Pallas kernels for 7% -> 17%
where the time goes in v2:
time: 113 us; the launch traced here: 112 us
  starting transfers between devices  38.2 us (34%)
  Pallas kernels  27.7 us (25%)
  waiting for transfers between devices  24 us (21%)
  local copies, waits for them, and re-layouts  20.6 us (18%)
    unnamed x68, local copies, waits for them, and re-layouts  20.6 us
    pallas_call x6, Pallas kernels, build_tiles(): pl.pallas_call(functools.partial(tile_kernel, plan), out_shape=(jax.Shape...  15.2 us
    ppermute x14, starting transfers between devices, around(): return lax.ppermute(x, 'dev', pairs)  14.8 us
    ppermute x9, starting transfers between devices, to_group(): return lax.ppermute(x, ('group', 'dev'), pairs)  13.1 us
    ppermute x10, starting transfers between devices, across(): return lax.ppermute(x, 'dev', [(i, i ^ bit) for i in range(dev_count)])  10.3 us
    ppermute x9, waiting for transfers between devices, to_group(): return lax.ppermute(x, ('group', 'dev'), pairs)  9.58 us
    ppermute x10, waiting for transfers between devices, across(): return lax.ppermute(x, 'dev', [(i, i ^ bit) for i in range(dev_count)])  9.5 us
    pallas_call x2, Pallas kernels, target_operand(): pl.pallas_call(target_kernel, out_shape=jax.ShapeDtypeStruct((blocks, wid...  6.1 us
  transfers between devices with their start and end apart: 33, of which 16 were waited for; matrix products, arithmetic and copies ran while one was open for 0% of the time, Pallas kernels for 17%

profile of v2, /device:TPU:0, one launch (start us, length us, event | category | flops | bytes accessed | tf_op | source)
XLA Modules:
  0.0 112.1 jit_solution(6086008831554900145)
XLA Ops:
  0.6 0.5 collective-permute-start.4
  1.2 1.0 copy-done.21
  2.2 0.7 copy-done.31
  2.9 0.7 copy-done.32
  3.6 0.7 copy-done.33
  4.4 2.6 %collective-permute-start = (f32[520,128]{1,0:T(8,128)S(1)}, f32[520,128]{1,0:T(8,128)S(1)}, u32[]{:S(2)}, u32[]{:S(2)}) collective-permute-start(f32[520,128]{1,0:T(8,128)S(1)} %get-tuple-element.48.refs_1_), channel_id=1, source_target_pairs={{0,4},{1,5},{4,8},{5,9},{8,12},{9,13},{12,14},{13,15},{14,10},{15,... | collective-permute-start | bytes 798728 | tf_op jit(solution)/shard_map/ppermute | solution.py:345
  6.9 2.0 %collective-permute-start.5 = (f32[520,128]{1,0:T(8,128)S(1)}, f32[520,128]{1,0:T(8,128)S(1)}, u32[]{:S(2)}, u32[]{:S(2)}) collective-permute-start(f32[520,128]{1,0:T(8,128)S(1)} %get-tuple-element.49.refs_2_), channel_id=1, source_target_pairs={{0,4},{1,5},{4,8},{5,9},{8,12},{9,13},{12,14},{13,15},{14,10},{15,... | collective-permute-start | bytes 798728 | tf_op jit(solution)/shard_map/ppermute | solution.py:345
  9.0 1.6 %copy-done.20 = f32[32,128,128]{2,1,0:T(8,128)S(1)} copy-done((f32[32,128,128]{2,1,0:T(8,128)S(1)}, f32[32,128,128]{2,1,0:T(8,128)}, u32[]{:S(2)}) %copy-start.20) | copy-done | bytes 2097176
  10.6 3.0 %target_operand.2.refs_3_.refs_5_ = bf16[32,128,256]{2,1,0:T(8,128)(2,1)S(1)} custom-call(f32[32,128,128]{2,1,0:T(8,128)S(1)} %copy-done.20), custom_call_target="tpu_custom_call" | custom-call | bytes 6291456 | tf_op jit(solution)/shard_map/target_operand/pallas_call | solution.py:65
  14.1 2.1 %collective-permute-done.1.refs_4_ = f32[520,128]{1,0:T(8,128)S(1)} collective-permute-done((f32[520,128]{1,0:T(8,128)S(1)}, f32[520,128]{1,0:T(8,128)S(1)}, u32[]{:S(2)}, u32[]{:S(2)}) %collective-permute-start.1) | collective-permute-done | bytes 266272 | tf_op jit(solution)/shard_map/ppermute | solution.py:345
  16.2 1.6 %collective-permute-start.2 = (f32[520,128]{1,0:T(8,128)S(1)}, f32[520,128]{1,0:T(8,128)}, u32[]{:S(2)}, u32[]{:S(2)}) collective-permute-start(f32[520,128]{1,0:T(8,128)S(1)} %collective-permute-done.refs_1_), channel_id=1, source_target_pairs={{0,4},{1,5},{4,8},{5,9},{8,12},{9,13},{12,14},{13,15},{14,10},{15,... | collective-permute-start | bytes 798728 | tf_op jit(solution)/shard_map/ppermute | solution.py:345
  17.8 0.7 copy-done.22
  18.9 0.7 copy-done.24
  19.8 2.0 %collective-permute-start.10 = (f32[520,128]{1,0:T(8,128)S(1)}, f32[520,128]{1,0:T(8,128)S(1)}, u32[]{:S(2)}, u32[]{:S(2)}) collective-permute-start(f32[520,128]{1,0:T(8,128)S(1)} %get-tuple-element.49.refs_2_), channel_id=1, source_target_pairs={{0,16},{1,17},{2,18},{3,19},{4,20},{5,21},{6,22},{7,23},{8,24},{9,... | collective-permute-start | bytes 798728 | tf_op jit(solution)/shard_map/ppermute | solution.py:356
  21.9 1.5 %collective-permute-start.9 = (f32[520,128]{1,0:T(8,128)S(1)}, f32[520,128]{1,0:T(8,128)}, u32[]{:S(2)}, u32[]{:S(2)}) collective-permute-start(f32[520,128]{1,0:T(8,128)S(1)} %get-tuple-element.48.refs_1_), channel_id=1, source_target_pairs={{0,16},{1,17},{2,18},{3,19},{4,20},{5,21},{6,22},{7,23},{8,24},{9,... | collective-permute-start | bytes 798728 | tf_op jit(solution)/shard_map/ppermute | solution.py:356
  23.4 2.0 %collective-permute-done.2.refs_1_ = f32[520,128]{1,0:T(8,128)} collective-permute-done((f32[520,128]{1,0:T(8,128)S(1)}, f32[520,128]{1,0:T(8,128)}, u32[]{:S(2)}, u32[]{:S(2)}) %collective-permute-start.2) | collective-permute-done | bytes 266272 | tf_op jit(solution)/shard_map/ppermute | solution.py:345
  25.4 1.8 %collective-permute-start.7 = (f32[520,128]{1,0:T(8,128)S(1)}, f32[520,128]{1,0:T(8,128)}, u32[]{:S(2)}, u32[]{:S(2)}) collective-permute-start(f32[520,128]{1,0:T(8,128)S(1)} %collective-permute-done.5.refs_2_), channel_id=1, source_target_pairs={{0,4},{1,5},{4,8},{5,9},{8,12},{9,13},{12,14},{13,15},{14,10},{15,... | collective-permute-start | bytes 798728 | tf_op jit(solution)/shard_map/ppermute | solution.py:345
  27.5 3.0 %target_operand.3.refs_4_.refs_6_ = bf16[32,128,256]{2,1,0:T(8,128)(2,1)S(1)} custom-call(f32[32,128,128]{2,1,0:T(8,128)S(1)} %collective-permute-done.4.emb_ref), custom_call_target="tpu_custom_call" | custom-call | bytes 6291456 | tf_op jit(solution)/shard_map/target_operand/pallas_call | solution.py:65
  30.5 1.4 %copy-done = bf16[32,128,256]{2,1,0:T(8,128)(2,1)} copy-done((bf16[32,128,256]{2,1,0:T(8,128)(2,1)}, bf16[32,128,256]{2,1,0:T(8,128)(2,1)S(1)}, u32[]{:S(2)}) %copy-start) | copy-done | bytes 2097176
  31.9 1.8 %collective-permute-start.11 = (f32[520,128]{1,0:T(8,128)}, f32[520,128]{1,0:T(8,128)}, u32[]{:S(2)}, u32[]{:S(2)}) collective-permute-start(f32[520,128]{1,0:T(8,128)} %collective-permute-done.2.refs_1_), channel_id=1, source_target_pairs={{0,4},{1,5},{4,8},{5,9},{8,12},{9,13},{12,14},{13,15},{14,10},{15,... | collective-permute-start | bytes 798728 | tf_op jit(solution)/shard_map/ppermute | solution.py:345
  33.9 2.5 %build_tiles.7 = (bf16[8,128,256]{2,1,0:T(8,128)(2,1)S(1)}, s32[8]{0:T(128)S(1)}, f32[8,128]{1,0:T(8,128)S(1)}, f32[8,128]{1,0:T(8,128)S(1)}) custom-call(s32[1]{0:T(128)} %bitcast.refs_0_, f32[520,128]{1,0:T(8,128)} %collective-permute-done.9.refs_1_, f32[520,128]{1,0:T(8,128)S(1)} %collective-permute-done.10.refs_2_, ...), custom_call_target="tpu_custom_call" | custom-call | flops 134217728 | bytes 2621440 | tf_op jit(solution)/shard_map/build_tiles/pallas_call | solution.py:206
  36.5 1.9 %build_tiles.6 = (bf16[10,128,256]{2,1,0:T(8,128)(2,1)S(1)}, s32[21]{0:T(128)S(1)}, f32[64,128]{1,0:T(8,128)S(1)}, f32[64,128]{1,0:T(8,128)S(1)}) custom-call(s32[1]{0:T(128)} %bitcast.refs_0_, f32[520,128]{1,0:T(8,128)S(1)} %get-tuple-element.48.refs_1_, f32[520,128]{1,0:T(8,128)S(1)} %get-tuple-element.49.refs_2_, ...), custom_call_target="tpu_custom_call" | custom-call | flops 167772160 | bytes 4849664 | tf_op jit(solution)/shard_map/build_tiles/pallas_call | solution.py:206
  38.4 0.8 copy-done.9
  39.3 1.8 %collective-permute-start.13 = (f32[520,128]{1,0:T(8,128)}, f32[520,128]{1,0:T(8,128)S(1)}, u32[]{:S(2)}, u32[]{:S(2)}) collective-permute-start(f32[520,128]{1,0:T(8,128)} %collective-permute-done.7.refs_2_), channel_id=1, source_target_pairs={{0,4},{1,5},{4,8},{5,9},{8,12},{9,13},{12,14},{13,15},{14,10},{15,... | collective-permute-start | bytes 798728 | tf_op jit(solution)/shard_map/ppermute | solution.py:345
  41.3 2.3 %build_tiles.8 = (bf16[20,128,256]{2,1,0:T(8,128)(2,1)S(1)}, s32[41]{0:T(128)S(1)}, f32[64,128]{1,0:T(8,128)S(1)}, f32[64,128]{1,0:T(8,128)S(1)}) custom-call(s32[1]{0:T(128)} %bitcast.refs_0_, f32[520,128]{1,0:T(8,128)S(1)} %copy-done.23, f32[520,128]{1,0:T(8,128)S(1)} %copy-done.27, f32[520,128]{1,0:T(8,128)S(1)} %copy-done.29, f32[520,128]{1,0:T(8,128)S(1)} %copy-done.25, ...), custom_call_target="tpu_custom_call" | custom-call | flops 335544320 | bytes 5505024 | tf_op jit(solution)/shard_map/build_tiles/pallas_call | solution.py:206
  43.6 1.9 %collective-permute-start.15 = (f32[520,128]{1,0:T(8,128)}, f32[520,128]{1,0:T(8,128)S(1)}, u32[]{:S(2)}, u32[]{:S(2)}) collective-permute-start(f32[520,128]{1,0:T(8,128)} %collective-permute-done.11.refs_1_), channel_id=1, source_target_pairs={{0,4},{1,5},{4,8},{5,9},{8,12},{9,13},{12,14},{13,15},{14,10},{15,... | collective-permute-start | bytes 798728 | tf_op jit(solution)/shard_map/ppermute | solution.py:345
  45.7 1.8 %collective-permute-start.17 = (f32[8,128]{1,0:T(8,128)S(1)}, f32[8,128]{1,0:T(8,128)S(1)}, u32[]{:S(2)}, u32[]{:S(2)}) collective-permute-start(f32[8,128]{1,0:T(8,128)S(1)} %get-tuple-element.77), channel_id=1, source_target_pairs={{0,16},{1,17},{2,18},{3,19},{4,20},{5,21},{6,22},{7,23},{8,24},{9,... | collective-permute-start | bytes 12296 | tf_op jit(solution)/shard_map/ppermute | solution.py:356
  47.4 3.4 %build_tiles.9 = (bf16[20,128,256]{2,1,0:T(8,128)(2,1)S(1)}, s32[41]{0:T(128)S(1)}, f32[64,128]{1,0:T(8,128)S(1)}, f32[64,128]{1,0:T(8,128)S(1)}) custom-call(s32[1]{0:T(128)} %bitcast.refs_0_, f32[520,128]{1,0:T(8,128)} %collective-permute-done.2.refs_1_, f32[520,128]{1,0:T(8,128)} %collective-permute-done.7.refs_2_, ...), custom_call_target="tpu_custom_call" | custom-call | flops 335544320 | bytes 5505024 | tf_op jit(solution)/shard_map/build_tiles/pallas_call | solution.py:206
  50.9 1.0 copy-done.2
  51.9 3.3 %build_tiles.10 = (bf16[20,128,256]{2,1,0:T(8,128)(2,1)S(1)}, s32[41]{0:T(128)S(1)}, f32[64,128]{1,0:T(8,128)S(1)}, f32[64,128]{1,0:T(8,128)S(1)}) custom-call(s32[1]{0:T(128)} %bitcast.refs_0_, f32[520,128]{1,0:T(8,128)} %collective-permute-done.11.refs_1_, f32[520,128]{1,0:T(8,128)S(1)} %collective-permute-done.13.refs_2_, ...), custom_call_target="tpu_custom_call" | custom-call | flops 335544320 | bytes 5505024 | tf_op jit(solution)/shard_map/build_tiles/pallas_call | solution.py:206
  55.2 1.1 copy-done.5
  56.3 1.9 %build_tiles.11 = (bf16[10,128,256]{2,1,0:T(8,128)(2,1)S(1)}, s32[21]{0:T(128)S(1)}, f32[64,128]{1,0:T(8,128)S(1)}, f32[64,128]{1,0:T(8,128)S(1)}) custom-call(s32[1]{0:T(128)} %bitcast.refs_0_, f32[520,128]{1,0:T(8,128)S(1)} %collective-permute-done.15.refs_1_, f32[520,128]{1,0:T(8,128)S(1)} %collective-permute-done.16.refs_2_, ...), custom_call_target="tpu_custom_call" | custom-call | flops 167772160 | bytes 4849664 | tf_op jit(solution)/shard_map/build_tiles/pallas_call | solution.py:206
  58.2 0.8 copy-done.12
  59.1 1.5 %collective-permute-start.18 = (f32[64,128]{1,0:T(8,128)S(1)}, f32[64,128]{1,0:T(8,128)S(1)}, u32[]{:S(2)}, u32[]{:S(2)}) collective-permute-start(f32[64,128]{1,0:T(8,128)S(1)} %get-tuple-element.80), channel_id=1, source_target_pairs={{0,2},{1,3},{2,0},{3,1},{4,6},{5,7},{6,4},{7,5},{8,10},{9,11},{10,... | collective-permute-start | bytes 98312 | tf_op jit(solution)/shard_map/ppermute | solution.py:348
  60.6 2.4 %collective-permute-done.18 = f32[64,128]{1,0:T(8,128)S(1)} collective-permute-done((f32[64,128]{1,0:T(8,128)S(1)}, f32[64,128]{1,0:T(8,128)S(1)}, u32[]{:S(2)}, u32[]{:S(2)}) %collective-permute-start.18) | collective-permute-done | bytes 32800 | tf_op jit(solution)/shard_map/ppermute | solution.py:348
  63.0 1.6 %collective-permute-start.19 = (f32[64,128]{1,0:T(8,128)S(1)}, f32[64,128]{1,0:T(8,128)S(1)}, u32[]{:S(2)}, u32[]{:S(2)}) collective-permute-start(f32[64,128]{1,0:T(8,128)S(1)} %add.56), channel_id=1, source_target_pairs={{0,4},{1,5},{2,6},{3,7},{4,0},{5,1},{6,2},{7,3},{8,12},{9,13},{10,... | collective-permute-start | bytes 98312 | tf_op jit(solution)/shard_map/ppermute | solution.py:348
  64.6 2.3 %collective-permute-done.19 = f32[64,128]{1,0:T(8,128)S(1)} collective-permute-done((f32[64,128]{1,0:T(8,128)S(1)}, f32[64,128]{1,0:T(8,128)S(1)}, u32[]{:S(2)}, u32[]{:S(2)}) %collective-permute-start.19) | collective-permute-done | bytes 32800 | tf_op jit(solution)/shard_map/ppermute | solution.py:348
  66.9 2.6 %collective-permute-start.20 = (f32[64,128]{1,0:T(8,128)S(1)}, f32[64,128]{1,0:T(8,128)S(1)}, u32[]{:S(2)}, u32[]{:S(2)}) collective-permute-start(f32[64,128]{1,0:T(8,128)S(1)} %add.57), channel_id=1, source_target_pairs={{0,8},{1,9},{2,10},{3,11},{4,12},{5,13},{6,14},{7,15},{8,0},{9,1},... | collective-permute-start | bytes 98312 | tf_op jit(solution)/shard_map/ppermute | solution.py:348
  70.0 1.3 %collective-permute-start.22 = (f32[8,128]{1,0:T(8,128)S(1)}, f32[8,128]{1,0:T(8,128)S(1)}, u32[]{:S(2)}, u32[]{:S(2)}) collective-permute-start(f32[8,128]{1,0:T(8,128)S(1)} %get-tuple-element.96), channel_id=1, source_target_pairs={{0,24},{1,25},{2,26},{3,27},{4,28},{5,29},{6,30},{7,31},{8,16},{9,... | collective-permute-start | bytes 12296 | tf_op jit(solution)/shard_map/ppermute | solution.py:356
  71.3 1.8 %collective-permute-done.21 = f32[8,128]{1,0:T(8,128)S(1)} collective-permute-done((f32[8,128]{1,0:T(8,128)S(1)}, f32[8,128]{1,0:T(8,128)S(1)}, u32[]{:S(2)}, u32[]{:S(2)}) %collective-permute-start.21) | collective-permute-done | bytes 4128 | tf_op jit(solution)/shard_map/ppermute | solution.py:356
  73.1 2.3 %collective-permute-done.22 = f32[8,128]{1,0:T(8,128)S(1)} collective-permute-done((f32[8,128]{1,0:T(8,128)S(1)}, f32[8,128]{1,0:T(8,128)S(1)}, u32[]{:S(2)}, u32[]{:S(2)}) %collective-permute-start.22) | collective-permute-done | bytes 4128 | tf_op jit(solution)/shard_map/ppermute | solution.py:356
  75.4 1.3 %copy-done.3 = bf16[20,128,256]{2,1,0:T(8,128)(2,1)S(1)} copy-done((bf16[20,128,256]{2,1,0:T(8,128)(2,1)S(1)}, bf16[20,128,256]{2,1,0:T(8,128)(2,1)}, u32[]{:S(2)}) %copy-start.3) | copy-done | bytes 1310744
  76.7 1.3 %copy-done.6 = bf16[20,128,256]{2,1,0:T(8,128)(2,1)S(1)} copy-done((bf16[20,128,256]{2,1,0:T(8,128)(2,1)S(1)}, bf16[20,128,256]{2,1,0:T(8,128)(2,1)}, u32[]{:S(2)}) %copy-start.6) | copy-done | bytes 1310744
  78.1 1.1 copy-done.10
  79.1 1.1 copy-done.13
  80.2 1.0 copy-done.17
  81.3 2.1 %column_sums.2 = (f32[64,128]{1,0:T(8,128)S(1)}, f32[8,128]{1,0:T(8,128)}) custom-call(s32[1]{0:T(128)} %bitcast.refs_0_, s32[21]{0:T(128)S(1)} %get-tuple-element.54.refs_1_.refs_0_, s32[41]{0:T(128)S(1)} %get-tuple-element.60.refs_2_.refs_1_, s32[41]{0:T(128)S(1)} %get-tuple-element.67.refs_3_.refs_2_, s32[41]{0:T(128)S(1)} %get-tuple-element.72.refs_4_.refs_3_, ...), custom_call_target="tpu_custom_call" | custom-call | flops 46137344 | bytes 5767168 | tf_op jit(solution)/shard_map/column_sums/pallas_call | solution.py:261
  83.4 0.5 collective-permute-start.24
  83.9 0.8 collective-permute-done.24.refs_9_
  84.7 2.2 %row_sums.1 = (f32[64,128]{1,0:T(8,128)S(1)}, f32[8,128]{1,0:T(8,128)S(1)}) custom-call(s32[21]{0:T(128)S(1)} %get-tuple-element.54.refs_1_.refs_0_, s32[41]{0:T(128)S(1)} %get-tuple-element.60.refs_2_.refs_1_, s32[41]{0:T(128)S(1)} %get-tuple-element.67.refs_3_.refs_2_, s32[41]{0:T(128)S(1)} %get-tuple-element.72.refs_4_.refs_3_, ...), custom_call_target="tpu_custom_call" | custom-call | flops 46137344 | bytes 5767168 | tf_op jit(solution)/shard_map/row_sums/pallas_call | solution.py:307
  87.0 1.6 %collective-permute-start.25 = (f32[64,128]{1,0:T(8,128)S(1)}, f32[64,128]{1,0:T(8,128)S(1)}, u32[]{:S(2)}, u32[]{:S(2)}) collective-permute-start(f32[64,128]{1,0:T(8,128)S(1)} %get-tuple-element.90), channel_id=1, source_target_pairs={{0,2},{1,3},{2,0},{3,1},{4,6},{5,7},{6,4},{7,5},{8,10},{9,11},{10,... | collective-permute-start | bytes 98312 | tf_op jit(solution)/shard_map/ppermute | solution.py:348
  88.5 1.5 %collective-permute-start.26 = (f32[8,128]{1,0:T(8,128)S(1)}, f32[8,128]{1,0:T(8,128)S(1)}, u32[]{:S(2)}, u32[]{:S(2)}) collective-permute-start(f32[8,128]{1,0:T(8,128)S(1)} %get-tuple-element.91), channel_id=1, source_target_pairs={{0,16},{1,17},{2,18},{3,19},{4,20},{5,21},{6,22},{7,23},{8,24},{9,... | collective-permute-start | bytes 12296 | tf_op jit(solution)/shard_map/ppermute | solution.py:356
  91.0 1.2 %collective-permute-done.26 = f32[8,128]{1,0:T(8,128)S(1)} collective-permute-done((f32[8,128]{1,0:T(8,128)S(1)}, f32[8,128]{1,0:T(8,128)S(1)}, u32[]{:S(2)}, u32[]{:S(2)}) %collective-permute-start.26) | collective-permute-done | bytes 4128 | tf_op jit(solution)/shard_map/ppermute | solution.py:356
  92.1 2.4 %collective-permute-done.27 = f32[8,128]{1,0:T(8,128)S(1)} collective-permute-done((f32[8,128]{1,0:T(8,128)S(1)}, f32[8,128]{1,0:T(8,128)S(1)}, u32[]{:S(2)}, u32[]{:S(2)}) %collective-permute-start.27) | collective-permute-done | bytes 4128 | tf_op jit(solution)/shard_map/ppermute | solution.py:356
  94.5 1.7 %collective-permute-start.28 = (f32[64,128]{1,0:T(8,128)S(1)}, f32[64,128]{1,0:T(8,128)S(1)}, u32[]{:S(2)}, u32[]{:S(2)}) collective-permute-start(f32[64,128]{1,0:T(8,128)S(1)} %add_dynamic-update-slice_fusion), channel_id=1, source_target_pairs={{0,4},{1,5},{2,6},{3,7},{4,0},{5,1},{6,2},{7,3},{8,12},{9,13},{10,... | collective-permute-start | bytes 98312 | tf_op jit(solution)/shard_map/ppermute | solution.py:348
  96.2 2.3 %collective-permute-done.28 = f32[64,128]{1,0:T(8,128)S(1)} collective-permute-done((f32[64,128]{1,0:T(8,128)S(1)}, f32[64,128]{1,0:T(8,128)S(1)}, u32[]{:S(2)}, u32[]{:S(2)}) %collective-permute-start.28) | collective-permute-done | bytes 32800 | tf_op jit(solution)/shard_map/ppermute | solution.py:348
  99.3 3.5 %collective-permute-start.31 = (f32[8,128]{1,0:T(8,128)S(1)}, f32[8,128]{1,0:T(8,128)S(1)}, u32[]{:S(2)}, u32[]{:S(2)}) collective-permute-start(f32[8,128]{1,0:T(8,128)S(1)} %get-tuple-element.94), channel_id=1, source_target_pairs={{0,24},{1,25},{2,26},{3,27},{4,28},{5,29},{6,30},{7,31},{8,16},{9,... | collective-permute-start | bytes 12296 | tf_op jit(solution)/shard_map/ppermute | solution.py:356
  102.9 1.9 %collective-permute-done.31 = f32[8,128]{1,0:T(8,128)S(1)} collective-permute-done((f32[8,128]{1,0:T(8,128)S(1)}, f32[8,128]{1,0:T(8,128)S(1)}, u32[]{:S(2)}, u32[]{:S(2)}) %collective-permute-start.31) | collective-permute-done | bytes 4128 | tf_op jit(solution)/shard_map/ppermute | solution.py:356
  104.8 1.3 %copy-done.8 = bf16[20,128,256]{2,1,0:T(8,128)(2,1)S(1)} copy-done((bf16[20,128,256]{2,1,0:T(8,128)(2,1)S(1)}, bf16[20,128,256]{2,1,0:T(8,128)(2,1)}, u32[]{:S(2)}) %copy-start.8) | copy-done | bytes 1310744
  106.1 1.1 copy-done.15
  107.2 1.0 copy-done.19
  108.2 2.0 %column_sums.3 = (f32[64,128]{1,0:T(8,128)S(1)}, f32[8,128]{1,0:T(8,128)}) custom-call(s32[1]{0:T(128)} %bitcast.refs_0_, s32[21]{0:T(128)S(1)} %get-tuple-element.54.refs_1_.refs_0_, s32[41]{0:T(128)S(1)} %get-tuple-element.60.refs_2_.refs_1_, s32[41]{0:T(128)S(1)} %get-tuple-element.67.refs_3_.refs_2_, s32[41]{0:T(128)S(1)} %get-tuple-element.72.refs_4_.refs_3_, ...), custom_call_target="tpu_custom_call" | custom-call | flops 46137344 | bytes 5767168 | tf_op jit(solution)/shard_map/column_sums/pallas_call | solution.py:261
  110.2 1.2 %collective-permute-done.32 = f32[64,128]{1,0:T(8,128)S(1)} collective-permute-done((f32[64,128]{1,0:T(8,128)S(1)}, f32[64,128]{1,0:T(8,128)S(1)}, u32[]{:S(2)}, u32[]{:S(2)}) %collective-permute-start.32) | collective-permute-done | bytes 32800 | tf_op jit(solution)/shard_map/ppermute | solution.py:348
  111.5 0.6 fusion
  (95 shorter events, 4.6 us)
Async XLA Ops:
  0.6 26.6 %collective-permute-start.4 = (f32[32,128,128]{2,1,0:T(8,128)}, f32[32,128,128]{2,1,0:T(8,128)S(1)}, u32[]{:S(2)}, u32[]{:S(2)}) collective-permute-start(f32[32,128,128]{2,1,0:T(8,128)} %emb_ref.1), channel_id=1, source_target_pairs={{0,1},{1,0},{2,3},{3,2},{4,5},{5,4},{6,7},{7,6},{8,9},{9,8},{10,11... | collective-permute-start | bytes 6291464 | tf_op jit(solution)/shard_map/ppermute | solution.py:348
  1.1 1.0 copy-start.21
  2.2 0.7 copy-start.31
  4.4 9.7 %collective-permute-start = (f32[520,128]{1,0:T(8,128)S(1)}, f32[520,128]{1,0:T(8,128)S(1)}, u32[]{:S(2)}, u32[]{:S(2)}) collective-permute-start(f32[520,128]{1,0:T(8,128)S(1)} %get-tuple-element.48.refs_1_), channel_id=1, source_target_pairs={{0,4},{1,5},{4,8},{5,9},{8,12},{9,13},{12,14},{13,15},{14,10},{15,... | collective-permute-start | bytes 798728 | tf_op jit(solution)/shard_map/ppermute | solution.py:345
  6.9 9.2 %collective-permute-start.1 = (f32[520,128]{1,0:T(8,128)S(1)}, f32[520,128]{1,0:T(8,128)S(1)}, u32[]{:S(2)}, u32[]{:S(2)}) collective-permute-start(f32[520,128]{1,0:T(8,128)S(1)} %get-tuple-element.49.refs_2_), channel_id=1, source_target_pairs={{0,2},{1,3},{4,0},{5,1},{8,4},{9,5},{12,8},{13,9},{14,12},{15,13},... | collective-permute-start | bytes 798728 | tf_op jit(solution)/shard_map/ppermute | solution.py:345
  6.9 12.9 %collective-permute-start.5 = (f32[520,128]{1,0:T(8,128)S(1)}, f32[520,128]{1,0:T(8,128)S(1)}, u32[]{:S(2)}, u32[]{:S(2)}) collective-permute-start(f32[520,128]{1,0:T(8,128)S(1)} %get-tuple-element.49.refs_2_), channel_id=1, source_target_pairs={{0,4},{1,5},{4,8},{5,9},{8,12},{9,13},{12,14},{13,15},{14,10},{15,... | collective-permute-start | bytes 798728 | tf_op jit(solution)/shard_map/ppermute | solution.py:345
  9.0 12.9 %collective-permute-start.6 = (f32[520,128]{1,0:T(8,128)S(1)}, f32[520,128]{1,0:T(8,128)S(1)}, u32[]{:S(2)}, u32[]{:S(2)}) collective-permute-start(f32[520,128]{1,0:T(8,128)S(1)} %get-tuple-element.48.refs_1_), channel_id=1, source_target_pairs={{0,2},{1,3},{4,0},{5,1},{8,4},{9,5},{12,8},{13,9},{14,12},{15,13},... | collective-permute-start | bytes 798728 | tf_op jit(solution)/shard_map/ppermute | solution.py:345
  9.0 1.6 %copy-start.20 = (f32[32,128,128]{2,1,0:T(8,128)S(1)}, f32[32,128,128]{2,1,0:T(8,128)}, u32[]{:S(2)}) copy-start(f32[32,128,128]{2,1,0:T(8,128)} %emb_ref.1) | copy-start | bytes 6291460
  16.2 9.3 %collective-permute-start.2 = (f32[520,128]{1,0:T(8,128)S(1)}, f32[520,128]{1,0:T(8,128)}, u32[]{:S(2)}, u32[]{:S(2)}) collective-permute-start(f32[520,128]{1,0:T(8,128)S(1)} %collective-permute-done.refs_1_), channel_id=1, source_target_pairs={{0,4},{1,5},{4,8},{5,9},{8,12},{9,13},{12,14},{13,15},{14,10},{15,... | collective-permute-start | bytes 798728 | tf_op jit(solution)/shard_map/ppermute | solution.py:345
  18.4 13.5 %collective-permute-start.3 = (f32[520,128]{1,0:T(8,128)S(1)}, f32[520,128]{1,0:T(8,128)}, u32[]{:S(2)}, u32[]{:S(2)}) collective-permute-start(f32[520,128]{1,0:T(8,128)S(1)} %collective-permute-done.1.refs_4_), channel_id=1, source_target_pairs={{0,2},{1,3},{4,0},{5,1},{8,4},{9,5},{12,8},{13,9},{14,12},{15,13},... | collective-permute-start | bytes 798728 | tf_op jit(solution)/shard_map/ppermute | solution.py:345
  18.9 0.7 copy-start.24
  19.8 10.7 %copy-start.26 = (f32[520,128]{1,0:T(8,128)}, f32[520,128]{1,0:T(8,128)S(1)}, u32[]{:S(2)}) copy-start(f32[520,128]{1,0:T(8,128)S(1)} %collective-permute-done.5.refs_2_) | copy-start | bytes 798724
  19.8 13.9 %collective-permute-start.10 = (f32[520,128]{1,0:T(8,128)S(1)}, f32[520,128]{1,0:T(8,128)S(1)}, u32[]{:S(2)}, u32[]{:S(2)}) collective-permute-start(f32[520,128]{1,0:T(8,128)S(1)} %get-tuple-element.49.refs_2_), channel_id=1, source_target_pairs={{0,16},{1,17},{2,18},{3,19},{4,20},{5,21},{6,22},{7,23},{8,24},{9,... | collective-permute-start | bytes 798728 | tf_op jit(solution)/shard_map/ppermute | solution.py:356
  21.9 8.6 %copy-start.28 = (f32[520,128]{1,0:T(8,128)}, f32[520,128]{1,0:T(8,128)S(1)}, u32[]{:S(2)}) copy-start(f32[520,128]{1,0:T(8,128)S(1)} %collective-permute-done.6.refs_3_) | copy-start | bytes 798724
  21.9 12.1 %collective-permute-start.9 = (f32[520,128]{1,0:T(8,128)S(1)}, f32[520,128]{1,0:T(8,128)}, u32[]{:S(2)}, u32[]{:S(2)}) collective-permute-start(f32[520,128]{1,0:T(8,128)S(1)} %get-tuple-element.48.refs_1_), channel_id=1, source_target_pairs={{0,16},{1,17},{2,18},{3,19},{4,20},{5,21},{6,22},{7,23},{8,24},{9,... | collective-permute-start | bytes 798728 | tf_op jit(solution)/shard_map/ppermute | solution.py:356
  25.4 13.8 %collective-permute-start.7 = (f32[520,128]{1,0:T(8,128)S(1)}, f32[520,128]{1,0:T(8,128)}, u32[]{:S(2)}, u32[]{:S(2)}) collective-permute-start(f32[520,128]{1,0:T(8,128)S(1)} %collective-permute-done.5.refs_2_), channel_id=1, source_target_pairs={{0,4},{1,5},{4,8},{5,9},{8,12},{9,13},{12,14},{13,15},{14,10},{15,... | collective-permute-start | bytes 798728 | tf_op jit(solution)/shard_map/ppermute | solution.py:345
  27.3 12.0 %collective-permute-start.8 = (f32[520,128]{1,0:T(8,128)S(1)}, f32[520,128]{1,0:T(8,128)}, u32[]{:S(2)}, u32[]{:S(2)}) collective-permute-start(f32[520,128]{1,0:T(8,128)S(1)} %collective-permute-done.6.refs_3_), channel_id=1, source_target_pairs={{0,2},{1,3},{4,0},{5,1},{8,4},{9,5},{12,8},{13,9},{14,12},{15,13},... | collective-permute-start | bytes 798728 | tf_op jit(solution)/shard_map/ppermute | solution.py:345
  30.5 1.4 %copy-start = (bf16[32,128,256]{2,1,0:T(8,128)(2,1)}, bf16[32,128,256]{2,1,0:T(8,128)(2,1)S(1)}, u32[]{:S(2)}) copy-start(bf16[32,128,256]{2,1,0:T(8,128)(2,1)S(1)} %target_operand.3.refs_4_.refs_6_) | copy-start | bytes 6291460
  31.9 11.7 %collective-permute-start.11 = (f32[520,128]{1,0:T(8,128)}, f32[520,128]{1,0:T(8,128)}, u32[]{:S(2)}, u32[]{:S(2)}) collective-permute-start(f32[520,128]{1,0:T(8,128)} %collective-permute-done.2.refs_1_), channel_id=1, source_target_pairs={{0,4},{1,5},{4,8},{5,9},{8,12},{9,13},{12,14},{13,15},{14,10},{15,... | collective-permute-start | bytes 798728 | tf_op jit(solution)/shard_map/ppermute | solution.py:345
  33.7 9.8 %collective-permute-start.12 = (f32[520,128]{1,0:T(8,128)}, f32[520,128]{1,0:T(8,128)}, u32[]{:S(2)}, u32[]{:S(2)}) collective-permute-start(f32[520,128]{1,0:T(8,128)} %collective-permute-done.3.refs_4_), channel_id=1, source_target_pairs={{0,2},{1,3},{4,0},{5,1},{8,4},{9,5},{12,8},{13,9},{14,12},{15,13},... | collective-permute-start | bytes 798728 | tf_op jit(solution)/shard_map/ppermute | solution.py:345
  33.9 2.5 %copy-start.1 = (bf16[32,128,256]{2,1,0:T(8,128)(2,1)S(1)}, bf16[32,128,256]{2,1,0:T(8,128)(2,1)}, u32[]{:S(2)}) copy-start(bf16[32,128,256]{2,1,0:T(8,128)(2,1)} %copy-done) | copy-start | bytes 6291460
  36.4 2.0 %copy-start.16 = (bf16[8,128,256]{2,1,0:T(8,128)(2,1)}, bf16[8,128,256]{2,1,0:T(8,128)(2,1)S(1)}, u32[]{:S(2)}) copy-start(bf16[8,128,256]{2,1,0:T(8,128)(2,1)S(1)} %get-tuple-element.88.refs_16_.refs_15_) | copy-start | bytes 1572868
  36.4 4.8 %copy-start.23 = (f32[520,128]{1,0:T(8,128)S(1)}, f32[520,128]{1,0:T(8,128)}, u32[]{:S(2)}) copy-start(f32[520,128]{1,0:T(8,128)} %copy-done.22) | copy-start | bytes 798724
  36.4 4.8 %copy-start.25 = (f32[520,128]{1,0:T(8,128)S(1)}, f32[520,128]{1,0:T(8,128)}, u32[]{:S(2)}) copy-start(f32[520,128]{1,0:T(8,128)} %copy-done.24) | copy-start | bytes 798724
  36.5 4.8 %copy-start.27 = (f32[520,128]{1,0:T(8,128)S(1)}, f32[520,128]{1,0:T(8,128)}, u32[]{:S(2)}) copy-start(f32[520,128]{1,0:T(8,128)} %copy-done.26) | copy-start | bytes 798724
  36.5 4.8 %copy-start.29 = (f32[520,128]{1,0:T(8,128)S(1)}, f32[520,128]{1,0:T(8,128)}, u32[]{:S(2)}) copy-start(f32[520,128]{1,0:T(8,128)} %copy-done.28) | copy-start | bytes 798724
  38.4 0.8 copy-start.9
  39.3 12.7 %collective-permute-start.13 = (f32[520,128]{1,0:T(8,128)}, f32[520,128]{1,0:T(8,128)S(1)}, u32[]{:S(2)}, u32[]{:S(2)}) collective-permute-start(f32[520,128]{1,0:T(8,128)} %collective-permute-done.7.refs_2_), channel_id=1, source_target_pairs={{0,4},{1,5},{4,8},{5,9},{8,12},{9,13},{12,14},{13,15},{14,10},{15,... | collective-permute-start | bytes 798728 | tf_op jit(solution)/shard_map/ppermute | solution.py:345
  41.1 10.8 %collective-permute-start.14 = (f32[520,128]{1,0:T(8,128)}, f32[520,128]{1,0:T(8,128)S(1)}, u32[]{:S(2)}, u32[]{:S(2)}) collective-permute-start(f32[520,128]{1,0:T(8,128)} %collective-permute-done.8.refs_3_), channel_id=1, source_target_pairs={{0,2},{1,3},{4,0},{5,1},{8,4},{9,5},{12,8},{13,9},{14,12},{15,13},... | collective-permute-start | bytes 798728 | tf_op jit(solution)/shard_map/ppermute | solution.py:345
  43.6 12.7 %collective-permute-start.15 = (f32[520,128]{1,0:T(8,128)}, f32[520,128]{1,0:T(8,128)S(1)}, u32[]{:S(2)}, u32[]{:S(2)}) collective-permute-start(f32[520,128]{1,0:T(8,128)} %collective-permute-done.11.refs_1_), channel_id=1, source_target_pairs={{0,4},{1,5},{4,8},{5,9},{8,12},{9,13},{12,14},{13,15},{14,10},{15,... | collective-permute-start | bytes 798728 | tf_op jit(solution)/shard_map/ppermute | solution.py:345
  45.5 10.9 %collective-permute-start.16 = (f32[520,128]{1,0:T(8,128)}, f32[520,128]{1,0:T(8,128)S(1)}, u32[]{:S(2)}, u32[]{:S(2)}) collective-permute-start(f32[520,128]{1,0:T(8,128)} %collective-permute-done.12.refs_4_), channel_id=1, source_target_pairs={{0,2},{1,3},{4,0},{5,1},{8,4},{9,5},{12,8},{13,9},{14,12},{15,13},... | collective-permute-start | bytes 798728 | tf_op jit(solution)/shard_map/ppermute | solution.py:345
  45.7 10.6 %collective-permute-start.17 = (f32[8,128]{1,0:T(8,128)S(1)}, f32[8,128]{1,0:T(8,128)S(1)}, u32[]{:S(2)}, u32[]{:S(2)}) collective-permute-start(f32[8,128]{1,0:T(8,128)S(1)} %get-tuple-element.77), channel_id=1, source_target_pairs={{0,16},{1,17},{2,18},{3,19},{4,20},{5,21},{6,22},{7,23},{8,24},{9,... | collective-permute-start | bytes 12296 | tf_op jit(solution)/shard_map/ppermute | solution.py:356
  50.9 1.1 copy-start.2
  55.2 1.1 copy-start.5
  58.2 0.8 copy-start.12
  59.1 3.9 %collective-permute-start.18 = (f32[64,128]{1,0:T(8,128)S(1)}, f32[64,128]{1,0:T(8,128)S(1)}, u32[]{:S(2)}, u32[]{:S(2)}) collective-permute-start(f32[64,128]{1,0:T(8,128)S(1)} %get-tuple-element.80), channel_id=1, source_target_pairs={{0,2},{1,3},{2,0},{3,1},{4,6},{5,7},{6,4},{7,5},{8,10},{9,11},{10,... | collective-permute-start | bytes 98312 | tf_op jit(solution)/shard_map/ppermute | solution.py:348
  63.0 3.9 %collective-permute-start.19 = (f32[64,128]{1,0:T(8,128)S(1)}, f32[64,128]{1,0:T(8,128)S(1)}, u32[]{:S(2)}, u32[]{:S(2)}) collective-permute-start(f32[64,128]{1,0:T(8,128)S(1)} %add.56), channel_id=1, source_target_pairs={{0,4},{1,5},{2,6},{3,7},{4,0},{5,1},{6,2},{7,3},{8,12},{9,13},{10,... | collective-permute-start | bytes 98312 | tf_op jit(solution)/shard_map/ppermute | solution.py:348
  66.9 8.5 %collective-permute-start.20 = (f32[64,128]{1,0:T(8,128)S(1)}, f32[64,128]{1,0:T(8,128)S(1)}, u32[]{:S(2)}, u32[]{:S(2)}) collective-permute-start(f32[64,128]{1,0:T(8,128)S(1)} %add.57), channel_id=1, source_target_pairs={{0,8},{1,9},{2,10},{3,11},{4,12},{5,13},{6,14},{7,15},{8,0},{9,1},... | collective-permute-start | bytes 98312 | tf_op jit(solution)/shard_map/ppermute | solution.py:348
  69.5 3.6 %collective-permute-start.21 = (f32[8,128]{1,0:T(8,128)S(1)}, f32[8,128]{1,0:T(8,128)S(1)}, u32[]{:S(2)}, u32[]{:S(2)}) collective-permute-start(f32[8,128]{1,0:T(8,128)S(1)} %get-tuple-element.97), channel_id=1, source_target_pairs={{0,16},{1,17},{2,18},{3,19},{4,20},{5,21},{6,22},{7,23},{8,24},{9,... | collective-permute-start | bytes 12296 | tf_op jit(solution)/shard_map/ppermute | solution.py:356
  70.0 5.4 %collective-permute-start.22 = (f32[8,128]{1,0:T(8,128)S(1)}, f32[8,128]{1,0:T(8,128)S(1)}, u32[]{:S(2)}, u32[]{:S(2)}) collective-permute-start(f32[8,128]{1,0:T(8,128)S(1)} %get-tuple-element.96), channel_id=1, source_target_pairs={{0,24},{1,25},{2,26},{3,27},{4,28},{5,29},{6,30},{7,31},{8,16},{9,... | collective-permute-start | bytes 12296 | tf_op jit(solution)/shard_map/ppermute | solution.py:356
  75.4 1.3 %copy-start.3 = (bf16[20,128,256]{2,1,0:T(8,128)(2,1)S(1)}, bf16[20,128,256]{2,1,0:T(8,128)(2,1)}, u32[]{:S(2)}) copy-start(bf16[20,128,256]{2,1,0:T(8,128)(2,1)} %copy-done.2) | copy-start | bytes 3932164
  76.7 1.3 %copy-start.6 = (bf16[20,128,256]{2,1,0:T(8,128)(2,1)S(1)}, bf16[20,128,256]{2,1,0:T(8,128)(2,1)}, u32[]{:S(2)}) copy-start(bf16[20,128,256]{2,1,0:T(8,128)(2,1)} %copy-done.5) | copy-start | bytes 3932164
  78.1 1.1 copy-start.10
  79.1 1.1 copy-start.13
  80.2 1.0 copy-start.17
  81.3 2.1 %copy-start.30 = (f32[32,128]{1,0:T(8,128)S(1)}, f32[32,128]{1,0:T(8,128)}, u32[]{:S(2)}) copy-start(f32[32,128]{1,0:T(8,128)} %refs_8_.1) | copy-start | bytes 49156
  81.3 3.4 %copy-start.4 = (bf16[20,128,256]{2,1,0:T(8,128)(2,1)S(1)}, bf16[20,128,256]{2,1,0:T(8,128)(2,1)}, u32[]{:S(2)}) copy-start(bf16[20,128,256]{2,1,0:T(8,128)(2,1)} %copy-done.2) | copy-start | bytes 3932164
  81.3 3.4 %copy-start.7 = (bf16[20,128,256]{2,1,0:T(8,128)(2,1)S(1)}, bf16[20,128,256]{2,1,0:T(8,128)(2,1)}, u32[]{:S(2)}) copy-start(bf16[20,128,256]{2,1,0:T(8,128)(2,1)} %copy-done.5) | copy-start | bytes 3932164
  81.3 3.4 %copy-start.11 = (bf16[10,128,256]{2,1,0:T(8,128)(2,1)S(1)}, bf16[10,128,256]{2,1,0:T(8,128)(2,1)}, u32[]{:S(2)}) copy-start(bf16[10,128,256]{2,1,0:T(8,128)(2,1)} %copy-done.9) | copy-start | bytes 1966084
  81.3 3.4 %copy-start.14 = (bf16[10,128,256]{2,1,0:T(8,128)(2,1)S(1)}, bf16[10,128,256]{2,1,0:T(8,128)(2,1)}, u32[]{:S(2)}) copy-start(bf16[10,128,256]{2,1,0:T(8,128)(2,1)} %copy-done.12) | copy-start | bytes 1966084
  81.3 3.4 %copy-start.18 = (bf16[8,128,256]{2,1,0:T(8,128)(2,1)S(1)}, bf16[8,128,256]{2,1,0:T(8,128)(2,1)}, u32[]{:S(2)}) copy-start(bf16[8,128,256]{2,1,0:T(8,128)(2,1)} %copy-done.16) | copy-start | bytes 1572868
  83.4 1.4 %collective-permute-start.23 = (f32[64,128]{1,0:T(8,128)S(1)}, f32[64,128]{1,0:T(8,128)S(1)}, u32[]{:S(2)}, u32[]{:S(2)}) collective-permute-start(f32[64,128]{1,0:T(8,128)S(1)} %get-tuple-element.89.refs_6_), channel_id=1, source_target_pairs={{0,1},{1,0},{2,3},{3,2},{4,5},{5,4},{6,7},{7,6},{8,9},{9,8},{10,11... | collective-permute-start | bytes 98312 | tf_op jit(solution)/shard_map/ppermute | solution.py:348
  83.4 1.3 %collective-permute-start.24 = (f32[32,128]{1,0:T(8,128)S(1)}, f32[32,128]{1,0:T(8,128)S(1)}, u32[]{:S(2)}, u32[]{:S(2)}) collective-permute-start(f32[32,128]{1,0:T(8,128)S(1)} %copy-done.30), channel_id=1, source_target_pairs={{0,1},{1,0},{2,3},{3,2},{4,5},{5,4},{6,7},{7,6},{8,9},{9,8},{10,11... | collective-permute-start | bytes 49160 | tf_op jit(solution)/shard_map/ppermute | solution.py:348
  87.0 4.0 %collective-permute-start.25 = (f32[64,128]{1,0:T(8,128)S(1)}, f32[64,128]{1,0:T(8,128)S(1)}, u32[]{:S(2)}, u32[]{:S(2)}) collective-permute-start(f32[64,128]{1,0:T(8,128)S(1)} %get-tuple-element.90), channel_id=1, source_target_pairs={{0,2},{1,3},{2,0},{3,1},{4,6},{5,7},{6,4},{7,5},{8,10},{9,11},{10,... | collective-permute-start | bytes 98312 | tf_op jit(solution)/shard_map/ppermute | solution.py:348
  88.5 3.6 %collective-permute-start.26 = (f32[8,128]{1,0:T(8,128)S(1)}, f32[8,128]{1,0:T(8,128)S(1)}, u32[]{:S(2)}, u32[]{:S(2)}) collective-permute-start(f32[8,128]{1,0:T(8,128)S(1)} %get-tuple-element.91), channel_id=1, source_target_pairs={{0,16},{1,17},{2,18},{3,19},{4,20},{5,21},{6,22},{7,23},{8,24},{9,... | collective-permute-start | bytes 12296 | tf_op jit(solution)/shard_map/ppermute | solution.py:356
  90.0 4.5 %collective-permute-start.27 = (f32[8,128]{1,0:T(8,128)S(1)}, f32[8,128]{1,0:T(8,128)S(1)}, u32[]{:S(2)}, u32[]{:S(2)}) collective-permute-start(f32[8,128]{1,0:T(8,128)S(1)} %get-tuple-element.91), channel_id=1, source_target_pairs={{0,18},{1,19},{2,16},{3,17},{4,22},{5,23},{6,20},{7,21},{8,26},{9,... | collective-permute-start | bytes 12296 | tf_op jit(solution)/shard_map/ppermute | solution.py:356
  94.5 3.9 %collective-permute-start.28 = (f32[64,128]{1,0:T(8,128)S(1)}, f32[64,128]{1,0:T(8,128)S(1)}, u32[]{:S(2)}, u32[]{:S(2)}) collective-permute-start(f32[64,128]{1,0:T(8,128)S(1)} %add_dynamic-update-slice_fusion), channel_id=1, source_target_pairs={{0,4},{1,5},{2,6},{3,7},{4,0},{5,1},{6,2},{7,3},{8,12},{9,13},{10,... | collective-permute-start | bytes 98312 | tf_op jit(solution)/shard_map/ppermute | solution.py:348
  98.5 6.3 %collective-permute-start.29 = (f32[64,128]{1,0:T(8,128)S(1)}, f32[64,128]{1,0:T(8,128)S(1)}, u32[]{:S(2)}, u32[]{:S(2)}) collective-permute-start(f32[64,128]{1,0:T(8,128)S(1)} %add.66), channel_id=1, source_target_pairs={{0,8},{1,9},{2,10},{3,11},{4,12},{5,13},{6,14},{7,15},{8,0},{9,1},... | collective-permute-start | bytes 98312 | tf_op jit(solution)/shard_map/ppermute | solution.py:348
  98.8 4.0 %collective-permute-start.30 = (f32[8,128]{1,0:T(8,128)S(1)}, f32[8,128]{1,0:T(8,128)S(1)}, u32[]{:S(2)}, u32[]{:S(2)}) collective-permute-start(f32[8,128]{1,0:T(8,128)S(1)} %get-tuple-element.95), channel_id=1, source_target_pairs={{0,16},{1,17},{2,18},{3,19},{4,20},{5,21},{6,22},{7,23},{8,24},{9,... | collective-permute-start | bytes 12296 | tf_op jit(solution)/shard_map/ppermute | solution.py:356
  99.3 5.4 %collective-permute-start.31 = (f32[8,128]{1,0:T(8,128)S(1)}, f32[8,128]{1,0:T(8,128)S(1)}, u32[]{:S(2)}, u32[]{:S(2)}) collective-permute-start(f32[8,128]{1,0:T(8,128)S(1)} %get-tuple-element.94), channel_id=1, source_target_pairs={{0,24},{1,25},{2,26},{3,27},{4,28},{5,29},{6,30},{7,31},{8,16},{9,... | collective-permute-start | bytes 12296 | tf_op jit(solution)/shard_map/ppermute | solution.py:356
  104.8 1.3 %copy-start.8 = (bf16[20,128,256]{2,1,0:T(8,128)(2,1)S(1)}, bf16[20,128,256]{2,1,0:T(8,128)(2,1)}, u32[]{:S(2)}) copy-start(bf16[20,128,256]{2,1,0:T(8,128)(2,1)} %copy-done.5) | copy-start | bytes 3932164
  106.1 1.1 copy-start.15
  107.2 1.0 copy-start.19
  110.2 1.2 %collective-permute-start.32 = (f32[64,128]{1,0:T(8,128)S(1)}, f32[64,128]{1,0:T(8,128)S(1)}, u32[]{:S(2)}, u32[]{:S(2)}) collective-permute-start(f32[64,128]{1,0:T(8,128)S(1)} %get-tuple-element.93), channel_id=1, source_target_pairs={{0,1},{1,0},{2,3},{3,2},{4,5},{5,4},{6,7},{7,6},{8,9},{9,8},{10,11... | collective-permute-start | bytes 98312 | tf_op jit(solution)/shard_map/ppermute | solution.py:348
  (3 other events, 2.1 us)

commit v3 on v2

v3 whole, which is shorter than its diff:
```python
import functools
import math

import jax
import jax.numpy as jnp
from jax import lax
from jax.experimental import pallas as pl
from jax.experimental.pallas import tpu as pltpu
from jax.sharding import PartitionSpec as P

ITERS = 2

entropic_regularizer = 0.1
dustbin = 0.5
epsilon = 1e-06

VMEM = pl.BlockSpec(memory_space=pltpu.VMEM)
SMEM = pl.BlockSpec(memory_space=pltpu.SMEM)
HBM = pl.BlockSpec(memory_space=pltpu.HBM)
LIGHT = pl.CostEstimate(flops=1, bytes_accessed=1, transcendentals=0)
NT = (((1,), (1,)), ((), ()))
NN = (((1,), (0,)), ((), ()))


def in_vmem(*arrays):
    return [pltpu.with_memory_space_constraint(x, pltpu.VMEM) for x in arrays]


def in_hbm(*arrays):
    return [pltpu.with_memory_space_constraint(x, pltpu.HBM) for x in arrays]


def split2(x):
    high = x.astype(jnp.bfloat16)
    low = (x - high.astype(jnp.float32)).astype(jnp.bfloat16)
    return high, low


def unit(x):
    return x * lax.rsqrt(jnp.mean(x * x, axis=-1, keepdims=True) + epsilon)


def stacked_parts(row):
    x = jnp.broadcast_to(row, (8, row.shape[1]))
    high = x.astype(jnp.bfloat16).astype(jnp.float32)
    rest = x - high
    low = rest.astype(jnp.bfloat16).astype(jnp.float32)
    place = lax.broadcasted_iota(jnp.int32, x.shape, 0)
    parts = jnp.where(place == 0, high, jnp.where(place == 1, low, jnp.where(place == 2, rest - low, 0.0)))
    return parts.astype(jnp.bfloat16)


def column_product(parts, tile):
    both = lax.dot_general(parts, tile, NN, preferred_element_type=jnp.float32)
    width = tile.shape[1] // 2
    return both[:, :width] + both[:, width:]


def row_product(parts, tile):
    return lax.dot_general(
        jnp.concatenate([parts, parts], axis=1), tile, NT, preferred_element_type=jnp.float32
    )


def target_kernel(emb_ref, out_ref, staged, arrived):
    parts = arrived.shape[0]
    share = emb_ref.shape[0] // parts
    copies = []
    for part in range(parts):
        spots = pl.ds(part * share, share)
        copies.append(pltpu.make_async_copy(emb_ref.at[spots], staged.at[spots], arrived.at[part]))
        copies[-1].start()

    def one(block, carry):
        high, low = split2(unit(staged[block]).T)
        out_ref[block] = jnp.concatenate([high, low], axis=1)
        return carry

    for part in range(parts):
        copies[part].wait()
        lax.fori_loop(part * share, (part + 1) * share, one, 0, unroll=4)


def target_operand(emb):
    blocks, rows, width = emb.shape
    parts = math.gcd(blocks, 8)
    return pl.pallas_call(
        target_kernel,
        out_shape=pltpu.VMEM((blocks, width, 2 * rows), jnp.bfloat16),
        in_specs=[pl.BlockSpec(memory_space=pl.ANY)],
        out_specs=VMEM,
        scratch_shapes=[pltpu.VMEM(emb.shape, jnp.float32), pltpu.SemaphoreType.DMA((parts,))],
        cost_estimate=LIGHT,
        compiler_params=pltpu.CompilerParams(vmem_limit_bytes=16 << 20),
        name="target_operand",
    )(emb)


def pack_kernel(device, emb, mass, cand_device, cand_block, upper, lower, both, named, blocks, arrived):
    sb, rows, width = emb.shape
    half, near = rows // 2, cand_device.shape[1]
    copies = [
        pltpu.make_async_copy(cand_device, named, arrived.at[0]),
        pltpu.make_async_copy(cand_block, blocks, arrived.at[1]),
        pltpu.make_async_copy(mass, lower.at[pl.ds(sb * half, sb)], arrived.at[2]),
    ]
    for block in range(sb):
        into = pl.ds(block * half, half)
        copies.append(pltpu.make_async_copy(emb.at[block, pl.ds(0, half)], upper.at[into], arrived.at[3 + 2 * block]))
        copies.append(
            pltpu.make_async_copy(emb.at[block, pl.ds(half, half)], lower.at[into], arrived.at[4 + 2 * block])
        )
    for copy in copies:
        copy.start()
    for copy in copies[:2]:
        copy.wait()
    upper[sb * half :] = jnp.zeros((sb, width), jnp.float32)
    upper[sb * half :, 0:near] = named[...].astype(jnp.float32)
    upper[sb * half :, near : near + blocks.shape[1]] = blocks[...].astype(jnp.float32)
    for copy in copies[2:]:
        copy.wait()
    count = upper.shape[0]
    both[0:count] = upper[...]
    both[count:] = lower[...]


def pack(device, emb, mass, cand_device, cand_block):
    sb, rows, width = emb.shape
    count = sb * (rows // 2 + 1)
    shape = pltpu.VMEM((count, width), jnp.float32)
    return pl.pallas_call(
        pack_kernel,
        out_shape=(shape, shape, pltpu.VMEM((2 * count, width), jnp.float32)),
        in_specs=[SMEM] + [HBM] * 4,
        out_specs=(VMEM, VMEM, VMEM),
        scratch_shapes=[
            pltpu.VMEM(cand_device.shape, jnp.int32),
            pltpu.VMEM(cand_block.shape, jnp.int32),
            pltpu.SemaphoreType.DMA((3 + 2 * sb,)),
        ],
        compiler_params=pltpu.CompilerParams(vmem_limit_bytes=16 << 20),
        name="pack",
    )(device, *in_hbm(emb, mass, cand_device, cand_block))


def chip_at(chips, chip, offset):
    odd = lax.rem(chip, 2)
    spot = jnp.where(odd == 1, chips - 1 - chip // 2, chip // 2) + offset
    spot = jnp.where(spot < 0, spot + chips, jnp.where(spot >= chips, spot - chips, spot))
    return jnp.where(spot < chips // 2, 2 * spot, 2 * chips - 1 - 2 * spot)


def tile_kernel(plan, *refs):
    chunks, slots, sb, half, tb, near, offsets, far, chained, closing = plan
    sides = 1 if far else 2
    refs = list(refs)
    device = refs.pop(0)
    if far:
        both = refs.pop(0)
        source = [both.at[pl.ds(start, sb * (half + 1))] for start in (0, sb * (half + 1))]
    else:
        source = [refs.pop(0) for _ in range(2 * chunks)]
    weight = [refs.pop(0) for _ in range(sides)]
    rows_in, mass_in = (refs.pop(0), refs.pop(0)) if chained else (None, None)
    back = refs.pop(0) if closing else None
    tiles, table, rows_out, mass_out, partial, staged, named, listed, arrived = refs
    count = chunks * sides * slots
    width = source[0].shape[1]
    scale = 1.0 / (width * entropic_regularizer)
    me = device[0]
    chips = rows_out.shape[0] // sb

    for chunk in range(chunks):
        staged[chunk * sb : (chunk + 1) * sb] = source[2 * chunk][sb * half :].astype(jnp.int32)
    copy = pltpu.make_async_copy(staged, named, arrived)
    copy.start()
    if chained:
        rows_out[...] = rows_in[...]
        mass_out[...] = mass_in[...]
    partial[...] = jnp.zeros_like(partial)
    place = lax.broadcasted_iota(jnp.int32, (8, 2 * width), 0)
    ones = jnp.where(place == 0, 1.0, 0.0).astype(jnp.bfloat16)
    copy.wait()

    chip_of = []
    for chunk in range(chunks):
        at_chip = jnp.int32(0) if far else chip_at(chips, me // 2, offsets[chunk])
        chip_of.append(at_chip)
        for side in range(sides):
            base = (chunk * sides + side) * slots
            if far:
                for j in range(sb):
                    listed[base + j] = j
                    table[j] = named[j, 2 * near]
                continue
            wanted = me if side == 0 else me + 1 - 2 * lax.rem(me, 2)
            filled = jnp.int32(0)
            for block in range(sb):
                found, which = jnp.int32(0), jnp.int32(0)
                for k in range(near):
                    hit = named[chunk * sb + block, k] == wanted
                    found = jnp.where(hit, 1, found)
                    which = jnp.where(hit, named[chunk * sb + block, near + k], which)
                listed[base + filled] = block
                table[count + base + filled] = which
                filled = filled + found
            for j in range(slots):
                valid = j < filled
                block = jnp.where(valid, listed[base + j], sb)
                which = jnp.where(valid, table[count + base + j], 2 * tb)
                listed[base + j] = block
                table[base + j] = jnp.where(valid, at_chip * sb + block, chips * sb)
                table[count + base + j] = jnp.where(valid, which + side * tb, 2 * tb)

    for chunk in range(chunks):
        upper, lower = source[2 * chunk], source[2 * chunk + 1]
        for side in range(sides):
            for j in range(slots):
                at = (chunk * sides + side) * slots + j
                block = listed[at]
                start = pl.multiple_of(lax.rem(block, sb) * half, half)
                left = jnp.concatenate([upper[pl.ds(start, half)], lower[pl.ds(start, half)]], axis=0)
                high, low = split2(unit(left))
                right = weight[side][table[at] if far else lax.rem(table[count + at], tb)]
                both = lax.dot_general(
                    jnp.concatenate([high, low], axis=1),
                    jnp.concatenate([right, right], axis=0),
                    NN,
                    preferred_element_type=jnp.float32,
                )
                nodes = both.shape[1] // 2
                affinity = both[:, :nodes] + both[:, nodes:]
                tile = jnp.exp(affinity * scale) * (1.0 / (8.0 * nodes))
                tile = jnp.concatenate(split2(tile), axis=1)
                tiles[at] = tile
                spot = chunk * (sb + 1) + block
                partial[spot] += lax.dot_general(ones, tile, NT, preferred_element_type=jnp.float32)
        start = pl.multiple_of(chip_of[chunk] * sb, sb)
        for block in range(sb):
            rows_out[pl.ds(start + block, 1)] = partial[chunk * (sb + 1) + block][0:1]
        mass_out[pl.ds(start, sb)] = lower[sb * half :]
    if closing:
        start = pl.multiple_of(me // 2 * sb, sb)
        rows_out[pl.ds(start, sb)] += back[...]


def build_tiles(device, source, weight, slots, sb, near, chips, offsets=(), chain=(), back=None):
    chunks, sides, far = max(1, len(source) // 2), len(weight), not offsets
    half, width = source[0].shape[0] // (sb * (1 + far)) - 1, source[0].shape[1]
    tb, nodes = weight[0].shape[0], weight[0].shape[2] // 2
    count = chunks * sides * slots
    plan = (chunks, slots, sb, half, tb, near, offsets, far, bool(chain), back is not None)
    operands = [device, *source, *in_vmem(*weight), *chain] + ([] if back is None else [back])
    rows = jax.ShapeDtypeStruct(((1 if far else chips) * sb, 2 * half), jnp.float32)
    return pl.pallas_call(
        functools.partial(tile_kernel, plan),
        out_shape=(
            pltpu.VMEM((count, 2 * half, 2 * nodes), jnp.bfloat16),
            jax.ShapeDtypeStruct((count if far else 2 * count + 1,), jnp.int32),
            rows,
            rows,
        ),
        in_specs=[SMEM] + [VMEM] * (len(operands) - 1),
        out_specs=(VMEM, SMEM, VMEM, VMEM),
        scratch_shapes=[
            pltpu.VMEM((chunks * (sb + 1), 8, 2 * half), jnp.float32),
            pltpu.VMEM((chunks * sb, width), jnp.int32),
            pltpu.SMEM((chunks * sb, width), jnp.int32),
            pltpu.SMEM((count + 1,), jnp.int32),
            pltpu.SemaphoreType.DMA,
        ],
        cost_estimate=LIGHT,
        compiler_params=pltpu.CompilerParams(vmem_limit_bytes=16 << 20),
        name="build_tiles",
    )(*operands)


SMALL = pltpu.CompilerParams(vmem_limit_bytes=16 << 20)


def add_kernel(device, mine, theirs, total, own):
    sb = own.shape[0]
    total[...] = mine[...] + theirs[...]
    own[...] = total[pl.ds(pl.multiple_of(device[0] // 2 * sb, sb), sb)]


def add_last(device, mine, theirs, sb):
    return pl.pallas_call(
        add_kernel,
        out_shape=(
            jax.ShapeDtypeStruct(mine.shape, jnp.float32),
            jax.ShapeDtypeStruct((sb, mine.shape[1]), jnp.float32),
        ),
        in_specs=[SMEM, VMEM, VMEM],
        out_specs=(VMEM, VMEM),
        compiler_params=SMALL,
        name="add_last",
    )(device, mine, theirs)


def insert_kernel(device, rows, part, out):
    out[...] = rows[...]
    out[pl.ds(pl.multiple_of(device[0] // 2 * part.shape[0], part.shape[0]), part.shape[0])] += part[...]


def add_own(device, rows, part):
    return pl.pallas_call(
        insert_kernel,
        out_shape=jax.ShapeDtypeStruct(rows.shape, jnp.float32),
        in_specs=[SMEM, VMEM, VMEM],
        out_specs=VMEM,
        compiler_params=SMALL,
        name="add_own",
    )(device, rows, part)


def column_kernel(counts, *refs):
    refs = list(refs)
    tables = [refs.pop(0) for _ in counts]
    rows, mass = refs.pop(0), refs.pop(0)
    tiles = [refs.pop(0) for _ in counts]
    out, scale, total = refs
    count = rows.shape[0]
    scale[0:count] = mass[...] / (dustbin + rows[...])
    scale[count:] = jnp.zeros((8, scale.shape[1]), jnp.float32)
    total[...] = jnp.zeros_like(total)
    for part, slots in enumerate(counts):
        for slot in range(slots):
            parts = stacked_parts(scale[pl.ds(tables[part][slot], 1), :])
            total[tables[part][slots + slot]] += column_product(parts, tiles[part][slot])
    for block in range(out.shape[0]):
        out[block : block + 1] = jnp.sum(total[block], axis=0, keepdims=True)


def column_sums(tables, rows, mass, tiles, targets):
    counts = tuple(t.shape[0] for t in tiles)
    width, nodes = rows.shape[1], tiles[0].shape[2] // 2
    return pl.pallas_call(
        functools.partial(column_kernel, counts),
        out_shape=jax.ShapeDtypeStruct((targets, nodes), jnp.float32),
        in_specs=[SMEM] * len(tables) + [VMEM] * (2 + len(tiles)),
        out_specs=VMEM,
        scratch_shapes=[
            pltpu.VMEM((rows.shape[0] + 8, width), jnp.float32),
            pltpu.VMEM((targets + 1, 8, nodes), jnp.float32),
        ],
        cost_estimate=LIGHT,
        compiler_params=SMALL,
        name="column_sums",
    )(*tables, rows, mass, *in_vmem(*tiles))


def far_column_kernel(far_at, sums, far_rows, far_mass, tiles, out, scale):
    far = tiles.shape[0]
    out[...] = sums[...]
    scale[...] = far_mass[...] / (dustbin + far_rows[...])
    for slot in range(far):
        product = column_product(stacked_parts(scale[slot : slot + 1, :]), tiles[slot])
        out[pl.ds(far_at[slot], 1)] += jnp.sum(product, axis=0, keepdims=True)


def far_column_sums(far_at, sums, far_rows, far_mass, tiles):
    return pl.pallas_call(
        far_column_kernel,
        out_shape=jax.ShapeDtypeStruct(sums.shape, jnp.float32),
        in_specs=[SMEM] + [VMEM] * 4,
        out_specs=VMEM,
        scratch_shapes=[pltpu.VMEM(far_mass.shape, jnp.float32)],
        cost_estimate=LIGHT,
        compiler_params=SMALL,
        name="far_column_sums",
    )(far_at, sums, far_rows, far_mass, *in_vmem(tiles))


def scale_kernel(rows, mass, mine, theirs, target_mass, src, tgt):
    blocks = tgt.shape[0]
    src[...] = mass[...] / (dustbin + rows[...])
    tgt[...] = target_mass[...] / (dustbin + mine[0:blocks] + theirs[blocks : 2 * blocks])


def scales(rows, mass, mine, theirs, target_mass):
    return pl.pallas_call(
        scale_kernel,
        out_shape=(
            jax.ShapeDtypeStruct(mass.shape, jnp.float32),
            jax.ShapeDtypeStruct(target_mass.shape, jnp.float32),
        ),
        in_specs=[VMEM] * 5,
        out_specs=(VMEM, VMEM),
        compiler_params=SMALL,
        name="scales",
    )(rows, mass, mine, theirs, target_mass)


def far_row_kernel(far_at, mine, theirs, mass, tiles, out, scale):
    blocks = mass.shape[0]
    scale[...] = mass[...] / (dustbin + mine[0:blocks] + theirs[blocks : 2 * blocks])
    for slot in range(tiles.shape[0]):
        product = row_product(stacked_parts(scale[pl.ds(far_at[slot], 1), :]), tiles[slot])
        out[slot : slot + 1] = jnp.sum(product, axis=0, keepdims=True)


def far_row_sums(far_at, mine, theirs, mass, tiles):
    return pl.pallas_call(
        far_row_kernel,
        out_shape=jax.ShapeDtypeStruct(tiles.shape[:2], jnp.float32),
        in_specs=[SMEM] + [VMEM] * 4,
        out_specs=VMEM,
        scratch_shapes=[pltpu.VMEM(mass.shape, jnp.float32)],
        cost_estimate=LIGHT,
        compiler_params=SMALL,
        name="far_row_sums",
    )(far_at, mine, theirs, mass, *in_vmem(tiles))


def row_kernel(counts, *refs):
    refs = list(refs)
    tables = [refs.pop(0) for _ in counts]
    mine, theirs, mass, other_mass = [refs.pop(0) for _ in range(4)]
    tiles = [refs.pop(0) for _ in counts]
    out, scale, total = refs
    blocks = mass.shape[0]
    scale[0:blocks] = mass[...] / (dustbin + mine[0:blocks] + theirs[blocks : 2 * blocks])
    scale[blocks : 2 * blocks] = other_mass[...] / (dustbin + mine[blocks : 2 * blocks] + theirs[0:blocks])
    scale[2 * blocks :] = jnp.zeros((8, scale.shape[1]), jnp.float32)
    total[...] = jnp.zeros_like(total)
    for part, slots in enumerate(counts):
        for slot in range(slots):
            parts = stacked_parts(scale[pl.ds(tables[part][slots + slot], 1), :])
            total[tables[part][slot]] += row_product(parts, tiles[part][slot])
    for block in range(out.shape[0]):
        out[block : block + 1] = jnp.sum(total[block], axis=0, keepdims=True)


def row_sums(tables, mine, theirs, mass, other_mass, tiles, sources):
    counts = tuple(t.shape[0] for t in tiles)
    width, nodes = tiles[0].shape[1], tiles[0].shape[2] // 2
    return pl.pallas_call(
        functools.partial(row_kernel, counts),
        out_shape=jax.ShapeDtypeStruct((sources, width), jnp.float32),
        in_specs=[SMEM] * len(tables) + [VMEM] * (4 + len(tiles)),
        out_specs=VMEM,
        scratch_shapes=[
            pltpu.VMEM((mine.shape[0] + 8, nodes), jnp.float32),
            pltpu.VMEM((sources + 1, 8, width), jnp.float32),
        ],
        cost_estimate=LIGHT,
        compiler_params=SMALL,
        name="row_sums",
    )(*tables, mine, theirs, mass, other_mass, *in_vmem(*tiles))


def local(source_emb, target_emb, source_mass, target_mass, cand_device, cand_block):
    dev_count = lax.axis_size("dev")
    group_count = lax.axis_size("group")
    chips = dev_count // 2
    sb, tb = source_emb.shape[0], target_emb.shape[0]
    near = cand_device.shape[1]
    slot_cap = (near * sb + dev_count - 1) // dev_count + 1
    steps = chips // 2
    ring = list(range(0, chips, 2)) + list(range(chips - 1, 0, -2))

    def around(x, by):
        pairs = [
            (2 * ring[i] + core, 2 * ring[(i + by) % chips] + core) for i in range(chips) for core in range(2)
        ]
        return lax.ppermute(x, "dev", pairs)

    def across(x, bit):
        return lax.ppermute(x, "dev", [(i, i ^ bit) for i in range(dev_count)])

    def to_group(x, by):
        return lax.ppermute(x, "group", [(g, (g + by) % group_count) for g in range(group_count)])

    device = lax.axis_index("dev").astype(jnp.int32)
    me = device.reshape(1)

    upper, lower, both = pack(me, source_emb, source_mass, cand_device, cand_block)
    sibling_emb, sibling_mass = across(target_emb, 1), across(target_mass, 1)
    far_both = [both]

    weights, tiles, tables, chain, far_parts = [], [], [], [], []
    build = functools.partial(build_tiles, me, sb=sb, near=near, chips=chips)

    def target_job(emb):
        weights.append(target_operand(emb))
        return weights[-1]

    def near_job(chunks, back=None):
        tile, table, *passed = build(
            [x for up, low, _ in chunks for x in (up, low)],
            weights,
            slots=slot_cap,
            offsets=tuple(offset for _, _, offset in chunks),
            chain=chain,
            back=back,
        )
        tiles.append(tile)
        tables.append(table)
        chain[:] = passed
        return chain[0]

    def far_job():
        tile, at, sums, mass = build([to_group(far_both[0], 1)], weights[:1], slots=sb)
        far_parts.extend((tile, at, mass, to_group(sums, -1)))
        return sums

    jobs = [
        (0, lambda: target_job(in_hbm(target_emb)[0])),
        (0, lambda: target_job(sibling_emb)),
        (0, lambda: near_job([(upper, lower, 0)])),
    ]

    def behind_job(step, *halves):
        if jobs and jobs[0][0] <= max(0, step - 2):
            halves = lax.optimization_barrier((halves, jobs.pop(0)[1]()))[0]
        return halves

    up_a, up_b, down_a, down_b = upper, lower, upper, lower
    for step in range(1, steps + 1):
        if step > 1:
            up_a, down_b = behind_job(step, up_a, down_b)
        up_a, down_b = around(up_a, 1), around(down_b, -1)
        if step < steps:
            up_b, down_a = behind_job(step, up_b, down_a)
            up_b, down_a = around(up_b, 1), around(down_a, -1)
            chunks = [(up_a, up_b, -step), (down_a, down_b, step)]
            jobs.append((step, functools.partial(near_job, chunks)))
        if step == 1:
            far_both[0] = lax.optimization_barrier((both, up_a))[0]
    far_job()
    for _, job in jobs:
        job()
    far_tiles, far_at, far_mass, from_far = far_parts
    near_job([(up_a, down_b, steps)], from_far)
    near_rows, all_mass = chain

    for sweep in range(ITERS):
        if sweep > 0:
            far_rows = far_row_sums(far_at, mine, theirs, target_mass, far_tiles)
            back = to_group(far_rows, -1)
            near_rows = row_sums(tables, mine, theirs, target_mass, sibling_mass, tiles, chips * sb)
            near_rows = add_own(me, near_rows, back)
        bit = 2
        while 2 * bit < dev_count:
            near_rows = near_rows + across(near_rows, bit)
            bit *= 2
        near_rows, own_rows = add_last(me, near_rows, across(near_rows, bit), sb)
        far_rows = to_group(own_rows, 1)
        mine = column_sums(tables, near_rows, all_mass, tiles, 2 * tb)
        mine = far_column_sums(far_at, mine, far_rows, far_mass, far_tiles)
        theirs = across(mine, 1)
    return scales(own_rows, source_mass, mine, theirs, target_mass)


def solution(mesh):
    placed = (
        P(("group", "dev"), None, None),
        P(("group", "dev"), None, None),
        P(("group", "dev"), None),
        P(("group", "dev"), None),
        P(("group", "dev"), None),
        P(("group", "dev"), None),
    )
    return jax.shard_map(
        local,
        mesh=mesh,
        in_specs=placed,
        out_specs=(P(("group", "dev"), None), P(("group", "dev"), None)),
        check_vma=False,
    )
```

time: 113 us -> 92.2 us (0.82)
  local copies, waits for them, and re-layouts: 20.6 us -> 0.01 us
  waiting for transfers between devices: 24 us -> 31.5 us
  starting transfers between devices: 38.2 us -> 33.6 us
  Pallas kernels: 27.7 us -> 26 us
    unnamed x68 -> x4, local copies, waits for them, and re-layouts: 20.6 us -> 0.01 us
    ppermute x10, waiting for transfers between devices: 9.5 us -> 17.5 us  [across(): return lax.ppermute(x, 'dev', [(i, i ^ bit) for i in range(dev_count)])]
    ppermute x9 -> x5, waiting for transfers between devices: 9.58 us -> 1.66 us  [to_group(): lax.ppermute(x, 'group', [(g, (g + by) % group_count) for g in range(grou...]
    ppermute x14, waiting for transfers between devices: 4.88 us -> 12.4 us  [around(): return lax.ppermute(x, 'dev', pairs)]
    ppermute x9 -> x5, starting transfers between devices: 13.1 us -> 7.42 us  [to_group(): lax.ppermute(x, 'group', [(g, (g + by) % group_count) for g in range(grou...]
    pallas_call x12 -> x19, Pallas kernels: 27.7 us -> 26 us  [the longest x6 11.7 us: build_tiles(): pl.pallas_call(functools.partial(tile_kernel, plan), out_shape=(pltpu.VME...]
  transfers between devices with their start and end apart: 33 -> 29, of which waited for: 16 -> 19; matrix products, arithmetic and copies ran while one was open for 0% -> 0% of each run, Pallas kernels for 17% -> 24%
where the time goes in v3:
time: 92.2 us; the launch traced here: 92 us
  starting transfers between devices  33.6 us (36%)
  waiting for transfers between devices  31.5 us (34%)
  Pallas kernels  26 us (28%)
    ppermute x10, waiting for transfers between devices, across(): return lax.ppermute(x, 'dev', [(i, i ^ bit) for i in range(dev_count)])  17.5 us
    ppermute x14, starting transfers between devices, around(): return lax.ppermute(x, 'dev', pairs)  14.9 us
    ppermute x14, waiting for transfers between devices, around(): return lax.ppermute(x, 'dev', pairs)  12.4 us
    pallas_call x6, Pallas kernels, build_tiles(): pl.pallas_call(functools.partial(tile_kernel, plan), out_shape=(pltpu.VME...  11.7 us
    ppermute x10, starting transfers between devices, across(): return lax.ppermute(x, 'dev', [(i, i ^ bit) for i in range(dev_count)])  11.3 us
    ppermute x5, starting transfers between devices, to_group(): lax.ppermute(x, 'group', [(g, (g + by) % group_count) for g in range(grou...  7.42 us
    pallas_call x2, Pallas kernels, target_operand(): pl.pallas_call(target_kernel, out_shape=pltpu.VMEM((blocks, width, 2 * ro...  5.09 us
    pallas_call x2, Pallas kernels, column_sums(): pl.pallas_call(functools.partial(column_kernel, counts), out_shape=jax.Sh...  2.93 us
  transfers between devices with their start and end apart: 29, of which 19 were waited for; matrix products, arithmetic and copies ran while one was open for 0% of the time, Pallas kernels for 24%

profile of v3, /device:TPU:0, one launch (start us, length us, event | category | flops | bytes accessed | tf_op | source)
XLA Modules:
  0.0 92.0 jit_solution(18362520093319659588)
XLA Ops:
  0.6 0.5 collective-permute-start
  1.1 1.2 %pack.1 = (f32[520,128]{1,0:T(8,128)S(1)}, f32[520,128]{1,0:T(8,128)S(1)}, f32[1040,128]{1,0:T(8,128)S(1)}) custom-call(s32[1]{0:T(128)} %bitcast.device.refs_0_, f32[8,128,128]{2,1,0:T(8,128)} %emb.1, f32[8,128]{1,0:T(8,128)} %mass.5, s32[8,7]{1,0:T(8,128)} %cand_device.1, s32[8,8]{1,0:T(8,128)} %cand_block.1), custom_call_target="tpu_custom_call" | custom-call | tf_op jit(solution)/shard_map/pack/pallas_call | solution.py:131
  2.4 2.6 %collective-permute-start.1 = (f32[520,128]{1,0:T(8,128)S(1)}, f32[520,128]{1,0:T(8,128)S(1)}, u32[]{:S(2)}, u32[]{:S(2)}) collective-permute-start(f32[520,128]{1,0:T(8,128)S(1)} %get-tuple-element.48.refs_1_), channel_id=1, source_target_pairs={{0,4},{1,5},{4,8},{5,9},{8,12},{9,13},{12,14},{13,15},{14,10},{15,... | collective-permute-start | bytes 798728 | tf_op jit(solution)/shard_map/ppermute | solution.py:467
  5.0 2.9 %target_operand.2.refs_3_.refs_5_.refs_2_ = bf16[32,128,256]{2,1,0:T(8,128)(2,1)S(1)} custom-call(f32[32,128,128]{2,1,0:T(8,128)} %emb_ref.1), custom_call_target="tpu_custom_call" | custom-call | flops 1 | bytes 1 | tf_op jit(solution)/shard_map/target_operand/pallas_call | solution.py:87
  8.0 2.1 %collective-permute-start.2 = (f32[520,128]{1,0:T(8,128)S(1)}, f32[520,128]{1,0:T(8,128)S(1)}, u32[]{:S(2)}, u32[]{:S(2)}) collective-permute-start(f32[520,128]{1,0:T(8,128)S(1)} %get-tuple-element.47.refs_2_), channel_id=1, source_target_pairs={{0,4},{1,5},{4,8},{5,9},{8,12},{9,13},{12,14},{13,15},{14,10},{15,... | collective-permute-start | bytes 798728 | tf_op jit(solution)/shard_map/ppermute | solution.py:467
  10.1 0.0 collective-permute-start.3
  10.1 0.0 collective-permute-done.emb_ref
  10.1 2.1 %target_operand.3.refs_4_.refs_6_ = bf16[32,128,256]{2,1,0:T(8,128)(2,1)S(1)} custom-call(f32[32,128,128]{2,1,0:T(8,128)S(1)} %collective-permute-done.emb_ref), custom_call_target="tpu_custom_call" | custom-call | flops 1 | bytes 1 | tf_op jit(solution)/shard_map/target_operand/pallas_call | solution.py:87
  12.2 2.0 %collective-permute-done.4.refs_4_ = f32[520,128]{1,0:T(8,128)S(1)} collective-permute-done((f32[520,128]{1,0:T(8,128)S(1)}, f32[520,128]{1,0:T(8,128)S(1)}, u32[]{:S(2)}, u32[]{:S(2)}) %collective-permute-start.4) | collective-permute-done | bytes 266272 | tf_op jit(solution)/shard_map/ppermute | solution.py:467
  14.3 1.6 %collective-permute-start.5 = (f32[520,128]{1,0:T(8,128)S(1)}, f32[520,128]{1,0:T(8,128)S(1)}, u32[]{:S(2)}, u32[]{:S(2)}) collective-permute-start(f32[520,128]{1,0:T(8,128)S(1)} %collective-permute-done.1.refs_1_), channel_id=1, source_target_pairs={{0,4},{1,5},{4,8},{5,9},{8,12},{9,13},{12,14},{13,15},{14,10},{15,... | collective-permute-start | bytes 798728 | tf_op jit(solution)/shard_map/ppermute | solution.py:467
  15.9 0.4 collective-permute-start.8
  16.3 1.5 %collective-permute-start.15 = (f32[1040,128]{1,0:T(8,128)S(1)}, f32[1040,128]{1,0:T(8,128)S(1)}, u32[]{:S(2)}, u32[]{:S(2)}) collective-permute-start(f32[1040,128]{1,0:T(8,128)S(1)} %get-tuple-element.69), channel_id=1, source_target_pairs={{0,16},{16,0},{1,17},{17,1},{2,18},{18,2},{3,19},{19,3},{4,20},{20... | collective-permute-start | bytes 1597448 | tf_op jit(solution)/shard_map/ppermute | solution.py:473
  17.8 1.9 %build_tiles.6 = (bf16[10,128,256]{2,1,0:T(8,128)(2,1)S(1)}, s32[21]{0:T(128)S(1)}, f32[64,128]{1,0:T(8,128)S(1)}, f32[64,128]{1,0:T(8,128)S(1)}) custom-call(s32[1]{0:T(128)} %bitcast.device.refs_0_, f32[520,128]{1,0:T(8,128)S(1)} %get-tuple-element.48.refs_1_, f32[520,128]{1,0:T(8,128)S(1)} %get-tuple-element.47.refs_2_, ...), custom_call_target="tpu_custom_call" | custom-call | flops 1 | bytes 1 | tf_op jit(solution)/shard_map/build_tiles/pallas_call | solution.py:255
  19.7 0.2 collective-permute-done.3.refs_3_
  20.0 1.6 %collective-permute-start.6 = (f32[520,128]{1,0:T(8,128)S(1)}, f32[520,128]{1,0:T(8,128)S(1)}, u32[]{:S(2)}, u32[]{:S(2)}) collective-permute-start(f32[520,128]{1,0:T(8,128)S(1)} %collective-permute-done.2.refs_2_), channel_id=1, source_target_pairs={{0,4},{1,5},{4,8},{5,9},{8,12},{9,13},{12,14},{13,15},{14,10},{15,... | collective-permute-start | bytes 798728 | tf_op jit(solution)/shard_map/ppermute | solution.py:467
  21.6 0.4 collective-permute-start.7
  22.0 2.2 %build_tiles.7 = (bf16[20,128,256]{2,1,0:T(8,128)(2,1)S(1)}, s32[41]{0:T(128)S(1)}, f32[64,128]{1,0:T(8,128)S(1)}, f32[64,128]{1,0:T(8,128)S(1)}) custom-call(s32[1]{0:T(128)} %bitcast.device.refs_0_, f32[520,128]{1,0:T(8,128)S(1)} %collective-permute-done.1.refs_1_, f32[520,128]{1,0:T(8,128)S(1)} %collective-permute-done.2.refs_2_, ...), custom_call_target="tpu_custom_call" | custom-call | flops 1 | bytes 1 | tf_op jit(solution)/shard_map/build_tiles/pallas_call | solution.py:255
  24.3 1.4 %collective-permute-done.8.refs_4_ = f32[520,128]{1,0:T(8,128)S(1)} collective-permute-done((f32[520,128]{1,0:T(8,128)S(1)}, f32[520,128]{1,0:T(8,128)S(1)}, u32[]{:S(2)}, u32[]{:S(2)}) %collective-permute-start.8) | collective-permute-done | bytes 266272 | tf_op jit(solution)/shard_map/ppermute | solution.py:467
  25.7 1.6 %collective-permute-start.9 = (f32[520,128]{1,0:T(8,128)S(1)}, f32[520,128]{1,0:T(8,128)S(1)}, u32[]{:S(2)}, u32[]{:S(2)}) collective-permute-start(f32[520,128]{1,0:T(8,128)S(1)} %collective-permute-done.5.refs_1_), channel_id=1, source_target_pairs={{0,4},{1,5},{4,8},{5,9},{8,12},{9,13},{12,14},{13,15},{14,10},{15,... | collective-permute-start | bytes 798728 | tf_op jit(solution)/shard_map/ppermute | solution.py:467
  27.3 0.4 collective-permute-start.12
  27.7 1.6 %collective-permute-done.6.refs_2_ = f32[520,128]{1,0:T(8,128)S(1)} collective-permute-done((f32[520,128]{1,0:T(8,128)S(1)}, f32[520,128]{1,0:T(8,128)S(1)}, u32[]{:S(2)}, u32[]{:S(2)}) %collective-permute-start.6) | collective-permute-done | bytes 266272 | tf_op jit(solution)/shard_map/ppermute | solution.py:467
  29.3 2.0 %collective-permute-start.10 = (f32[520,128]{1,0:T(8,128)S(1)}, f32[520,128]{1,0:T(8,128)S(1)}, u32[]{:S(2)}, u32[]{:S(2)}) collective-permute-start(f32[520,128]{1,0:T(8,128)S(1)} %collective-permute-done.6.refs_2_), channel_id=1, source_target_pairs={{0,4},{1,5},{4,8},{5,9},{8,12},{9,13},{12,14},{13,15},{14,10},{15,... | collective-permute-start | bytes 798728 | tf_op jit(solution)/shard_map/ppermute | solution.py:467
  31.3 0.0 collective-permute-done.7.refs_3_
  31.4 2.2 %build_tiles.8 = (bf16[20,128,256]{2,1,0:T(8,128)(2,1)S(1)}, s32[41]{0:T(128)S(1)}, f32[64,128]{1,0:T(8,128)S(1)}, f32[64,128]{1,0:T(8,128)S(1)}) custom-call(s32[1]{0:T(128)} %bitcast.device.refs_0_, f32[520,128]{1,0:T(8,128)S(1)} %collective-permute-done.5.refs_1_, f32[520,128]{1,0:T(8,128)S(1)} %collective-permute-done.6.refs_2_, ...), custom_call_target="tpu_custom_call" | custom-call | flops 1 | bytes 1 | tf_op jit(solution)/shard_map/build_tiles/pallas_call | solution.py:255
  33.6 1.4 %collective-permute-done.9.refs_1_ = f32[520,128]{1,0:T(8,128)S(1)} collective-permute-done((f32[520,128]{1,0:T(8,128)S(1)}, f32[520,128]{1,0:T(8,128)S(1)}, u32[]{:S(2)}, u32[]{:S(2)}) %collective-permute-start.9) | collective-permute-done | bytes 266272 | tf_op jit(solution)/shard_map/ppermute | solution.py:467
  35.0 2.1 %collective-permute-done.12.refs_4_ = f32[520,128]{1,0:T(8,128)S(1)} collective-permute-done((f32[520,128]{1,0:T(8,128)S(1)}, f32[520,128]{1,0:T(8,128)S(1)}, u32[]{:S(2)}, u32[]{:S(2)}) %collective-permute-start.12) | collective-permute-done | bytes 266272 | tf_op jit(solution)/shard_map/ppermute | solution.py:467
  37.1 1.6 %collective-permute-start.13 = (f32[520,128]{1,0:T(8,128)S(1)}, f32[520,128]{1,0:T(8,128)S(1)}, u32[]{:S(2)}, u32[]{:S(2)}) collective-permute-start(f32[520,128]{1,0:T(8,128)S(1)} %collective-permute-done.9.refs_1_), channel_id=1, source_target_pairs={{0,4},{1,5},{4,8},{5,9},{8,12},{9,13},{12,14},{13,15},{14,10},{15,... | collective-permute-start | bytes 798728 | tf_op jit(solution)/shard_map/ppermute | solution.py:467
  38.7 0.4 collective-permute-start.14
  39.1 1.2 %build_tiles.10 = (bf16[8,128,256]{2,1,0:T(8,128)(2,1)S(1)}, s32[8]{0:T(128)S(1)}, f32[8,128]{1,0:T(8,128)S(1)}, f32[8,128]{1,0:T(8,128)S(1)}) custom-call(s32[1]{0:T(128)} %bitcast.device.refs_0_, f32[1040,128]{1,0:T(8,128)S(1)} %collective-permute-done.15.refs_1_, bf16[32,128,256]{2,1,0:T(8,128)(2,1)S(1)} %target_operand.2.refs_3_.refs_5_.refs_2_), custom_call_target="tpu_custom_call" | custom-call | flops 1 | bytes 1 | tf_op jit(solution)/shard_map/build_tiles/pallas_call | solution.py:255
  40.4 1.6 %collective-permute-start.16 = (f32[8,128]{1,0:T(8,128)S(1)}, f32[8,128]{1,0:T(8,128)S(1)}, u32[]{:S(2)}, u32[]{:S(2)}) collective-permute-start(f32[8,128]{1,0:T(8,128)S(1)} %get-tuple-element.70), channel_id=1, source_target_pairs={{0,16},{16,0},{1,17},{17,1},{2,18},{18,2},{3,19},{19,3},{4,20},{20... | collective-permute-start | bytes 12296 | tf_op jit(solution)/shard_map/ppermute | solution.py:473
  42.0 0.8 collective-permute-done.11.refs_3_
  42.8 2.2 %build_tiles.9 = (bf16[20,128,256]{2,1,0:T(8,128)(2,1)S(1)}, s32[41]{0:T(128)S(1)}, f32[64,128]{1,0:T(8,128)S(1)}, f32[64,128]{1,0:T(8,128)S(1)}) custom-call(s32[1]{0:T(128)} %bitcast.device.refs_0_, f32[520,128]{1,0:T(8,128)S(1)} %collective-permute-done.9.refs_1_, f32[520,128]{1,0:T(8,128)S(1)} %collective-permute-done.10.refs_2_, ...), custom_call_target="tpu_custom_call" | custom-call | flops 1 | bytes 1 | tf_op jit(solution)/shard_map/build_tiles/pallas_call | solution.py:255
  45.1 1.2 %collective-permute-done.13.refs_1_ = f32[520,128]{1,0:T(8,128)S(1)} collective-permute-done((f32[520,128]{1,0:T(8,128)S(1)}, f32[520,128]{1,0:T(8,128)S(1)}, u32[]{:S(2)}, u32[]{:S(2)}) %collective-permute-start.13) | collective-permute-done | bytes 266272 | tf_op jit(solution)/shard_map/ppermute | solution.py:467
  46.2 1.5 %collective-permute-done.14.refs_2_ = f32[520,128]{1,0:T(8,128)S(1)} collective-permute-done((f32[520,128]{1,0:T(8,128)S(1)}, f32[520,128]{1,0:T(8,128)S(1)}, u32[]{:S(2)}, u32[]{:S(2)}) %collective-permute-start.14) | collective-permute-done | bytes 266272 | tf_op jit(solution)/shard_map/ppermute | solution.py:467
  47.8 1.9 %build_tiles.11 = (bf16[10,128,256]{2,1,0:T(8,128)(2,1)S(1)}, s32[21]{0:T(128)S(1)}, f32[64,128]{1,0:T(8,128)S(1)}, f32[64,128]{1,0:T(8,128)S(1)}) custom-call(s32[1]{0:T(128)} %bitcast.device.refs_0_, f32[520,128]{1,0:T(8,128)S(1)} %collective-permute-done.13.refs_1_, f32[520,128]{1,0:T(8,128)S(1)} %collective-permute-done.14.refs_2_, ...), custom_call_target="tpu_custom_call" | custom-call | flops 1 | bytes 1 | tf_op jit(solution)/shard_map/build_tiles/pallas_call | solution.py:255
  49.7 0.3 collective-permute-start.17
  50.0 3.6 %collective-permute-done.17 = f32[64,128]{1,0:T(8,128)S(1)} collective-permute-done((f32[64,128]{1,0:T(8,128)S(1)}, f32[64,128]{1,0:T(8,128)S(1)}, u32[]{:S(2)}, u32[]{:S(2)}) %collective-permute-start.17) | collective-permute-done | bytes 32800 | tf_op jit(solution)/shard_map/ppermute | solution.py:470
  53.7 1.6 %collective-permute-start.18 = (f32[64,128]{1,0:T(8,128)S(1)}, f32[64,128]{1,0:T(8,128)S(1)}, u32[]{:S(2)}, u32[]{:S(2)}) collective-permute-start(f32[64,128]{1,0:T(8,128)S(1)} %add.12), channel_id=1, source_target_pairs={{0,4},{1,5},{2,6},{3,7},{4,0},{5,1},{6,2},{7,3},{8,12},{9,13},{10,... | collective-permute-start | bytes 98312 | tf_op jit(solution)/shard_map/ppermute | solution.py:470
  55.2 2.3 %collective-permute-done.18 = f32[64,128]{1,0:T(8,128)S(1)} collective-permute-done((f32[64,128]{1,0:T(8,128)S(1)}, f32[64,128]{1,0:T(8,128)S(1)}, u32[]{:S(2)}, u32[]{:S(2)}) %collective-permute-start.18) | collective-permute-done | bytes 32800 | tf_op jit(solution)/shard_map/ppermute | solution.py:470
  57.6 2.9 %collective-permute-start.19 = (f32[64,128]{1,0:T(8,128)S(1)}, f32[64,128]{1,0:T(8,128)S(1)}, u32[]{:S(2)}, u32[]{:S(2)}) collective-permute-start(f32[64,128]{1,0:T(8,128)S(1)} %add.13.mine), channel_id=1, source_target_pairs={{0,8},{1,9},{2,10},{3,11},{4,12},{5,13},{6,14},{7,15},{8,0},{9,1},... | collective-permute-start | bytes 98312 | tf_op jit(solution)/shard_map/ppermute | solution.py:470
  60.5 1.9 %collective-permute-done.19.theirs = f32[64,128]{1,0:T(8,128)S(1)} collective-permute-done((f32[64,128]{1,0:T(8,128)S(1)}, f32[64,128]{1,0:T(8,128)S(1)}, u32[]{:S(2)}, u32[]{:S(2)}) %collective-permute-start.19) | collective-permute-done | bytes 32800 | tf_op jit(solution)/shard_map/ppermute | solution.py:470
  62.4 1.6 %collective-permute-start.20 = (f32[8,128]{1,0:T(8,128)S(1)}, f32[8,128]{1,0:T(8,128)S(1)}, u32[]{:S(2)}, u32[]{:S(2)}) collective-permute-start(f32[8,128]{1,0:T(8,128)S(1)} %get-tuple-element.81), channel_id=1, source_target_pairs={{0,16},{16,0},{1,17},{17,1},{2,18},{18,2},{3,19},{19,3},{4,20},{20... | collective-permute-start | bytes 12296 | tf_op jit(solution)/shard_map/ppermute | solution.py:473
  64.0 1.5 %column_sums.2.sums = f32[64,128]{1,0:T(8,128)S(1)} custom-call(s32[21]{0:T(128)S(1)} %get-tuple-element.46.refs_0_, s32[41]{0:T(128)S(1)} %get-tuple-element.51.refs_1_, s32[41]{0:T(128)S(1)} %get-tuple-element.58.refs_2_, s32[41]{0:T(128)S(1)} %get-tuple-element.63.refs_3_, s32[21]{0:T(128)S(1)} %get-tuple-element.71.refs_4_, ...), custom_call_target="tpu_custom_call" | custom-call | flops 1 | bytes 1 | tf_op jit(solution)/shard_map/column_sums/pallas_call | solution.py:338
  65.5 0.6 collective-permute-done.20.far_rows
  66.1 0.7 far_column_sums.2.refs_5_.mine
  66.8 0.1 collective-permute-start.21
  66.9 0.5 collective-permute-start.22
  67.4 0.7 collective-permute-done.21.refs_6_.theirs
  68.1 0.8 far_row_sums.1
  68.9 1.6 %collective-permute-start.23 = (f32[8,128]{1,0:T(8,128)S(1)}, f32[8,128]{1,0:T(8,128)S(1)}, u32[]{:S(2)}, u32[]{:S(2)}) collective-permute-start(f32[8,128]{1,0:T(8,128)S(1)} %far_row_sums.1), channel_id=1, source_target_pairs={{0,16},{16,0},{1,17},{17,1},{2,18},{18,2},{3,19},{19,3},{4,20},{20... | collective-permute-start | bytes 12296 | tf_op jit(solution)/shard_map/ppermute | solution.py:473
  70.5 2.1 %row_sums.1.rows = f32[64,128]{1,0:T(8,128)S(1)} custom-call(s32[21]{0:T(128)S(1)} %get-tuple-element.46.refs_0_, s32[41]{0:T(128)S(1)} %get-tuple-element.51.refs_1_, s32[41]{0:T(128)S(1)} %get-tuple-element.58.refs_2_, s32[41]{0:T(128)S(1)} %get-tuple-element.63.refs_3_, s32[21]{0:T(128)S(1)} %get-tuple-element.71.refs_4_, ...), custom_call_target="tpu_custom_call" | custom-call | flops 1 | bytes 1 | tf_op jit(solution)/shard_map/row_sums/pallas_call | solution.py:438
  72.6 0.5 collective-permute-start.24
  73.1 3.5 %collective-permute-done.24 = f32[64,128]{1,0:T(8,128)S(1)} collective-permute-done((f32[64,128]{1,0:T(8,128)S(1)}, f32[64,128]{1,0:T(8,128)S(1)}, u32[]{:S(2)}, u32[]{:S(2)}) %collective-permute-start.24) | collective-permute-done | bytes 32800 | tf_op jit(solution)/shard_map/ppermute | solution.py:470
  76.6 1.6 %collective-permute-start.25 = (f32[64,128]{1,0:T(8,128)S(1)}, f32[64,128]{1,0:T(8,128)S(1)}, u32[]{:S(2)}, u32[]{:S(2)}) collective-permute-start(f32[64,128]{1,0:T(8,128)S(1)} %add.14), channel_id=1, source_target_pairs={{0,4},{1,5},{2,6},{3,7},{4,0},{5,1},{6,2},{7,3},{8,12},{9,13},{10,... | collective-permute-start | bytes 98312 | tf_op jit(solution)/shard_map/ppermute | solution.py:470
  78.2 2.3 %collective-permute-done.25 = f32[64,128]{1,0:T(8,128)S(1)} collective-permute-done((f32[64,128]{1,0:T(8,128)S(1)}, f32[64,128]{1,0:T(8,128)S(1)}, u32[]{:S(2)}, u32[]{:S(2)}) %collective-permute-start.25) | collective-permute-done | bytes 32800 | tf_op jit(solution)/shard_map/ppermute | solution.py:470
  80.5 3.3 %collective-permute-start.26 = (f32[64,128]{1,0:T(8,128)S(1)}, f32[64,128]{1,0:T(8,128)S(1)}, u32[]{:S(2)}, u32[]{:S(2)}) collective-permute-start(f32[64,128]{1,0:T(8,128)S(1)} %add.15.mine), channel_id=1, source_target_pairs={{0,8},{1,9},{2,10},{3,11},{4,12},{5,13},{6,14},{7,15},{8,0},{9,1},... | collective-permute-start | bytes 98312 | tf_op jit(solution)/shard_map/ppermute | solution.py:470
  83.8 1.9 %collective-permute-done.26.theirs = f32[64,128]{1,0:T(8,128)S(1)} collective-permute-done((f32[64,128]{1,0:T(8,128)S(1)}, f32[64,128]{1,0:T(8,128)S(1)}, u32[]{:S(2)}, u32[]{:S(2)}) %collective-permute-start.26) | collective-permute-done | bytes 32800 | tf_op jit(solution)/shard_map/ppermute | solution.py:470
  85.7 1.2 %collective-permute-start.27 = (f32[8,128]{1,0:T(8,128)S(1)}, f32[8,128]{1,0:T(8,128)S(1)}, u32[]{:S(2)}, u32[]{:S(2)}) collective-permute-start(f32[8,128]{1,0:T(8,128)S(1)} %get-tuple-element.84.rows), channel_id=1, source_target_pairs={{0,16},{16,0},{1,17},{17,1},{2,18},{18,2},{3,19},{19,3},{4,20},{20... | collective-permute-start | bytes 12296 | tf_op jit(solution)/shard_map/ppermute | solution.py:473
  86.9 1.5 %column_sums.3.sums = f32[64,128]{1,0:T(8,128)S(1)} custom-call(s32[21]{0:T(128)S(1)} %get-tuple-element.46.refs_0_, s32[41]{0:T(128)S(1)} %get-tuple-element.51.refs_1_, s32[41]{0:T(128)S(1)} %get-tuple-element.58.refs_2_, s32[41]{0:T(128)S(1)} %get-tuple-element.63.refs_3_, s32[21]{0:T(128)S(1)} %get-tuple-element.71.refs_4_, ...), custom_call_target="tpu_custom_call" | custom-call | flops 1 | bytes 1 | tf_op jit(solution)/shard_map/column_sums/pallas_call | solution.py:338
  88.3 1.0 %collective-permute-done.27.far_rows = f32[8,128]{1,0:T(8,128)S(1)} collective-permute-done((f32[8,128]{1,0:T(8,128)S(1)}, f32[8,128]{1,0:T(8,128)S(1)}, u32[]{:S(2)}, u32[]{:S(2)}) %collective-permute-start.27) | collective-permute-done | bytes 4128 | tf_op jit(solution)/shard_map/ppermute | solution.py:473
  89.4 0.7 far_column_sums.3.mine
  90.1 0.1 collective-permute-start.28
  90.2 1.2 %collective-permute-done.28.theirs = f32[64,128]{1,0:T(8,128)S(1)} collective-permute-done((f32[64,128]{1,0:T(8,128)S(1)}, f32[64,128]{1,0:T(8,128)S(1)}, u32[]{:S(2)}, u32[]{:S(2)}) %collective-permute-start.28) | collective-permute-done | bytes 32800 | tf_op jit(solution)/shard_map/ppermute | solution.py:470
  91.4 0.6 scales.1
  (21 shorter events, 0.1 us)
Async XLA Ops:
  0.6 9.5 %collective-permute-start = (f32[32,128,128]{2,1,0:T(8,128)}, f32[32,128,128]{2,1,0:T(8,128)S(1)}, u32[]{:S(2)}, u32[]{:S(2)}) collective-permute-start(f32[32,128,128]{2,1,0:T(8,128)} %emb_ref.1), channel_id=1, source_target_pairs={{0,1},{1,0},{2,3},{3,2},{4,5},{5,4},{6,7},{7,6},{8,9},{9,8},{10,11... | collective-permute-start | bytes 6291464 | tf_op jit(solution)/shard_map/ppermute | solution.py:470
  2.4 9.8 %collective-permute-start.1 = (f32[520,128]{1,0:T(8,128)S(1)}, f32[520,128]{1,0:T(8,128)S(1)}, u32[]{:S(2)}, u32[]{:S(2)}) collective-permute-start(f32[520,128]{1,0:T(8,128)S(1)} %get-tuple-element.48.refs_1_), channel_id=1, source_target_pairs={{0,4},{1,5},{4,8},{5,9},{8,12},{9,13},{12,14},{13,15},{14,10},{15,... | collective-permute-start | bytes 798728 | tf_op jit(solution)/shard_map/ppermute | solution.py:467
  5.0 9.2 %collective-permute-start.4 = (f32[520,128]{1,0:T(8,128)S(1)}, f32[520,128]{1,0:T(8,128)S(1)}, u32[]{:S(2)}, u32[]{:S(2)}) collective-permute-start(f32[520,128]{1,0:T(8,128)S(1)} %get-tuple-element.47.refs_2_), channel_id=1, source_target_pairs={{0,2},{1,3},{4,0},{5,1},{8,4},{9,5},{12,8},{13,9},{14,12},{15,13},... | collective-permute-start | bytes 798728 | tf_op jit(solution)/shard_map/ppermute | solution.py:467
  8.0 11.7 %collective-permute-start.2 = (f32[520,128]{1,0:T(8,128)S(1)}, f32[520,128]{1,0:T(8,128)S(1)}, u32[]{:S(2)}, u32[]{:S(2)}) collective-permute-start(f32[520,128]{1,0:T(8,128)S(1)} %get-tuple-element.47.refs_2_), channel_id=1, source_target_pairs={{0,4},{1,5},{4,8},{5,9},{8,12},{9,13},{12,14},{13,15},{14,10},{15,... | collective-permute-start | bytes 798728 | tf_op jit(solution)/shard_map/ppermute | solution.py:467
  10.1 9.9 %collective-permute-start.3 = (f32[520,128]{1,0:T(8,128)S(1)}, f32[520,128]{1,0:T(8,128)S(1)}, u32[]{:S(2)}, u32[]{:S(2)}) collective-permute-start(f32[520,128]{1,0:T(8,128)S(1)} %get-tuple-element.48.refs_1_), channel_id=1, source_target_pairs={{0,2},{1,3},{4,0},{5,1},{8,4},{9,5},{12,8},{13,9},{14,12},{15,13},... | collective-permute-start | bytes 798728 | tf_op jit(solution)/shard_map/ppermute | solution.py:467
  14.3 10.0 %collective-permute-start.5 = (f32[520,128]{1,0:T(8,128)S(1)}, f32[520,128]{1,0:T(8,128)S(1)}, u32[]{:S(2)}, u32[]{:S(2)}) collective-permute-start(f32[520,128]{1,0:T(8,128)S(1)} %collective-permute-done.1.refs_1_), channel_id=1, source_target_pairs={{0,4},{1,5},{4,8},{5,9},{8,12},{9,13},{12,14},{13,15},{14,10},{15,... | collective-permute-start | bytes 798728 | tf_op jit(solution)/shard_map/ppermute | solution.py:467
  15.9 9.8 %collective-permute-start.8 = (f32[520,128]{1,0:T(8,128)S(1)}, f32[520,128]{1,0:T(8,128)S(1)}, u32[]{:S(2)}, u32[]{:S(2)}) collective-permute-start(f32[520,128]{1,0:T(8,128)S(1)} %collective-permute-done.4.refs_4_), channel_id=1, source_target_pairs={{0,2},{1,3},{4,0},{5,1},{8,4},{9,5},{12,8},{13,9},{14,12},{15,13},... | collective-permute-start | bytes 798728 | tf_op jit(solution)/shard_map/ppermute | solution.py:467
  16.3 22.8 %collective-permute-start.15 = (f32[1040,128]{1,0:T(8,128)S(1)}, f32[1040,128]{1,0:T(8,128)S(1)}, u32[]{:S(2)}, u32[]{:S(2)}) collective-permute-start(f32[1040,128]{1,0:T(8,128)S(1)} %get-tuple-element.69), channel_id=1, source_target_pairs={{0,16},{16,0},{1,17},{17,1},{2,18},{18,2},{3,19},{19,3},{4,20},{20... | collective-permute-start | bytes 1597448 | tf_op jit(solution)/shard_map/ppermute | solution.py:473
  20.0 9.3 %collective-permute-start.6 = (f32[520,128]{1,0:T(8,128)S(1)}, f32[520,128]{1,0:T(8,128)S(1)}, u32[]{:S(2)}, u32[]{:S(2)}) collective-permute-start(f32[520,128]{1,0:T(8,128)S(1)} %collective-permute-done.2.refs_2_), channel_id=1, source_target_pairs={{0,4},{1,5},{4,8},{5,9},{8,12},{9,13},{12,14},{13,15},{14,10},{15,... | collective-permute-start | bytes 798728 | tf_op jit(solution)/shard_map/ppermute | solution.py:467
  21.6 9.8 %collective-permute-start.7 = (f32[520,128]{1,0:T(8,128)S(1)}, f32[520,128]{1,0:T(8,128)S(1)}, u32[]{:S(2)}, u32[]{:S(2)}) collective-permute-start(f32[520,128]{1,0:T(8,128)S(1)} %collective-permute-done.3.refs_3_), channel_id=1, source_target_pairs={{0,2},{1,3},{4,0},{5,1},{8,4},{9,5},{12,8},{13,9},{14,12},{15,13},... | collective-permute-start | bytes 798728 | tf_op jit(solution)/shard_map/ppermute | solution.py:467
  25.7 9.3 %collective-permute-start.9 = (f32[520,128]{1,0:T(8,128)S(1)}, f32[520,128]{1,0:T(8,128)S(1)}, u32[]{:S(2)}, u32[]{:S(2)}) collective-permute-start(f32[520,128]{1,0:T(8,128)S(1)} %collective-permute-done.5.refs_1_), channel_id=1, source_target_pairs={{0,4},{1,5},{4,8},{5,9},{8,12},{9,13},{12,14},{13,15},{14,10},{15,... | collective-permute-start | bytes 798728 | tf_op jit(solution)/shard_map/ppermute | solution.py:467
  27.3 9.8 %collective-permute-start.12 = (f32[520,128]{1,0:T(8,128)S(1)}, f32[520,128]{1,0:T(8,128)S(1)}, u32[]{:S(2)}, u32[]{:S(2)}) collective-permute-start(f32[520,128]{1,0:T(8,128)S(1)} %collective-permute-done.8.refs_4_), channel_id=1, source_target_pairs={{0,2},{1,3},{4,0},{5,1},{8,4},{9,5},{12,8},{13,9},{14,12},{15,13},... | collective-permute-start | bytes 798728 | tf_op jit(solution)/shard_map/ppermute | solution.py:467
  29.3 12.6 %collective-permute-start.10 = (f32[520,128]{1,0:T(8,128)S(1)}, f32[520,128]{1,0:T(8,128)S(1)}, u32[]{:S(2)}, u32[]{:S(2)}) collective-permute-start(f32[520,128]{1,0:T(8,128)S(1)} %collective-permute-done.6.refs_2_), channel_id=1, source_target_pairs={{0,4},{1,5},{4,8},{5,9},{8,12},{9,13},{12,14},{13,15},{14,10},{15,... | collective-permute-start | bytes 798728 | tf_op jit(solution)/shard_map/ppermute | solution.py:467
  31.4 11.4 %collective-permute-start.11 = (f32[520,128]{1,0:T(8,128)S(1)}, f32[520,128]{1,0:T(8,128)S(1)}, u32[]{:S(2)}, u32[]{:S(2)}) collective-permute-start(f32[520,128]{1,0:T(8,128)S(1)} %collective-permute-done.7.refs_3_), channel_id=1, source_target_pairs={{0,2},{1,3},{4,0},{5,1},{8,4},{9,5},{12,8},{13,9},{14,12},{15,13},... | collective-permute-start | bytes 798728 | tf_op jit(solution)/shard_map/ppermute | solution.py:467
  37.1 9.1 %collective-permute-start.13 = (f32[520,128]{1,0:T(8,128)S(1)}, f32[520,128]{1,0:T(8,128)S(1)}, u32[]{:S(2)}, u32[]{:S(2)}) collective-permute-start(f32[520,128]{1,0:T(8,128)S(1)} %collective-permute-done.9.refs_1_), channel_id=1, source_target_pairs={{0,4},{1,5},{4,8},{5,9},{8,12},{9,13},{12,14},{13,15},{14,10},{15,... | collective-permute-start | bytes 798728 | tf_op jit(solution)/shard_map/ppermute | solution.py:467
  38.7 9.1 %collective-permute-start.14 = (f32[520,128]{1,0:T(8,128)S(1)}, f32[520,128]{1,0:T(8,128)S(1)}, u32[]{:S(2)}, u32[]{:S(2)}) collective-permute-start(f32[520,128]{1,0:T(8,128)S(1)} %collective-permute-done.12.refs_4_), channel_id=1, source_target_pairs={{0,2},{1,3},{4,0},{5,1},{8,4},{9,5},{12,8},{13,9},{14,12},{15,13},... | collective-permute-start | bytes 798728 | tf_op jit(solution)/shard_map/ppermute | solution.py:467
  40.4 4.7 %collective-permute-start.16 = (f32[8,128]{1,0:T(8,128)S(1)}, f32[8,128]{1,0:T(8,128)S(1)}, u32[]{:S(2)}, u32[]{:S(2)}) collective-permute-start(f32[8,128]{1,0:T(8,128)S(1)} %get-tuple-element.70), channel_id=1, source_target_pairs={{0,16},{16,0},{1,17},{17,1},{2,18},{18,2},{3,19},{19,3},{4,20},{20... | collective-permute-start | bytes 12296 | tf_op jit(solution)/shard_map/ppermute | solution.py:473
  49.7 4.0 %collective-permute-start.17 = (f32[64,128]{1,0:T(8,128)S(1)}, f32[64,128]{1,0:T(8,128)S(1)}, u32[]{:S(2)}, u32[]{:S(2)}) collective-permute-start(f32[64,128]{1,0:T(8,128)S(1)} %get-tuple-element.73), channel_id=1, source_target_pairs={{0,2},{1,3},{2,0},{3,1},{4,6},{5,7},{6,4},{7,5},{8,10},{9,11},{10,... | collective-permute-start | bytes 98312 | tf_op jit(solution)/shard_map/ppermute | solution.py:470
  53.7 3.9 %collective-permute-start.18 = (f32[64,128]{1,0:T(8,128)S(1)}, f32[64,128]{1,0:T(8,128)S(1)}, u32[]{:S(2)}, u32[]{:S(2)}) collective-permute-start(f32[64,128]{1,0:T(8,128)S(1)} %add.12), channel_id=1, source_target_pairs={{0,4},{1,5},{2,6},{3,7},{4,0},{5,1},{6,2},{7,3},{8,12},{9,13},{10,... | collective-permute-start | bytes 98312 | tf_op jit(solution)/shard_map/ppermute | solution.py:470
  57.6 4.8 %collective-permute-start.19 = (f32[64,128]{1,0:T(8,128)S(1)}, f32[64,128]{1,0:T(8,128)S(1)}, u32[]{:S(2)}, u32[]{:S(2)}) collective-permute-start(f32[64,128]{1,0:T(8,128)S(1)} %add.13.mine), channel_id=1, source_target_pairs={{0,8},{1,9},{2,10},{3,11},{4,12},{5,13},{6,14},{7,15},{8,0},{9,1},... | collective-permute-start | bytes 98312 | tf_op jit(solution)/shard_map/ppermute | solution.py:470
  62.4 3.7 %collective-permute-start.20 = (f32[8,128]{1,0:T(8,128)S(1)}, f32[8,128]{1,0:T(8,128)S(1)}, u32[]{:S(2)}, u32[]{:S(2)}) collective-permute-start(f32[8,128]{1,0:T(8,128)S(1)} %get-tuple-element.81), channel_id=1, source_target_pairs={{0,16},{16,0},{1,17},{17,1},{2,18},{18,2},{3,19},{19,3},{4,20},{20... | collective-permute-start | bytes 12296 | tf_op jit(solution)/shard_map/ppermute | solution.py:473
  64.0 2.9 %copy-start = (f32[32,128]{1,0:T(8,128)S(1)}, f32[32,128]{1,0:T(8,128)}, u32[]{:S(2)}) copy-start(f32[32,128]{1,0:T(8,128)} %target_mass.1) | copy-start | bytes 49156
  66.8 1.3 %collective-permute-start.21 = (f32[64,128]{1,0:T(8,128)S(1)}, f32[64,128]{1,0:T(8,128)S(1)}, u32[]{:S(2)}, u32[]{:S(2)}) collective-permute-start(f32[64,128]{1,0:T(8,128)S(1)} %far_column_sums.2.refs_5_.mine), channel_id=1, source_target_pairs={{0,1},{1,0},{2,3},{3,2},{4,5},{5,4},{6,7},{7,6},{8,9},{9,8},{10,11... | collective-permute-start | bytes 98312 | tf_op jit(solution)/shard_map/ppermute | solution.py:470
  66.9 3.6 %collective-permute-start.22 = (f32[32,128]{1,0:T(8,128)S(1)}, f32[32,128]{1,0:T(8,128)S(1)}, u32[]{:S(2)}, u32[]{:S(2)}) collective-permute-start(f32[32,128]{1,0:T(8,128)S(1)} %copy-done), channel_id=1, source_target_pairs={{0,1},{1,0},{2,3},{3,2},{4,5},{5,4},{6,7},{7,6},{8,9},{9,8},{10,11... | collective-permute-start | bytes 49160 | tf_op jit(solution)/shard_map/ppermute | solution.py:470
  68.9 3.7 %collective-permute-start.23 = (f32[8,128]{1,0:T(8,128)S(1)}, f32[8,128]{1,0:T(8,128)S(1)}, u32[]{:S(2)}, u32[]{:S(2)}) collective-permute-start(f32[8,128]{1,0:T(8,128)S(1)} %far_row_sums.1), channel_id=1, source_target_pairs={{0,16},{16,0},{1,17},{17,1},{2,18},{18,2},{3,19},{19,3},{4,20},{20... | collective-permute-start | bytes 12296 | tf_op jit(solution)/shard_map/ppermute | solution.py:473
  72.6 4.0 %collective-permute-start.24 = (f32[64,128]{1,0:T(8,128)S(1)}, f32[64,128]{1,0:T(8,128)S(1)}, u32[]{:S(2)}, u32[]{:S(2)}) collective-permute-start(f32[64,128]{1,0:T(8,128)S(1)} %add_own.1), channel_id=1, source_target_pairs={{0,2},{1,3},{2,0},{3,1},{4,6},{5,7},{6,4},{7,5},{8,10},{9,11},{10,... | collective-permute-start | bytes 98312 | tf_op jit(solution)/shard_map/ppermute | solution.py:470
  76.6 3.9 %collective-permute-start.25 = (f32[64,128]{1,0:T(8,128)S(1)}, f32[64,128]{1,0:T(8,128)S(1)}, u32[]{:S(2)}, u32[]{:S(2)}) collective-permute-start(f32[64,128]{1,0:T(8,128)S(1)} %add.14), channel_id=1, source_target_pairs={{0,4},{1,5},{2,6},{3,7},{4,0},{5,1},{6,2},{7,3},{8,12},{9,13},{10,... | collective-permute-start | bytes 98312 | tf_op jit(solution)/shard_map/ppermute | solution.py:470
  80.5 5.2 %collective-permute-start.26 = (f32[64,128]{1,0:T(8,128)S(1)}, f32[64,128]{1,0:T(8,128)S(1)}, u32[]{:S(2)}, u32[]{:S(2)}) collective-permute-start(f32[64,128]{1,0:T(8,128)S(1)} %add.15.mine), channel_id=1, source_target_pairs={{0,8},{1,9},{2,10},{3,11},{4,12},{5,13},{6,14},{7,15},{8,0},{9,1},... | collective-permute-start | bytes 98312 | tf_op jit(solution)/shard_map/ppermute | solution.py:470
  85.7 3.7 %collective-permute-start.27 = (f32[8,128]{1,0:T(8,128)S(1)}, f32[8,128]{1,0:T(8,128)S(1)}, u32[]{:S(2)}, u32[]{:S(2)}) collective-permute-start(f32[8,128]{1,0:T(8,128)S(1)} %get-tuple-element.84.rows), channel_id=1, source_target_pairs={{0,16},{16,0},{1,17},{17,1},{2,18},{18,2},{3,19},{19,3},{4,20},{20... | collective-permute-start | bytes 12296 | tf_op jit(solution)/shard_map/ppermute | solution.py:473
  86.9 4.5 %copy-start.1 = (f32[8,128]{1,0:T(8,128)S(1)}, f32[8,128]{1,0:T(8,128)}, u32[]{:S(2)}) copy-start(f32[8,128]{1,0:T(8,128)} %mass.5) | copy-start | bytes 12292
  90.1 1.3 %collective-permute-start.28 = (f32[64,128]{1,0:T(8,128)S(1)}, f32[64,128]{1,0:T(8,128)S(1)}, u32[]{:S(2)}, u32[]{:S(2)}) collective-permute-start(f32[64,128]{1,0:T(8,128)S(1)} %far_column_sums.3.mine), channel_id=1, source_target_pairs={{0,1},{1,0},{2,3},{3,2},{4,5},{5,4},{6,7},{7,6},{8,9},{9,8},{10,11... | collective-permute-start | bytes 98312 | tf_op jit(solution)/shard_map/ppermute | solution.py:470

commit v4 on v3

--- a/solution.py
+++ b/solution.py
@@ -24,6 +24,10 @@
 
 def in_vmem(*arrays):
     return [pltpu.with_memory_space_constraint(x, pltpu.VMEM) for x in arrays]
+
+
+def in_smem(*arrays):
+    return [pltpu.with_memory_space_constraint(x, pltpu.SMEM) for x in arrays]
 
 
 def in_hbm(*arrays):
@@ -163,7 +167,7 @@
     weight = [refs.pop(0) for _ in range(sides)]
     rows_in, mass_in = (refs.pop(0), refs.pop(0)) if chained else (None, None)
     back = refs.pop(0) if closing else None
-    tiles, table, rows_out, mass_out, partial, staged, named, listed, arrived = refs
+    tiles, table, rows_out, mass_out, partial, units, staged, named, listed, arrived = refs
     count = chunks * sides * slots
     width = source[0].shape[1]
     scale = 1.0 / (width * entropic_regularizer)
@@ -180,6 +184,11 @@
     partial[...] = jnp.zeros_like(partial)
     place = lax.broadcasted_iota(jnp.int32, (8, 2 * width), 0)
     ones = jnp.where(place == 0, 1.0, 0.0).astype(jnp.bfloat16)
+    for chunk in range(chunks):
+        for block in range(sb):
+            rows = pl.ds(block * half, half)
+            left = jnp.concatenate([source[2 * chunk][rows], source[2 * chunk + 1][rows]], axis=0)
+            units[chunk * sb + block] = jnp.concatenate(split2(unit(left)), axis=1)
     copy.wait()
 
     chip_of = []
@@ -213,17 +222,14 @@
                 table[count + base + j] = jnp.where(valid, which + side * tb, 2 * tb)
 
     for chunk in range(chunks):
-        upper, lower = source[2 * chunk], source[2 * chunk + 1]
+        lower = source[2 * chunk + 1]
         for side in range(sides):
             for j in range(slots):
                 at = (chunk * sides + side) * slots + j
                 block = listed[at]
-                start = pl.multiple_of(lax.rem(block, sb) * half, half)
-                left = jnp.concatenate([upper[pl.ds(start, half)], lower[pl.ds(start, half)]], axis=0)
-                high, low = split2(unit(left))
                 right = weight[side][table[at] if far else lax.rem(table[count + at], tb)]
                 both = lax.dot_general(
-                    jnp.concatenate([high, low], axis=1),
+                    units[chunk * sb + lax.rem(block, sb)],
                     jnp.concatenate([right, right], axis=0),
                     NN,
                     preferred_element_type=jnp.float32,
@@ -256,7 +262,7 @@
         functools.partial(tile_kernel, plan),
         out_shape=(
             pltpu.VMEM((count, 2 * half, 2 * nodes), jnp.bfloat16),
-            jax.ShapeDtypeStruct((count if far else 2 * count + 1,), jnp.int32),
+            pltpu.SMEM((count if far else 2 * count + 1,), jnp.int32),
             rows,
             rows,
         ),
@@ -264,6 +270,7 @@
         out_specs=(VMEM, SMEM, VMEM, VMEM),
         scratch_shapes=[
             pltpu.VMEM((chunks * (sb + 1), 8, 2 * half), jnp.float32),
+            pltpu.VMEM((chunks * sb, 2 * half, 2 * width), jnp.bfloat16),
             pltpu.VMEM((chunks * sb, width), jnp.int32),
             pltpu.SMEM((chunks * sb, width), jnp.int32),
             pltpu.SMEM((count + 1,), jnp.int32),
@@ -278,24 +285,25 @@
 SMALL = pltpu.CompilerParams(vmem_limit_bytes=16 << 20)
 
 
-def add_kernel(device, mine, theirs, total, own):
+def add_kernel(device, *refs):
+    parts, total, own = refs[:-2], refs[-2], refs[-1]
     sb = own.shape[0]
-    total[...] = mine[...] + theirs[...]
+    total[...] = sum([part[...] for part in parts[1:]], parts[0][...])
     own[...] = total[pl.ds(pl.multiple_of(device[0] // 2 * sb, sb), sb)]
 
 
-def add_last(device, mine, theirs, sb):
+def add_last(device, parts, sb):
     return pl.pallas_call(
         add_kernel,
         out_shape=(
-            jax.ShapeDtypeStruct(mine.shape, jnp.float32),
-            jax.ShapeDtypeStruct((sb, mine.shape[1]), jnp.float32),
+            jax.ShapeDtypeStruct(parts[0].shape, jnp.float32),
+            jax.ShapeDtypeStruct((sb, parts[0].shape[1]), jnp.float32),
         ),
-        in_specs=[SMEM, VMEM, VMEM],
+        in_specs=[SMEM] + [VMEM] * len(parts),
         out_specs=(VMEM, VMEM),
         compiler_params=SMALL,
         name="add_last",
-    )(device, mine, theirs)
+    )(device, *parts)
 
 
 def insert_kernel(device, rows, part, out):
@@ -347,7 +355,7 @@
         cost_estimate=LIGHT,
         compiler_params=SMALL,
         name="column_sums",
-    )(*tables, rows, mass, *in_vmem(*tiles))
+    )(*in_smem(*tables), rows, mass, *in_vmem(*tiles))
 
 
 def far_column_kernel(far_at, sums, far_rows, far_mass, tiles, out, scale):
@@ -369,7 +377,7 @@
         cost_estimate=LIGHT,
         compiler_params=SMALL,
         name="far_column_sums",
-    )(far_at, sums, far_rows, far_mass, *in_vmem(tiles))
+    )(*in_smem(far_at), sums, far_rows, far_mass, *in_vmem(tiles))
 
 
 def scale_kernel(rows, mass, mine, theirs, target_mass, src, tgt):
@@ -410,7 +418,7 @@
         cost_estimate=LIGHT,
         compiler_params=SMALL,
         name="far_row_sums",
-    )(far_at, mine, theirs, mass, *in_vmem(tiles))
+    )(*in_smem(far_at), mine, theirs, mass, *in_vmem(tiles))
 
 
 def row_kernel(counts, *refs):
@@ -447,7 +455,7 @@
         cost_estimate=LIGHT,
         compiler_params=SMALL,
         name="row_sums",
-    )(*tables, mine, theirs, mass, other_mass, *in_vmem(*tiles))
+    )(*in_smem(*tables), mine, theirs, mass, other_mass, *in_vmem(*tiles))
 
 
 def local(source_emb, target_emb, source_mass, target_mass, cand_device, cand_block):
@@ -513,7 +521,7 @@
 
     def behind_job(step, *halves):
         if jobs and jobs[0][0] <= max(0, step - 2):
-            halves = lax.optimization_barrier((halves, jobs.pop(0)[1]()))[0]
+            halves = lax.optimization_barrier((halves, jobs.pop(0)[1](), sibling_mass))[0]
         return halves
 
     up_a, up_b, down_a, down_b = upper, lower, upper, lower
@@ -541,11 +549,14 @@
             back = to_group(far_rows, -1)
             near_rows = row_sums(tables, mine, theirs, target_mass, sibling_mass, tiles, chips * sb)
             near_rows = add_own(me, near_rows, back)
-        bit = 2
-        while 2 * bit < dev_count:
-            near_rows = near_rows + across(near_rows, bit)
-            bit *= 2
-        near_rows, own_rows = add_last(me, near_rows, across(near_rows, bit), sb)
+        bits = [1 << k for k in range(1, dev_count.bit_length() - 1)]
+        parts = [near_rows]
+        while bits:
+            ways = [bits.pop() for _ in range(2 - len(bits) % 2)]
+            ways = ways + [sum(ways)] if len(ways) == 2 else ways
+            total = sum(parts[1:], parts[0])
+            parts = [total] + [across(total, way) for way in ways]
+        near_rows, own_rows = add_last(me, parts, sb)
         far_rows = to_group(own_rows, 1)
         mine = column_sums(tables, near_rows, all_mass, tiles, 2 * tb)
         mine = far_column_sums(far_at, mine, far_rows, far_mass, far_tiles)

time: 92.2 us -> 88 us (0.954)
  waiting for transfers between devices: 31.5 us -> 27.6 us
  Pallas kernels: 26 us -> 23.2 us
  starting transfers between devices: 33.6 us -> 36 us
    ppermute x10 -> x12, waiting for transfers between devices: 17.5 us -> 13.3 us  [across(): return lax.ppermute(x, 'dev', [(i, i ^ bit) for i in range(dev_count)])]
    ppermute x10 -> x12, starting transfers between devices: 11.3 us -> 13.3 us  [across(): return lax.ppermute(x, 'dev', [(i, i ^ bit) for i in range(dev_count)])]
    ppermute x5, waiting for transfers between devices: 1.66 us -> 2.91 us  [to_group(): lax.ppermute(x, 'group', [(g, (g + by) % group_count) for g in range(grou...]
    pallas_call x2, Pallas kernels: 2.93 us -> 1.78 us  [column_sums(): pl.pallas_call(functools.partial(column_kernel, counts), out_shape=jax.Sh...]
    pallas_call x2, Pallas kernels: 1.46 us -> 0.38 us  [far_column_sums(): pl.pallas_call(far_column_kernel, out_shape=jax.ShapeDtypeStruct(sums.sha...]
    ppermute x14, waiting for transfers between devices: 12.4 us -> 11.4 us  [around(): return lax.ppermute(x, 'dev', pairs)]
  transfers between devices with their start and end apart: 29 -> 31, of which waited for: 19 -> 22; matrix products, arithmetic and copies ran while one was open for 0% -> 0% of each run, Pallas kernels for 24% -> 23%
where the time goes in v4:
time: 88 us; the launch traced here: 87.8 us
  starting transfers between devices  36 us (41%)
  waiting for transfers between devices  27.6 us (31%)
  Pallas kernels  23.2 us (26%)
    ppermute x14, starting transfers between devices, around(): return lax.ppermute(x, 'dev', pairs)  14.9 us
    ppermute x12, starting transfers between devices, across(): return lax.ppermute(x, 'dev', [(i, i ^ bit) for i in range(dev_count)])  13.3 us
    ppermute x12, waiting for transfers between devices, across(): return lax.ppermute(x, 'dev', [(i, i ^ bit) for i in range(dev_count)])  13.3 us
    pallas_call x6, Pallas kernels, build_tiles(): pl.pallas_call(functools.partial(tile_kernel, plan), out_shape=(pltpu.VME...  12.3 us
    ppermute x14, waiting for transfers between devices, around(): return lax.ppermute(x, 'dev', pairs)  11.4 us
    ppermute x5, starting transfers between devices, to_group(): lax.ppermute(x, 'group', [(g, (g + by) % group_count) for g in range(grou...  7.86 us
    pallas_call x2, Pallas kernels, target_operand(): pl.pallas_call(target_kernel, out_shape=pltpu.VMEM((blocks, width, 2 * ro...  5.09 us
    ppermute x5, waiting for transfers between devices, to_group(): lax.ppermute(x, 'group', [(g, (g + by) % group_count) for g in range(grou...  2.91 us
  transfers between devices with their start and end apart: 31, of which 22 were waited for; matrix products, arithmetic and copies ran while one was open for 0% of the time, Pallas kernels for 23%

profile of v4, /device:TPU:0, one launch (start us, length us, event | category | flops | bytes accessed | tf_op | source)
XLA Modules:
  0.0 87.8 jit_solution(11609727148128861256)
XLA Ops:
  0.6 0.5 collective-permute-start
  1.1 1.2 %pack.1 = (f32[520,128]{1,0:T(8,128)S(1)}, f32[520,128]{1,0:T(8,128)S(1)}, f32[1040,128]{1,0:T(8,128)S(1)}) custom-call(s32[1]{0:T(128)} %bitcast.device.refs_0_, f32[8,128,128]{2,1,0:T(8,128)} %emb.1, f32[8,128]{1,0:T(8,128)} %mass.5, s32[8,7]{1,0:T(8,128)} %cand_device.1, s32[8,8]{1,0:T(8,128)} %cand_block.1), custom_call_target="tpu_custom_call" | custom-call | tf_op jit(solution)/shard_map/pack/pallas_call | solution.py:135
  2.4 2.6 %collective-permute-start.1 = (f32[520,128]{1,0:T(8,128)S(1)}, f32[520,128]{1,0:T(8,128)S(1)}, u32[]{:S(2)}, u32[]{:S(2)}) collective-permute-start(f32[520,128]{1,0:T(8,128)S(1)} %get-tuple-element.48.refs_1_), channel_id=1, source_target_pairs={{0,4},{1,5},{4,8},{5,9},{8,12},{9,13},{12,14},{13,15},{14,10},{15,... | collective-permute-start | bytes 798728 | tf_op jit(solution)/shard_map/ppermute | solution.py:475
  5.0 0.2 collective-permute-start.2
  5.3 2.9 %target_operand.2.refs_3_.refs_5_.refs_2_ = bf16[32,128,256]{2,1,0:T(8,128)(2,1)S(1)} custom-call(f32[32,128,128]{2,1,0:T(8,128)} %emb_ref.1), custom_call_target="tpu_custom_call" | custom-call | flops 1 | bytes 1 | tf_op jit(solution)/shard_map/target_operand/pallas_call | solution.py:91
  8.2 1.9 %collective-permute-start.3 = (f32[520,128]{1,0:T(8,128)S(1)}, f32[520,128]{1,0:T(8,128)S(1)}, u32[]{:S(2)}, u32[]{:S(2)}) collective-permute-start(f32[520,128]{1,0:T(8,128)S(1)} %get-tuple-element.47.refs_2_), channel_id=1, source_target_pairs={{0,4},{1,5},{4,8},{5,9},{8,12},{9,13},{12,14},{13,15},{14,10},{15,... | collective-permute-start | bytes 798728 | tf_op jit(solution)/shard_map/ppermute | solution.py:475
  10.1 0.2 collective-permute-start.4
  10.3 2.1 %target_operand.3.refs_4_.refs_6_ = bf16[32,128,256]{2,1,0:T(8,128)(2,1)S(1)} custom-call(f32[32,128,128]{2,1,0:T(8,128)S(1)} %collective-permute-done.emb_ref), custom_call_target="tpu_custom_call" | custom-call | flops 1 | bytes 1 | tf_op jit(solution)/shard_map/target_operand/pallas_call | solution.py:91
  12.5 1.7 %collective-permute-done.5.refs_4_ = f32[520,128]{1,0:T(8,128)S(1)} collective-permute-done((f32[520,128]{1,0:T(8,128)S(1)}, f32[520,128]{1,0:T(8,128)S(1)}, u32[]{:S(2)}, u32[]{:S(2)}) %collective-permute-start.5) | collective-permute-done | bytes 266272 | tf_op jit(solution)/shard_map/ppermute | solution.py:475
  14.1 1.6 %collective-permute-start.6 = (f32[520,128]{1,0:T(8,128)S(1)}, f32[520,128]{1,0:T(8,128)S(1)}, u32[]{:S(2)}, u32[]{:S(2)}) collective-permute-start(f32[520,128]{1,0:T(8,128)S(1)} %collective-permute-done.1.refs_1_), channel_id=1, source_target_pairs={{0,4},{1,5},{4,8},{5,9},{8,12},{9,13},{12,14},{13,15},{14,10},{15,... | collective-permute-start | bytes 798728 | tf_op jit(solution)/shard_map/ppermute | solution.py:475
  15.7 0.4 collective-permute-start.9
  16.1 1.5 %collective-permute-start.16 = (f32[1040,128]{1,0:T(8,128)S(1)}, f32[1040,128]{1,0:T(8,128)S(1)}, u32[]{:S(2)}, u32[]{:S(2)}) collective-permute-start(f32[1040,128]{1,0:T(8,128)S(1)} %get-tuple-element.69), channel_id=1, source_target_pairs={{0,16},{16,0},{1,17},{17,1},{2,18},{18,2},{3,19},{19,3},{4,20},{20... | collective-permute-start | bytes 1597448 | tf_op jit(solution)/shard_map/ppermute | solution.py:481
  17.7 1.7 %build_tiles.6 = (bf16[10,128,256]{2,1,0:T(8,128)(2,1)S(1)}, s32[21]{0:T(128)S(4)}, f32[64,128]{1,0:T(8,128)S(1)}, f32[64,128]{1,0:T(8,128)S(1)}) custom-call(s32[1]{0:T(128)} %bitcast.device.refs_0_, f32[520,128]{1,0:T(8,128)S(1)} %get-tuple-element.48.refs_1_, f32[520,128]{1,0:T(8,128)S(1)} %get-tuple-element.47.refs_2_, ...), custom_call_target="tpu_custom_call" | custom-call | flops 1 | bytes 1 | tf_op jit(solution)/shard_map/build_tiles/pallas_call | solution.py:261
  19.4 0.5 collective-permute-done.4.refs_3_
  19.8 1.6 %collective-permute-start.7 = (f32[520,128]{1,0:T(8,128)S(1)}, f32[520,128]{1,0:T(8,128)S(1)}, u32[]{:S(2)}, u32[]{:S(2)}) collective-permute-start(f32[520,128]{1,0:T(8,128)S(1)} %collective-permute-done.3.refs_2_), channel_id=1, source_target_pairs={{0,4},{1,5},{4,8},{5,9},{8,12},{9,13},{12,14},{13,15},{14,10},{15,... | collective-permute-start | bytes 798728 | tf_op jit(solution)/shard_map/ppermute | solution.py:475
  21.4 0.4 collective-permute-start.8
  21.9 2.5 %build_tiles.7 = (bf16[20,128,256]{2,1,0:T(8,128)(2,1)S(1)}, s32[41]{0:T(128)S(4)}, f32[64,128]{1,0:T(8,128)S(1)}, f32[64,128]{1,0:T(8,128)S(1)}) custom-call(s32[1]{0:T(128)} %bitcast.device.refs_0_, f32[520,128]{1,0:T(8,128)S(1)} %collective-permute-done.1.refs_1_, f32[520,128]{1,0:T(8,128)S(1)} %collective-permute-done.3.refs_2_, ...), custom_call_target="tpu_custom_call" | custom-call | flops 1 | bytes 1 | tf_op jit(solution)/shard_map/build_tiles/pallas_call | solution.py:261
  24.4 1.1 %collective-permute-done.9.refs_4_ = f32[520,128]{1,0:T(8,128)S(1)} collective-permute-done((f32[520,128]{1,0:T(8,128)S(1)}, f32[520,128]{1,0:T(8,128)S(1)}, u32[]{:S(2)}, u32[]{:S(2)}) %collective-permute-start.9) | collective-permute-done | bytes 266272 | tf_op jit(solution)/shard_map/ppermute | solution.py:475
  25.5 1.6 %collective-permute-start.10 = (f32[520,128]{1,0:T(8,128)S(1)}, f32[520,128]{1,0:T(8,128)S(1)}, u32[]{:S(2)}, u32[]{:S(2)}) collective-permute-start(f32[520,128]{1,0:T(8,128)S(1)} %collective-permute-done.6.refs_1_), channel_id=1, source_target_pairs={{0,4},{1,5},{4,8},{5,9},{8,12},{9,13},{12,14},{13,15},{14,10},{15,... | collective-permute-start | bytes 798728 | tf_op jit(solution)/shard_map/ppermute | solution.py:475
  27.1 0.4 collective-permute-start.13
  27.6 1.8 %collective-permute-done.7.refs_2_ = f32[520,128]{1,0:T(8,128)S(1)} collective-permute-done((f32[520,128]{1,0:T(8,128)S(1)}, f32[520,128]{1,0:T(8,128)S(1)}, u32[]{:S(2)}, u32[]{:S(2)}) %collective-permute-start.7) | collective-permute-done | bytes 266272 | tf_op jit(solution)/shard_map/ppermute | solution.py:475
  29.3 2.0 %collective-permute-start.11 = (f32[520,128]{1,0:T(8,128)S(1)}, f32[520,128]{1,0:T(8,128)S(1)}, u32[]{:S(2)}, u32[]{:S(2)}) collective-permute-start(f32[520,128]{1,0:T(8,128)S(1)} %collective-permute-done.7.refs_2_), channel_id=1, source_target_pairs={{0,4},{1,5},{4,8},{5,9},{8,12},{9,13},{12,14},{13,15},{14,10},{15,... | collective-permute-start | bytes 798728 | tf_op jit(solution)/shard_map/ppermute | solution.py:475
  31.4 2.5 %build_tiles.8 = (bf16[20,128,256]{2,1,0:T(8,128)(2,1)S(1)}, s32[41]{0:T(128)S(4)}, f32[64,128]{1,0:T(8,128)S(1)}, f32[64,128]{1,0:T(8,128)S(1)}) custom-call(s32[1]{0:T(128)} %bitcast.device.refs_0_, f32[520,128]{1,0:T(8,128)S(1)} %collective-permute-done.6.refs_1_, f32[520,128]{1,0:T(8,128)S(1)} %collective-permute-done.7.refs_2_, ...), custom_call_target="tpu_custom_call" | custom-call | flops 1 | bytes 1 | tf_op jit(solution)/shard_map/build_tiles/pallas_call | solution.py:261
  33.9 1.1 %collective-permute-done.10.refs_1_ = f32[520,128]{1,0:T(8,128)S(1)} collective-permute-done((f32[520,128]{1,0:T(8,128)S(1)}, f32[520,128]{1,0:T(8,128)S(1)}, u32[]{:S(2)}, u32[]{:S(2)}) %collective-permute-start.10) | collective-permute-done | bytes 266272 | tf_op jit(solution)/shard_map/ppermute | solution.py:475
  35.0 1.9 %collective-permute-done.13.refs_4_ = f32[520,128]{1,0:T(8,128)S(1)} collective-permute-done((f32[520,128]{1,0:T(8,128)S(1)}, f32[520,128]{1,0:T(8,128)S(1)}, u32[]{:S(2)}, u32[]{:S(2)}) %collective-permute-start.13) | collective-permute-done | bytes 266272 | tf_op jit(solution)/shard_map/ppermute | solution.py:475
  36.9 1.6 %collective-permute-start.14 = (f32[520,128]{1,0:T(8,128)S(1)}, f32[520,128]{1,0:T(8,128)S(1)}, u32[]{:S(2)}, u32[]{:S(2)}) collective-permute-start(f32[520,128]{1,0:T(8,128)S(1)} %collective-permute-done.10.refs_1_), channel_id=1, source_target_pairs={{0,4},{1,5},{4,8},{5,9},{8,12},{9,13},{12,14},{13,15},{14,10},{15,... | collective-permute-start | bytes 798728 | tf_op jit(solution)/shard_map/ppermute | solution.py:475
  38.5 0.4 collective-permute-start.15
  39.0 1.3 %build_tiles.10 = (bf16[8,128,256]{2,1,0:T(8,128)(2,1)S(1)}, s32[8]{0:T(128)S(4)}, f32[8,128]{1,0:T(8,128)S(1)}, f32[8,128]{1,0:T(8,128)S(1)}) custom-call(s32[1]{0:T(128)} %bitcast.device.refs_0_, f32[1040,128]{1,0:T(8,128)S(1)} %collective-permute-done.16.refs_1_, bf16[32,128,256]{2,1,0:T(8,128)(2,1)S(1)} %target_operand.2.refs_3_.refs_5_.refs_2_), custom_call_target="tpu_custom_call" | custom-call | flops 1 | bytes 1 | tf_op jit(solution)/shard_map/build_tiles/pallas_call | solution.py:261
  40.3 1.6 %collective-permute-start.17 = (f32[8,128]{1,0:T(8,128)S(1)}, f32[8,128]{1,0:T(8,128)S(1)}, u32[]{:S(2)}, u32[]{:S(2)}) collective-permute-start(f32[8,128]{1,0:T(8,128)S(1)} %get-tuple-element.70), channel_id=1, source_target_pairs={{0,16},{16,0},{1,17},{17,1},{2,18},{18,2},{3,19},{19,3},{4,20},{20... | collective-permute-start | bytes 12296 | tf_op jit(solution)/shard_map/ppermute | solution.py:481
  41.9 0.7 collective-permute-done.12.refs_3_
  42.6 2.5 %build_tiles.9 = (bf16[20,128,256]{2,1,0:T(8,128)(2,1)S(1)}, s32[41]{0:T(128)S(4)}, f32[64,128]{1,0:T(8,128)S(1)}, f32[64,128]{1,0:T(8,128)S(1)}) custom-call(s32[1]{0:T(128)} %bitcast.device.refs_0_, f32[520,128]{1,0:T(8,128)S(1)} %collective-permute-done.10.refs_1_, f32[520,128]{1,0:T(8,128)S(1)} %collective-permute-done.11.refs_2_, ...), custom_call_target="tpu_custom_call" | custom-call | flops 1 | bytes 1 | tf_op jit(solution)/shard_map/build_tiles/pallas_call | solution.py:261
  45.2 1.0 %collective-permute-done.14.refs_1_ = f32[520,128]{1,0:T(8,128)S(1)} collective-permute-done((f32[520,128]{1,0:T(8,128)S(1)}, f32[520,128]{1,0:T(8,128)S(1)}, u32[]{:S(2)}, u32[]{:S(2)}) %collective-permute-start.14) | collective-permute-done | bytes 266272 | tf_op jit(solution)/shard_map/ppermute | solution.py:475
  46.2 1.5 %collective-permute-done.15.refs_2_ = f32[520,128]{1,0:T(8,128)S(1)} collective-permute-done((f32[520,128]{1,0:T(8,128)S(1)}, f32[520,128]{1,0:T(8,128)S(1)}, u32[]{:S(2)}, u32[]{:S(2)}) %collective-permute-start.15) | collective-permute-done | bytes 266272 | tf_op jit(solution)/shard_map/ppermute | solution.py:475
  47.8 1.7 %build_tiles.11 = (bf16[10,128,256]{2,1,0:T(8,128)(2,1)S(1)}, s32[21]{0:T(128)S(4)}, f32[64,128]{1,0:T(8,128)S(1)}, f32[64,128]{1,0:T(8,128)S(1)}) custom-call(s32[1]{0:T(128)} %bitcast.device.refs_0_, f32[520,128]{1,0:T(8,128)S(1)} %collective-permute-done.14.refs_1_, f32[520,128]{1,0:T(8,128)S(1)} %collective-permute-done.15.refs_2_, ...), custom_call_target="tpu_custom_call" | custom-call | flops 1 | bytes 1 | tf_op jit(solution)/shard_map/build_tiles/pallas_call | solution.py:261
  49.5 2.7 %collective-permute-start.18 = (f32[64,128]{1,0:T(8,128)S(1)}, f32[64,128]{1,0:T(8,128)S(1)}, u32[]{:S(2)}, u32[]{:S(2)}) collective-permute-start(f32[64,128]{1,0:T(8,128)S(1)} %get-tuple-element.73), channel_id=1, source_target_pairs={{0,8},{1,9},{2,10},{3,11},{4,12},{5,13},{6,14},{7,15},{8,0},{9,1},... | collective-permute-start | bytes 98312 | tf_op jit(solution)/shard_map/ppermute | solution.py:478
  52.1 2.2 %collective-permute-done.18 = f32[64,128]{1,0:T(8,128)S(1)} collective-permute-done((f32[64,128]{1,0:T(8,128)S(1)}, f32[64,128]{1,0:T(8,128)S(1)}, u32[]{:S(2)}, u32[]{:S(2)}) %collective-permute-start.18) | collective-permute-done | bytes 32800 | tf_op jit(solution)/shard_map/ppermute | solution.py:478
  54.4 1.6 %collective-permute-start.19 = (f32[64,128]{1,0:T(8,128)S(1)}, f32[64,128]{1,0:T(8,128)S(1)}, u32[]{:S(2)}, u32[]{:S(2)}) collective-permute-start(f32[64,128]{1,0:T(8,128)S(1)} %add.6.refs_0_), channel_id=1, source_target_pairs={{0,4},{1,5},{2,6},{3,7},{4,0},{5,1},{6,2},{7,3},{8,12},{9,13},{10,... | collective-permute-start | bytes 98312 | tf_op jit(solution)/shard_map/ppermute | solution.py:478
  55.9 0.4 collective-permute-start.20
  56.3 1.5 %collective-permute-start.21 = (f32[64,128]{1,0:T(8,128)S(1)}, f32[64,128]{1,0:T(8,128)S(1)}, u32[]{:S(2)}, u32[]{:S(2)}) collective-permute-start(f32[64,128]{1,0:T(8,128)S(1)} %add.6.refs_0_), channel_id=1, source_target_pairs={{0,6},{1,7},{2,4},{3,5},{4,2},{5,3},{6,0},{7,1},{8,14},{9,15},{10,... | collective-permute-start | bytes 98312 | tf_op jit(solution)/shard_map/ppermute | solution.py:478
  57.9 0.7 collective-permute-done.19.refs_1_
  58.5 1.3 %collective-permute-done.20.refs_2_ = f32[64,128]{1,0:T(8,128)S(1)} collective-permute-done((f32[64,128]{1,0:T(8,128)S(1)}, f32[64,128]{1,0:T(8,128)S(1)}, u32[]{:S(2)}, u32[]{:S(2)}) %collective-permute-start.20) | collective-permute-done | bytes 32800 | tf_op jit(solution)/shard_map/ppermute | solution.py:478
  59.9 1.3 %collective-permute-done.21.refs_3_ = f32[64,128]{1,0:T(8,128)S(1)} collective-permute-done((f32[64,128]{1,0:T(8,128)S(1)}, f32[64,128]{1,0:T(8,128)S(1)}, u32[]{:S(2)}, u32[]{:S(2)}) %collective-permute-start.21) | collective-permute-done | bytes 32800 | tf_op jit(solution)/shard_map/ppermute | solution.py:478
  61.1 1.6 %collective-permute-start.22 = (f32[8,128]{1,0:T(8,128)S(1)}, f32[8,128]{1,0:T(8,128)S(1)}, u32[]{:S(2)}, u32[]{:S(2)}) collective-permute-start(f32[8,128]{1,0:T(8,128)S(1)} %get-tuple-element.81), channel_id=1, source_target_pairs={{0,16},{16,0},{1,17},{17,1},{2,18},{18,2},{3,19},{19,3},{4,20},{20... | collective-permute-start | bytes 12296 | tf_op jit(solution)/shard_map/ppermute | solution.py:481
  62.7 0.9 %column_sums.2.sums = f32[64,128]{1,0:T(8,128)S(1)} custom-call(s32[21]{0:T(128)S(4)} %get-tuple-element.46.refs_0_, s32[41]{0:T(128)S(4)} %get-tuple-element.51.refs_1_, s32[41]{0:T(128)S(4)} %get-tuple-element.58.refs_2_, s32[41]{0:T(128)S(4)} %get-tuple-element.63.refs_3_, s32[21]{0:T(128)S(4)} %get-tuple-element.71.refs_4_, ...), custom_call_target="tpu_custom_call" | custom-call | flops 1 | bytes 1 | tf_op jit(solution)/shard_map/column_sums/pallas_call | solution.py:346
  63.6 1.2 %collective-permute-done.22.far_rows = f32[8,128]{1,0:T(8,128)S(1)} collective-permute-done((f32[8,128]{1,0:T(8,128)S(1)}, f32[8,128]{1,0:T(8,128)S(1)}, u32[]{:S(2)}, u32[]{:S(2)}) %collective-permute-start.22) | collective-permute-done | bytes 4128 | tf_op jit(solution)/shard_map/ppermute | solution.py:481
  64.8 0.2 far_column_sums.2.refs_5_.mine
  65.1 1.2 %collective-permute-done.23.refs_6_.theirs = f32[64,128]{1,0:T(8,128)S(1)} collective-permute-done((f32[64,128]{1,0:T(8,128)S(1)}, f32[64,128]{1,0:T(8,128)S(1)}, u32[]{:S(2)}, u32[]{:S(2)}) %collective-permute-start.23) | collective-permute-done | bytes 32800 | tf_op jit(solution)/shard_map/ppermute | solution.py:478
  66.3 0.2 far_row_sums.1
  66.5 1.6 %collective-permute-start.24 = (f32[8,128]{1,0:T(8,128)S(1)}, f32[8,128]{1,0:T(8,128)S(1)}, u32[]{:S(2)}, u32[]{:S(2)}) collective-permute-start(f32[8,128]{1,0:T(8,128)S(1)} %far_row_sums.1), channel_id=1, source_target_pairs={{0,16},{16,0},{1,17},{17,1},{2,18},{18,2},{3,19},{19,3},{4,20},{20... | collective-permute-start | bytes 12296 | tf_op jit(solution)/shard_map/ppermute | solution.py:481
  68.1 1.6 %row_sums.1.rows = f32[64,128]{1,0:T(8,128)S(1)} custom-call(s32[21]{0:T(128)S(4)} %get-tuple-element.46.refs_0_, s32[41]{0:T(128)S(4)} %get-tuple-element.51.refs_1_, s32[41]{0:T(128)S(4)} %get-tuple-element.58.refs_2_, s32[41]{0:T(128)S(4)} %get-tuple-element.63.refs_3_, s32[21]{0:T(128)S(4)} %get-tuple-element.71.refs_4_, ...), custom_call_target="tpu_custom_call" | custom-call | flops 1 | bytes 1 | tf_op jit(solution)/shard_map/row_sums/pallas_call | solution.py:446
  69.7 0.5 collective-permute-done.24.part
  70.2 2.8 %collective-permute-start.25 = (f32[64,128]{1,0:T(8,128)S(1)}, f32[64,128]{1,0:T(8,128)S(1)}, u32[]{:S(2)}, u32[]{:S(2)}) collective-permute-start(f32[64,128]{1,0:T(8,128)S(1)} %add_own.1), channel_id=1, source_target_pairs={{0,8},{1,9},{2,10},{3,11},{4,12},{5,13},{6,14},{7,15},{8,0},{9,1},... | collective-permute-start | bytes 98312 | tf_op jit(solution)/shard_map/ppermute | solution.py:478
  73.0 2.2 %collective-permute-done.25 = f32[64,128]{1,0:T(8,128)S(1)} collective-permute-done((f32[64,128]{1,0:T(8,128)S(1)}, f32[64,128]{1,0:T(8,128)S(1)}, u32[]{:S(2)}, u32[]{:S(2)}) %collective-permute-start.25) | collective-permute-done | bytes 32800 | tf_op jit(solution)/shard_map/ppermute | solution.py:478
  75.2 0.2 collective-permute-start.26
  75.4 1.7 %collective-permute-start.27 = (f32[64,128]{1,0:T(8,128)S(1)}, f32[64,128]{1,0:T(8,128)S(1)}, u32[]{:S(2)}, u32[]{:S(2)}) collective-permute-start(f32[64,128]{1,0:T(8,128)S(1)} %add.7.refs_0_), channel_id=1, source_target_pairs={{0,2},{1,3},{2,0},{3,1},{4,6},{5,7},{6,4},{7,5},{8,10},{9,11},{10,... | collective-permute-start | bytes 98312 | tf_op jit(solution)/shard_map/ppermute | solution.py:478
  77.2 1.5 %collective-permute-start.28 = (f32[64,128]{1,0:T(8,128)S(1)}, f32[64,128]{1,0:T(8,128)S(1)}, u32[]{:S(2)}, u32[]{:S(2)}) collective-permute-start(f32[64,128]{1,0:T(8,128)S(1)} %add.7.refs_0_), channel_id=1, source_target_pairs={{0,6},{1,7},{2,4},{3,5},{4,2},{5,3},{6,0},{7,1},{8,14},{9,15},{10,... | collective-permute-start | bytes 98312 | tf_op jit(solution)/shard_map/ppermute | solution.py:478
  78.7 0.4 collective-permute-done.26.refs_1_
  79.1 0.2 collective-permute-done.27.refs_2_
  79.3 2.6 %collective-permute-done.28.refs_3_ = f32[64,128]{1,0:T(8,128)S(1)} collective-permute-done((f32[64,128]{1,0:T(8,128)S(1)}, f32[64,128]{1,0:T(8,128)S(1)}, u32[]{:S(2)}, u32[]{:S(2)}) %collective-permute-start.28) | collective-permute-done | bytes 32800 | tf_op jit(solution)/shard_map/ppermute | solution.py:478
  82.0 1.6 %collective-permute-start.29 = (f32[8,128]{1,0:T(8,128)S(1)}, f32[8,128]{1,0:T(8,128)S(1)}, u32[]{:S(2)}, u32[]{:S(2)}) collective-permute-start(f32[8,128]{1,0:T(8,128)S(1)} %get-tuple-element.84.rows), channel_id=1, source_target_pairs={{0,16},{16,0},{1,17},{17,1},{2,18},{18,2},{3,19},{19,3},{4,20},{20... | collective-permute-start | bytes 12296 | tf_op jit(solution)/shard_map/ppermute | solution.py:481
  83.6 0.9 %column_sums.3.sums = f32[64,128]{1,0:T(8,128)S(1)} custom-call(s32[21]{0:T(128)S(4)} %get-tuple-element.46.refs_0_, s32[41]{0:T(128)S(4)} %get-tuple-element.51.refs_1_, s32[41]{0:T(128)S(4)} %get-tuple-element.58.refs_2_, s32[41]{0:T(128)S(4)} %get-tuple-element.63.refs_3_, s32[21]{0:T(128)S(4)} %get-tuple-element.71.refs_4_, ...), custom_call_target="tpu_custom_call" | custom-call | flops 1 | bytes 1 | tf_op jit(solution)/shard_map/column_sums/pallas_call | solution.py:346
  84.5 1.2 %collective-permute-done.29.far_rows = f32[8,128]{1,0:T(8,128)S(1)} collective-permute-done((f32[8,128]{1,0:T(8,128)S(1)}, f32[8,128]{1,0:T(8,128)S(1)}, u32[]{:S(2)}, u32[]{:S(2)}) %collective-permute-start.29) | collective-permute-done | bytes 4128 | tf_op jit(solution)/shard_map/ppermute | solution.py:481
  85.9 1.2 %collective-permute-done.30.theirs = f32[64,128]{1,0:T(8,128)S(1)} collective-permute-done((f32[64,128]{1,0:T(8,128)S(1)}, f32[64,128]{1,0:T(8,128)S(1)}, u32[]{:S(2)}, u32[]{:S(2)}) %collective-permute-start.30) | collective-permute-done | bytes 32800 | tf_op jit(solution)/shard_map/ppermute | solution.py:478
  87.1 0.6 scales.1
  (23 shorter events, 0.4 us)
Async XLA Ops:
  0.6 9.7 %collective-permute-start = (f32[32,128,128]{2,1,0:T(8,128)}, f32[32,128,128]{2,1,0:T(8,128)S(1)}, u32[]{:S(2)}, u32[]{:S(2)}) collective-permute-start(f32[32,128,128]{2,1,0:T(8,128)} %emb_ref.1), channel_id=1, source_target_pairs={{0,1},{1,0},{2,3},{3,2},{4,5},{5,4},{6,7},{7,6},{8,9},{9,8},{10,11... | collective-permute-start | bytes 6291464 | tf_op jit(solution)/shard_map/ppermute | solution.py:478
  2.4 10.1 %collective-permute-start.1 = (f32[520,128]{1,0:T(8,128)S(1)}, f32[520,128]{1,0:T(8,128)S(1)}, u32[]{:S(2)}, u32[]{:S(2)}) collective-permute-start(f32[520,128]{1,0:T(8,128)S(1)} %get-tuple-element.48.refs_1_), channel_id=1, source_target_pairs={{0,4},{1,5},{4,8},{5,9},{8,12},{9,13},{12,14},{13,15},{14,10},{15,... | collective-permute-start | bytes 798728 | tf_op jit(solution)/shard_map/ppermute | solution.py:475
  5.0 9.1 %collective-permute-start.5 = (f32[520,128]{1,0:T(8,128)S(1)}, f32[520,128]{1,0:T(8,128)S(1)}, u32[]{:S(2)}, u32[]{:S(2)}) collective-permute-start(f32[520,128]{1,0:T(8,128)S(1)} %get-tuple-element.47.refs_2_), channel_id=1, source_target_pairs={{0,2},{1,3},{4,0},{5,1},{8,4},{9,5},{12,8},{13,9},{14,12},{15,13},... | collective-permute-start | bytes 798728 | tf_op jit(solution)/shard_map/ppermute | solution.py:475
  5.0 3.2 %collective-permute-start.2 = (f32[32,128]{1,0:T(8,128)}, f32[32,128]{1,0:T(8,128)S(1)}, u32[]{:S(2)}, u32[]{:S(2)}) collective-permute-start(f32[32,128]{1,0:T(8,128)} %target_mass.1), channel_id=1, source_target_pairs={{0,1},{1,0},{2,3},{3,2},{4,5},{5,4},{6,7},{7,6},{8,9},{9,8},{10,11... | collective-permute-start | bytes 49160 | tf_op jit(solution)/shard_map/ppermute | solution.py:478
  8.2 11.1 %collective-permute-start.3 = (f32[520,128]{1,0:T(8,128)S(1)}, f32[520,128]{1,0:T(8,128)S(1)}, u32[]{:S(2)}, u32[]{:S(2)}) collective-permute-start(f32[520,128]{1,0:T(8,128)S(1)} %get-tuple-element.47.refs_2_), channel_id=1, source_target_pairs={{0,4},{1,5},{4,8},{5,9},{8,12},{9,13},{12,14},{13,15},{14,10},{15,... | collective-permute-start | bytes 798728 | tf_op jit(solution)/shard_map/ppermute | solution.py:475
  10.1 9.7 %collective-permute-start.4 = (f32[520,128]{1,0:T(8,128)S(1)}, f32[520,128]{1,0:T(8,128)S(1)}, u32[]{:S(2)}, u32[]{:S(2)}) collective-permute-start(f32[520,128]{1,0:T(8,128)S(1)} %get-tuple-element.48.refs_1_), channel_id=1, source_target_pairs={{0,2},{1,3},{4,0},{5,1},{8,4},{9,5},{12,8},{13,9},{14,12},{15,13},... | collective-permute-start | bytes 798728 | tf_op jit(solution)/shard_map/ppermute | solution.py:475
  14.1 10.3 %collective-permute-start.6 = (f32[520,128]{1,0:T(8,128)S(1)}, f32[520,128]{1,0:T(8,128)S(1)}, u32[]{:S(2)}, u32[]{:S(2)}) collective-permute-start(f32[520,128]{1,0:T(8,128)S(1)} %collective-permute-done.1.refs_1_), channel_id=1, source_target_pairs={{0,4},{1,5},{4,8},{5,9},{8,12},{9,13},{12,14},{13,15},{14,10},{15,... | collective-permute-start | bytes 798728 | tf_op jit(solution)/shard_map/ppermute | solution.py:475
  15.7 9.8 %collective-permute-start.9 = (f32[520,128]{1,0:T(8,128)S(1)}, f32[520,128]{1,0:T(8,128)S(1)}, u32[]{:S(2)}, u32[]{:S(2)}) collective-permute-start(f32[520,128]{1,0:T(8,128)S(1)} %collective-permute-done.5.refs_4_), channel_id=1, source_target_pairs={{0,2},{1,3},{4,0},{5,1},{8,4},{9,5},{12,8},{13,9},{14,12},{15,13},... | collective-permute-start | bytes 798728 | tf_op jit(solution)/shard_map/ppermute | solution.py:475
  16.1 22.8 %collective-permute-start.16 = (f32[1040,128]{1,0:T(8,128)S(1)}, f32[1040,128]{1,0:T(8,128)S(1)}, u32[]{:S(2)}, u32[]{:S(2)}) collective-permute-start(f32[1040,128]{1,0:T(8,128)S(1)} %get-tuple-element.69), channel_id=1, source_target_pairs={{0,16},{16,0},{1,17},{17,1},{2,18},{18,2},{3,19},{19,3},{4,20},{20... | collective-permute-start | bytes 1597448 | tf_op jit(solution)/shard_map/ppermute | solution.py:481
  19.8 9.5 %collective-permute-start.7 = (f32[520,128]{1,0:T(8,128)S(1)}, f32[520,128]{1,0:T(8,128)S(1)}, u32[]{:S(2)}, u32[]{:S(2)}) collective-permute-start(f32[520,128]{1,0:T(8,128)S(1)} %collective-permute-done.3.refs_2_), channel_id=1, source_target_pairs={{0,4},{1,5},{4,8},{5,9},{8,12},{9,13},{12,14},{13,15},{14,10},{15,... | collective-permute-start | bytes 798728 | tf_op jit(solution)/shard_map/ppermute | solution.py:475
  21.4 9.9 %collective-permute-start.8 = (f32[520,128]{1,0:T(8,128)S(1)}, f32[520,128]{1,0:T(8,128)S(1)}, u32[]{:S(2)}, u32[]{:S(2)}) collective-permute-start(f32[520,128]{1,0:T(8,128)S(1)} %collective-permute-done.4.refs_3_), channel_id=1, source_target_pairs={{0,2},{1,3},{4,0},{5,1},{8,4},{9,5},{12,8},{13,9},{14,12},{15,13},... | collective-permute-start | bytes 798728 | tf_op jit(solution)/shard_map/ppermute | solution.py:475
  25.5 9.5 %collective-permute-start.10 = (f32[520,128]{1,0:T(8,128)S(1)}, f32[520,128]{1,0:T(8,128)S(1)}, u32[]{:S(2)}, u32[]{:S(2)}) collective-permute-start(f32[520,128]{1,0:T(8,128)S(1)} %collective-permute-done.6.refs_1_), channel_id=1, source_target_pairs={{0,4},{1,5},{4,8},{5,9},{8,12},{9,13},{12,14},{13,15},{14,10},{15,... | collective-permute-start | bytes 798728 | tf_op jit(solution)/shard_map/ppermute | solution.py:475
  27.1 9.8 %collective-permute-start.13 = (f32[520,128]{1,0:T(8,128)S(1)}, f32[520,128]{1,0:T(8,128)S(1)}, u32[]{:S(2)}, u32[]{:S(2)}) collective-permute-start(f32[520,128]{1,0:T(8,128)S(1)} %collective-permute-done.9.refs_4_), channel_id=1, source_target_pairs={{0,2},{1,3},{4,0},{5,1},{8,4},{9,5},{12,8},{13,9},{14,12},{15,13},... | collective-permute-start | bytes 798728 | tf_op jit(solution)/shard_map/ppermute | solution.py:475
  29.3 12.6 %collective-permute-start.11 = (f32[520,128]{1,0:T(8,128)S(1)}, f32[520,128]{1,0:T(8,128)S(1)}, u32[]{:S(2)}, u32[]{:S(2)}) collective-permute-start(f32[520,128]{1,0:T(8,128)S(1)} %collective-permute-done.7.refs_2_), channel_id=1, source_target_pairs={{0,4},{1,5},{4,8},{5,9},{8,12},{9,13},{12,14},{13,15},{14,10},{15,... | collective-permute-start | bytes 798728 | tf_op jit(solution)/shard_map/ppermute | solution.py:475
  31.3 11.3 %collective-permute-start.12 = (f32[520,128]{1,0:T(8,128)S(1)}, f32[520,128]{1,0:T(8,128)S(1)}, u32[]{:S(2)}, u32[]{:S(2)}) collective-permute-start(f32[520,128]{1,0:T(8,128)S(1)} %collective-permute-done.8.refs_3_), channel_id=1, source_target_pairs={{0,2},{1,3},{4,0},{5,1},{8,4},{9,5},{12,8},{13,9},{14,12},{15,13},... | collective-permute-start | bytes 798728 | tf_op jit(solution)/shard_map/ppermute | solution.py:475
  36.9 9.3 %collective-permute-start.14 = (f32[520,128]{1,0:T(8,128)S(1)}, f32[520,128]{1,0:T(8,128)S(1)}, u32[]{:S(2)}, u32[]{:S(2)}) collective-permute-start(f32[520,128]{1,0:T(8,128)S(1)} %collective-permute-done.10.refs_1_), channel_id=1, source_target_pairs={{0,4},{1,5},{4,8},{5,9},{8,12},{9,13},{12,14},{13,15},{14,10},{15,... | collective-permute-start | bytes 798728 | tf_op jit(solution)/shard_map/ppermute | solution.py:475
  38.5 9.3 %collective-permute-start.15 = (f32[520,128]{1,0:T(8,128)S(1)}, f32[520,128]{1,0:T(8,128)S(1)}, u32[]{:S(2)}, u32[]{:S(2)}) collective-permute-start(f32[520,128]{1,0:T(8,128)S(1)} %collective-permute-done.13.refs_4_), channel_id=1, source_target_pairs={{0,2},{1,3},{4,0},{5,1},{8,4},{9,5},{12,8},{13,9},{14,12},{15,13},... | collective-permute-start | bytes 798728 | tf_op jit(solution)/shard_map/ppermute | solution.py:475
  40.3 4.9 %collective-permute-start.17 = (f32[8,128]{1,0:T(8,128)S(1)}, f32[8,128]{1,0:T(8,128)S(1)}, u32[]{:S(2)}, u32[]{:S(2)}) collective-permute-start(f32[8,128]{1,0:T(8,128)S(1)} %get-tuple-element.70), channel_id=1, source_target_pairs={{0,16},{16,0},{1,17},{17,1},{2,18},{18,2},{3,19},{19,3},{4,20},{20... | collective-permute-start | bytes 12296 | tf_op jit(solution)/shard_map/ppermute | solution.py:481
  49.5 4.9 %collective-permute-start.18 = (f32[64,128]{1,0:T(8,128)S(1)}, f32[64,128]{1,0:T(8,128)S(1)}, u32[]{:S(2)}, u32[]{:S(2)}) collective-permute-start(f32[64,128]{1,0:T(8,128)S(1)} %get-tuple-element.73), channel_id=1, source_target_pairs={{0,8},{1,9},{2,10},{3,11},{4,12},{5,13},{6,14},{7,15},{8,0},{9,1},... | collective-permute-start | bytes 98312 | tf_op jit(solution)/shard_map/ppermute | solution.py:478
  54.4 4.2 %collective-permute-start.19 = (f32[64,128]{1,0:T(8,128)S(1)}, f32[64,128]{1,0:T(8,128)S(1)}, u32[]{:S(2)}, u32[]{:S(2)}) collective-permute-start(f32[64,128]{1,0:T(8,128)S(1)} %add.6.refs_0_), channel_id=1, source_target_pairs={{0,4},{1,5},{2,6},{3,7},{4,0},{5,1},{6,2},{7,3},{8,12},{9,13},{10,... | collective-permute-start | bytes 98312 | tf_op jit(solution)/shard_map/ppermute | solution.py:478
  55.9 3.9 %collective-permute-start.20 = (f32[64,128]{1,0:T(8,128)S(1)}, f32[64,128]{1,0:T(8,128)S(1)}, u32[]{:S(2)}, u32[]{:S(2)}) collective-permute-start(f32[64,128]{1,0:T(8,128)S(1)} %add.6.refs_0_), channel_id=1, source_target_pairs={{0,2},{1,3},{2,0},{3,1},{4,6},{5,7},{6,4},{7,5},{8,10},{9,11},{10,... | collective-permute-start | bytes 98312 | tf_op jit(solution)/shard_map/ppermute | solution.py:478
  56.3 4.8 %collective-permute-start.21 = (f32[64,128]{1,0:T(8,128)S(1)}, f32[64,128]{1,0:T(8,128)S(1)}, u32[]{:S(2)}, u32[]{:S(2)}) collective-permute-start(f32[64,128]{1,0:T(8,128)S(1)} %add.6.refs_0_), channel_id=1, source_target_pairs={{0,6},{1,7},{2,4},{3,5},{4,2},{5,3},{6,0},{7,1},{8,14},{9,15},{10,... | collective-permute-start | bytes 98312 | tf_op jit(solution)/shard_map/ppermute | solution.py:478
  61.1 3.7 %collective-permute-start.22 = (f32[8,128]{1,0:T(8,128)S(1)}, f32[8,128]{1,0:T(8,128)S(1)}, u32[]{:S(2)}, u32[]{:S(2)}) collective-permute-start(f32[8,128]{1,0:T(8,128)S(1)} %get-tuple-element.81), channel_id=1, source_target_pairs={{0,16},{16,0},{1,17},{17,1},{2,18},{18,2},{3,19},{19,3},{4,20},{20... | collective-permute-start | bytes 12296 | tf_op jit(solution)/shard_map/ppermute | solution.py:481
  62.7 3.6 %copy-start = (f32[32,128]{1,0:T(8,128)S(1)}, f32[32,128]{1,0:T(8,128)}, u32[]{:S(2)}) copy-start(f32[32,128]{1,0:T(8,128)} %target_mass.1) | copy-start | bytes 49156
  65.0 1.3 %collective-permute-start.23 = (f32[64,128]{1,0:T(8,128)S(1)}, f32[64,128]{1,0:T(8,128)S(1)}, u32[]{:S(2)}, u32[]{:S(2)}) collective-permute-start(f32[64,128]{1,0:T(8,128)S(1)} %far_column_sums.2.refs_5_.mine), channel_id=1, source_target_pairs={{0,1},{1,0},{2,3},{3,2},{4,5},{5,4},{6,7},{7,6},{8,9},{9,8},{10,11... | collective-permute-start | bytes 98312 | tf_op jit(solution)/shard_map/ppermute | solution.py:478
  66.5 3.7 %collective-permute-start.24 = (f32[8,128]{1,0:T(8,128)S(1)}, f32[8,128]{1,0:T(8,128)S(1)}, u32[]{:S(2)}, u32[]{:S(2)}) collective-permute-start(f32[8,128]{1,0:T(8,128)S(1)} %far_row_sums.1), channel_id=1, source_target_pairs={{0,16},{16,0},{1,17},{17,1},{2,18},{18,2},{3,19},{19,3},{4,20},{20... | collective-permute-start | bytes 12296 | tf_op jit(solution)/shard_map/ppermute | solution.py:481
  70.2 5.0 %collective-permute-start.25 = (f32[64,128]{1,0:T(8,128)S(1)}, f32[64,128]{1,0:T(8,128)S(1)}, u32[]{:S(2)}, u32[]{:S(2)}) collective-permute-start(f32[64,128]{1,0:T(8,128)S(1)} %add_own.1), channel_id=1, source_target_pairs={{0,8},{1,9},{2,10},{3,11},{4,12},{5,13},{6,14},{7,15},{8,0},{9,1},... | collective-permute-start | bytes 98312 | tf_op jit(solution)/shard_map/ppermute | solution.py:478
  75.2 3.9 %collective-permute-start.26 = (f32[64,128]{1,0:T(8,128)S(1)}, f32[64,128]{1,0:T(8,128)S(1)}, u32[]{:S(2)}, u32[]{:S(2)}) collective-permute-start(f32[64,128]{1,0:T(8,128)S(1)} %add.7.refs_0_), channel_id=1, source_target_pairs={{0,4},{1,5},{2,6},{3,7},{4,0},{5,1},{6,2},{7,3},{8,12},{9,13},{10,... | collective-permute-start | bytes 98312 | tf_op jit(solution)/shard_map/ppermute | solution.py:478
  75.4 3.9 %collective-permute-start.27 = (f32[64,128]{1,0:T(8,128)S(1)}, f32[64,128]{1,0:T(8,128)S(1)}, u32[]{:S(2)}, u32[]{:S(2)}) collective-permute-start(f32[64,128]{1,0:T(8,128)S(1)} %add.7.refs_0_), channel_id=1, source_target_pairs={{0,2},{1,3},{2,0},{3,1},{4,6},{5,7},{6,4},{7,5},{8,10},{9,11},{10,... | collective-permute-start | bytes 98312 | tf_op jit(solution)/shard_map/ppermute | solution.py:478
  77.2 4.8 %collective-permute-start.28 = (f32[64,128]{1,0:T(8,128)S(1)}, f32[64,128]{1,0:T(8,128)S(1)}, u32[]{:S(2)}, u32[]{:S(2)}) collective-permute-start(f32[64,128]{1,0:T(8,128)S(1)} %add.7.refs_0_), channel_id=1, source_target_pairs={{0,6},{1,7},{2,4},{3,5},{4,2},{5,3},{6,0},{7,1},{8,14},{9,15},{10,... | collective-permute-start | bytes 98312 | tf_op jit(solution)/shard_map/ppermute | solution.py:478
  82.0 3.7 %collective-permute-start.29 = (f32[8,128]{1,0:T(8,128)S(1)}, f32[8,128]{1,0:T(8,128)S(1)}, u32[]{:S(2)}, u32[]{:S(2)}) collective-permute-start(f32[8,128]{1,0:T(8,128)S(1)} %get-tuple-element.84.rows), channel_id=1, source_target_pairs={{0,16},{16,0},{1,17},{17,1},{2,18},{18,2},{3,19},{19,3},{4,20},{20... | collective-permute-start | bytes 12296 | tf_op jit(solution)/shard_map/ppermute | solution.py:481
  83.6 3.6 %copy-start.1 = (f32[8,128]{1,0:T(8,128)S(1)}, f32[8,128]{1,0:T(8,128)}, u32[]{:S(2)}) copy-start(f32[8,128]{1,0:T(8,128)} %mass.5) | copy-start | bytes 12292
  85.9 1.3 %collective-permute-start.30 = (f32[64,128]{1,0:T(8,128)S(1)}, f32[64,128]{1,0:T(8,128)S(1)}, u32[]{:S(2)}, u32[]{:S(2)}) collective-permute-start(f32[64,128]{1,0:T(8,128)S(1)} %far_column_sums.3.mine), channel_id=1, source_target_pairs={{0,1},{1,0},{2,3},{3,2},{4,5},{5,4},{6,7},{7,6},{8,9},{9,8},{10,11... | collective-permute-start | bytes 98312 | tf_op jit(solution)/shard_map/ppermute | solution.py:478

commit v5 on v4

--- a/solution.py
+++ b/solution.py
@@ -155,7 +155,7 @@
 
 
 def tile_kernel(plan, *refs):
-    chunks, slots, sb, half, tb, near, offsets, far, chained, closing = plan
+    chunks, slots, sb, half, tb, near, offsets, far, chained, closing, planned = plan
     sides = 1 if far else 2
     refs = list(refs)
     device = refs.pop(0)
@@ -167,17 +167,18 @@
     weight = [refs.pop(0) for _ in range(sides)]
     rows_in, mass_in = (refs.pop(0), refs.pop(0)) if chained else (None, None)
     back = refs.pop(0) if closing else None
-    tiles, table, rows_out, mass_out, partial, units, staged, named, listed, arrived = refs
+    if planned:
+        table, listed, tiles, rows_out, mass_out, partial, units = refs
+    else:
+        tiles, table, rows_out, mass_out, partial, units, staged, named, listed, arrived = refs
     count = chunks * sides * slots
     width = source[0].shape[1]
     scale = 1.0 / (width * entropic_regularizer)
     me = device[0]
     chips = rows_out.shape[0] // sb
 
-    for chunk in range(chunks):
-        staged[chunk * sb : (chunk + 1) * sb] = source[2 * chunk][sb * half :].astype(jnp.int32)
-    copy = pltpu.make_async_copy(staged, named, arrived)
-    copy.start()
+    if not planned:
+        copy = fetch_named([source[2 * chunk] for chunk in range(chunks)], staged, named, arrived, sb, half)
     if chained:
         rows_out[...] = rows_in[...]
         mass_out[...] = mass_in[...]
@@ -189,37 +190,16 @@
             rows = pl.ds(block * half, half)
             left = jnp.concatenate([source[2 * chunk][rows], source[2 * chunk + 1][rows]], axis=0)
             units[chunk * sb + block] = jnp.concatenate(split2(unit(left)), axis=1)
-    copy.wait()
-
-    chip_of = []
-    for chunk in range(chunks):
-        at_chip = jnp.int32(0) if far else chip_at(chips, me // 2, offsets[chunk])
-        chip_of.append(at_chip)
-        for side in range(sides):
-            base = (chunk * sides + side) * slots
+    chip_of = [jnp.int32(0) if far else chip_at(chips, me // 2, offsets[chunk]) for chunk in range(chunks)]
+    if not planned:
+        copy.wait()
+        for chunk in range(chunks):
             if far:
                 for j in range(sb):
-                    listed[base + j] = j
+                    listed[j] = j
                     table[j] = named[j, 2 * near]
-                continue
-            wanted = me if side == 0 else me + 1 - 2 * lax.rem(me, 2)
-            filled = jnp.int32(0)
-            for block in range(sb):
-                found, which = jnp.int32(0), jnp.int32(0)
-                for k in range(near):
-                    hit = named[chunk * sb + block, k] == wanted
-                    found = jnp.where(hit, 1, found)
-                    which = jnp.where(hit, named[chunk * sb + block, near + k], which)
-                listed[base + filled] = block
-                table[count + base + filled] = which
-                filled = filled + found
-            for j in range(slots):
-                valid = j < filled
-                block = jnp.where(valid, listed[base + j], sb)
-                which = jnp.where(valid, table[count + base + j], 2 * tb)
-                listed[base + j] = block
-                table[base + j] = jnp.where(valid, at_chip * sb + block, chips * sb)
-                table[count + base + j] = jnp.where(valid, which + side * tb, 2 * tb)
+            else:
+                list_slots(named, listed, table, me, chip_of[chunk], chunk, slots, sb, tb, near, chips, count)
 
     for chunk in range(chunks):
         lower = source[2 * chunk + 1]
@@ -250,60 +230,125 @@
         rows_out[pl.ds(start, sb)] += back[...]
 
 
-def build_tiles(device, source, weight, slots, sb, near, chips, offsets=(), chain=(), back=None):
+def fetch_named(uppers, staged, named, arrived, sb, half):
+    for chunk, upper in enumerate(uppers):
+        staged[chunk * sb : (chunk + 1) * sb] = upper[sb * half :].astype(jnp.int32)
+    copy = pltpu.make_async_copy(staged, named, arrived)
+    copy.start()
+    return copy
+
+
+def list_slots(named, listed, table, me, at_chip, chunk, slots, sb, tb, near, chips, count):
+    for side in range(2):
+        base = (chunk * 2 + side) * slots
+        wanted = me if side == 0 else me + 1 - 2 * lax.rem(me, 2)
+        filled = jnp.int32(0)
+        for block in range(sb):
+            found, which = jnp.int32(0), jnp.int32(0)
+            for k in range(near):
+                hit = named[chunk * sb + block, k] == wanted
+                found = jnp.where(hit, 1, found)
+                which = jnp.where(hit, named[chunk * sb + block, near + k], which)
+            listed[base + filled] = block
+            table[count + base + filled] = which
+            filled = filled + found
+        for j in range(slots):
+            valid = j < filled
+            block = jnp.where(valid, listed[base + j], sb)
+            which = jnp.where(valid, table[count + base + j], 2 * tb)
+            listed[base + j] = block
+            table[base + j] = jnp.where(valid, at_chip * sb + block, chips * sb)
+            table[count + base + j] = jnp.where(valid, which + side * tb, 2 * tb)
+
+
+def plan_kernel(plan, device, upper, table, listed, staged, named, arrived):
+    slots, sb, half, tb, near, chips, offset = plan
+    copy = fetch_named([upper], staged, named, arrived, sb, half)
+    me = device[0]
+    copy.wait()
+    list_slots(
+        named, listed, table, me, chip_at(chips, me // 2, offset), 0, slots, sb, tb, near, chips, 2 * slots
+    )
+
+
+def plan_tiles(device, upper, slots, sb, tb, near, chips, offset):
+    half, width = upper.shape[0] // sb - 1, upper.shape[1]
+    return pl.pallas_call(
+        functools.partial(plan_kernel, (slots, sb, half, tb, near, chips, offset)),
+        out_shape=(pltpu.SMEM((4 * slots + 1,), jnp.int32), pltpu.SMEM((2 * slots + 1,), jnp.int32)),
+        in_specs=[SMEM, VMEM],
+        out_specs=(SMEM, SMEM),
+        scratch_shapes=[
+            pltpu.VMEM((sb, width), jnp.int32),
+            pltpu.SMEM((sb, width), jnp.int32),
+            pltpu.SemaphoreType.DMA,
+        ],
+        cost_estimate=LIGHT,
+        compiler_params=SMALL,
+        name="plan_tiles",
+    )(device, upper)
+
+
+def build_tiles(device, source, weight, slots, sb, near, chips, offsets=(), chain=(), back=None, planned=()):
     chunks, sides, far = max(1, len(source) // 2), len(weight), not offsets
     half, width = source[0].shape[0] // (sb * (1 + far)) - 1, source[0].shape[1]
     tb, nodes = weight[0].shape[0], weight[0].shape[2] // 2
     count = chunks * sides * slots
-    plan = (chunks, slots, sb, half, tb, near, offsets, far, bool(chain), back is not None)
-    operands = [device, *source, *in_vmem(*weight), *chain] + ([] if back is None else [back])
+    plan = (
+        *(chunks, slots, sb, half, tb, near, offsets, far),
+        *(bool(chain), back is not None, bool(planned)),
+    )
+    operands = [*source, *in_vmem(*weight), *chain] + ([] if back is None else [back])
     rows = jax.ShapeDtypeStruct(((1 if far else chips) * sb, 2 * half), jnp.float32)
-    return pl.pallas_call(
+    out_shape = [
+        pltpu.VMEM((count, 2 * half, 2 * nodes), jnp.bfloat16),
+        pltpu.SMEM((count if far else 2 * count + 1,), jnp.int32),
+        rows,
+        rows,
+    ]
+    out_specs = [VMEM, SMEM, VMEM, VMEM]
+    scratch = [
+        pltpu.VMEM((chunks * (sb + 1), 8, 2 * half), jnp.float32),
+        pltpu.VMEM((chunks * sb, 2 * half, 2 * width), jnp.bfloat16),
+        pltpu.VMEM((chunks * sb, width), jnp.int32),
+        pltpu.SMEM((chunks * sb, width), jnp.int32),
+        pltpu.SMEM((count + 1,), jnp.int32),
+        pltpu.SemaphoreType.DMA,
+    ]
+    if planned:
+        out_shape.pop(1)
+        out_specs.pop(1)
+        scratch = scratch[:2]
+    out = pl.pallas_call(
         functools.partial(tile_kernel, plan),
-        out_shape=(
-            pltpu.VMEM((count, 2 * half, 2 * nodes), jnp.bfloat16),
-            pltpu.SMEM((count if far else 2 * count + 1,), jnp.int32),
-            rows,
-            rows,
-        ),
-        in_specs=[SMEM] + [VMEM] * (len(operands) - 1),
-        out_specs=(VMEM, SMEM, VMEM, VMEM),
-        scratch_shapes=[
-            pltpu.VMEM((chunks * (sb + 1), 8, 2 * half), jnp.float32),
-            pltpu.VMEM((chunks * sb, 2 * half, 2 * width), jnp.bfloat16),
-            pltpu.VMEM((chunks * sb, width), jnp.int32),
-            pltpu.SMEM((chunks * sb, width), jnp.int32),
-            pltpu.SMEM((count + 1,), jnp.int32),
-            pltpu.SemaphoreType.DMA,
-        ],
+        out_shape=out_shape,
+        in_specs=[SMEM] + [VMEM] * len(operands) + [SMEM] * len(planned),
+        out_specs=out_specs,
+        scratch_shapes=scratch,
         cost_estimate=LIGHT,
         compiler_params=pltpu.CompilerParams(vmem_limit_bytes=16 << 20),
         name="build_tiles",
-    )(*operands)
+    )(device, *operands, *in_smem(*planned))
+    return [out[0], planned[0], *out[1:]] if planned else out
 
 
 SMALL = pltpu.CompilerParams(vmem_limit_bytes=16 << 20)
 
 
-def add_kernel(device, *refs):
-    parts, total, own = refs[:-2], refs[-2], refs[-1]
-    sb = own.shape[0]
+def add_kernel(*refs):
+    parts, total = refs[:-1], refs[-1]
     total[...] = sum([part[...] for part in parts[1:]], parts[0][...])
-    own[...] = total[pl.ds(pl.multiple_of(device[0] // 2 * sb, sb), sb)]
-
-
-def add_last(device, parts, sb):
+
+
+def add_all(parts):
     return pl.pallas_call(
         add_kernel,
-        out_shape=(
-            jax.ShapeDtypeStruct(parts[0].shape, jnp.float32),
-            jax.ShapeDtypeStruct((sb, parts[0].shape[1]), jnp.float32),
-        ),
-        in_specs=[SMEM] + [VMEM] * len(parts),
-        out_specs=(VMEM, VMEM),
+        out_shape=jax.ShapeDtypeStruct(parts[0].shape, jnp.float32),
+        in_specs=[VMEM] * len(parts),
+        out_specs=VMEM,
         compiler_params=SMALL,
-        name="add_last",
-    )(device, *parts)
+        name="add_all",
+    )(*parts)
 
 
 def insert_kernel(device, rows, part, out):
@@ -327,8 +372,8 @@
     tables = [refs.pop(0) for _ in counts]
     rows, mass = refs.pop(0), refs.pop(0)
     tiles = [refs.pop(0) for _ in counts]
-    out, scale, total = refs
-    count = rows.shape[0]
+    own, other, scale, total = refs
+    count, blocks = rows.shape[0], own.shape[0]
     scale[0:count] = mass[...] / (dustbin + rows[...])
     scale[count:] = jnp.zeros((8, scale.shape[1]), jnp.float32)
     total[...] = jnp.zeros_like(total)
@@ -336,8 +381,9 @@
         for slot in range(slots):
             parts = stacked_parts(scale[pl.ds(tables[part][slot], 1), :])
             total[tables[part][slots + slot]] += column_product(parts, tiles[part][slot])
-    for block in range(out.shape[0]):
-        out[block : block + 1] = jnp.sum(total[block], axis=0, keepdims=True)
+    for block in range(blocks):
+        own[block : block + 1] = jnp.sum(total[block], axis=0, keepdims=True)
+        other[block : block + 1] = jnp.sum(total[blocks + block], axis=0, keepdims=True)
 
 
 def column_sums(tables, rows, mass, tiles, targets):
@@ -345,12 +391,12 @@
     width, nodes = rows.shape[1], tiles[0].shape[2] // 2
     return pl.pallas_call(
         functools.partial(column_kernel, counts),
-        out_shape=jax.ShapeDtypeStruct((targets, nodes), jnp.float32),
+        out_shape=(jax.ShapeDtypeStruct((targets, nodes), jnp.float32),) * 2,
         in_specs=[SMEM] * len(tables) + [VMEM] * (2 + len(tiles)),
-        out_specs=VMEM,
+        out_specs=(VMEM, VMEM),
         scratch_shapes=[
             pltpu.VMEM((rows.shape[0] + 8, width), jnp.float32),
-            pltpu.VMEM((targets + 1, 8, nodes), jnp.float32),
+            pltpu.VMEM((2 * targets + 1, 8, nodes), jnp.float32),
         ],
         cost_estimate=LIGHT,
         compiler_params=SMALL,
@@ -358,78 +404,58 @@
     )(*in_smem(*tables), rows, mass, *in_vmem(*tiles))
 
 
-def far_column_kernel(far_at, sums, far_rows, far_mass, tiles, out, scale):
-    far = tiles.shape[0]
-    out[...] = sums[...]
-    scale[...] = far_mass[...] / (dustbin + far_rows[...])
-    for slot in range(far):
+def closing_kernel(last, *refs):
+    device, far_at, far_rows, far_mass, mine, theirs, target_mass, tiles = refs[:8]
+    tgt, total = refs[-3], refs[-1]
+    sb, slots = far_mass.shape[0], range(tiles.shape[0])
+    start = pl.multiple_of(device[0] // 2 * sb, sb)
+    scale = refs[-2]
+    scale[...] = far_mass[...] / (dustbin + far_rows[pl.ds(start, sb)])
+    total[...] = mine[...] + theirs[...]
+    for slot in slots:
         product = column_product(stacked_parts(scale[slot : slot + 1, :]), tiles[slot])
-        out[pl.ds(far_at[slot], 1)] += jnp.sum(product, axis=0, keepdims=True)
-
-
-def far_column_sums(far_at, sums, far_rows, far_mass, tiles):
-    return pl.pallas_call(
-        far_column_kernel,
-        out_shape=jax.ShapeDtypeStruct(sums.shape, jnp.float32),
-        in_specs=[SMEM] + [VMEM] * 4,
-        out_specs=VMEM,
-        scratch_shapes=[pltpu.VMEM(far_mass.shape, jnp.float32)],
+        total[pl.ds(far_at[slot], 1)] += jnp.sum(product, axis=0, keepdims=True)
+    tgt[...] = target_mass[...] / (dustbin + total[...])
+    if last:
+        rows, mass, src = refs[8:11]
+        src[...] = mass[...] / (dustbin + rows[pl.ds(start, sb)])
+    else:
+        back = refs[8]
+        for slot in slots:
+            product = row_product(stacked_parts(tgt[pl.ds(far_at[slot], 1), :]), tiles[slot])
+            back[slot : slot + 1] = jnp.sum(product, axis=0, keepdims=True)
+
+
+def closing(device, far_at, far_rows, far_mass, mine, theirs, target_mass, tiles, rows=None, mass=None):
+    last = mass is not None
+    side = far_mass if mass is None else mass
+    return pl.pallas_call(
+        functools.partial(closing_kernel, last),
+        out_shape=(
+            jax.ShapeDtypeStruct(side.shape, jnp.float32),
+            jax.ShapeDtypeStruct(target_mass.shape, jnp.float32),
+        ),
+        in_specs=[SMEM] * 2 + [VMEM] * (8 if last else 6),
+        out_specs=(VMEM, VMEM),
+        scratch_shapes=[pltpu.VMEM(far_mass.shape, jnp.float32), pltpu.VMEM(target_mass.shape, jnp.float32)],
         cost_estimate=LIGHT,
         compiler_params=SMALL,
-        name="far_column_sums",
-    )(*in_smem(far_at), sums, far_rows, far_mass, *in_vmem(tiles))
-
-
-def scale_kernel(rows, mass, mine, theirs, target_mass, src, tgt):
-    blocks = tgt.shape[0]
-    src[...] = mass[...] / (dustbin + rows[...])
-    tgt[...] = target_mass[...] / (dustbin + mine[0:blocks] + theirs[blocks : 2 * blocks])
-
-
-def scales(rows, mass, mine, theirs, target_mass):
-    return pl.pallas_call(
-        scale_kernel,
-        out_shape=(
-            jax.ShapeDtypeStruct(mass.shape, jnp.float32),
-            jax.ShapeDtypeStruct(target_mass.shape, jnp.float32),
-        ),
-        in_specs=[VMEM] * 5,
-        out_specs=(VMEM, VMEM),
-        compiler_params=SMALL,
-        name="scales",
-    )(rows, mass, mine, theirs, target_mass)
-
-
-def far_row_kernel(far_at, mine, theirs, mass, tiles, out, scale):
-    blocks = mass.shape[0]
-    scale[...] = mass[...] / (dustbin + mine[0:blocks] + theirs[blocks : 2 * blocks])
-    for slot in range(tiles.shape[0]):
-        product = row_product(stacked_parts(scale[pl.ds(far_at[slot], 1), :]), tiles[slot])
-        out[slot : slot + 1] = jnp.sum(product, axis=0, keepdims=True)
-
-
-def far_row_sums(far_at, mine, theirs, mass, tiles):
-    return pl.pallas_call(
-        far_row_kernel,
-        out_shape=jax.ShapeDtypeStruct(tiles.shape[:2], jnp.float32),
-        in_specs=[SMEM] + [VMEM] * 4,
-        out_specs=VMEM,
-        scratch_shapes=[pltpu.VMEM(mass.shape, jnp.float32)],
-        cost_estimate=LIGHT,
-        compiler_params=SMALL,
-        name="far_row_sums",
-    )(*in_smem(far_at), mine, theirs, mass, *in_vmem(tiles))
+        name="closing",
+    )(
+        *(device, *in_smem(far_at), far_rows, far_mass, mine, theirs, target_mass, *in_vmem(tiles)),
+        *((rows, mass) if last else ()),
+    )
 
 
 def row_kernel(counts, *refs):
     refs = list(refs)
     tables = [refs.pop(0) for _ in counts]
-    mine, theirs, mass, other_mass = [refs.pop(0) for _ in range(4)]
+    mine, theirs = refs.pop(0), refs.pop(0)
     tiles = [refs.pop(0) for _ in counts]
     out, scale, total = refs
-    blocks = mass.shape[0]
-    scale[0:blocks] = mass[...] / (dustbin + mine[0:blocks] + theirs[blocks : 2 * blocks])
-    scale[blocks : 2 * blocks] = other_mass[...] / (dustbin + mine[blocks : 2 * blocks] + theirs[0:blocks])
+    blocks = mine.shape[0]
+    scale[0:blocks] = mine[...]
+    scale[blocks : 2 * blocks] = theirs[...]
     scale[2 * blocks :] = jnp.zeros((8, scale.shape[1]), jnp.float32)
     total[...] = jnp.zeros_like(total)
     for part, slots in enumerate(counts):
@@ -440,22 +466,22 @@
         out[block : block + 1] = jnp.sum(total[block], axis=0, keepdims=True)
 
 
-def row_sums(tables, mine, theirs, mass, other_mass, tiles, sources):
+def row_sums(tables, mine, theirs, tiles, sources):
     counts = tuple(t.shape[0] for t in tiles)
     width, nodes = tiles[0].shape[1], tiles[0].shape[2] // 2
     return pl.pallas_call(
         functools.partial(row_kernel, counts),
         out_shape=jax.ShapeDtypeStruct((sources, width), jnp.float32),
-        in_specs=[SMEM] * len(tables) + [VMEM] * (4 + len(tiles)),
+        in_specs=[SMEM] * len(tables) + [VMEM] * (2 + len(tiles)),
         out_specs=VMEM,
         scratch_shapes=[
-            pltpu.VMEM((mine.shape[0] + 8, nodes), jnp.float32),
+            pltpu.VMEM((2 * mine.shape[0] + 8, nodes), jnp.float32),
             pltpu.VMEM((sources + 1, 8, width), jnp.float32),
         ],
         cost_estimate=LIGHT,
         compiler_params=SMALL,
         name="row_sums",
-    )(*in_smem(*tables), mine, theirs, mass, other_mass, *in_vmem(*tiles))
+    )(*in_smem(*tables), mine, theirs, *in_vmem(*tiles))
 
 
 def local(source_emb, target_emb, source_mass, target_mass, cand_device, cand_block):
@@ -484,7 +510,7 @@
     me = device.reshape(1)
 
     upper, lower, both = pack(me, source_emb, source_mass, cand_device, cand_block)
-    sibling_emb, sibling_mass = across(target_emb, 1), across(target_mass, 1)
+    sibling_emb = across(target_emb, 1)
     far_both = [both]
 
     weights, tiles, tables, chain, far_parts = [], [], [], [], []
@@ -494,7 +520,7 @@
         weights.append(target_operand(emb))
         return weights[-1]
 
-    def near_job(chunks, back=None):
+    def near_job(chunks, back=None, planned=()):
         tile, table, *passed = build(
             [x for up, low, _ in chunks for x in (up, low)],
             weights,
@@ -502,6 +528,7 @@
             offsets=tuple(offset for _, _, offset in chunks),
             chain=chain,
             back=back,
+            planned=planned,
         )
         tiles.append(tile)
         tables.append(table)
@@ -521,7 +548,7 @@
 
     def behind_job(step, *halves):
         if jobs and jobs[0][0] <= max(0, step - 2):
-            halves = lax.optimization_barrier((halves, jobs.pop(0)[1](), sibling_mass))[0]
+            halves, _ = lax.optimization_barrier((halves, jobs.pop(0)[1]()))
         return halves
 
     up_a, up_b, down_a, down_b = upper, lower, upper, lower
@@ -540,28 +567,31 @@
     for _, job in jobs:
         job()
     far_tiles, far_at, far_mass, from_far = far_parts
-    near_job([(up_a, down_b, steps)], from_far)
+    planned = plan_tiles(me, up_a, slot_cap, sb, target_emb.shape[0], near, chips, steps)
+    near_job([(up_a, down_b, steps)], from_far, planned)
     near_rows, all_mass = chain
 
     for sweep in range(ITERS):
         if sweep > 0:
-            far_rows = far_row_sums(far_at, mine, theirs, target_mass, far_tiles)
-            back = to_group(far_rows, -1)
-            near_rows = row_sums(tables, mine, theirs, target_mass, sibling_mass, tiles, chips * sb)
+            back = to_group(extra, -1)
+            near_rows = row_sums(tables, scale, across(scale, 1), tiles, chips * sb)
             near_rows = add_own(me, near_rows, back)
         bits = [1 << k for k in range(1, dev_count.bit_length() - 1)]
         parts = [near_rows]
         while bits:
             ways = [bits.pop() for _ in range(2 - len(bits) % 2)]
-            ways = ways + [sum(ways)] if len(ways) == 2 else ways
+            ways = [sum(ways)] + ways if len(ways) == 2 else ways
             total = sum(parts[1:], parts[0])
             parts = [total] + [across(total, way) for way in ways]
-        near_rows, own_rows = add_last(me, parts, sb)
-        far_rows = to_group(own_rows, 1)
-        mine = column_sums(tables, near_rows, all_mass, tiles, 2 * tb)
-        mine = far_column_sums(far_at, mine, far_rows, far_mass, far_tiles)
-        theirs = across(mine, 1)
-    return scales(own_rows, source_mass, mine, theirs, target_mass)
+        near_rows = add_all(parts)
+        all_rows = to_group(near_rows, 1)
+        mine, other = column_sums(tables, near_rows, all_mass, tiles, target_emb.shape[0])
+        theirs = across(other, 1)
+        own = (near_rows, source_mass) if sweep == ITERS - 1 else ()
+        extra, scale = closing(
+            me, far_at, all_rows, far_mass, mine, theirs, target_mass, far_tiles, *own
+        )
+    return (extra, scale)
 
 
 def solution(mesh):

time: 88 us -> 84.6 us (0.961)
  waiting for transfers between devices: 27.6 us -> 25.1 us
    ppermute x5, waiting for transfers between devices: 2.91 us -> 1.33 us  [to_group(): lax.ppermute(x, 'group', [(g, (g + by) % group_count) for g in range(grou...]
    pallas_call x14 -> x13, Pallas kernels: 15.3 us -> 15.3 us  [the longest x6 11.4 us: build_tiles(): pl.pallas_call(functools.partial(tile_kernel, plan), out_shape=out_shape,...]
  transfers between devices with their start and end apart: 31 -> 31, of which waited for: 22 -> 22; matrix products, arithmetic and copies ran while one was open for 0% -> 0% of each run, Pallas kernels for 23% -> 25%
where the time goes in v5:
time: 84.6 us; the launch traced here: 84.4 us
  starting transfers between devices  35.2 us (42%)
  waiting for transfers between devices  25.1 us (30%)
  Pallas kernels  23.2 us (27%)
    ppermute x14, starting transfers between devices, around(): return lax.ppermute(x, 'dev', pairs)  14.9 us
    ppermute x12, waiting for transfers between devices, across(): return lax.ppermute(x, 'dev', [(i, i ^ bit) for i in range(dev_count)])  13 us
    ppermute x12, starting transfers between devices, across(): return lax.ppermute(x, 'dev', [(i, i ^ bit) for i in range(dev_count)])  12.8 us
    pallas_call x6, Pallas kernels, build_tiles(): pl.pallas_call(functools.partial(tile_kernel, plan), out_shape=out_shape,...  11.4 us
    ppermute x14, waiting for transfers between devices, around(): return lax.ppermute(x, 'dev', pairs)  10.8 us
    ppermute x5, starting transfers between devices, to_group(): lax.ppermute(x, 'group', [(g, (g + by) % group_count) for g in range(grou...  7.55 us
    pallas_call x2, Pallas kernels, target_operand(): pl.pallas_call(target_kernel, out_shape=pltpu.VMEM((blocks, width, 2 * ro...  5.09 us
    pallas_call x2, Pallas kernels, column_sums(): pl.pallas_call(functools.partial(column_kernel, counts), out_shape=(jax.S...  1.78 us
  transfers between devices with their start and end apart: 31, of which 22 were waited for; matrix products, arithmetic and copies ran while one was open for 0% of the time, Pallas kernels for 25%

profile of v5, /device:TPU:0, one launch (start us, length us, event | category | flops | bytes accessed | tf_op | source)
XLA Modules:
  0.0 84.4 jit_solution(8408934291462358281)
XLA Ops:
  0.6 0.5 collective-permute-start.2
  1.1 1.2 %pack.1 = (f32[520,128]{1,0:T(8,128)S(1)}, f32[520,128]{1,0:T(8,128)S(1)}, f32[1040,128]{1,0:T(8,128)S(1)}) custom-call(s32[1]{0:T(128)} %bitcast.device.refs_0_, f32[8,128,128]{2,1,0:T(8,128)} %emb.1, f32[8,128]{1,0:T(8,128)} %refs_9_.1, s32[8,7]{1,0:T(8,128)} %cand_device.1, s32[8,8]{1,0:T(8,128)} %cand_block.1), custom_call_target="tpu_custom_call" | custom-call | tf_op jit(solution)/shard_map/pack/pallas_call | solution.py:135
  2.4 2.6 %collective-permute-start = (f32[520,128]{1,0:T(8,128)S(1)}, f32[520,128]{1,0:T(8,128)S(1)}, u32[]{:S(2)}, u32[]{:S(2)}) collective-permute-start(f32[520,128]{1,0:T(8,128)S(1)} %get-tuple-element.54.refs_1_), channel_id=1, source_target_pairs={{0,4},{1,5},{4,8},{5,9},{8,12},{9,13},{12,14},{13,15},{14,10},{15,... | collective-permute-start | bytes 798728 | tf_op jit(solution)/shard_map/ppermute | solution.py:501
  5.0 2.9 %target_operand.2.refs_2_.refs_3_.refs_5_ = bf16[32,128,256]{2,1,0:T(8,128)(2,1)S(1)} custom-call(f32[32,128,128]{2,1,0:T(8,128)} %emb_ref.1), custom_call_target="tpu_custom_call" | custom-call | flops 1 | bytes 1 | tf_op jit(solution)/shard_map/target_operand/pallas_call | solution.py:91
  8.0 2.1 %collective-permute-start.3 = (f32[520,128]{1,0:T(8,128)S(1)}, f32[520,128]{1,0:T(8,128)S(1)}, u32[]{:S(2)}, u32[]{:S(2)}) collective-permute-start(f32[520,128]{1,0:T(8,128)S(1)} %get-tuple-element.53.refs_2_), channel_id=1, source_target_pairs={{0,4},{1,5},{4,8},{5,9},{8,12},{9,13},{12,14},{13,15},{14,10},{15,... | collective-permute-start | bytes 798728 | tf_op jit(solution)/shard_map/ppermute | solution.py:501
  10.1 2.1 %target_operand.3.refs_4_.refs_6_ = bf16[32,128,256]{2,1,0:T(8,128)(2,1)S(1)} custom-call(f32[32,128,128]{2,1,0:T(8,128)S(1)} %collective-permute-done.2.emb_ref), custom_call_target="tpu_custom_call" | custom-call | flops 1 | bytes 1 | tf_op jit(solution)/shard_map/target_operand/pallas_call | solution.py:91
  12.2 2.0 %collective-permute-done.5.refs_4_ = f32[520,128]{1,0:T(8,128)S(1)} collective-permute-done((f32[520,128]{1,0:T(8,128)S(1)}, f32[520,128]{1,0:T(8,128)S(1)}, u32[]{:S(2)}, u32[]{:S(2)}) %collective-permute-start.5) | collective-permute-done | bytes 266272 | tf_op jit(solution)/shard_map/ppermute | solution.py:501
  14.3 1.6 %collective-permute-start.6 = (f32[520,128]{1,0:T(8,128)S(1)}, f32[520,128]{1,0:T(8,128)S(1)}, u32[]{:S(2)}, u32[]{:S(2)}) collective-permute-start(f32[520,128]{1,0:T(8,128)S(1)} %collective-permute-done.refs_1_), channel_id=1, source_target_pairs={{0,4},{1,5},{4,8},{5,9},{8,12},{9,13},{12,14},{13,15},{14,10},{15,... | collective-permute-start | bytes 798728 | tf_op jit(solution)/shard_map/ppermute | solution.py:501
  15.9 0.4 collective-permute-start.9
  16.3 1.5 %collective-permute-start.1 = (f32[1040,128]{1,0:T(8,128)S(1)}, f32[1040,128]{1,0:T(8,128)S(1)}, u32[]{:S(2)}, u32[]{:S(2)}) collective-permute-start(f32[1040,128]{1,0:T(8,128)S(1)} %get-tuple-element.49), channel_id=1, source_target_pairs={{0,16},{16,0},{1,17},{17,1},{2,18},{18,2},{3,19},{19,3},{4,20},{20... | collective-permute-start | bytes 1597448 | tf_op jit(solution)/shard_map/ppermute | solution.py:507
  17.8 1.7 %build_tiles.7 = (bf16[10,128,256]{2,1,0:T(8,128)(2,1)S(1)}, s32[21]{0:T(128)S(4)}, f32[64,128]{1,0:T(8,128)S(1)}, f32[64,128]{1,0:T(8,128)S(1)}) custom-call(s32[1]{0:T(128)} %bitcast.device.refs_0_, f32[520,128]{1,0:T(8,128)S(1)} %get-tuple-element.54.refs_1_, f32[520,128]{1,0:T(8,128)S(1)} %get-tuple-element.53.refs_2_, ...), custom_call_target="tpu_custom_call" | custom-call | flops 1 | bytes 1 | tf_op jit(solution)/shard_map/build_tiles/pallas_call | solution.py:322
  19.5 0.5 collective-permute-done.4.refs_3_
  20.0 1.6 %collective-permute-start.7 = (f32[520,128]{1,0:T(8,128)S(1)}, f32[520,128]{1,0:T(8,128)S(1)}, u32[]{:S(2)}, u32[]{:S(2)}) collective-permute-start(f32[520,128]{1,0:T(8,128)S(1)} %collective-permute-done.3.refs_2_), channel_id=1, source_target_pairs={{0,4},{1,5},{4,8},{5,9},{8,12},{9,13},{12,14},{13,15},{14,10},{15,... | collective-permute-start | bytes 798728 | tf_op jit(solution)/shard_map/ppermute | solution.py:501
  21.6 0.4 collective-permute-start.8
  22.0 2.5 %build_tiles.8 = (bf16[20,128,256]{2,1,0:T(8,128)(2,1)S(1)}, s32[41]{0:T(128)S(4)}, f32[64,128]{1,0:T(8,128)S(1)}, f32[64,128]{1,0:T(8,128)S(1)}) custom-call(s32[1]{0:T(128)} %bitcast.device.refs_0_, f32[520,128]{1,0:T(8,128)S(1)} %collective-permute-done.refs_1_, f32[520,128]{1,0:T(8,128)S(1)} %collective-permute-done.3.refs_2_, ...), custom_call_target="tpu_custom_call" | custom-call | flops 1 | bytes 1 | tf_op jit(solution)/shard_map/build_tiles/pallas_call | solution.py:322
  24.5 1.1 %collective-permute-done.9.refs_4_ = f32[520,128]{1,0:T(8,128)S(1)} collective-permute-done((f32[520,128]{1,0:T(8,128)S(1)}, f32[520,128]{1,0:T(8,128)S(1)}, u32[]{:S(2)}, u32[]{:S(2)}) %collective-permute-start.9) | collective-permute-done | bytes 266272 | tf_op jit(solution)/shard_map/ppermute | solution.py:501
  25.7 1.6 %collective-permute-start.10 = (f32[520,128]{1,0:T(8,128)S(1)}, f32[520,128]{1,0:T(8,128)S(1)}, u32[]{:S(2)}, u32[]{:S(2)}) collective-permute-start(f32[520,128]{1,0:T(8,128)S(1)} %collective-permute-done.6.refs_1_), channel_id=1, source_target_pairs={{0,4},{1,5},{4,8},{5,9},{8,12},{9,13},{12,14},{13,15},{14,10},{15,... | collective-permute-start | bytes 798728 | tf_op jit(solution)/shard_map/ppermute | solution.py:501
  27.3 0.4 collective-permute-start.13
  27.7 1.6 %collective-permute-done.7.refs_2_ = f32[520,128]{1,0:T(8,128)S(1)} collective-permute-done((f32[520,128]{1,0:T(8,128)S(1)}, f32[520,128]{1,0:T(8,128)S(1)}, u32[]{:S(2)}, u32[]{:S(2)}) %collective-permute-start.7) | collective-permute-done | bytes 266272 | tf_op jit(solution)/shard_map/ppermute | solution.py:501
  29.3 2.0 %collective-permute-start.11 = (f32[520,128]{1,0:T(8,128)S(1)}, f32[520,128]{1,0:T(8,128)S(1)}, u32[]{:S(2)}, u32[]{:S(2)}) collective-permute-start(f32[520,128]{1,0:T(8,128)S(1)} %collective-permute-done.7.refs_2_), channel_id=1, source_target_pairs={{0,4},{1,5},{4,8},{5,9},{8,12},{9,13},{12,14},{13,15},{14,10},{15,... | collective-permute-start | bytes 798728 | tf_op jit(solution)/shard_map/ppermute | solution.py:501
  31.4 2.5 %build_tiles.9 = (bf16[20,128,256]{2,1,0:T(8,128)(2,1)S(1)}, s32[41]{0:T(128)S(4)}, f32[64,128]{1,0:T(8,128)S(1)}, f32[64,128]{1,0:T(8,128)S(1)}) custom-call(s32[1]{0:T(128)} %bitcast.device.refs_0_, f32[520,128]{1,0:T(8,128)S(1)} %collective-permute-done.6.refs_1_, f32[520,128]{1,0:T(8,128)S(1)} %collective-permute-done.7.refs_2_, ...), custom_call_target="tpu_custom_call" | custom-call | flops 1 | bytes 1 | tf_op jit(solution)/shard_map/build_tiles/pallas_call | solution.py:322
  33.9 1.1 %collective-permute-done.10.refs_1_ = f32[520,128]{1,0:T(8,128)S(1)} collective-permute-done((f32[520,128]{1,0:T(8,128)S(1)}, f32[520,128]{1,0:T(8,128)S(1)}, u32[]{:S(2)}, u32[]{:S(2)}) %collective-permute-start.10) | collective-permute-done | bytes 266272 | tf_op jit(solution)/shard_map/ppermute | solution.py:501
  35.0 2.1 %collective-permute-done.13.refs_4_ = f32[520,128]{1,0:T(8,128)S(1)} collective-permute-done((f32[520,128]{1,0:T(8,128)S(1)}, f32[520,128]{1,0:T(8,128)S(1)}, u32[]{:S(2)}, u32[]{:S(2)}) %collective-permute-start.13) | collective-permute-done | bytes 266272 | tf_op jit(solution)/shard_map/ppermute | solution.py:501
  37.1 1.6 %collective-permute-start.14 = (f32[520,128]{1,0:T(8,128)S(1)}, f32[520,128]{1,0:T(8,128)S(1)}, u32[]{:S(2)}, u32[]{:S(2)}) collective-permute-start(f32[520,128]{1,0:T(8,128)S(1)} %collective-permute-done.10.refs_1_), channel_id=1, source_target_pairs={{0,4},{1,5},{4,8},{5,9},{8,12},{9,13},{12,14},{13,15},{14,10},{15,... | collective-permute-start | bytes 798728 | tf_op jit(solution)/shard_map/ppermute | solution.py:501
  38.7 0.4 collective-permute-start.15
  39.1 1.3 %build_tiles.6 = (bf16[8,128,256]{2,1,0:T(8,128)(2,1)S(1)}, s32[8]{0:T(128)S(4)}, f32[8,128]{1,0:T(8,128)S(1)}, f32[8,128]{1,0:T(8,128)S(1)}) custom-call(s32[1]{0:T(128)} %bitcast.device.refs_0_, f32[1040,128]{1,0:T(8,128)S(1)} %collective-permute-done.1.refs_1_, bf16[32,128,256]{2,1,0:T(8,128)(2,1)S(1)} %target_operand.2.refs_2_.refs_3_.refs_5_), custom_call_target="tpu_custom_call" | custom-call | flops 1 | bytes 1 | tf_op jit(solution)/shard_map/build_tiles/pallas_call | solution.py:322
  40.5 1.6 %collective-permute-start.16 = (f32[8,128]{1,0:T(8,128)S(1)}, f32[8,128]{1,0:T(8,128)S(1)}, u32[]{:S(2)}, u32[]{:S(2)}) collective-permute-start(f32[8,128]{1,0:T(8,128)S(1)} %get-tuple-element.75), channel_id=1, source_target_pairs={{0,16},{16,0},{1,17},{17,1},{2,18},{18,2},{3,19},{19,3},{4,20},{20... | collective-permute-start | bytes 12296 | tf_op jit(solution)/shard_map/ppermute | solution.py:507
  42.1 0.7 collective-permute-done.12.refs_3_
  42.8 2.5 %build_tiles.10 = (bf16[20,128,256]{2,1,0:T(8,128)(2,1)S(1)}, s32[41]{0:T(128)S(4)}, f32[64,128]{1,0:T(8,128)S(1)}, f32[64,128]{1,0:T(8,128)S(1)}) custom-call(s32[1]{0:T(128)} %bitcast.device.refs_0_, f32[520,128]{1,0:T(8,128)S(1)} %collective-permute-done.10.refs_1_, f32[520,128]{1,0:T(8,128)S(1)} %collective-permute-done.11.refs_2_, ...), custom_call_target="tpu_custom_call" | custom-call | flops 1 | bytes 1 | tf_op jit(solution)/shard_map/build_tiles/pallas_call | solution.py:322
  45.3 0.9 %collective-permute-done.14.upper.refs_1_ = f32[520,128]{1,0:T(8,128)S(1)} collective-permute-done((f32[520,128]{1,0:T(8,128)S(1)}, f32[520,128]{1,0:T(8,128)S(1)}, u32[]{:S(2)}, u32[]{:S(2)}) %collective-permute-start.14) | collective-permute-done | bytes 266272 | tf_op jit(solution)/shard_map/ppermute | solution.py:501
  46.2 0.9 %plan_tiles.1 = (s32[21]{0:T(128)S(4)}, s32[11]{0:T(128)S(4)}) custom-call(s32[1]{0:T(128)} %bitcast.device.refs_0_, f32[520,128]{1,0:T(8,128)S(1)} %collective-permute-done.14.upper.refs_1_), custom_call_target="tpu_custom_call" | custom-call | flops 1 | bytes 1 | tf_op jit(solution)/shard_map/plan_tiles/pallas_call | solution.py:276
  47.1 0.6 collective-permute-done.15.refs_2_
  47.8 0.8 build_tiles.11
  48.6 2.6 %collective-permute-start.17 = (f32[64,128]{1,0:T(8,128)S(1)}, f32[64,128]{1,0:T(8,128)S(1)}, u32[]{:S(2)}, u32[]{:S(2)}) collective-permute-start(f32[64,128]{1,0:T(8,128)S(1)} %get-tuple-element.77), channel_id=1, source_target_pairs={{0,8},{1,9},{2,10},{3,11},{4,12},{5,13},{6,14},{7,15},{8,0},{9,1},... | collective-permute-start | bytes 98312 | tf_op jit(solution)/shard_map/ppermute | solution.py:504
  51.2 2.2 %collective-permute-done.17 = f32[64,128]{1,0:T(8,128)S(1)} collective-permute-done((f32[64,128]{1,0:T(8,128)S(1)}, f32[64,128]{1,0:T(8,128)S(1)}, u32[]{:S(2)}, u32[]{:S(2)}) %collective-permute-start.17) | collective-permute-done | bytes 32800 | tf_op jit(solution)/shard_map/ppermute | solution.py:504
  53.4 2.1 %collective-permute-start.18 = (f32[64,128]{1,0:T(8,128)S(1)}, f32[64,128]{1,0:T(8,128)S(1)}, u32[]{:S(2)}, u32[]{:S(2)}) collective-permute-start(f32[64,128]{1,0:T(8,128)S(1)} %add.6.refs_0_), channel_id=1, source_target_pairs={{0,6},{1,7},{2,4},{3,5},{4,2},{5,3},{6,0},{7,1},{8,14},{9,15},{10,... | collective-permute-start | bytes 98312 | tf_op jit(solution)/shard_map/ppermute | solution.py:504
  55.6 0.6 collective-permute-start.19
  56.1 0.8 collective-permute-start.20
  56.9 1.3 %collective-permute-done.18.refs_1_ = f32[64,128]{1,0:T(8,128)S(1)} collective-permute-done((f32[64,128]{1,0:T(8,128)S(1)}, f32[64,128]{1,0:T(8,128)S(1)}, u32[]{:S(2)}, u32[]{:S(2)}) %collective-permute-start.18) | collective-permute-done | bytes 32800 | tf_op jit(solution)/shard_map/ppermute | solution.py:504
  58.3 1.2 %collective-permute-done.19.refs_2_ = f32[64,128]{1,0:T(8,128)S(1)} collective-permute-done((f32[64,128]{1,0:T(8,128)S(1)}, f32[64,128]{1,0:T(8,128)S(1)}, u32[]{:S(2)}, u32[]{:S(2)}) %collective-permute-start.19) | collective-permute-done | bytes 32800 | tf_op jit(solution)/shard_map/ppermute | solution.py:504
  59.5 0.6 collective-permute-done.20.refs_3_
  60.1 1.6 %collective-permute-start.21 = (f32[64,128]{1,0:T(8,128)S(1)}, f32[64,128]{1,0:T(8,128)S(1)}, u32[]{:S(2)}, u32[]{:S(2)}) collective-permute-start(f32[64,128]{1,0:T(8,128)S(1)} %add_all.2.refs_5_), channel_id=1, source_target_pairs={{0,16},{16,0},{1,17},{17,1},{2,18},{18,2},{3,19},{19,3},{4,20},{20... | collective-permute-start | bytes 98312 | tf_op jit(solution)/shard_map/ppermute | solution.py:507
  61.6 0.9 %column_sums.2 = (f32[32,128]{1,0:T(8,128)S(1)}, f32[32,128]{1,0:T(8,128)S(1)}) custom-call(s32[21]{0:T(128)S(4)} %get-tuple-element.52.refs_0_, s32[41]{0:T(128)S(4)} %get-tuple-element.57.refs_1_, s32[41]{0:T(128)S(4)} %get-tuple-element.64.refs_2_, s32[41]{0:T(128)S(4)} %get-tuple-element.69.refs_3_, s32[21]{0:T(128)S(4)} %get-tuple-element.71.refs_8_.refs_4_, ...), custom_call_target="tpu_custom_call" | custom-call | flops 1 | bytes 1 | tf_op jit(solution)/shard_map/column_sums/pallas_call | solution.py:392
  62.5 0.1 collective-permute-start.22
  62.6 1.2 %collective-permute-done.22.refs_5_ = f32[32,128]{1,0:T(8,128)S(1)} collective-permute-done((f32[32,128]{1,0:T(8,128)S(1)}, f32[32,128]{1,0:T(8,128)S(1)}, u32[]{:S(2)}, u32[]{:S(2)}) %collective-permute-start.22) | collective-permute-done | bytes 16416 | tf_op jit(solution)/shard_map/ppermute | solution.py:504
  63.8 0.2 collective-permute-done.21.refs_2_
  64.0 0.4 closing.2
  64.5 0.1 collective-permute-start.23
  64.6 1.6 %collective-permute-start.24 = (f32[8,128]{1,0:T(8,128)S(1)}, f32[8,128]{1,0:T(8,128)S(1)}, u32[]{:S(2)}, u32[]{:S(2)}) collective-permute-start(f32[8,128]{1,0:T(8,128)S(1)} %get-tuple-element.89), channel_id=1, source_target_pairs={{0,16},{16,0},{1,17},{17,1},{2,18},{18,2},{3,19},{19,3},{4,20},{20... | collective-permute-start | bytes 12296 | tf_op jit(solution)/shard_map/ppermute | solution.py:507
  66.2 1.6 %row_sums.1.rows = f32[64,128]{1,0:T(8,128)S(1)} custom-call(s32[21]{0:T(128)S(4)} %get-tuple-element.52.refs_0_, s32[41]{0:T(128)S(4)} %get-tuple-element.57.refs_1_, s32[41]{0:T(128)S(4)} %get-tuple-element.64.refs_2_, s32[41]{0:T(128)S(4)} %get-tuple-element.69.refs_3_, s32[21]{0:T(128)S(4)} %get-tuple-element.71.refs_8_.refs_4_, ...), custom_call_target="tpu_custom_call" | custom-call | flops 1 | bytes 1 | tf_op jit(solution)/shard_map/row_sums/pallas_call | solution.py:472
  67.7 0.5 collective-permute-done.24.part
  68.2 2.5 %collective-permute-start.25 = (f32[64,128]{1,0:T(8,128)S(1)}, f32[64,128]{1,0:T(8,128)S(1)}, u32[]{:S(2)}, u32[]{:S(2)}) collective-permute-start(f32[64,128]{1,0:T(8,128)S(1)} %add_own.1), channel_id=1, source_target_pairs={{0,8},{1,9},{2,10},{3,11},{4,12},{5,13},{6,14},{7,15},{8,0},{9,1},... | collective-permute-start | bytes 98312 | tf_op jit(solution)/shard_map/ppermute | solution.py:504
  70.8 2.5 %collective-permute-done.25 = f32[64,128]{1,0:T(8,128)S(1)} collective-permute-done((f32[64,128]{1,0:T(8,128)S(1)}, f32[64,128]{1,0:T(8,128)S(1)}, u32[]{:S(2)}, u32[]{:S(2)}) %collective-permute-start.25) | collective-permute-done | bytes 32800 | tf_op jit(solution)/shard_map/ppermute | solution.py:504
  73.3 1.6 %collective-permute-start.26 = (f32[64,128]{1,0:T(8,128)S(1)}, f32[64,128]{1,0:T(8,128)S(1)}, u32[]{:S(2)}, u32[]{:S(2)}) collective-permute-start(f32[64,128]{1,0:T(8,128)S(1)} %add.7.refs_0_), channel_id=1, source_target_pairs={{0,6},{1,7},{2,4},{3,5},{4,2},{5,3},{6,0},{7,1},{8,14},{9,15},{10,... | collective-permute-start | bytes 98312 | tf_op jit(solution)/shard_map/ppermute | solution.py:504
  74.9 0.8 collective-permute-start.27
  75.6 1.1 %collective-permute-start.28 = (f32[64,128]{1,0:T(8,128)S(1)}, f32[64,128]{1,0:T(8,128)S(1)}, u32[]{:S(2)}, u32[]{:S(2)}) collective-permute-start(f32[64,128]{1,0:T(8,128)S(1)} %add.7.refs_0_), channel_id=1, source_target_pairs={{0,2},{1,3},{2,0},{3,1},{4,6},{5,7},{6,4},{7,5},{8,10},{9,11},{10,... | collective-permute-start | bytes 98312 | tf_op jit(solution)/shard_map/ppermute | solution.py:504
  76.7 1.3 %collective-permute-done.26.refs_1_ = f32[64,128]{1,0:T(8,128)S(1)} collective-permute-done((f32[64,128]{1,0:T(8,128)S(1)}, f32[64,128]{1,0:T(8,128)S(1)}, u32[]{:S(2)}, u32[]{:S(2)}) %collective-permute-start.26) | collective-permute-done | bytes 32800 | tf_op jit(solution)/shard_map/ppermute | solution.py:504
  78.1 0.7 collective-permute-done.27.refs_2_
  78.8 0.8 collective-permute-done.28.refs_3_
  79.6 1.3 %collective-permute-start.29 = (f32[64,128]{1,0:T(8,128)S(1)}, f32[64,128]{1,0:T(8,128)S(1)}, u32[]{:S(2)}, u32[]{:S(2)}) collective-permute-start(f32[64,128]{1,0:T(8,128)S(1)} %add_all.3.refs_5_.refs_8_), channel_id=1, source_target_pairs={{0,16},{16,0},{1,17},{17,1},{2,18},{18,2},{3,19},{19,3},{4,20},{20... | collective-permute-start | bytes 98312 | tf_op jit(solution)/shard_map/ppermute | solution.py:507
  80.9 0.9 %column_sums.3 = (f32[32,128]{1,0:T(8,128)S(1)}, f32[32,128]{1,0:T(8,128)S(1)}) custom-call(s32[21]{0:T(128)S(4)} %get-tuple-element.52.refs_0_, s32[41]{0:T(128)S(4)} %get-tuple-element.57.refs_1_, s32[41]{0:T(128)S(4)} %get-tuple-element.64.refs_2_, s32[41]{0:T(128)S(4)} %get-tuple-element.69.refs_3_, s32[21]{0:T(128)S(4)} %get-tuple-element.71.refs_8_.refs_4_, ...), custom_call_target="tpu_custom_call" | custom-call | flops 1 | bytes 1 | tf_op jit(solution)/shard_map/column_sums/pallas_call | solution.py:392
  81.8 1.2 %collective-permute-done.30.refs_5_ = f32[32,128]{1,0:T(8,128)S(1)} collective-permute-done((f32[32,128]{1,0:T(8,128)S(1)}, f32[32,128]{1,0:T(8,128)S(1)}, u32[]{:S(2)}, u32[]{:S(2)}) %collective-permute-start.30) | collective-permute-done | bytes 16416 | tf_op jit(solution)/shard_map/ppermute | solution.py:504
  83.0 0.6 collective-permute-done.29.refs_2_
  83.6 0.8 closing.3
  (22 shorter events, 0.2 us)
Async XLA Ops:
  0.6 9.5 %collective-permute-start.2 = (f32[32,128,128]{2,1,0:T(8,128)}, f32[32,128,128]{2,1,0:T(8,128)S(1)}, u32[]{:S(2)}, u32[]{:S(2)}) collective-permute-start(f32[32,128,128]{2,1,0:T(8,128)} %emb_ref.1), channel_id=1, source_target_pairs={{0,1},{1,0},{2,3},{3,2},{4,5},{5,4},{6,7},{7,6},{8,9},{9,8},{10,11... | collective-permute-start | bytes 6291464 | tf_op jit(solution)/shard_map/ppermute | solution.py:504
  2.4 9.8 %collective-permute-start = (f32[520,128]{1,0:T(8,128)S(1)}, f32[520,128]{1,0:T(8,128)S(1)}, u32[]{:S(2)}, u32[]{:S(2)}) collective-permute-start(f32[520,128]{1,0:T(8,128)S(1)} %get-tuple-element.54.refs_1_), channel_id=1, source_target_pairs={{0,4},{1,5},{4,8},{5,9},{8,12},{9,13},{12,14},{13,15},{14,10},{15,... | collective-permute-start | bytes 798728 | tf_op jit(solution)/shard_map/ppermute | solution.py:501
  5.0 9.2 %collective-permute-start.5 = (f32[520,128]{1,0:T(8,128)S(1)}, f32[520,128]{1,0:T(8,128)S(1)}, u32[]{:S(2)}, u32[]{:S(2)}) collective-permute-start(f32[520,128]{1,0:T(8,128)S(1)} %get-tuple-element.53.refs_2_), channel_id=1, source_target_pairs={{0,2},{1,3},{4,0},{5,1},{8,4},{9,5},{12,8},{13,9},{14,12},{15,13},... | collective-permute-start | bytes 798728 | tf_op jit(solution)/shard_map/ppermute | solution.py:501
  8.0 11.5 %collective-permute-start.3 = (f32[520,128]{1,0:T(8,128)S(1)}, f32[520,128]{1,0:T(8,128)S(1)}, u32[]{:S(2)}, u32[]{:S(2)}) collective-permute-start(f32[520,128]{1,0:T(8,128)S(1)} %get-tuple-element.53.refs_2_), channel_id=1, source_target_pairs={{0,4},{1,5},{4,8},{5,9},{8,12},{9,13},{12,14},{13,15},{14,10},{15,... | collective-permute-start | bytes 798728 | tf_op jit(solution)/shard_map/ppermute | solution.py:501
  10.1 9.9 %collective-permute-start.4 = (f32[520,128]{1,0:T(8,128)S(1)}, f32[520,128]{1,0:T(8,128)S(1)}, u32[]{:S(2)}, u32[]{:S(2)}) collective-permute-start(f32[520,128]{1,0:T(8,128)S(1)} %get-tuple-element.54.refs_1_), channel_id=1, source_target_pairs={{0,2},{1,3},{4,0},{5,1},{8,4},{9,5},{12,8},{13,9},{14,12},{15,13},... | collective-permute-start | bytes 798728 | tf_op jit(solution)/shard_map/ppermute | solution.py:501
  14.3 10.3 %collective-permute-start.6 = (f32[520,128]{1,0:T(8,128)S(1)}, f32[520,128]{1,0:T(8,128)S(1)}, u32[]{:S(2)}, u32[]{:S(2)}) collective-permute-start(f32[520,128]{1,0:T(8,128)S(1)} %collective-permute-done.refs_1_), channel_id=1, source_target_pairs={{0,4},{1,5},{4,8},{5,9},{8,12},{9,13},{12,14},{13,15},{14,10},{15,... | collective-permute-start | bytes 798728 | tf_op jit(solution)/shard_map/ppermute | solution.py:501
  15.9 9.8 %collective-permute-start.9 = (f32[520,128]{1,0:T(8,128)S(1)}, f32[520,128]{1,0:T(8,128)S(1)}, u32[]{:S(2)}, u32[]{:S(2)}) collective-permute-start(f32[520,128]{1,0:T(8,128)S(1)} %collective-permute-done.5.refs_4_), channel_id=1, source_target_pairs={{0,2},{1,3},{4,0},{5,1},{8,4},{9,5},{12,8},{13,9},{14,12},{15,13},... | collective-permute-start | bytes 798728 | tf_op jit(solution)/shard_map/ppermute | solution.py:501
  16.3 22.8 %collective-permute-start.1 = (f32[1040,128]{1,0:T(8,128)S(1)}, f32[1040,128]{1,0:T(8,128)S(1)}, u32[]{:S(2)}, u32[]{:S(2)}) collective-permute-start(f32[1040,128]{1,0:T(8,128)S(1)} %get-tuple-element.49), channel_id=1, source_target_pairs={{0,16},{16,0},{1,17},{17,1},{2,18},{18,2},{3,19},{19,3},{4,20},{20... | collective-permute-start | bytes 1597448 | tf_op jit(solution)/shard_map/ppermute | solution.py:507
  20.0 9.3 %collective-permute-start.7 = (f32[520,128]{1,0:T(8,128)S(1)}, f32[520,128]{1,0:T(8,128)S(1)}, u32[]{:S(2)}, u32[]{:S(2)}) collective-permute-start(f32[520,128]{1,0:T(8,128)S(1)} %collective-permute-done.3.refs_2_), channel_id=1, source_target_pairs={{0,4},{1,5},{4,8},{5,9},{8,12},{9,13},{12,14},{13,15},{14,10},{15,... | collective-permute-start | bytes 798728 | tf_op jit(solution)/shard_map/ppermute | solution.py:501
  21.6 9.8 %collective-permute-start.8 = (f32[520,128]{1,0:T(8,128)S(1)}, f32[520,128]{1,0:T(8,128)S(1)}, u32[]{:S(2)}, u32[]{:S(2)}) collective-permute-start(f32[520,128]{1,0:T(8,128)S(1)} %collective-permute-done.4.refs_3_), channel_id=1, source_target_pairs={{0,2},{1,3},{4,0},{5,1},{8,4},{9,5},{12,8},{13,9},{14,12},{15,13},... | collective-permute-start | bytes 798728 | tf_op jit(solution)/shard_map/ppermute | solution.py:501
  25.7 9.3 %collective-permute-start.10 = (f32[520,128]{1,0:T(8,128)S(1)}, f32[520,128]{1,0:T(8,128)S(1)}, u32[]{:S(2)}, u32[]{:S(2)}) collective-permute-start(f32[520,128]{1,0:T(8,128)S(1)} %collective-permute-done.6.refs_1_), channel_id=1, source_target_pairs={{0,4},{1,5},{4,8},{5,9},{8,12},{9,13},{12,14},{13,15},{14,10},{15,... | collective-permute-start | bytes 798728 | tf_op jit(solution)/shard_map/ppermute | solution.py:501
  27.3 9.8 %collective-permute-start.13 = (f32[520,128]{1,0:T(8,128)S(1)}, f32[520,128]{1,0:T(8,128)S(1)}, u32[]{:S(2)}, u32[]{:S(2)}) collective-permute-start(f32[520,128]{1,0:T(8,128)S(1)} %collective-permute-done.9.refs_4_), channel_id=1, source_target_pairs={{0,2},{1,3},{4,0},{5,1},{8,4},{9,5},{12,8},{13,9},{14,12},{15,13},... | collective-permute-start | bytes 798728 | tf_op jit(solution)/shard_map/ppermute | solution.py:501
  29.3 12.7 %collective-permute-start.11 = (f32[520,128]{1,0:T(8,128)S(1)}, f32[520,128]{1,0:T(8,128)S(1)}, u32[]{:S(2)}, u32[]{:S(2)}) collective-permute-start(f32[520,128]{1,0:T(8,128)S(1)} %collective-permute-done.7.refs_2_), channel_id=1, source_target_pairs={{0,4},{1,5},{4,8},{5,9},{8,12},{9,13},{12,14},{13,15},{14,10},{15,... | collective-permute-start | bytes 798728 | tf_op jit(solution)/shard_map/ppermute | solution.py:501
  31.4 11.4 %collective-permute-start.12 = (f32[520,128]{1,0:T(8,128)S(1)}, f32[520,128]{1,0:T(8,128)S(1)}, u32[]{:S(2)}, u32[]{:S(2)}) collective-permute-start(f32[520,128]{1,0:T(8,128)S(1)} %collective-permute-done.8.refs_3_), channel_id=1, source_target_pairs={{0,2},{1,3},{4,0},{5,1},{8,4},{9,5},{12,8},{13,9},{14,12},{15,13},... | collective-permute-start | bytes 798728 | tf_op jit(solution)/shard_map/ppermute | solution.py:501
  37.1 9.1 %collective-permute-start.14 = (f32[520,128]{1,0:T(8,128)S(1)}, f32[520,128]{1,0:T(8,128)S(1)}, u32[]{:S(2)}, u32[]{:S(2)}) collective-permute-start(f32[520,128]{1,0:T(8,128)S(1)} %collective-permute-done.10.refs_1_), channel_id=1, source_target_pairs={{0,4},{1,5},{4,8},{5,9},{8,12},{9,13},{12,14},{13,15},{14,10},{15,... | collective-permute-start | bytes 798728 | tf_op jit(solution)/shard_map/ppermute | solution.py:501
  38.7 9.1 %collective-permute-start.15 = (f32[520,128]{1,0:T(8,128)S(1)}, f32[520,128]{1,0:T(8,128)S(1)}, u32[]{:S(2)}, u32[]{:S(2)}) collective-permute-start(f32[520,128]{1,0:T(8,128)S(1)} %collective-permute-done.13.refs_4_), channel_id=1, source_target_pairs={{0,2},{1,3},{4,0},{5,1},{8,4},{9,5},{12,8},{13,9},{14,12},{15,13},... | collective-permute-start | bytes 798728 | tf_op jit(solution)/shard_map/ppermute | solution.py:501
  40.5 6.7 %collective-permute-start.16 = (f32[8,128]{1,0:T(8,128)S(1)}, f32[8,128]{1,0:T(8,128)S(1)}, u32[]{:S(2)}, u32[]{:S(2)}) collective-permute-start(f32[8,128]{1,0:T(8,128)S(1)} %get-tuple-element.75), channel_id=1, source_target_pairs={{0,16},{16,0},{1,17},{17,1},{2,18},{18,2},{3,19},{19,3},{4,20},{20... | collective-permute-start | bytes 12296 | tf_op jit(solution)/shard_map/ppermute | solution.py:507
  48.6 4.8 %collective-permute-start.17 = (f32[64,128]{1,0:T(8,128)S(1)}, f32[64,128]{1,0:T(8,128)S(1)}, u32[]{:S(2)}, u32[]{:S(2)}) collective-permute-start(f32[64,128]{1,0:T(8,128)S(1)} %get-tuple-element.77), channel_id=1, source_target_pairs={{0,8},{1,9},{2,10},{3,11},{4,12},{5,13},{6,14},{7,15},{8,0},{9,1},... | collective-permute-start | bytes 98312 | tf_op jit(solution)/shard_map/ppermute | solution.py:504
  53.4 4.8 %collective-permute-start.18 = (f32[64,128]{1,0:T(8,128)S(1)}, f32[64,128]{1,0:T(8,128)S(1)}, u32[]{:S(2)}, u32[]{:S(2)}) collective-permute-start(f32[64,128]{1,0:T(8,128)S(1)} %add.6.refs_0_), channel_id=1, source_target_pairs={{0,6},{1,7},{2,4},{3,5},{4,2},{5,3},{6,0},{7,1},{8,14},{9,15},{10,... | collective-permute-start | bytes 98312 | tf_op jit(solution)/shard_map/ppermute | solution.py:504
  55.6 3.9 %collective-permute-start.19 = (f32[64,128]{1,0:T(8,128)S(1)}, f32[64,128]{1,0:T(8,128)S(1)}, u32[]{:S(2)}, u32[]{:S(2)}) collective-permute-start(f32[64,128]{1,0:T(8,128)S(1)} %add.6.refs_0_), channel_id=1, source_target_pairs={{0,4},{1,5},{2,6},{3,7},{4,0},{5,1},{6,2},{7,3},{8,12},{9,13},{10,... | collective-permute-start | bytes 98312 | tf_op jit(solution)/shard_map/ppermute | solution.py:504
  56.1 3.9 %collective-permute-start.20 = (f32[64,128]{1,0:T(8,128)S(1)}, f32[64,128]{1,0:T(8,128)S(1)}, u32[]{:S(2)}, u32[]{:S(2)}) collective-permute-start(f32[64,128]{1,0:T(8,128)S(1)} %add.6.refs_0_), channel_id=1, source_target_pairs={{0,2},{1,3},{2,0},{3,1},{4,6},{5,7},{6,4},{7,5},{8,10},{9,11},{10,... | collective-permute-start | bytes 98312 | tf_op jit(solution)/shard_map/ppermute | solution.py:504
  60.1 4.0 %collective-permute-start.21 = (f32[64,128]{1,0:T(8,128)S(1)}, f32[64,128]{1,0:T(8,128)S(1)}, u32[]{:S(2)}, u32[]{:S(2)}) collective-permute-start(f32[64,128]{1,0:T(8,128)S(1)} %add_all.2.refs_5_), channel_id=1, source_target_pairs={{0,16},{16,0},{1,17},{17,1},{2,18},{18,2},{3,19},{19,3},{4,20},{20... | collective-permute-start | bytes 98312 | tf_op jit(solution)/shard_map/ppermute | solution.py:507
  61.6 2.4 %copy-start = (f32[32,128]{1,0:T(8,128)S(1)}, f32[32,128]{1,0:T(8,128)}, u32[]{:S(2)}) copy-start(f32[32,128]{1,0:T(8,128)} %refs_6_.3) | copy-start | bytes 49156
  62.5 1.2 %collective-permute-start.22 = (f32[32,128]{1,0:T(8,128)S(1)}, f32[32,128]{1,0:T(8,128)S(1)}, u32[]{:S(2)}, u32[]{:S(2)}) collective-permute-start(f32[32,128]{1,0:T(8,128)S(1)} %get-tuple-element.86), channel_id=1, source_target_pairs={{0,1},{1,0},{2,3},{3,2},{4,5},{5,4},{6,7},{7,6},{8,9},{9,8},{10,11... | collective-permute-start | bytes 49160 | tf_op jit(solution)/shard_map/ppermute | solution.py:504
  64.5 1.7 %collective-permute-start.23 = (f32[32,128]{1,0:T(8,128)S(1)}, f32[32,128]{1,0:T(8,128)S(1)}, u32[]{:S(2)}, u32[]{:S(2)}) collective-permute-start(f32[32,128]{1,0:T(8,128)S(1)} %get-tuple-element.88.refs_5_), channel_id=1, source_target_pairs={{0,1},{1,0},{2,3},{3,2},{4,5},{5,4},{6,7},{7,6},{8,9},{9,8},{10,11... | collective-permute-start | bytes 49160 | tf_op jit(solution)/shard_map/ppermute | solution.py:504
  64.6 3.7 %collective-permute-start.24 = (f32[8,128]{1,0:T(8,128)S(1)}, f32[8,128]{1,0:T(8,128)S(1)}, u32[]{:S(2)}, u32[]{:S(2)}) collective-permute-start(f32[8,128]{1,0:T(8,128)S(1)} %get-tuple-element.89), channel_id=1, source_target_pairs={{0,16},{16,0},{1,17},{17,1},{2,18},{18,2},{3,19},{19,3},{4,20},{20... | collective-permute-start | bytes 12296 | tf_op jit(solution)/shard_map/ppermute | solution.py:507
  68.2 5.0 %collective-permute-start.25 = (f32[64,128]{1,0:T(8,128)S(1)}, f32[64,128]{1,0:T(8,128)S(1)}, u32[]{:S(2)}, u32[]{:S(2)}) collective-permute-start(f32[64,128]{1,0:T(8,128)S(1)} %add_own.1), channel_id=1, source_target_pairs={{0,8},{1,9},{2,10},{3,11},{4,12},{5,13},{6,14},{7,15},{8,0},{9,1},... | collective-permute-start | bytes 98312 | tf_op jit(solution)/shard_map/ppermute | solution.py:504
  73.3 4.8 %collective-permute-start.26 = (f32[64,128]{1,0:T(8,128)S(1)}, f32[64,128]{1,0:T(8,128)S(1)}, u32[]{:S(2)}, u32[]{:S(2)}) collective-permute-start(f32[64,128]{1,0:T(8,128)S(1)} %add.7.refs_0_), channel_id=1, source_target_pairs={{0,6},{1,7},{2,4},{3,5},{4,2},{5,3},{6,0},{7,1},{8,14},{9,15},{10,... | collective-permute-start | bytes 98312 | tf_op jit(solution)/shard_map/ppermute | solution.py:504
  74.9 3.9 %collective-permute-start.27 = (f32[64,128]{1,0:T(8,128)S(1)}, f32[64,128]{1,0:T(8,128)S(1)}, u32[]{:S(2)}, u32[]{:S(2)}) collective-permute-start(f32[64,128]{1,0:T(8,128)S(1)} %add.7.refs_0_), channel_id=1, source_target_pairs={{0,4},{1,5},{2,6},{3,7},{4,0},{5,1},{6,2},{7,3},{8,12},{9,13},{10,... | collective-permute-start | bytes 98312 | tf_op jit(solution)/shard_map/ppermute | solution.py:504
  75.6 3.9 %collective-permute-start.28 = (f32[64,128]{1,0:T(8,128)S(1)}, f32[64,128]{1,0:T(8,128)S(1)}, u32[]{:S(2)}, u32[]{:S(2)}) collective-permute-start(f32[64,128]{1,0:T(8,128)S(1)} %add.7.refs_0_), channel_id=1, source_target_pairs={{0,2},{1,3},{2,0},{3,1},{4,6},{5,7},{6,4},{7,5},{8,10},{9,11},{10,... | collective-permute-start | bytes 98312 | tf_op jit(solution)/shard_map/ppermute | solution.py:504
  79.6 4.0 %copy-start.1 = (f32[8,128]{1,0:T(8,128)S(1)}, f32[8,128]{1,0:T(8,128)}, u32[]{:S(2)}) copy-start(f32[8,128]{1,0:T(8,128)} %refs_9_.1) | copy-start | bytes 12292
  79.6 4.0 %collective-permute-start.29 = (f32[64,128]{1,0:T(8,128)S(1)}, f32[64,128]{1,0:T(8,128)S(1)}, u32[]{:S(2)}, u32[]{:S(2)}) collective-permute-start(f32[64,128]{1,0:T(8,128)S(1)} %add_all.3.refs_5_.refs_8_), channel_id=1, source_target_pairs={{0,16},{16,0},{1,17},{17,1},{2,18},{18,2},{3,19},{19,3},{4,20},{20... | collective-permute-start | bytes 98312 | tf_op jit(solution)/shard_map/ppermute | solution.py:507
  81.8 1.2 %collective-permute-start.30 = (f32[32,128]{1,0:T(8,128)S(1)}, f32[32,128]{1,0:T(8,128)S(1)}, u32[]{:S(2)}, u32[]{:S(2)}) collective-permute-start(f32[32,128]{1,0:T(8,128)S(1)} %get-tuple-element.91), channel_id=1, source_target_pairs={{0,1},{1,0},{2,3},{3,2},{4,5},{5,4},{6,7},{7,6},{8,9},{9,8},{10,11... | collective-permute-start | bytes 49160 | tf_op jit(solution)/shard_map/ppermute | solution.py:504

commit v6 on v5

--- a/solution.py
+++ b/solution.py
@@ -17,7 +17,6 @@
 VMEM = pl.BlockSpec(memory_space=pltpu.VMEM)
 SMEM = pl.BlockSpec(memory_space=pltpu.SMEM)
 HBM = pl.BlockSpec(memory_space=pltpu.HBM)
-LIGHT = pl.CostEstimate(flops=1, bytes_accessed=1, transcendentals=0)
 NT = (((1,), (1,)), ((), ()))
 NN = (((1,), (0,)), ((), ()))
 
@@ -94,7 +93,6 @@
         in_specs=[pl.BlockSpec(memory_space=pl.ANY)],
         out_specs=VMEM,
         scratch_shapes=[pltpu.VMEM(emb.shape, jnp.float32), pltpu.SemaphoreType.DMA((parts,))],
-        cost_estimate=LIGHT,
         compiler_params=pltpu.CompilerParams(vmem_limit_bytes=16 << 20),
         name="target_operand",
     )(emb)
@@ -167,10 +165,13 @@
     weight = [refs.pop(0) for _ in range(sides)]
     rows_in, mass_in = (refs.pop(0), refs.pop(0)) if chained else (None, None)
     back = refs.pop(0) if closing else None
+    turned = None
     if planned:
         table, listed, tiles, rows_out, mass_out, partial, units = refs
+    elif far:
+        tiles, table, rows_out, mass_out, partial, units, staged, named, listed, arrived = refs
     else:
-        tiles, table, rows_out, mass_out, partial, units, staged, named, listed, arrived = refs
+        tiles, table, rows_out, mass_out, turned, partial, units, staged, named, listed, arrived = refs
     count = chunks * sides * slots
     width = source[0].shape[1]
     scale = 1.0 / (width * entropic_regularizer)
@@ -217,6 +218,8 @@
                 nodes = both.shape[1] // 2
                 affinity = both[:, :nodes] + both[:, nodes:]
                 tile = jnp.exp(affinity * scale) * (1.0 / (8.0 * nodes))
+                if turned is not None:
+                    turned[at] = jnp.concatenate(split2(tile.T), axis=1)
                 tile = jnp.concatenate(split2(tile), axis=1)
                 tiles[at] = tile
                 spot = chunk * (sb + 1) + block
@@ -283,7 +286,6 @@
             pltpu.SMEM((sb, width), jnp.int32),
             pltpu.SemaphoreType.DMA,
         ],
-        cost_estimate=LIGHT,
         compiler_params=SMALL,
         name="plan_tiles",
     )(device, upper)
@@ -307,6 +309,9 @@
         rows,
     ]
     out_specs = [VMEM, SMEM, VMEM, VMEM]
+    if not far and not planned:
+        out_shape.append(pltpu.VMEM((count, nodes, 4 * half), jnp.bfloat16))
+        out_specs.append(VMEM)
     scratch = [
         pltpu.VMEM((chunks * (sb + 1), 8, 2 * half), jnp.float32),
         pltpu.VMEM((chunks * sb, 2 * half, 2 * width), jnp.bfloat16),
@@ -325,7 +330,6 @@
         in_specs=[SMEM] + [VMEM] * len(operands) + [SMEM] * len(planned),
         out_specs=out_specs,
         scratch_shapes=scratch,
-        cost_estimate=LIGHT,
         compiler_params=pltpu.CompilerParams(vmem_limit_bytes=16 << 20),
         name="build_tiles",
     )(device, *operands, *in_smem(*planned))
@@ -398,7 +402,6 @@
             pltpu.VMEM((rows.shape[0] + 8, width), jnp.float32),
             pltpu.VMEM((2 * targets + 1, 8, nodes), jnp.float32),
         ],
-        cost_estimate=LIGHT,
         compiler_params=SMALL,
         name="column_sums",
     )(*in_smem(*tables), rows, mass, *in_vmem(*tiles))
@@ -438,7 +441,6 @@
         in_specs=[SMEM] * 2 + [VMEM] * (8 if last else 6),
         out_specs=(VMEM, VMEM),
         scratch_shapes=[pltpu.VMEM(far_mass.shape, jnp.float32), pltpu.VMEM(target_mass.shape, jnp.float32)],
-        cost_estimate=LIGHT,
         compiler_params=SMALL,
         name="closing",
     )(
@@ -461,7 +463,8 @@
     for part, slots in enumerate(counts):
         for slot in range(slots):
             parts = stacked_parts(scale[pl.ds(tables[part][slots + slot], 1), :])
-            total[tables[part][slot]] += row_product(parts, tiles[part][slot])
+            product = row_product if part == len(counts) - 1 else column_product
+            total[tables[part][slot]] += product(parts, tiles[part][slot])
     for block in range(out.shape[0]):
         out[block : block + 1] = jnp.sum(total[block], axis=0, keepdims=True)
 
@@ -478,7 +481,6 @@
             pltpu.VMEM((2 * mine.shape[0] + 8, nodes), jnp.float32),
             pltpu.VMEM((sources + 1, 8, width), jnp.float32),
         ],
-        cost_estimate=LIGHT,
         compiler_params=SMALL,
         name="row_sums",
     )(*in_smem(*tables), mine, theirs, *in_vmem(*tiles))
@@ -513,7 +515,7 @@
     sibling_emb = across(target_emb, 1)
     far_both = [both]
 
-    weights, tiles, tables, chain, far_parts = [], [], [], [], []
+    weights, tiles, row_tiles, tables, chain, far_parts = [], [], [], [], [], []
     build = functools.partial(build_tiles, me, sb=sb, near=near, chips=chips)
 
     def target_job(emb):
@@ -521,7 +523,7 @@
         return weights[-1]
 
     def near_job(chunks, back=None, planned=()):
-        tile, table, *passed = build(
+        tile, table, rows, mass, *turned = build(
             [x for up, low, _ in chunks for x in (up, low)],
             weights,
             slots=slot_cap,
@@ -532,7 +534,8 @@
         )
         tiles.append(tile)
         tables.append(table)
-        chain[:] = passed
+        row_tiles.append(turned[0] if turned else tile)
+        chain[:] = [rows, mass]
         return chain[0]
 
     def far_job():
@@ -574,7 +577,7 @@
     for sweep in range(ITERS):
         if sweep > 0:
             back = to_group(extra, -1)
-            near_rows = row_sums(tables, scale, across(scale, 1), tiles, chips * sb)
+            near_rows = row_sums(tables, scale, across(scale, 1), row_tiles, chips * sb)
             near_rows = add_own(me, near_rows, back)
         bits = [1 << k for k in range(1, dev_count.bit_length() - 1)]
         parts = [near_rows]

time: 84.6 us -> 84.3 us (level)
  transfers between devices with their start and end apart: 31 -> 31, of which waited for: 22 -> 22; matrix products, arithmetic and copies ran while one was open for 0% -> 0% of each run, Pallas kernels for 25% -> 24%
where the time goes in v6:
time: 84.3 us; the launch traced here: 84.1 us
  starting transfers between devices  35.6 us (42%)
  waiting for transfers between devices  25 us (30%)
  Pallas kernels  22.6 us (27%)
    ppermute x14, starting transfers between devices, around(): return lax.ppermute(x, 'dev', pairs)  14.9 us
    ppermute x12, starting transfers between devices, across(): return lax.ppermute(x, 'dev', [(i, i ^ bit) for i in range(dev_count)])  12.8 us
    ppermute x12, waiting for transfers between devices, across(): return lax.ppermute(x, 'dev', [(i, i ^ bit) for i in range(dev_count)])  12.7 us
    pallas_call x6, Pallas kernels, build_tiles(): pl.pallas_call(functools.partial(tile_kernel, plan), out_shape=out_shape,...  11.4 us
    ppermute x14, waiting for transfers between devices, around(): return lax.ppermute(x, 'dev', pairs)  10.8 us
    ppermute x5, starting transfers between devices, to_group(): lax.ppermute(x, 'group', [(g, (g + by) % group_count) for g in range(grou...  7.87 us
    pallas_call x2, Pallas kernels, target_operand(): pl.pallas_call(target_kernel, out_shape=pltpu.VMEM((blocks, width, 2 * ro...  5.09 us
    pallas_call x2, Pallas kernels, column_sums(): pl.pallas_call(functools.partial(column_kernel, counts), out_shape=(jax.S...  1.79 us
  transfers between devices with their start and end apart: 31, of which 22 were waited for; matrix products, arithmetic and copies ran while one was open for 0% of the time, Pallas kernels for 24%

profile of v6, /device:TPU:0, one launch (start us, length us, event | category | flops | bytes accessed | tf_op | source)
XLA Modules:
  0.0 84.1 jit_solution(6275541128716418599)
XLA Ops:
  0.6 0.5 collective-permute-start.2
  1.1 1.2 %pack.1 = (f32[520,128]{1,0:T(8,128)S(1)}, f32[520,128]{1,0:T(8,128)S(1)}, f32[1040,128]{1,0:T(8,128)S(1)}) custom-call(s32[1]{0:T(128)} %bitcast.device.refs_0_, f32[8,128,128]{2,1,0:T(8,128)} %emb.1, f32[8,128]{1,0:T(8,128)} %refs_9_.1, s32[8,7]{1,0:T(8,128)} %cand_device.1, s32[8,8]{1,0:T(8,128)} %cand_block.1), custom_call_target="tpu_custom_call" | custom-call | tf_op jit(solution)/shard_map/pack/pallas_call | solution.py:133
  2.4 2.6 %collective-permute-start = (f32[520,128]{1,0:T(8,128)S(1)}, f32[520,128]{1,0:T(8,128)S(1)}, u32[]{:S(2)}, u32[]{:S(2)}) collective-permute-start(f32[520,128]{1,0:T(8,128)S(1)} %get-tuple-element.58.refs_1_), channel_id=1, source_target_pairs={{0,4},{1,5},{4,8},{5,9},{8,12},{9,13},{12,14},{13,15},{14,10},{15,... | collective-permute-start | bytes 798728 | tf_op jit(solution)/shard_map/ppermute | solution.py:503
  5.0 2.9 %target_operand.2.refs_2_.refs_3_.refs_5_ = bf16[32,128,256]{2,1,0:T(8,128)(2,1)S(1)} custom-call(f32[32,128,128]{2,1,0:T(8,128)} %emb_ref.1), custom_call_target="tpu_custom_call" | custom-call | tf_op jit(solution)/shard_map/target_operand/pallas_call | solution.py:90
  8.0 2.1 %collective-permute-start.3 = (f32[520,128]{1,0:T(8,128)S(1)}, f32[520,128]{1,0:T(8,128)S(1)}, u32[]{:S(2)}, u32[]{:S(2)}) collective-permute-start(f32[520,128]{1,0:T(8,128)S(1)} %get-tuple-element.57.refs_2_), channel_id=1, source_target_pairs={{0,4},{1,5},{4,8},{5,9},{8,12},{9,13},{12,14},{13,15},{14,10},{15,... | collective-permute-start | bytes 798728 | tf_op jit(solution)/shard_map/ppermute | solution.py:503
  10.1 2.1 %target_operand.3.refs_4_.refs_6_ = bf16[32,128,256]{2,1,0:T(8,128)(2,1)S(1)} custom-call(f32[32,128,128]{2,1,0:T(8,128)S(1)} %collective-permute-done.2.emb_ref), custom_call_target="tpu_custom_call" | custom-call | tf_op jit(solution)/shard_map/target_operand/pallas_call | solution.py:90
  12.2 2.0 %collective-permute-done.5.refs_4_ = f32[520,128]{1,0:T(8,128)S(1)} collective-permute-done((f32[520,128]{1,0:T(8,128)S(1)}, f32[520,128]{1,0:T(8,128)S(1)}, u32[]{:S(2)}, u32[]{:S(2)}) %collective-permute-start.5) | collective-permute-done | bytes 266272 | tf_op jit(solution)/shard_map/ppermute | solution.py:503
  14.3 1.6 %collective-permute-start.6 = (f32[520,128]{1,0:T(8,128)S(1)}, f32[520,128]{1,0:T(8,128)S(1)}, u32[]{:S(2)}, u32[]{:S(2)}) collective-permute-start(f32[520,128]{1,0:T(8,128)S(1)} %collective-permute-done.refs_1_), channel_id=1, source_target_pairs={{0,4},{1,5},{4,8},{5,9},{8,12},{9,13},{12,14},{13,15},{14,10},{15,... | collective-permute-start | bytes 798728 | tf_op jit(solution)/shard_map/ppermute | solution.py:503
  15.9 0.4 collective-permute-start.9
  16.3 1.5 %collective-permute-start.1 = (f32[1040,128]{1,0:T(8,128)S(1)}, f32[1040,128]{1,0:T(8,128)S(1)}, u32[]{:S(2)}, u32[]{:S(2)}) collective-permute-start(f32[1040,128]{1,0:T(8,128)S(1)} %get-tuple-element.53), channel_id=1, source_target_pairs={{0,16},{16,0},{1,17},{17,1},{2,18},{18,2},{3,19},{19,3},{4,20},{20... | collective-permute-start | bytes 1597448 | tf_op jit(solution)/shard_map/ppermute | solution.py:509
  17.8 1.7 %build_tiles.7 = (bf16[10,128,256]{2,1,0:T(8,128)(2,1)S(1)}, s32[21]{0:T(128)S(4)}, f32[64,128]{1,0:T(8,128)S(1)}, f32[64,128]{1,0:T(8,128)S(1)}, bf16[10,128,256]{2,1,0:T(8,128)(2,1)S(1)}) custom-call(s32[1]{0:T(128)} %bitcast.device.refs_0_, f32[520,128]{1,0:T(8,128)S(1)} %get-tuple-element.58.refs_1_, f32[520,128]{1,0:T(8,128)S(1)} %get-tuple-element.57.refs_2_, ...), custom_call_target="tpu_custom_call" | custom-call | tf_op jit(solution)/shard_map/build_tiles/pallas_call | solution.py:327
  19.5 0.5 collective-permute-done.4.refs_3_
  20.0 1.6 %collective-permute-start.7 = (f32[520,128]{1,0:T(8,128)S(1)}, f32[520,128]{1,0:T(8,128)S(1)}, u32[]{:S(2)}, u32[]{:S(2)}) collective-permute-start(f32[520,128]{1,0:T(8,128)S(1)} %collective-permute-done.3.refs_2_), channel_id=1, source_target_pairs={{0,4},{1,5},{4,8},{5,9},{8,12},{9,13},{12,14},{13,15},{14,10},{15,... | collective-permute-start | bytes 798728 | tf_op jit(solution)/shard_map/ppermute | solution.py:503
  21.6 0.4 collective-permute-start.8
  22.0 2.5 %build_tiles.8 = (bf16[20,128,256]{2,1,0:T(8,128)(2,1)S(1)}, s32[41]{0:T(128)S(4)}, f32[64,128]{1,0:T(8,128)S(1)}, f32[64,128]{1,0:T(8,128)S(1)}, bf16[20,128,256]{2,1,0:T(8,128)(2,1)S(1)}) custom-call(s32[1]{0:T(128)} %bitcast.device.refs_0_, f32[520,128]{1,0:T(8,128)S(1)} %collective-permute-done.refs_1_, f32[520,128]{1,0:T(8,128)S(1)} %collective-permute-done.3.refs_2_, ...), custom_call_target="tpu_custom_call" | custom-call | tf_op jit(solution)/shard_map/build_tiles/pallas_call | solution.py:327
  24.5 1.1 %collective-permute-done.9.refs_4_ = f32[520,128]{1,0:T(8,128)S(1)} collective-permute-done((f32[520,128]{1,0:T(8,128)S(1)}, f32[520,128]{1,0:T(8,128)S(1)}, u32[]{:S(2)}, u32[]{:S(2)}) %collective-permute-start.9) | collective-permute-done | bytes 266272 | tf_op jit(solution)/shard_map/ppermute | solution.py:503
  25.7 1.6 %collective-permute-start.10 = (f32[520,128]{1,0:T(8,128)S(1)}, f32[520,128]{1,0:T(8,128)S(1)}, u32[]{:S(2)}, u32[]{:S(2)}) collective-permute-start(f32[520,128]{1,0:T(8,128)S(1)} %collective-permute-done.6.refs_1_), channel_id=1, source_target_pairs={{0,4},{1,5},{4,8},{5,9},{8,12},{9,13},{12,14},{13,15},{14,10},{15,... | collective-permute-start | bytes 798728 | tf_op jit(solution)/shard_map/ppermute | solution.py:503
  27.3 0.4 collective-permute-start.13
  27.7 1.6 %collective-permute-done.7.refs_2_ = f32[520,128]{1,0:T(8,128)S(1)} collective-permute-done((f32[520,128]{1,0:T(8,128)S(1)}, f32[520,128]{1,0:T(8,128)S(1)}, u32[]{:S(2)}, u32[]{:S(2)}) %collective-permute-start.7) | collective-permute-done | bytes 266272 | tf_op jit(solution)/shard_map/ppermute | solution.py:503
  29.3 2.0 %collective-permute-start.11 = (f32[520,128]{1,0:T(8,128)S(1)}, f32[520,128]{1,0:T(8,128)S(1)}, u32[]{:S(2)}, u32[]{:S(2)}) collective-permute-start(f32[520,128]{1,0:T(8,128)S(1)} %collective-permute-done.7.refs_2_), channel_id=1, source_target_pairs={{0,4},{1,5},{4,8},{5,9},{8,12},{9,13},{12,14},{13,15},{14,10},{15,... | collective-permute-start | bytes 798728 | tf_op jit(solution)/shard_map/ppermute | solution.py:503
  31.4 2.5 %build_tiles.9 = (bf16[20,128,256]{2,1,0:T(8,128)(2,1)S(1)}, s32[41]{0:T(128)S(4)}, f32[64,128]{1,0:T(8,128)S(1)}, f32[64,128]{1,0:T(8,128)S(1)}, bf16[20,128,256]{2,1,0:T(8,128)(2,1)S(1)}) custom-call(s32[1]{0:T(128)} %bitcast.device.refs_0_, f32[520,128]{1,0:T(8,128)S(1)} %collective-permute-done.6.refs_1_, f32[520,128]{1,0:T(8,128)S(1)} %collective-permute-done.7.refs_2_, ...), custom_call_target="tpu_custom_call" | custom-call | tf_op jit(solution)/shard_map/build_tiles/pallas_call | solution.py:327
  33.9 1.1 %collective-permute-done.10.refs_1_ = f32[520,128]{1,0:T(8,128)S(1)} collective-permute-done((f32[520,128]{1,0:T(8,128)S(1)}, f32[520,128]{1,0:T(8,128)S(1)}, u32[]{:S(2)}, u32[]{:S(2)}) %collective-permute-start.10) | collective-permute-done | bytes 266272 | tf_op jit(solution)/shard_map/ppermute | solution.py:503
  35.0 2.1 %collective-permute-done.13.refs_4_ = f32[520,128]{1,0:T(8,128)S(1)} collective-permute-done((f32[520,128]{1,0:T(8,128)S(1)}, f32[520,128]{1,0:T(8,128)S(1)}, u32[]{:S(2)}, u32[]{:S(2)}) %collective-permute-start.13) | collective-permute-done | bytes 266272 | tf_op jit(solution)/shard_map/ppermute | solution.py:503
  37.1 1.6 %collective-permute-start.14 = (f32[520,128]{1,0:T(8,128)S(1)}, f32[520,128]{1,0:T(8,128)S(1)}, u32[]{:S(2)}, u32[]{:S(2)}) collective-permute-start(f32[520,128]{1,0:T(8,128)S(1)} %collective-permute-done.10.refs_1_), channel_id=1, source_target_pairs={{0,4},{1,5},{4,8},{5,9},{8,12},{9,13},{12,14},{13,15},{14,10},{15,... | collective-permute-start | bytes 798728 | tf_op jit(solution)/shard_map/ppermute | solution.py:503
  38.7 0.4 collective-permute-start.15
  39.1 1.3 %build_tiles.6 = (bf16[8,128,256]{2,1,0:T(8,128)(2,1)S(1)}, s32[8]{0:T(128)S(4)}, f32[8,128]{1,0:T(8,128)S(1)}, f32[8,128]{1,0:T(8,128)S(1)}) custom-call(s32[1]{0:T(128)} %bitcast.device.refs_0_, f32[1040,128]{1,0:T(8,128)S(1)} %collective-permute-done.1.refs_1_, bf16[32,128,256]{2,1,0:T(8,128)(2,1)S(1)} %target_operand.2.refs_2_.refs_3_.refs_5_), custom_call_target="tpu_custom_call" | custom-call | tf_op jit(solution)/shard_map/build_tiles/pallas_call | solution.py:327
  40.5 1.6 %collective-permute-start.16 = (f32[8,128]{1,0:T(8,128)S(1)}, f32[8,128]{1,0:T(8,128)S(1)}, u32[]{:S(2)}, u32[]{:S(2)}) collective-permute-start(f32[8,128]{1,0:T(8,128)S(1)} %get-tuple-element.79), channel_id=1, source_target_pairs={{0,16},{16,0},{1,17},{17,1},{2,18},{18,2},{3,19},{19,3},{4,20},{20... | collective-permute-start | bytes 12296 | tf_op jit(solution)/shard_map/ppermute | solution.py:509
  42.1 0.7 collective-permute-done.12.refs_3_
  42.8 2.5 %build_tiles.10 = (bf16[20,128,256]{2,1,0:T(8,128)(2,1)S(1)}, s32[41]{0:T(128)S(4)}, f32[64,128]{1,0:T(8,128)S(1)}, f32[64,128]{1,0:T(8,128)S(1)}, bf16[20,128,256]{2,1,0:T(8,128)(2,1)S(1)}) custom-call(s32[1]{0:T(128)} %bitcast.device.refs_0_, f32[520,128]{1,0:T(8,128)S(1)} %collective-permute-done.10.refs_1_, ...), custom_call_target="tpu_custom_call" | custom-call | tf_op jit(solution)/shard_map/build_tiles/pallas_call | solution.py:327
  45.3 0.9 %collective-permute-done.14.upper.refs_1_ = f32[520,128]{1,0:T(8,128)S(1)} collective-permute-done((f32[520,128]{1,0:T(8,128)S(1)}, f32[520,128]{1,0:T(8,128)S(1)}, u32[]{:S(2)}, u32[]{:S(2)}) %collective-permute-start.14) | collective-permute-done | bytes 266272 | tf_op jit(solution)/shard_map/ppermute | solution.py:503
  46.2 0.9 %plan_tiles.1 = (s32[21]{0:T(128)S(4)}, s32[11]{0:T(128)S(4)}) custom-call(s32[1]{0:T(128)} %bitcast.device.refs_0_, f32[520,128]{1,0:T(8,128)S(1)} %collective-permute-done.14.upper.refs_1_), custom_call_target="tpu_custom_call" | custom-call | tf_op jit(solution)/shard_map/plan_tiles/pallas_call | solution.py:279
  47.1 0.6 collective-permute-done.15.refs_2_
  47.8 0.8 build_tiles.11
  48.6 2.6 %collective-permute-start.17 = (f32[64,128]{1,0:T(8,128)S(1)}, f32[64,128]{1,0:T(8,128)S(1)}, u32[]{:S(2)}, u32[]{:S(2)}) collective-permute-start(f32[64,128]{1,0:T(8,128)S(1)} %get-tuple-element.81), channel_id=1, source_target_pairs={{0,8},{1,9},{2,10},{3,11},{4,12},{5,13},{6,14},{7,15},{8,0},{9,1},... | collective-permute-start | bytes 98312 | tf_op jit(solution)/shard_map/ppermute | solution.py:506
  51.2 2.2 %collective-permute-done.17 = f32[64,128]{1,0:T(8,128)S(1)} collective-permute-done((f32[64,128]{1,0:T(8,128)S(1)}, f32[64,128]{1,0:T(8,128)S(1)}, u32[]{:S(2)}, u32[]{:S(2)}) %collective-permute-start.17) | collective-permute-done | bytes 32800 | tf_op jit(solution)/shard_map/ppermute | solution.py:506
  53.4 2.1 %collective-permute-start.18 = (f32[64,128]{1,0:T(8,128)S(1)}, f32[64,128]{1,0:T(8,128)S(1)}, u32[]{:S(2)}, u32[]{:S(2)}) collective-permute-start(f32[64,128]{1,0:T(8,128)S(1)} %add.6.refs_0_), channel_id=1, source_target_pairs={{0,6},{1,7},{2,4},{3,5},{4,2},{5,3},{6,0},{7,1},{8,14},{9,15},{10,... | collective-permute-start | bytes 98312 | tf_op jit(solution)/shard_map/ppermute | solution.py:506
  55.6 0.6 collective-permute-start.19
  56.1 0.8 collective-permute-start.20
  56.9 1.3 %collective-permute-done.18.refs_1_ = f32[64,128]{1,0:T(8,128)S(1)} collective-permute-done((f32[64,128]{1,0:T(8,128)S(1)}, f32[64,128]{1,0:T(8,128)S(1)}, u32[]{:S(2)}, u32[]{:S(2)}) %collective-permute-start.18) | collective-permute-done | bytes 32800 | tf_op jit(solution)/shard_map/ppermute | solution.py:506
  58.3 1.2 %collective-permute-done.19.refs_2_ = f32[64,128]{1,0:T(8,128)S(1)} collective-permute-done((f32[64,128]{1,0:T(8,128)S(1)}, f32[64,128]{1,0:T(8,128)S(1)}, u32[]{:S(2)}, u32[]{:S(2)}) %collective-permute-start.19) | collective-permute-done | bytes 32800 | tf_op jit(solution)/shard_map/ppermute | solution.py:506
  59.5 0.6 collective-permute-done.20.refs_3_
  60.1 1.6 %collective-permute-start.21 = (f32[64,128]{1,0:T(8,128)S(1)}, f32[64,128]{1,0:T(8,128)S(1)}, u32[]{:S(2)}, u32[]{:S(2)}) collective-permute-start(f32[64,128]{1,0:T(8,128)S(1)} %add_all.2.refs_5_), channel_id=1, source_target_pairs={{0,16},{16,0},{1,17},{17,1},{2,18},{18,2},{3,19},{19,3},{4,20},{20... | collective-permute-start | bytes 98312 | tf_op jit(solution)/shard_map/ppermute | solution.py:509
  61.7 0.9 %column_sums.2 = (f32[32,128]{1,0:T(8,128)S(1)}, f32[32,128]{1,0:T(8,128)S(1)}) custom-call(s32[21]{0:T(128)S(4)} %get-tuple-element.56.refs_0_, s32[41]{0:T(128)S(4)} %get-tuple-element.61.refs_1_, s32[41]{0:T(128)S(4)} %get-tuple-element.68.refs_2_, s32[41]{0:T(128)S(4)} %get-tuple-element.73.refs_3_, s32[21]{0:T(128)S(4)} %get-tuple-element.75.refs_8_.refs_4_, ...), custom_call_target="tpu_custom_call" | custom-call | tf_op jit(solution)/shard_map/column_sums/pallas_call | solution.py:396
  62.6 0.1 collective-permute-start.22
  62.6 1.2 %collective-permute-done.22.refs_5_ = f32[32,128]{1,0:T(8,128)S(1)} collective-permute-done((f32[32,128]{1,0:T(8,128)S(1)}, f32[32,128]{1,0:T(8,128)S(1)}, u32[]{:S(2)}, u32[]{:S(2)}) %collective-permute-start.22) | collective-permute-done | bytes 16416 | tf_op jit(solution)/shard_map/ppermute | solution.py:506
  63.8 0.2 collective-permute-done.21.refs_2_
  64.0 0.4 closing.2
  64.5 0.1 collective-permute-start.23
  64.6 1.6 %collective-permute-start.24 = (f32[8,128]{1,0:T(8,128)S(1)}, f32[8,128]{1,0:T(8,128)S(1)}, u32[]{:S(2)}, u32[]{:S(2)}) collective-permute-start(f32[8,128]{1,0:T(8,128)S(1)} %get-tuple-element.97), channel_id=1, source_target_pairs={{0,16},{16,0},{1,17},{17,1},{2,18},{18,2},{3,19},{19,3},{4,20},{20... | collective-permute-start | bytes 12296 | tf_op jit(solution)/shard_map/ppermute | solution.py:509
  66.2 1.0 %row_sums.1.rows = f32[64,128]{1,0:T(8,128)S(1)} custom-call(s32[21]{0:T(128)S(4)} %get-tuple-element.56.refs_0_, s32[41]{0:T(128)S(4)} %get-tuple-element.61.refs_1_, s32[41]{0:T(128)S(4)} %get-tuple-element.68.refs_2_, s32[41]{0:T(128)S(4)} %get-tuple-element.73.refs_3_, s32[21]{0:T(128)S(4)} %get-tuple-element.75.refs_8_.refs_4_, ...), custom_call_target="tpu_custom_call" | custom-call | tf_op jit(solution)/shard_map/row_sums/pallas_call | solution.py:475
  67.1 1.1 %collective-permute-done.24.part = f32[8,128]{1,0:T(8,128)S(1)} collective-permute-done((f32[8,128]{1,0:T(8,128)S(1)}, f32[8,128]{1,0:T(8,128)S(1)}, u32[]{:S(2)}, u32[]{:S(2)}) %collective-permute-start.24) | collective-permute-done | bytes 4128 | tf_op jit(solution)/shard_map/ppermute | solution.py:509
  68.3 2.5 %collective-permute-start.25 = (f32[64,128]{1,0:T(8,128)S(1)}, f32[64,128]{1,0:T(8,128)S(1)}, u32[]{:S(2)}, u32[]{:S(2)}) collective-permute-start(f32[64,128]{1,0:T(8,128)S(1)} %add_own.1), channel_id=1, source_target_pairs={{0,8},{1,9},{2,10},{3,11},{4,12},{5,13},{6,14},{7,15},{8,0},{9,1},... | collective-permute-start | bytes 98312 | tf_op jit(solution)/shard_map/ppermute | solution.py:506
  70.8 2.3 %collective-permute-done.25 = f32[64,128]{1,0:T(8,128)S(1)} collective-permute-done((f32[64,128]{1,0:T(8,128)S(1)}, f32[64,128]{1,0:T(8,128)S(1)}, u32[]{:S(2)}, u32[]{:S(2)}) %collective-permute-start.25) | collective-permute-done | bytes 32800 | tf_op jit(solution)/shard_map/ppermute | solution.py:506
  73.1 1.8 %collective-permute-start.26 = (f32[64,128]{1,0:T(8,128)S(1)}, f32[64,128]{1,0:T(8,128)S(1)}, u32[]{:S(2)}, u32[]{:S(2)}) collective-permute-start(f32[64,128]{1,0:T(8,128)S(1)} %add.7.refs_0_), channel_id=1, source_target_pairs={{0,6},{1,7},{2,4},{3,5},{4,2},{5,3},{6,0},{7,1},{8,14},{9,15},{10,... | collective-permute-start | bytes 98312 | tf_op jit(solution)/shard_map/ppermute | solution.py:506
  74.9 0.4 collective-permute-start.27
  75.3 1.2 %collective-permute-start.28 = (f32[64,128]{1,0:T(8,128)S(1)}, f32[64,128]{1,0:T(8,128)S(1)}, u32[]{:S(2)}, u32[]{:S(2)}) collective-permute-start(f32[64,128]{1,0:T(8,128)S(1)} %add.7.refs_0_), channel_id=1, source_target_pairs={{0,2},{1,3},{2,0},{3,1},{4,6},{5,7},{6,4},{7,5},{8,10},{9,11},{10,... | collective-permute-start | bytes 98312 | tf_op jit(solution)/shard_map/ppermute | solution.py:506
  76.6 1.3 %collective-permute-done.26.refs_1_ = f32[64,128]{1,0:T(8,128)S(1)} collective-permute-done((f32[64,128]{1,0:T(8,128)S(1)}, f32[64,128]{1,0:T(8,128)S(1)}, u32[]{:S(2)}, u32[]{:S(2)}) %collective-permute-start.26) | collective-permute-done | bytes 32800 | tf_op jit(solution)/shard_map/ppermute | solution.py:506
  77.9 0.9 %collective-permute-done.27.refs_2_ = f32[64,128]{1,0:T(8,128)S(1)} collective-permute-done((f32[64,128]{1,0:T(8,128)S(1)}, f32[64,128]{1,0:T(8,128)S(1)}, u32[]{:S(2)}, u32[]{:S(2)}) %collective-permute-start.27) | collective-permute-done | bytes 32800 | tf_op jit(solution)/shard_map/ppermute | solution.py:506
  78.8 0.4 collective-permute-done.28.refs_3_
  79.3 1.6 %collective-permute-start.29 = (f32[64,128]{1,0:T(8,128)S(1)}, f32[64,128]{1,0:T(8,128)S(1)}, u32[]{:S(2)}, u32[]{:S(2)}) collective-permute-start(f32[64,128]{1,0:T(8,128)S(1)} %add_all.3.refs_5_.refs_8_), channel_id=1, source_target_pairs={{0,16},{16,0},{1,17},{17,1},{2,18},{18,2},{3,19},{19,3},{4,20},{20... | collective-permute-start | bytes 98312 | tf_op jit(solution)/shard_map/ppermute | solution.py:509
  80.9 0.9 %column_sums.3 = (f32[32,128]{1,0:T(8,128)S(1)}, f32[32,128]{1,0:T(8,128)S(1)}) custom-call(s32[21]{0:T(128)S(4)} %get-tuple-element.56.refs_0_, s32[41]{0:T(128)S(4)} %get-tuple-element.61.refs_1_, s32[41]{0:T(128)S(4)} %get-tuple-element.68.refs_2_, s32[41]{0:T(128)S(4)} %get-tuple-element.73.refs_3_, s32[21]{0:T(128)S(4)} %get-tuple-element.75.refs_8_.refs_4_, ...), custom_call_target="tpu_custom_call" | custom-call | tf_op jit(solution)/shard_map/column_sums/pallas_call | solution.py:396
  81.8 1.2 %collective-permute-done.30.refs_5_ = f32[32,128]{1,0:T(8,128)S(1)} collective-permute-done((f32[32,128]{1,0:T(8,128)S(1)}, f32[32,128]{1,0:T(8,128)S(1)}, u32[]{:S(2)}, u32[]{:S(2)}) %collective-permute-start.30) | collective-permute-done | bytes 16416 | tf_op jit(solution)/shard_map/ppermute | solution.py:506
  83.0 0.2 collective-permute-done.29.refs_2_
  83.3 0.8 closing.3
  (22 shorter events, 0.2 us)
Async XLA Ops:
  0.6 9.5 %collective-permute-start.2 = (f32[32,128,128]{2,1,0:T(8,128)}, f32[32,128,128]{2,1,0:T(8,128)S(1)}, u32[]{:S(2)}, u32[]{:S(2)}) collective-permute-start(f32[32,128,128]{2,1,0:T(8,128)} %emb_ref.1), channel_id=1, source_target_pairs={{0,1},{1,0},{2,3},{3,2},{4,5},{5,4},{6,7},{7,6},{8,9},{9,8},{10,11... | collective-permute-start | bytes 6291464 | tf_op jit(solution)/shard_map/ppermute | solution.py:506
  2.4 9.8 %collective-permute-start = (f32[520,128]{1,0:T(8,128)S(1)}, f32[520,128]{1,0:T(8,128)S(1)}, u32[]{:S(2)}, u32[]{:S(2)}) collective-permute-start(f32[520,128]{1,0:T(8,128)S(1)} %get-tuple-element.58.refs_1_), channel_id=1, source_target_pairs={{0,4},{1,5},{4,8},{5,9},{8,12},{9,13},{12,14},{13,15},{14,10},{15,... | collective-permute-start | bytes 798728 | tf_op jit(solution)/shard_map/ppermute | solution.py:503
  5.0 9.2 %collective-permute-start.5 = (f32[520,128]{1,0:T(8,128)S(1)}, f32[520,128]{1,0:T(8,128)S(1)}, u32[]{:S(2)}, u32[]{:S(2)}) collective-permute-start(f32[520,128]{1,0:T(8,128)S(1)} %get-tuple-element.57.refs_2_), channel_id=1, source_target_pairs={{0,2},{1,3},{4,0},{5,1},{8,4},{9,5},{12,8},{13,9},{14,12},{15,13},... | collective-permute-start | bytes 798728 | tf_op jit(solution)/shard_map/ppermute | solution.py:503
  8.0 11.5 %collective-permute-start.3 = (f32[520,128]{1,0:T(8,128)S(1)}, f32[520,128]{1,0:T(8,128)S(1)}, u32[]{:S(2)}, u32[]{:S(2)}) collective-permute-start(f32[520,128]{1,0:T(8,128)S(1)} %get-tuple-element.57.refs_2_), channel_id=1, source_target_pairs={{0,4},{1,5},{4,8},{5,9},{8,12},{9,13},{12,14},{13,15},{14,10},{15,... | collective-permute-start | bytes 798728 | tf_op jit(solution)/shard_map/ppermute | solution.py:503
  10.1 9.9 %collective-permute-start.4 = (f32[520,128]{1,0:T(8,128)S(1)}, f32[520,128]{1,0:T(8,128)S(1)}, u32[]{:S(2)}, u32[]{:S(2)}) collective-permute-start(f32[520,128]{1,0:T(8,128)S(1)} %get-tuple-element.58.refs_1_), channel_id=1, source_target_pairs={{0,2},{1,3},{4,0},{5,1},{8,4},{9,5},{12,8},{13,9},{14,12},{15,13},... | collective-permute-start | bytes 798728 | tf_op jit(solution)/shard_map/ppermute | solution.py:503
  14.3 10.3 %collective-permute-start.6 = (f32[520,128]{1,0:T(8,128)S(1)}, f32[520,128]{1,0:T(8,128)S(1)}, u32[]{:S(2)}, u32[]{:S(2)}) collective-permute-start(f32[520,128]{1,0:T(8,128)S(1)} %collective-permute-done.refs_1_), channel_id=1, source_target_pairs={{0,4},{1,5},{4,8},{5,9},{8,12},{9,13},{12,14},{13,15},{14,10},{15,... | collective-permute-start | bytes 798728 | tf_op jit(solution)/shard_map/ppermute | solution.py:503
  15.9 9.8 %collective-permute-start.9 = (f32[520,128]{1,0:T(8,128)S(1)}, f32[520,128]{1,0:T(8,128)S(1)}, u32[]{:S(2)}, u32[]{:S(2)}) collective-permute-start(f32[520,128]{1,0:T(8,128)S(1)} %collective-permute-done.5.refs_4_), channel_id=1, source_target_pairs={{0,2},{1,3},{4,0},{5,1},{8,4},{9,5},{12,8},{13,9},{14,12},{15,13},... | collective-permute-start | bytes 798728 | tf_op jit(solution)/shard_map/ppermute | solution.py:503
  16.3 22.8 %collective-permute-start.1 = (f32[1040,128]{1,0:T(8,128)S(1)}, f32[1040,128]{1,0:T(8,128)S(1)}, u32[]{:S(2)}, u32[]{:S(2)}) collective-permute-start(f32[1040,128]{1,0:T(8,128)S(1)} %get-tuple-element.53), channel_id=1, source_target_pairs={{0,16},{16,0},{1,17},{17,1},{2,18},{18,2},{3,19},{19,3},{4,20},{20... | collective-permute-start | bytes 1597448 | tf_op jit(solution)/shard_map/ppermute | solution.py:509
  20.0 9.3 %collective-permute-start.7 = (f32[520,128]{1,0:T(8,128)S(1)}, f32[520,128]{1,0:T(8,128)S(1)}, u32[]{:S(2)}, u32[]{:S(2)}) collective-permute-start(f32[520,128]{1,0:T(8,128)S(1)} %collective-permute-done.3.refs_2_), channel_id=1, source_target_pairs={{0,4},{1,5},{4,8},{5,9},{8,12},{9,13},{12,14},{13,15},{14,10},{15,... | collective-permute-start | bytes 798728 | tf_op jit(solution)/shard_map/ppermute | solution.py:503
  21.6 9.8 %collective-permute-start.8 = (f32[520,128]{1,0:T(8,128)S(1)}, f32[520,128]{1,0:T(8,128)S(1)}, u32[]{:S(2)}, u32[]{:S(2)}) collective-permute-start(f32[520,128]{1,0:T(8,128)S(1)} %collective-permute-done.4.refs_3_), channel_id=1, source_target_pairs={{0,2},{1,3},{4,0},{5,1},{8,4},{9,5},{12,8},{13,9},{14,12},{15,13},... | collective-permute-start | bytes 798728 | tf_op jit(solution)/shard_map/ppermute | solution.py:503
  25.7 9.3 %collective-permute-start.10 = (f32[520,128]{1,0:T(8,128)S(1)}, f32[520,128]{1,0:T(8,128)S(1)}, u32[]{:S(2)}, u32[]{:S(2)}) collective-permute-start(f32[520,128]{1,0:T(8,128)S(1)} %collective-permute-done.6.refs_1_), channel_id=1, source_target_pairs={{0,4},{1,5},{4,8},{5,9},{8,12},{9,13},{12,14},{13,15},{14,10},{15,... | collective-permute-start | bytes 798728 | tf_op jit(solution)/shard_map/ppermute | solution.py:503
  27.3 9.8 %collective-permute-start.13 = (f32[520,128]{1,0:T(8,128)S(1)}, f32[520,128]{1,0:T(8,128)S(1)}, u32[]{:S(2)}, u32[]{:S(2)}) collective-permute-start(f32[520,128]{1,0:T(8,128)S(1)} %collective-permute-done.9.refs_4_), channel_id=1, source_target_pairs={{0,2},{1,3},{4,0},{5,1},{8,4},{9,5},{12,8},{13,9},{14,12},{15,13},... | collective-permute-start | bytes 798728 | tf_op jit(solution)/shard_map/ppermute | solution.py:503
  29.3 12.7 %collective-permute-start.11 = (f32[520,128]{1,0:T(8,128)S(1)}, f32[520,128]{1,0:T(8,128)S(1)}, u32[]{:S(2)}, u32[]{:S(2)}) collective-permute-start(f32[520,128]{1,0:T(8,128)S(1)} %collective-permute-done.7.refs_2_), channel_id=1, source_target_pairs={{0,4},{1,5},{4,8},{5,9},{8,12},{9,13},{12,14},{13,15},{14,10},{15,... | collective-permute-start | bytes 798728 | tf_op jit(solution)/shard_map/ppermute | solution.py:503
  31.4 11.4 %collective-permute-start.12 = (f32[520,128]{1,0:T(8,128)S(1)}, f32[520,128]{1,0:T(8,128)S(1)}, u32[]{:S(2)}, u32[]{:S(2)}) collective-permute-start(f32[520,128]{1,0:T(8,128)S(1)} %collective-permute-done.8.refs_3_), channel_id=1, source_target_pairs={{0,2},{1,3},{4,0},{5,1},{8,4},{9,5},{12,8},{13,9},{14,12},{15,13},... | collective-permute-start | bytes 798728 | tf_op jit(solution)/shard_map/ppermute | solution.py:503
  37.1 9.1 %collective-permute-start.14 = (f32[520,128]{1,0:T(8,128)S(1)}, f32[520,128]{1,0:T(8,128)S(1)}, u32[]{:S(2)}, u32[]{:S(2)}) collective-permute-start(f32[520,128]{1,0:T(8,128)S(1)} %collective-permute-done.10.refs_1_), channel_id=1, source_target_pairs={{0,4},{1,5},{4,8},{5,9},{8,12},{9,13},{12,14},{13,15},{14,10},{15,... | collective-permute-start | bytes 798728 | tf_op jit(solution)/shard_map/ppermute | solution.py:503
  38.7 9.1 %collective-permute-start.15 = (f32[520,128]{1,0:T(8,128)S(1)}, f32[520,128]{1,0:T(8,128)S(1)}, u32[]{:S(2)}, u32[]{:S(2)}) collective-permute-start(f32[520,128]{1,0:T(8,128)S(1)} %collective-permute-done.13.refs_4_), channel_id=1, source_target_pairs={{0,2},{1,3},{4,0},{5,1},{8,4},{9,5},{12,8},{13,9},{14,12},{15,13},... | collective-permute-start | bytes 798728 | tf_op jit(solution)/shard_map/ppermute | solution.py:503
  40.5 6.7 %collective-permute-start.16 = (f32[8,128]{1,0:T(8,128)S(1)}, f32[8,128]{1,0:T(8,128)S(1)}, u32[]{:S(2)}, u32[]{:S(2)}) collective-permute-start(f32[8,128]{1,0:T(8,128)S(1)} %get-tuple-element.79), channel_id=1, source_target_pairs={{0,16},{16,0},{1,17},{17,1},{2,18},{18,2},{3,19},{19,3},{4,20},{20... | collective-permute-start | bytes 12296 | tf_op jit(solution)/shard_map/ppermute | solution.py:509
  48.6 4.8 %collective-permute-start.17 = (f32[64,128]{1,0:T(8,128)S(1)}, f32[64,128]{1,0:T(8,128)S(1)}, u32[]{:S(2)}, u32[]{:S(2)}) collective-permute-start(f32[64,128]{1,0:T(8,128)S(1)} %get-tuple-element.81), channel_id=1, source_target_pairs={{0,8},{1,9},{2,10},{3,11},{4,12},{5,13},{6,14},{7,15},{8,0},{9,1},... | collective-permute-start | bytes 98312 | tf_op jit(solution)/shard_map/ppermute | solution.py:506
  53.4 4.8 %collective-permute-start.18 = (f32[64,128]{1,0:T(8,128)S(1)}, f32[64,128]{1,0:T(8,128)S(1)}, u32[]{:S(2)}, u32[]{:S(2)}) collective-permute-start(f32[64,128]{1,0:T(8,128)S(1)} %add.6.refs_0_), channel_id=1, source_target_pairs={{0,6},{1,7},{2,4},{3,5},{4,2},{5,3},{6,0},{7,1},{8,14},{9,15},{10,... | collective-permute-start | bytes 98312 | tf_op jit(solution)/shard_map/ppermute | solution.py:506
  55.6 3.9 %collective-permute-start.19 = (f32[64,128]{1,0:T(8,128)S(1)}, f32[64,128]{1,0:T(8,128)S(1)}, u32[]{:S(2)}, u32[]{:S(2)}) collective-permute-start(f32[64,128]{1,0:T(8,128)S(1)} %add.6.refs_0_), channel_id=1, source_target_pairs={{0,4},{1,5},{2,6},{3,7},{4,0},{5,1},{6,2},{7,3},{8,12},{9,13},{10,... | collective-permute-start | bytes 98312 | tf_op jit(solution)/shard_map/ppermute | solution.py:506
  56.1 3.9 %collective-permute-start.20 = (f32[64,128]{1,0:T(8,128)S(1)}, f32[64,128]{1,0:T(8,128)S(1)}, u32[]{:S(2)}, u32[]{:S(2)}) collective-permute-start(f32[64,128]{1,0:T(8,128)S(1)} %add.6.refs_0_), channel_id=1, source_target_pairs={{0,2},{1,3},{2,0},{3,1},{4,6},{5,7},{6,4},{7,5},{8,10},{9,11},{10,... | collective-permute-start | bytes 98312 | tf_op jit(solution)/shard_map/ppermute | solution.py:506
  60.1 4.0 %collective-permute-start.21 = (f32[64,128]{1,0:T(8,128)S(1)}, f32[64,128]{1,0:T(8,128)S(1)}, u32[]{:S(2)}, u32[]{:S(2)}) collective-permute-start(f32[64,128]{1,0:T(8,128)S(1)} %add_all.2.refs_5_), channel_id=1, source_target_pairs={{0,16},{16,0},{1,17},{17,1},{2,18},{18,2},{3,19},{19,3},{4,20},{20... | collective-permute-start | bytes 98312 | tf_op jit(solution)/shard_map/ppermute | solution.py:509
  61.7 2.4 %copy-start = (f32[32,128]{1,0:T(8,128)S(1)}, f32[32,128]{1,0:T(8,128)}, u32[]{:S(2)}) copy-start(f32[32,128]{1,0:T(8,128)} %refs_6_.3) | copy-start | bytes 49156
  62.6 1.2 %collective-permute-start.22 = (f32[32,128]{1,0:T(8,128)S(1)}, f32[32,128]{1,0:T(8,128)S(1)}, u32[]{:S(2)}, u32[]{:S(2)}) collective-permute-start(f32[32,128]{1,0:T(8,128)S(1)} %get-tuple-element.90), channel_id=1, source_target_pairs={{0,1},{1,0},{2,3},{3,2},{4,5},{5,4},{6,7},{7,6},{8,9},{9,8},{10,11... | collective-permute-start | bytes 49160 | tf_op jit(solution)/shard_map/ppermute | solution.py:506
  64.5 1.7 %collective-permute-start.23 = (f32[32,128]{1,0:T(8,128)S(1)}, f32[32,128]{1,0:T(8,128)S(1)}, u32[]{:S(2)}, u32[]{:S(2)}) collective-permute-start(f32[32,128]{1,0:T(8,128)S(1)} %get-tuple-element.92.refs_5_), channel_id=1, source_target_pairs={{0,1},{1,0},{2,3},{3,2},{4,5},{5,4},{6,7},{7,6},{8,9},{9,8},{10,11... | collective-permute-start | bytes 49160 | tf_op jit(solution)/shard_map/ppermute | solution.py:506
  64.6 3.7 %collective-permute-start.24 = (f32[8,128]{1,0:T(8,128)S(1)}, f32[8,128]{1,0:T(8,128)S(1)}, u32[]{:S(2)}, u32[]{:S(2)}) collective-permute-start(f32[8,128]{1,0:T(8,128)S(1)} %get-tuple-element.97), channel_id=1, source_target_pairs={{0,16},{16,0},{1,17},{17,1},{2,18},{18,2},{3,19},{19,3},{4,20},{20... | collective-permute-start | bytes 12296 | tf_op jit(solution)/shard_map/ppermute | solution.py:509
  68.3 4.8 %collective-permute-start.25 = (f32[64,128]{1,0:T(8,128)S(1)}, f32[64,128]{1,0:T(8,128)S(1)}, u32[]{:S(2)}, u32[]{:S(2)}) collective-permute-start(f32[64,128]{1,0:T(8,128)S(1)} %add_own.1), channel_id=1, source_target_pairs={{0,8},{1,9},{2,10},{3,11},{4,12},{5,13},{6,14},{7,15},{8,0},{9,1},... | collective-permute-start | bytes 98312 | tf_op jit(solution)/shard_map/ppermute | solution.py:506
  73.1 4.8 %collective-permute-start.26 = (f32[64,128]{1,0:T(8,128)S(1)}, f32[64,128]{1,0:T(8,128)S(1)}, u32[]{:S(2)}, u32[]{:S(2)}) collective-permute-start(f32[64,128]{1,0:T(8,128)S(1)} %add.7.refs_0_), channel_id=1, source_target_pairs={{0,6},{1,7},{2,4},{3,5},{4,2},{5,3},{6,0},{7,1},{8,14},{9,15},{10,... | collective-permute-start | bytes 98312 | tf_op jit(solution)/shard_map/ppermute | solution.py:506
  74.9 3.9 %collective-permute-start.27 = (f32[64,128]{1,0:T(8,128)S(1)}, f32[64,128]{1,0:T(8,128)S(1)}, u32[]{:S(2)}, u32[]{:S(2)}) collective-permute-start(f32[64,128]{1,0:T(8,128)S(1)} %add.7.refs_0_), channel_id=1, source_target_pairs={{0,4},{1,5},{2,6},{3,7},{4,0},{5,1},{6,2},{7,3},{8,12},{9,13},{10,... | collective-permute-start | bytes 98312 | tf_op jit(solution)/shard_map/ppermute | solution.py:506
  75.3 3.9 %collective-permute-start.28 = (f32[64,128]{1,0:T(8,128)S(1)}, f32[64,128]{1,0:T(8,128)S(1)}, u32[]{:S(2)}, u32[]{:S(2)}) collective-permute-start(f32[64,128]{1,0:T(8,128)S(1)} %add.7.refs_0_), channel_id=1, source_target_pairs={{0,2},{1,3},{2,0},{3,1},{4,6},{5,7},{6,4},{7,5},{8,10},{9,11},{10,... | collective-permute-start | bytes 98312 | tf_op jit(solution)/shard_map/ppermute | solution.py:506
  79.3 4.0 %copy-start.1 = (f32[8,128]{1,0:T(8,128)S(1)}, f32[8,128]{1,0:T(8,128)}, u32[]{:S(2)}) copy-start(f32[8,128]{1,0:T(8,128)} %refs_9_.1) | copy-start | bytes 12292
  79.3 4.0 %collective-permute-start.29 = (f32[64,128]{1,0:T(8,128)S(1)}, f32[64,128]{1,0:T(8,128)S(1)}, u32[]{:S(2)}, u32[]{:S(2)}) collective-permute-start(f32[64,128]{1,0:T(8,128)S(1)} %add_all.3.refs_5_.refs_8_), channel_id=1, source_target_pairs={{0,16},{16,0},{1,17},{17,1},{2,18},{18,2},{3,19},{19,3},{4,20},{20... | collective-permute-start | bytes 98312 | tf_op jit(solution)/shard_map/ppermute | solution.py:509
  81.8 1.2 %collective-permute-start.30 = (f32[32,128]{1,0:T(8,128)S(1)}, f32[32,128]{1,0:T(8,128)S(1)}, u32[]{:S(2)}, u32[]{:S(2)}) collective-permute-start(f32[32,128]{1,0:T(8,128)S(1)} %get-tuple-element.99), channel_id=1, source_target_pairs={{0,1},{1,0},{2,3},{3,2},{4,5},{5,4},{6,7},{7,6},{8,9},{9,8},{10,11... | collective-permute-start | bytes 49160 | tf_op jit(solution)/shard_map/ppermute | solution.py:506

commit v7 on v6

--- a/solution.py
+++ b/solution.py
@@ -179,7 +179,7 @@
     chips = rows_out.shape[0] // sb
 
     if not planned:
-        copy = fetch_named([source[2 * chunk] for chunk in range(chunks)], staged, named, arrived, sb, half)
+        copy = fetch_named([source[2 * chunk] for chunk in range(chunks)], staged, named, arrived, sb, half, me, near)
     if chained:
         rows_out[...] = rows_in[...]
         mass_out[...] = mass_in[...]
@@ -200,7 +200,7 @@
                     listed[j] = j
                     table[j] = named[j, 2 * near]
             else:
-                list_slots(named, listed, table, me, chip_of[chunk], chunk, slots, sb, tb, near, chips, count)
+                list_slots(named, listed, table, chip_of[chunk], chunk, slots, sb, tb, chips, count)
 
     for chunk in range(chunks):
         lower = source[2 * chunk + 1]
@@ -233,28 +233,30 @@
         rows_out[pl.ds(start, sb)] += back[...]
 
 
-def fetch_named(uppers, staged, named, arrived, sb, half):
+def fetch_named(uppers, staged, named, arrived, sb, half, me, near):
     for chunk, upper in enumerate(uppers):
-        staged[chunk * sb : (chunk + 1) * sb] = upper[sb * half :].astype(jnp.int32)
+        rows = upper[sb * half :]
+        lane = lax.broadcasted_iota(jnp.int32, rows.shape, 1)
+        blocks = pltpu.roll(rows, rows.shape[1] - near, 1)
+        out = rows
+        for side, wanted in enumerate((me, me + 1 - 2 * lax.rem(me, 2))):
+            hit = jnp.where((rows.astype(jnp.int32) == wanted) & (lane < near), 1.0, 0.0)
+            out = jnp.where(lane == 2 * side, jnp.sum(hit, axis=1, keepdims=True), out)
+            out = jnp.where(lane == 2 * side + 1, jnp.sum(hit * blocks, axis=1, keepdims=True), out)
+        staged[chunk * sb : (chunk + 1) * sb] = out.astype(jnp.int32)
     copy = pltpu.make_async_copy(staged, named, arrived)
     copy.start()
     return copy
 
 
-def list_slots(named, listed, table, me, at_chip, chunk, slots, sb, tb, near, chips, count):
+def list_slots(named, listed, table, at_chip, chunk, slots, sb, tb, chips, count):
     for side in range(2):
         base = (chunk * 2 + side) * slots
-        wanted = me if side == 0 else me + 1 - 2 * lax.rem(me, 2)
         filled = jnp.int32(0)
         for block in range(sb):
-            found, which = jnp.int32(0), jnp.int32(0)
-            for k in range(near):
-                hit = named[chunk * sb + block, k] == wanted
-                found = jnp.where(hit, 1, found)
-                which = jnp.where(hit, named[chunk * sb + block, near + k], which)
             listed[base + filled] = block
-            table[count + base + filled] = which
-            filled = filled + found
+            table[count + base + filled] = named[chunk * sb + block, 2 * side + 1]
+            filled = filled + named[chunk * sb + block, 2 * side]
         for j in range(slots):
             valid = j < filled
             block = jnp.where(valid, listed[base + j], sb)
@@ -266,12 +268,10 @@
 
 def plan_kernel(plan, device, upper, table, listed, staged, named, arrived):
     slots, sb, half, tb, near, chips, offset = plan
-    copy = fetch_named([upper], staged, named, arrived, sb, half)
     me = device[0]
+    copy = fetch_named([upper], staged, named, arrived, sb, half, me, near)
     copy.wait()
-    list_slots(
-        named, listed, table, me, chip_at(chips, me // 2, offset), 0, slots, sb, tb, near, chips, 2 * slots
-    )
+    list_slots(named, listed, table, chip_at(chips, me // 2, offset), 0, slots, sb, tb, chips, 2 * slots)
 
 
 def plan_tiles(device, upper, slots, sb, tb, near, chips, offset):

time: 84.3 us -> 84.3 us (level)
  waiting for transfers between devices: 25 us -> 26.8 us
  Pallas kernels: 22.6 us -> 20.9 us
    ppermute x14, waiting for transfers between devices: 10.8 us -> 12.6 us  [around(): return lax.ppermute(x, 'dev', pairs)]
    pallas_call x6, Pallas kernels: 11.4 us -> 9.57 us  [build_tiles(): pl.pallas_call(functools.partial(tile_kernel, plan), out_shape=out_shape,...]
  transfers between devices with their start and end apart: 31 -> 31, of which waited for: 22 -> 22; matrix products, arithmetic and copies ran while one was open for 0% -> 0% of each run, Pallas kernels for 24% -> 22%
where the time goes in v7:
time: 84.3 us; the launch traced here: 84.1 us
  starting transfers between devices  35.6 us (42%)
  waiting for transfers between devices  26.8 us (32%)
  Pallas kernels  20.9 us (25%)
    ppermute x14, starting transfers between devices, around(): return lax.ppermute(x, 'dev', pairs)  14.9 us
    ppermute x12, starting transfers between devices, across(): return lax.ppermute(x, 'dev', [(i, i ^ bit) for i in range(dev_count)])  12.8 us
    ppermute x12, waiting for transfers between devices, across(): return lax.ppermute(x, 'dev', [(i, i ^ bit) for i in range(dev_count)])  12.7 us
    ppermute x14, waiting for transfers between devices, around(): return lax.ppermute(x, 'dev', pairs)  12.6 us
    pallas_call x6, Pallas kernels, build_tiles(): pl.pallas_call(functools.partial(tile_kernel, plan), out_shape=out_shape,...  9.57 us
    ppermute x5, starting transfers between devices, to_group(): lax.ppermute(x, 'group', [(g, (g + by) % group_count) for g in range(grou...  7.86 us
    pallas_call x2, Pallas kernels, target_operand(): pl.pallas_call(target_kernel, out_shape=pltpu.VMEM((blocks, width, 2 * ro...  5.09 us
    pallas_call x2, Pallas kernels, column_sums(): pl.pallas_call(functools.partial(column_kernel, counts), out_shape=(jax.S...  1.81 us
  transfers between devices with their start and end apart: 31, of which 22 were waited for; matrix products, arithmetic and copies ran while one was open for 0% of the time, Pallas kernels for 22%

profile of v7, /device:TPU:0, one launch (start us, length us, event | category | flops | bytes accessed | tf_op | source)
XLA Modules:
  0.0 84.1 jit_solution(9196144994400945173)
XLA Ops:
  0.6 0.5 collective-permute-start.2
  1.1 1.2 %pack.1 = (f32[520,128]{1,0:T(8,128)S(1)}, f32[520,128]{1,0:T(8,128)S(1)}, f32[1040,128]{1,0:T(8,128)S(1)}) custom-call(s32[1]{0:T(128)} %bitcast.device.refs_0_, f32[8,128,128]{2,1,0:T(8,128)} %emb.1, f32[8,128]{1,0:T(8,128)} %refs_9_.1, s32[8,7]{1,0:T(8,128)} %cand_device.1, s32[8,8]{1,0:T(8,128)} %cand_block.1), custom_call_target="tpu_custom_call" | custom-call | tf_op jit(solution)/shard_map/pack/pallas_call | solution.py:133
  2.4 2.6 %collective-permute-start = (f32[520,128]{1,0:T(8,128)S(1)}, f32[520,128]{1,0:T(8,128)S(1)}, u32[]{:S(2)}, u32[]{:S(2)}) collective-permute-start(f32[520,128]{1,0:T(8,128)S(1)} %get-tuple-element.58.refs_1_), channel_id=1, source_target_pairs={{0,4},{1,5},{4,8},{5,9},{8,12},{9,13},{12,14},{13,15},{14,10},{15,... | collective-permute-start | bytes 798728 | tf_op jit(solution)/shard_map/ppermute | solution.py:503
  5.0 2.9 %target_operand.2.refs_2_.refs_3_.refs_5_ = bf16[32,128,256]{2,1,0:T(8,128)(2,1)S(1)} custom-call(f32[32,128,128]{2,1,0:T(8,128)} %emb_ref.1), custom_call_target="tpu_custom_call" | custom-call | tf_op jit(solution)/shard_map/target_operand/pallas_call | solution.py:90
  8.0 2.1 %collective-permute-start.3 = (f32[520,128]{1,0:T(8,128)S(1)}, f32[520,128]{1,0:T(8,128)S(1)}, u32[]{:S(2)}, u32[]{:S(2)}) collective-permute-start(f32[520,128]{1,0:T(8,128)S(1)} %get-tuple-element.57.refs_2_), channel_id=1, source_target_pairs={{0,4},{1,5},{4,8},{5,9},{8,12},{9,13},{12,14},{13,15},{14,10},{15,... | collective-permute-start | bytes 798728 | tf_op jit(solution)/shard_map/ppermute | solution.py:503
  10.1 2.1 %target_operand.3.refs_4_.refs_6_ = bf16[32,128,256]{2,1,0:T(8,128)(2,1)S(1)} custom-call(f32[32,128,128]{2,1,0:T(8,128)S(1)} %collective-permute-done.2.emb_ref), custom_call_target="tpu_custom_call" | custom-call | tf_op jit(solution)/shard_map/target_operand/pallas_call | solution.py:90
  12.2 2.0 %collective-permute-done.5.refs_4_ = f32[520,128]{1,0:T(8,128)S(1)} collective-permute-done((f32[520,128]{1,0:T(8,128)S(1)}, f32[520,128]{1,0:T(8,128)S(1)}, u32[]{:S(2)}, u32[]{:S(2)}) %collective-permute-start.5) | collective-permute-done | bytes 266272 | tf_op jit(solution)/shard_map/ppermute | solution.py:503
  14.3 1.6 %collective-permute-start.6 = (f32[520,128]{1,0:T(8,128)S(1)}, f32[520,128]{1,0:T(8,128)S(1)}, u32[]{:S(2)}, u32[]{:S(2)}) collective-permute-start(f32[520,128]{1,0:T(8,128)S(1)} %collective-permute-done.refs_1_), channel_id=1, source_target_pairs={{0,4},{1,5},{4,8},{5,9},{8,12},{9,13},{12,14},{13,15},{14,10},{15,... | collective-permute-start | bytes 798728 | tf_op jit(solution)/shard_map/ppermute | solution.py:503
  15.9 0.4 collective-permute-start.9
  16.3 1.5 %collective-permute-start.1 = (f32[1040,128]{1,0:T(8,128)S(1)}, f32[1040,128]{1,0:T(8,128)S(1)}, u32[]{:S(2)}, u32[]{:S(2)}) collective-permute-start(f32[1040,128]{1,0:T(8,128)S(1)} %get-tuple-element.53), channel_id=1, source_target_pairs={{0,16},{16,0},{1,17},{17,1},{2,18},{18,2},{3,19},{19,3},{4,20},{20... | collective-permute-start | bytes 1597448 | tf_op jit(solution)/shard_map/ppermute | solution.py:509
  17.8 1.5 %build_tiles.7 = (bf16[10,128,256]{2,1,0:T(8,128)(2,1)S(1)}, s32[21]{0:T(128)S(4)}, f32[64,128]{1,0:T(8,128)S(1)}, f32[64,128]{1,0:T(8,128)S(1)}, bf16[10,128,256]{2,1,0:T(8,128)(2,1)S(1)}) custom-call(s32[1]{0:T(128)} %bitcast.device.refs_0_, f32[520,128]{1,0:T(8,128)S(1)} %get-tuple-element.58.refs_1_, f32[520,128]{1,0:T(8,128)S(1)} %get-tuple-element.57.refs_2_, ...), custom_call_target="tpu_custom_call" | custom-call | tf_op jit(solution)/shard_map/build_tiles/pallas_call | solution.py:327
  19.3 0.7 collective-permute-done.4.refs_3_
  20.0 1.6 %collective-permute-start.7 = (f32[520,128]{1,0:T(8,128)S(1)}, f32[520,128]{1,0:T(8,128)S(1)}, u32[]{:S(2)}, u32[]{:S(2)}) collective-permute-start(f32[520,128]{1,0:T(8,128)S(1)} %collective-permute-done.3.refs_2_), channel_id=1, source_target_pairs={{0,4},{1,5},{4,8},{5,9},{8,12},{9,13},{12,14},{13,15},{14,10},{15,... | collective-permute-start | bytes 798728 | tf_op jit(solution)/shard_map/ppermute | solution.py:503
  21.6 0.4 collective-permute-start.8
  22.0 2.0 %build_tiles.8 = (bf16[20,128,256]{2,1,0:T(8,128)(2,1)S(1)}, s32[41]{0:T(128)S(4)}, f32[64,128]{1,0:T(8,128)S(1)}, f32[64,128]{1,0:T(8,128)S(1)}, bf16[20,128,256]{2,1,0:T(8,128)(2,1)S(1)}) custom-call(s32[1]{0:T(128)} %bitcast.device.refs_0_, f32[520,128]{1,0:T(8,128)S(1)} %collective-permute-done.refs_1_, f32[520,128]{1,0:T(8,128)S(1)} %collective-permute-done.3.refs_2_, ...), custom_call_target="tpu_custom_call" | custom-call | tf_op jit(solution)/shard_map/build_tiles/pallas_call | solution.py:327
  24.0 1.7 %collective-permute-done.9.refs_4_ = f32[520,128]{1,0:T(8,128)S(1)} collective-permute-done((f32[520,128]{1,0:T(8,128)S(1)}, f32[520,128]{1,0:T(8,128)S(1)}, u32[]{:S(2)}, u32[]{:S(2)}) %collective-permute-start.9) | collective-permute-done | bytes 266272 | tf_op jit(solution)/shard_map/ppermute | solution.py:503
  25.7 1.6 %collective-permute-start.10 = (f32[520,128]{1,0:T(8,128)S(1)}, f32[520,128]{1,0:T(8,128)S(1)}, u32[]{:S(2)}, u32[]{:S(2)}) collective-permute-start(f32[520,128]{1,0:T(8,128)S(1)} %collective-permute-done.6.refs_1_), channel_id=1, source_target_pairs={{0,4},{1,5},{4,8},{5,9},{8,12},{9,13},{12,14},{13,15},{14,10},{15,... | collective-permute-start | bytes 798728 | tf_op jit(solution)/shard_map/ppermute | solution.py:503
  27.3 0.4 collective-permute-start.13
  27.7 1.6 %collective-permute-done.7.refs_2_ = f32[520,128]{1,0:T(8,128)S(1)} collective-permute-done((f32[520,128]{1,0:T(8,128)S(1)}, f32[520,128]{1,0:T(8,128)S(1)}, u32[]{:S(2)}, u32[]{:S(2)}) %collective-permute-start.7) | collective-permute-done | bytes 266272 | tf_op jit(solution)/shard_map/ppermute | solution.py:503
  29.3 2.0 %collective-permute-start.11 = (f32[520,128]{1,0:T(8,128)S(1)}, f32[520,128]{1,0:T(8,128)S(1)}, u32[]{:S(2)}, u32[]{:S(2)}) collective-permute-start(f32[520,128]{1,0:T(8,128)S(1)} %collective-permute-done.7.refs_2_), channel_id=1, source_target_pairs={{0,4},{1,5},{4,8},{5,9},{8,12},{9,13},{12,14},{13,15},{14,10},{15,... | collective-permute-start | bytes 798728 | tf_op jit(solution)/shard_map/ppermute | solution.py:503
  31.4 2.0 %build_tiles.9 = (bf16[20,128,256]{2,1,0:T(8,128)(2,1)S(1)}, s32[41]{0:T(128)S(4)}, f32[64,128]{1,0:T(8,128)S(1)}, f32[64,128]{1,0:T(8,128)S(1)}, bf16[20,128,256]{2,1,0:T(8,128)(2,1)S(1)}) custom-call(s32[1]{0:T(128)} %bitcast.device.refs_0_, f32[520,128]{1,0:T(8,128)S(1)} %collective-permute-done.6.refs_1_, f32[520,128]{1,0:T(8,128)S(1)} %collective-permute-done.7.refs_2_, ...), custom_call_target="tpu_custom_call" | custom-call | tf_op jit(solution)/shard_map/build_tiles/pallas_call | solution.py:327
  33.4 1.6 %collective-permute-done.10.refs_1_ = f32[520,128]{1,0:T(8,128)S(1)} collective-permute-done((f32[520,128]{1,0:T(8,128)S(1)}, f32[520,128]{1,0:T(8,128)S(1)}, u32[]{:S(2)}, u32[]{:S(2)}) %collective-permute-start.10) | collective-permute-done | bytes 266272 | tf_op jit(solution)/shard_map/ppermute | solution.py:503
  35.0 2.1 %collective-permute-done.13.refs_4_ = f32[520,128]{1,0:T(8,128)S(1)} collective-permute-done((f32[520,128]{1,0:T(8,128)S(1)}, f32[520,128]{1,0:T(8,128)S(1)}, u32[]{:S(2)}, u32[]{:S(2)}) %collective-permute-start.13) | collective-permute-done | bytes 266272 | tf_op jit(solution)/shard_map/ppermute | solution.py:503
  37.1 1.6 %collective-permute-start.14 = (f32[520,128]{1,0:T(8,128)S(1)}, f32[520,128]{1,0:T(8,128)S(1)}, u32[]{:S(2)}, u32[]{:S(2)}) collective-permute-start(f32[520,128]{1,0:T(8,128)S(1)} %collective-permute-done.10.refs_1_), channel_id=1, source_target_pairs={{0,4},{1,5},{4,8},{5,9},{8,12},{9,13},{12,14},{13,15},{14,10},{15,... | collective-permute-start | bytes 798728 | tf_op jit(solution)/shard_map/ppermute | solution.py:503
  38.7 0.4 collective-permute-start.15
  39.1 1.3 %build_tiles.6 = (bf16[8,128,256]{2,1,0:T(8,128)(2,1)S(1)}, s32[8]{0:T(128)S(4)}, f32[8,128]{1,0:T(8,128)S(1)}, f32[8,128]{1,0:T(8,128)S(1)}) custom-call(s32[1]{0:T(128)} %bitcast.device.refs_0_, f32[1040,128]{1,0:T(8,128)S(1)} %collective-permute-done.1.refs_1_, bf16[32,128,256]{2,1,0:T(8,128)(2,1)S(1)} %target_operand.2.refs_2_.refs_3_.refs_5_), custom_call_target="tpu_custom_call" | custom-call | tf_op jit(solution)/shard_map/build_tiles/pallas_call | solution.py:327
  40.5 1.6 %collective-permute-start.16 = (f32[8,128]{1,0:T(8,128)S(1)}, f32[8,128]{1,0:T(8,128)S(1)}, u32[]{:S(2)}, u32[]{:S(2)}) collective-permute-start(f32[8,128]{1,0:T(8,128)S(1)} %get-tuple-element.79), channel_id=1, source_target_pairs={{0,16},{16,0},{1,17},{17,1},{2,18},{18,2},{3,19},{19,3},{4,20},{20... | collective-permute-start | bytes 12296 | tf_op jit(solution)/shard_map/ppermute | solution.py:509
  42.0 0.8 collective-permute-done.12.refs_3_
  42.8 2.0 %build_tiles.10 = (bf16[20,128,256]{2,1,0:T(8,128)(2,1)S(1)}, s32[41]{0:T(128)S(4)}, f32[64,128]{1,0:T(8,128)S(1)}, f32[64,128]{1,0:T(8,128)S(1)}, bf16[20,128,256]{2,1,0:T(8,128)(2,1)S(1)}) custom-call(s32[1]{0:T(128)} %bitcast.device.refs_0_, f32[520,128]{1,0:T(8,128)S(1)} %collective-permute-done.10.refs_1_, ...), custom_call_target="tpu_custom_call" | custom-call | tf_op jit(solution)/shard_map/build_tiles/pallas_call | solution.py:327
  44.8 1.4 %collective-permute-done.14.upper.refs_1_ = f32[520,128]{1,0:T(8,128)S(1)} collective-permute-done((f32[520,128]{1,0:T(8,128)S(1)}, f32[520,128]{1,0:T(8,128)S(1)}, u32[]{:S(2)}, u32[]{:S(2)}) %collective-permute-start.14) | collective-permute-done | bytes 266272 | tf_op jit(solution)/shard_map/ppermute | solution.py:503
  46.2 0.9 %plan_tiles.1 = (s32[21]{0:T(128)S(4)}, s32[11]{0:T(128)S(4)}) custom-call(s32[1]{0:T(128)} %bitcast.device.refs_0_, f32[520,128]{1,0:T(8,128)S(1)} %collective-permute-done.14.upper.refs_1_), custom_call_target="tpu_custom_call" | custom-call | tf_op jit(solution)/shard_map/plan_tiles/pallas_call | solution.py:279
  47.1 0.7 collective-permute-done.15.refs_2_
  47.8 0.8 build_tiles.11
  48.6 2.6 %collective-permute-start.17 = (f32[64,128]{1,0:T(8,128)S(1)}, f32[64,128]{1,0:T(8,128)S(1)}, u32[]{:S(2)}, u32[]{:S(2)}) collective-permute-start(f32[64,128]{1,0:T(8,128)S(1)} %get-tuple-element.81), channel_id=1, source_target_pairs={{0,8},{1,9},{2,10},{3,11},{4,12},{5,13},{6,14},{7,15},{8,0},{9,1},... | collective-permute-start | bytes 98312 | tf_op jit(solution)/shard_map/ppermute | solution.py:506
  51.2 2.2 %collective-permute-done.17 = f32[64,128]{1,0:T(8,128)S(1)} collective-permute-done((f32[64,128]{1,0:T(8,128)S(1)}, f32[64,128]{1,0:T(8,128)S(1)}, u32[]{:S(2)}, u32[]{:S(2)}) %collective-permute-start.17) | collective-permute-done | bytes 32800 | tf_op jit(solution)/shard_map/ppermute | solution.py:506
  53.4 2.1 %collective-permute-start.18 = (f32[64,128]{1,0:T(8,128)S(1)}, f32[64,128]{1,0:T(8,128)S(1)}, u32[]{:S(2)}, u32[]{:S(2)}) collective-permute-start(f32[64,128]{1,0:T(8,128)S(1)} %add.6.refs_0_), channel_id=1, source_target_pairs={{0,6},{1,7},{2,4},{3,5},{4,2},{5,3},{6,0},{7,1},{8,14},{9,15},{10,... | collective-permute-start | bytes 98312 | tf_op jit(solution)/shard_map/ppermute | solution.py:506
  55.5 0.6 collective-permute-start.19
  56.1 0.8 %collective-permute-start.20 = (f32[64,128]{1,0:T(8,128)S(1)}, f32[64,128]{1,0:T(8,128)S(1)}, u32[]{:S(2)}, u32[]{:S(2)}) collective-permute-start(f32[64,128]{1,0:T(8,128)S(1)} %add.6.refs_0_), channel_id=1, source_target_pairs={{0,2},{1,3},{2,0},{3,1},{4,6},{5,7},{6,4},{7,5},{8,10},{9,11},{10,... | collective-permute-start | bytes 98312 | tf_op jit(solution)/shard_map/ppermute | solution.py:506
  56.9 1.3 %collective-permute-done.18.refs_1_ = f32[64,128]{1,0:T(8,128)S(1)} collective-permute-done((f32[64,128]{1,0:T(8,128)S(1)}, f32[64,128]{1,0:T(8,128)S(1)}, u32[]{:S(2)}, u32[]{:S(2)}) %collective-permute-start.18) | collective-permute-done | bytes 32800 | tf_op jit(solution)/shard_map/ppermute | solution.py:506
  58.3 1.2 %collective-permute-done.19.refs_2_ = f32[64,128]{1,0:T(8,128)S(1)} collective-permute-done((f32[64,128]{1,0:T(8,128)S(1)}, f32[64,128]{1,0:T(8,128)S(1)}, u32[]{:S(2)}, u32[]{:S(2)}) %collective-permute-start.19) | collective-permute-done | bytes 32800 | tf_op jit(solution)/shard_map/ppermute | solution.py:506
  59.5 0.6 collective-permute-done.20.refs_3_
  60.0 1.6 %collective-permute-start.21 = (f32[64,128]{1,0:T(8,128)S(1)}, f32[64,128]{1,0:T(8,128)S(1)}, u32[]{:S(2)}, u32[]{:S(2)}) collective-permute-start(f32[64,128]{1,0:T(8,128)S(1)} %add_all.2.refs_5_), channel_id=1, source_target_pairs={{0,16},{16,0},{1,17},{17,1},{2,18},{18,2},{3,19},{19,3},{4,20},{20... | collective-permute-start | bytes 98312 | tf_op jit(solution)/shard_map/ppermute | solution.py:509
  61.6 0.9 %column_sums.2 = (f32[32,128]{1,0:T(8,128)S(1)}, f32[32,128]{1,0:T(8,128)S(1)}) custom-call(s32[21]{0:T(128)S(4)} %get-tuple-element.56.refs_0_, s32[41]{0:T(128)S(4)} %get-tuple-element.61.refs_1_, s32[41]{0:T(128)S(4)} %get-tuple-element.68.refs_2_, s32[41]{0:T(128)S(4)} %get-tuple-element.73.refs_3_, s32[21]{0:T(128)S(4)} %get-tuple-element.75.refs_8_.refs_4_, ...), custom_call_target="tpu_custom_call" | custom-call | tf_op jit(solution)/shard_map/column_sums/pallas_call | solution.py:396
  62.6 1.2 %collective-permute-done.22.refs_5_ = f32[32,128]{1,0:T(8,128)S(1)} collective-permute-done((f32[32,128]{1,0:T(8,128)S(1)}, f32[32,128]{1,0:T(8,128)S(1)}, u32[]{:S(2)}, u32[]{:S(2)}) %collective-permute-start.22) | collective-permute-done | bytes 16416 | tf_op jit(solution)/shard_map/ppermute | solution.py:506
  63.8 0.2 collective-permute-done.21.refs_2_
  64.0 0.4 closing.2
  64.5 0.1 collective-permute-start.23
  64.5 1.6 %collective-permute-start.24 = (f32[8,128]{1,0:T(8,128)S(1)}, f32[8,128]{1,0:T(8,128)S(1)}, u32[]{:S(2)}, u32[]{:S(2)}) collective-permute-start(f32[8,128]{1,0:T(8,128)S(1)} %get-tuple-element.97), channel_id=1, source_target_pairs={{0,16},{16,0},{1,17},{17,1},{2,18},{18,2},{3,19},{19,3},{4,20},{20... | collective-permute-start | bytes 12296 | tf_op jit(solution)/shard_map/ppermute | solution.py:509
  66.1 1.0 %row_sums.1.rows = f32[64,128]{1,0:T(8,128)S(1)} custom-call(s32[21]{0:T(128)S(4)} %get-tuple-element.56.refs_0_, s32[41]{0:T(128)S(4)} %get-tuple-element.61.refs_1_, s32[41]{0:T(128)S(4)} %get-tuple-element.68.refs_2_, s32[41]{0:T(128)S(4)} %get-tuple-element.73.refs_3_, s32[21]{0:T(128)S(4)} %get-tuple-element.75.refs_8_.refs_4_, ...), custom_call_target="tpu_custom_call" | custom-call | tf_op jit(solution)/shard_map/row_sums/pallas_call | solution.py:475
  67.1 1.1 %collective-permute-done.24.part = f32[8,128]{1,0:T(8,128)S(1)} collective-permute-done((f32[8,128]{1,0:T(8,128)S(1)}, f32[8,128]{1,0:T(8,128)S(1)}, u32[]{:S(2)}, u32[]{:S(2)}) %collective-permute-start.24) | collective-permute-done | bytes 4128 | tf_op jit(solution)/shard_map/ppermute | solution.py:509
  68.2 2.5 %collective-permute-start.25 = (f32[64,128]{1,0:T(8,128)S(1)}, f32[64,128]{1,0:T(8,128)S(1)}, u32[]{:S(2)}, u32[]{:S(2)}) collective-permute-start(f32[64,128]{1,0:T(8,128)S(1)} %add_own.1), channel_id=1, source_target_pairs={{0,8},{1,9},{2,10},{3,11},{4,12},{5,13},{6,14},{7,15},{8,0},{9,1},... | collective-permute-start | bytes 98312 | tf_op jit(solution)/shard_map/ppermute | solution.py:506
  70.7 2.3 %collective-permute-done.25 = f32[64,128]{1,0:T(8,128)S(1)} collective-permute-done((f32[64,128]{1,0:T(8,128)S(1)}, f32[64,128]{1,0:T(8,128)S(1)}, u32[]{:S(2)}, u32[]{:S(2)}) %collective-permute-start.25) | collective-permute-done | bytes 32800 | tf_op jit(solution)/shard_map/ppermute | solution.py:506
  73.0 1.9 %collective-permute-start.26 = (f32[64,128]{1,0:T(8,128)S(1)}, f32[64,128]{1,0:T(8,128)S(1)}, u32[]{:S(2)}, u32[]{:S(2)}) collective-permute-start(f32[64,128]{1,0:T(8,128)S(1)} %add.7.refs_0_), channel_id=1, source_target_pairs={{0,6},{1,7},{2,4},{3,5},{4,2},{5,3},{6,0},{7,1},{8,14},{9,15},{10,... | collective-permute-start | bytes 98312 | tf_op jit(solution)/shard_map/ppermute | solution.py:506
  74.9 0.4 collective-permute-start.27
  75.3 1.2 %collective-permute-start.28 = (f32[64,128]{1,0:T(8,128)S(1)}, f32[64,128]{1,0:T(8,128)S(1)}, u32[]{:S(2)}, u32[]{:S(2)}) collective-permute-start(f32[64,128]{1,0:T(8,128)S(1)} %add.7.refs_0_), channel_id=1, source_target_pairs={{0,2},{1,3},{2,0},{3,1},{4,6},{5,7},{6,4},{7,5},{8,10},{9,11},{10,... | collective-permute-start | bytes 98312 | tf_op jit(solution)/shard_map/ppermute | solution.py:506
  76.5 1.3 %collective-permute-done.26.refs_1_ = f32[64,128]{1,0:T(8,128)S(1)} collective-permute-done((f32[64,128]{1,0:T(8,128)S(1)}, f32[64,128]{1,0:T(8,128)S(1)}, u32[]{:S(2)}, u32[]{:S(2)}) %collective-permute-start.26) | collective-permute-done | bytes 32800 | tf_op jit(solution)/shard_map/ppermute | solution.py:506
  77.8 1.0 %collective-permute-done.27.refs_2_ = f32[64,128]{1,0:T(8,128)S(1)} collective-permute-done((f32[64,128]{1,0:T(8,128)S(1)}, f32[64,128]{1,0:T(8,128)S(1)}, u32[]{:S(2)}, u32[]{:S(2)}) %collective-permute-start.27) | collective-permute-done | bytes 32800 | tf_op jit(solution)/shard_map/ppermute | solution.py:506
  78.8 0.4 collective-permute-done.28.refs_3_
  79.3 1.6 %collective-permute-start.29 = (f32[64,128]{1,0:T(8,128)S(1)}, f32[64,128]{1,0:T(8,128)S(1)}, u32[]{:S(2)}, u32[]{:S(2)}) collective-permute-start(f32[64,128]{1,0:T(8,128)S(1)} %add_all.3.refs_5_.refs_8_), channel_id=1, source_target_pairs={{0,16},{16,0},{1,17},{17,1},{2,18},{18,2},{3,19},{19,3},{4,20},{20... | collective-permute-start | bytes 98312 | tf_op jit(solution)/shard_map/ppermute | solution.py:509
  80.9 0.9 %column_sums.3 = (f32[32,128]{1,0:T(8,128)S(1)}, f32[32,128]{1,0:T(8,128)S(1)}) custom-call(s32[21]{0:T(128)S(4)} %get-tuple-element.56.refs_0_, s32[41]{0:T(128)S(4)} %get-tuple-element.61.refs_1_, s32[41]{0:T(128)S(4)} %get-tuple-element.68.refs_2_, s32[41]{0:T(128)S(4)} %get-tuple-element.73.refs_3_, s32[21]{0:T(128)S(4)} %get-tuple-element.75.refs_8_.refs_4_, ...), custom_call_target="tpu_custom_call" | custom-call | tf_op jit(solution)/shard_map/column_sums/pallas_call | solution.py:396
  81.8 0.1 collective-permute-start.30
  81.9 1.2 %collective-permute-done.30.refs_5_ = f32[32,128]{1,0:T(8,128)S(1)} collective-permute-done((f32[32,128]{1,0:T(8,128)S(1)}, f32[32,128]{1,0:T(8,128)S(1)}, u32[]{:S(2)}, u32[]{:S(2)}) %collective-permute-start.30) | collective-permute-done | bytes 16416 | tf_op jit(solution)/shard_map/ppermute | solution.py:506
  83.0 0.2 collective-permute-done.29.refs_2_
  83.3 0.8 closing.3
  (22 shorter events, 0.2 us)
Async XLA Ops:
  0.6 9.5 %collective-permute-start.2 = (f32[32,128,128]{2,1,0:T(8,128)}, f32[32,128,128]{2,1,0:T(8,128)S(1)}, u32[]{:S(2)}, u32[]{:S(2)}) collective-permute-start(f32[32,128,128]{2,1,0:T(8,128)} %emb_ref.1), channel_id=1, source_target_pairs={{0,1},{1,0},{2,3},{3,2},{4,5},{5,4},{6,7},{7,6},{8,9},{9,8},{10,11... | collective-permute-start | bytes 6291464 | tf_op jit(solution)/shard_map/ppermute | solution.py:506
  2.4 9.8 %collective-permute-start = (f32[520,128]{1,0:T(8,128)S(1)}, f32[520,128]{1,0:T(8,128)S(1)}, u32[]{:S(2)}, u32[]{:S(2)}) collective-permute-start(f32[520,128]{1,0:T(8,128)S(1)} %get-tuple-element.58.refs_1_), channel_id=1, source_target_pairs={{0,4},{1,5},{4,8},{5,9},{8,12},{9,13},{12,14},{13,15},{14,10},{15,... | collective-permute-start | bytes 798728 | tf_op jit(solution)/shard_map/ppermute | solution.py:503
  5.0 9.2 %collective-permute-start.5 = (f32[520,128]{1,0:T(8,128)S(1)}, f32[520,128]{1,0:T(8,128)S(1)}, u32[]{:S(2)}, u32[]{:S(2)}) collective-permute-start(f32[520,128]{1,0:T(8,128)S(1)} %get-tuple-element.57.refs_2_), channel_id=1, source_target_pairs={{0,2},{1,3},{4,0},{5,1},{8,4},{9,5},{12,8},{13,9},{14,12},{15,13},... | collective-permute-start | bytes 798728 | tf_op jit(solution)/shard_map/ppermute | solution.py:503
  8.0 11.3 %collective-permute-start.3 = (f32[520,128]{1,0:T(8,128)S(1)}, f32[520,128]{1,0:T(8,128)S(1)}, u32[]{:S(2)}, u32[]{:S(2)}) collective-permute-start(f32[520,128]{1,0:T(8,128)S(1)} %get-tuple-element.57.refs_2_), channel_id=1, source_target_pairs={{0,4},{1,5},{4,8},{5,9},{8,12},{9,13},{12,14},{13,15},{14,10},{15,... | collective-permute-start | bytes 798728 | tf_op jit(solution)/shard_map/ppermute | solution.py:503
  10.1 9.9 %collective-permute-start.4 = (f32[520,128]{1,0:T(8,128)S(1)}, f32[520,128]{1,0:T(8,128)S(1)}, u32[]{:S(2)}, u32[]{:S(2)}) collective-permute-start(f32[520,128]{1,0:T(8,128)S(1)} %get-tuple-element.58.refs_1_), channel_id=1, source_target_pairs={{0,2},{1,3},{4,0},{5,1},{8,4},{9,5},{12,8},{13,9},{14,12},{15,13},... | collective-permute-start | bytes 798728 | tf_op jit(solution)/shard_map/ppermute | solution.py:503
  14.3 9.7 %collective-permute-start.6 = (f32[520,128]{1,0:T(8,128)S(1)}, f32[520,128]{1,0:T(8,128)S(1)}, u32[]{:S(2)}, u32[]{:S(2)}) collective-permute-start(f32[520,128]{1,0:T(8,128)S(1)} %collective-permute-done.refs_1_), channel_id=1, source_target_pairs={{0,4},{1,5},{4,8},{5,9},{8,12},{9,13},{12,14},{13,15},{14,10},{15,... | collective-permute-start | bytes 798728 | tf_op jit(solution)/shard_map/ppermute | solution.py:503
  15.9 9.8 %collective-permute-start.9 = (f32[520,128]{1,0:T(8,128)S(1)}, f32[520,128]{1,0:T(8,128)S(1)}, u32[]{:S(2)}, u32[]{:S(2)}) collective-permute-start(f32[520,128]{1,0:T(8,128)S(1)} %collective-permute-done.5.refs_4_), channel_id=1, source_target_pairs={{0,2},{1,3},{4,0},{5,1},{8,4},{9,5},{12,8},{13,9},{14,12},{15,13},... | collective-permute-start | bytes 798728 | tf_op jit(solution)/shard_map/ppermute | solution.py:503
  16.3 22.8 %collective-permute-start.1 = (f32[1040,128]{1,0:T(8,128)S(1)}, f32[1040,128]{1,0:T(8,128)S(1)}, u32[]{:S(2)}, u32[]{:S(2)}) collective-permute-start(f32[1040,128]{1,0:T(8,128)S(1)} %get-tuple-element.53), channel_id=1, source_target_pairs={{0,16},{16,0},{1,17},{17,1},{2,18},{18,2},{3,19},{19,3},{4,20},{20... | collective-permute-start | bytes 1597448 | tf_op jit(solution)/shard_map/ppermute | solution.py:509
  20.0 9.3 %collective-permute-start.7 = (f32[520,128]{1,0:T(8,128)S(1)}, f32[520,128]{1,0:T(8,128)S(1)}, u32[]{:S(2)}, u32[]{:S(2)}) collective-permute-start(f32[520,128]{1,0:T(8,128)S(1)} %collective-permute-done.3.refs_2_), channel_id=1, source_target_pairs={{0,4},{1,5},{4,8},{5,9},{8,12},{9,13},{12,14},{13,15},{14,10},{15,... | collective-permute-start | bytes 798728 | tf_op jit(solution)/shard_map/ppermute | solution.py:503
  21.6 9.8 %collective-permute-start.8 = (f32[520,128]{1,0:T(8,128)S(1)}, f32[520,128]{1,0:T(8,128)S(1)}, u32[]{:S(2)}, u32[]{:S(2)}) collective-permute-start(f32[520,128]{1,0:T(8,128)S(1)} %collective-permute-done.4.refs_3_), channel_id=1, source_target_pairs={{0,2},{1,3},{4,0},{5,1},{8,4},{9,5},{12,8},{13,9},{14,12},{15,13},... | collective-permute-start | bytes 798728 | tf_op jit(solution)/shard_map/ppermute | solution.py:503
  25.7 9.3 %collective-permute-start.10 = (f32[520,128]{1,0:T(8,128)S(1)}, f32[520,128]{1,0:T(8,128)S(1)}, u32[]{:S(2)}, u32[]{:S(2)}) collective-permute-start(f32[520,128]{1,0:T(8,128)S(1)} %collective-permute-done.6.refs_1_), channel_id=1, source_target_pairs={{0,4},{1,5},{4,8},{5,9},{8,12},{9,13},{12,14},{13,15},{14,10},{15,... | collective-permute-start | bytes 798728 | tf_op jit(solution)/shard_map/ppermute | solution.py:503
  27.3 9.8 %collective-permute-start.13 = (f32[520,128]{1,0:T(8,128)S(1)}, f32[520,128]{1,0:T(8,128)S(1)}, u32[]{:S(2)}, u32[]{:S(2)}) collective-permute-start(f32[520,128]{1,0:T(8,128)S(1)} %collective-permute-done.9.refs_4_), channel_id=1, source_target_pairs={{0,2},{1,3},{4,0},{5,1},{8,4},{9,5},{12,8},{13,9},{14,12},{15,13},... | collective-permute-start | bytes 798728 | tf_op jit(solution)/shard_map/ppermute | solution.py:503
  29.3 12.7 %collective-permute-start.11 = (f32[520,128]{1,0:T(8,128)S(1)}, f32[520,128]{1,0:T(8,128)S(1)}, u32[]{:S(2)}, u32[]{:S(2)}) collective-permute-start(f32[520,128]{1,0:T(8,128)S(1)} %collective-permute-done.7.refs_2_), channel_id=1, source_target_pairs={{0,4},{1,5},{4,8},{5,9},{8,12},{9,13},{12,14},{13,15},{14,10},{15,... | collective-permute-start | bytes 798728 | tf_op jit(solution)/shard_map/ppermute | solution.py:503
  31.4 11.4 %collective-permute-start.12 = (f32[520,128]{1,0:T(8,128)S(1)}, f32[520,128]{1,0:T(8,128)S(1)}, u32[]{:S(2)}, u32[]{:S(2)}) collective-permute-start(f32[520,128]{1,0:T(8,128)S(1)} %collective-permute-done.8.refs_3_), channel_id=1, source_target_pairs={{0,2},{1,3},{4,0},{5,1},{8,4},{9,5},{12,8},{13,9},{14,12},{15,13},... | collective-permute-start | bytes 798728 | tf_op jit(solution)/shard_map/ppermute | solution.py:503
  37.1 9.1 %collective-permute-start.14 = (f32[520,128]{1,0:T(8,128)S(1)}, f32[520,128]{1,0:T(8,128)S(1)}, u32[]{:S(2)}, u32[]{:S(2)}) collective-permute-start(f32[520,128]{1,0:T(8,128)S(1)} %collective-permute-done.10.refs_1_), channel_id=1, source_target_pairs={{0,4},{1,5},{4,8},{5,9},{8,12},{9,13},{12,14},{13,15},{14,10},{15,... | collective-permute-start | bytes 798728 | tf_op jit(solution)/shard_map/ppermute | solution.py:503
  38.7 9.1 %collective-permute-start.15 = (f32[520,128]{1,0:T(8,128)S(1)}, f32[520,128]{1,0:T(8,128)S(1)}, u32[]{:S(2)}, u32[]{:S(2)}) collective-permute-start(f32[520,128]{1,0:T(8,128)S(1)} %collective-permute-done.13.refs_4_), channel_id=1, source_target_pairs={{0,2},{1,3},{4,0},{5,1},{8,4},{9,5},{12,8},{13,9},{14,12},{15,13},... | collective-permute-start | bytes 798728 | tf_op jit(solution)/shard_map/ppermute | solution.py:503
  40.5 6.6 %collective-permute-start.16 = (f32[8,128]{1,0:T(8,128)S(1)}, f32[8,128]{1,0:T(8,128)S(1)}, u32[]{:S(2)}, u32[]{:S(2)}) collective-permute-start(f32[8,128]{1,0:T(8,128)S(1)} %get-tuple-element.79), channel_id=1, source_target_pairs={{0,16},{16,0},{1,17},{17,1},{2,18},{18,2},{3,19},{19,3},{4,20},{20... | collective-permute-start | bytes 12296 | tf_op jit(solution)/shard_map/ppermute | solution.py:509
  48.6 4.8 %collective-permute-start.17 = (f32[64,128]{1,0:T(8,128)S(1)}, f32[64,128]{1,0:T(8,128)S(1)}, u32[]{:S(2)}, u32[]{:S(2)}) collective-permute-start(f32[64,128]{1,0:T(8,128)S(1)} %get-tuple-element.81), channel_id=1, source_target_pairs={{0,8},{1,9},{2,10},{3,11},{4,12},{5,13},{6,14},{7,15},{8,0},{9,1},... | collective-permute-start | bytes 98312 | tf_op jit(solution)/shard_map/ppermute | solution.py:506
  53.4 4.8 %collective-permute-start.18 = (f32[64,128]{1,0:T(8,128)S(1)}, f32[64,128]{1,0:T(8,128)S(1)}, u32[]{:S(2)}, u32[]{:S(2)}) collective-permute-start(f32[64,128]{1,0:T(8,128)S(1)} %add.6.refs_0_), channel_id=1, source_target_pairs={{0,6},{1,7},{2,4},{3,5},{4,2},{5,3},{6,0},{7,1},{8,14},{9,15},{10,... | collective-permute-start | bytes 98312 | tf_op jit(solution)/shard_map/ppermute | solution.py:506
  55.5 3.9 %collective-permute-start.19 = (f32[64,128]{1,0:T(8,128)S(1)}, f32[64,128]{1,0:T(8,128)S(1)}, u32[]{:S(2)}, u32[]{:S(2)}) collective-permute-start(f32[64,128]{1,0:T(8,128)S(1)} %add.6.refs_0_), channel_id=1, source_target_pairs={{0,4},{1,5},{2,6},{3,7},{4,0},{5,1},{6,2},{7,3},{8,12},{9,13},{10,... | collective-permute-start | bytes 98312 | tf_op jit(solution)/shard_map/ppermute | solution.py:506
  56.1 3.9 %collective-permute-start.20 = (f32[64,128]{1,0:T(8,128)S(1)}, f32[64,128]{1,0:T(8,128)S(1)}, u32[]{:S(2)}, u32[]{:S(2)}) collective-permute-start(f32[64,128]{1,0:T(8,128)S(1)} %add.6.refs_0_), channel_id=1, source_target_pairs={{0,2},{1,3},{2,0},{3,1},{4,6},{5,7},{6,4},{7,5},{8,10},{9,11},{10,... | collective-permute-start | bytes 98312 | tf_op jit(solution)/shard_map/ppermute | solution.py:506
  60.0 4.0 %collective-permute-start.21 = (f32[64,128]{1,0:T(8,128)S(1)}, f32[64,128]{1,0:T(8,128)S(1)}, u32[]{:S(2)}, u32[]{:S(2)}) collective-permute-start(f32[64,128]{1,0:T(8,128)S(1)} %add_all.2.refs_5_), channel_id=1, source_target_pairs={{0,16},{16,0},{1,17},{17,1},{2,18},{18,2},{3,19},{19,3},{4,20},{20... | collective-permute-start | bytes 98312 | tf_op jit(solution)/shard_map/ppermute | solution.py:509
  61.6 2.4 %copy-start = (f32[32,128]{1,0:T(8,128)S(1)}, f32[32,128]{1,0:T(8,128)}, u32[]{:S(2)}) copy-start(f32[32,128]{1,0:T(8,128)} %refs_6_.3) | copy-start | bytes 49156
  62.5 1.2 %collective-permute-start.22 = (f32[32,128]{1,0:T(8,128)S(1)}, f32[32,128]{1,0:T(8,128)S(1)}, u32[]{:S(2)}, u32[]{:S(2)}) collective-permute-start(f32[32,128]{1,0:T(8,128)S(1)} %get-tuple-element.90), channel_id=1, source_target_pairs={{0,1},{1,0},{2,3},{3,2},{4,5},{5,4},{6,7},{7,6},{8,9},{9,8},{10,11... | collective-permute-start | bytes 49160 | tf_op jit(solution)/shard_map/ppermute | solution.py:506
  64.5 1.7 %collective-permute-start.23 = (f32[32,128]{1,0:T(8,128)S(1)}, f32[32,128]{1,0:T(8,128)S(1)}, u32[]{:S(2)}, u32[]{:S(2)}) collective-permute-start(f32[32,128]{1,0:T(8,128)S(1)} %get-tuple-element.92.refs_5_), channel_id=1, source_target_pairs={{0,1},{1,0},{2,3},{3,2},{4,5},{5,4},{6,7},{7,6},{8,9},{9,8},{10,11... | collective-permute-start | bytes 49160 | tf_op jit(solution)/shard_map/ppermute | solution.py:506
  64.5 3.7 %collective-permute-start.24 = (f32[8,128]{1,0:T(8,128)S(1)}, f32[8,128]{1,0:T(8,128)S(1)}, u32[]{:S(2)}, u32[]{:S(2)}) collective-permute-start(f32[8,128]{1,0:T(8,128)S(1)} %get-tuple-element.97), channel_id=1, source_target_pairs={{0,16},{16,0},{1,17},{17,1},{2,18},{18,2},{3,19},{19,3},{4,20},{20... | collective-permute-start | bytes 12296 | tf_op jit(solution)/shard_map/ppermute | solution.py:509
  68.2 4.8 %collective-permute-start.25 = (f32[64,128]{1,0:T(8,128)S(1)}, f32[64,128]{1,0:T(8,128)S(1)}, u32[]{:S(2)}, u32[]{:S(2)}) collective-permute-start(f32[64,128]{1,0:T(8,128)S(1)} %add_own.1), channel_id=1, source_target_pairs={{0,8},{1,9},{2,10},{3,11},{4,12},{5,13},{6,14},{7,15},{8,0},{9,1},... | collective-permute-start | bytes 98312 | tf_op jit(solution)/shard_map/ppermute | solution.py:506
  73.0 4.8 %collective-permute-start.26 = (f32[64,128]{1,0:T(8,128)S(1)}, f32[64,128]{1,0:T(8,128)S(1)}, u32[]{:S(2)}, u32[]{:S(2)}) collective-permute-start(f32[64,128]{1,0:T(8,128)S(1)} %add.7.refs_0_), channel_id=1, source_target_pairs={{0,6},{1,7},{2,4},{3,5},{4,2},{5,3},{6,0},{7,1},{8,14},{9,15},{10,... | collective-permute-start | bytes 98312 | tf_op jit(solution)/shard_map/ppermute | solution.py:506
  74.9 3.9 %collective-permute-start.27 = (f32[64,128]{1,0:T(8,128)S(1)}, f32[64,128]{1,0:T(8,128)S(1)}, u32[]{:S(2)}, u32[]{:S(2)}) collective-permute-start(f32[64,128]{1,0:T(8,128)S(1)} %add.7.refs_0_), channel_id=1, source_target_pairs={{0,4},{1,5},{2,6},{3,7},{4,0},{5,1},{6,2},{7,3},{8,12},{9,13},{10,... | collective-permute-start | bytes 98312 | tf_op jit(solution)/shard_map/ppermute | solution.py:506
  75.3 3.9 %collective-permute-start.28 = (f32[64,128]{1,0:T(8,128)S(1)}, f32[64,128]{1,0:T(8,128)S(1)}, u32[]{:S(2)}, u32[]{:S(2)}) collective-permute-start(f32[64,128]{1,0:T(8,128)S(1)} %add.7.refs_0_), channel_id=1, source_target_pairs={{0,2},{1,3},{2,0},{3,1},{4,6},{5,7},{6,4},{7,5},{8,10},{9,11},{10,... | collective-permute-start | bytes 98312 | tf_op jit(solution)/shard_map/ppermute | solution.py:506
  79.3 4.0 %copy-start.1 = (f32[8,128]{1,0:T(8,128)S(1)}, f32[8,128]{1,0:T(8,128)}, u32[]{:S(2)}) copy-start(f32[8,128]{1,0:T(8,128)} %refs_9_.1) | copy-start | bytes 12292
  79.3 4.0 %collective-permute-start.29 = (f32[64,128]{1,0:T(8,128)S(1)}, f32[64,128]{1,0:T(8,128)S(1)}, u32[]{:S(2)}, u32[]{:S(2)}) collective-permute-start(f32[64,128]{1,0:T(8,128)S(1)} %add_all.3.refs_5_.refs_8_), channel_id=1, source_target_pairs={{0,16},{16,0},{1,17},{17,1},{2,18},{18,2},{3,19},{19,3},{4,20},{20... | collective-permute-start | bytes 98312 | tf_op jit(solution)/shard_map/ppermute | solution.py:509
  81.8 1.2 %collective-permute-start.30 = (f32[32,128]{1,0:T(8,128)S(1)}, f32[32,128]{1,0:T(8,128)S(1)}, u32[]{:S(2)}, u32[]{:S(2)}) collective-permute-start(f32[32,128]{1,0:T(8,128)S(1)} %get-tuple-element.99), channel_id=1, source_target_pairs={{0,1},{1,0},{2,3},{3,2},{4,5},{5,4},{6,7},{7,6},{8,9},{9,8},{10,11... | collective-permute-start | bytes 49160 | tf_op jit(solution)/shard_map/ppermute | solution.py:506

commit v8 on v7

--- a/solution.py
+++ b/solution.py
@@ -547,11 +547,14 @@
         (0, lambda: target_job(in_hbm(target_emb)[0])),
         (0, lambda: target_job(sibling_emb)),
         (0, lambda: near_job([(upper, lower, 0)])),
+        (0, None),
     ]
 
     def behind_job(step, *halves):
         if jobs and jobs[0][0] <= max(0, step - 2):
-            halves, _ = lax.optimization_barrier((halves, jobs.pop(0)[1]()))
+            job = jobs.pop(0)[1]
+            if job is not None:
+                halves, _ = lax.optimization_barrier((halves, job()))
         return halves
 
     up_a, up_b, down_a, down_b = upper, lower, upper, lower

time: 84.3 us -> 84.3 us (level)
  no operation moved by 1% of the time
where the time goes in v8:
time: 84.3 us; the launch traced here: 84.1 us
  starting transfers between devices  35.6 us (42%)
  waiting for transfers between devices  26.8 us (32%)
  Pallas kernels  20.9 us (25%)
    ppermute x14, starting transfers between devices, around(): return lax.ppermute(x, 'dev', pairs)  14.9 us
    ppermute x12, starting transfers between devices, across(): return lax.ppermute(x, 'dev', [(i, i ^ bit) for i in range(dev_count)])  12.8 us
    ppermute x12, waiting for transfers between devices, across(): return lax.ppermute(x, 'dev', [(i, i ^ bit) for i in range(dev_count)])  12.7 us
    ppermute x14, waiting for transfers between devices, around(): return lax.ppermute(x, 'dev', pairs)  12.6 us
    pallas_call x6, Pallas kernels, build_tiles(): pl.pallas_call(functools.partial(tile_kernel, plan), out_shape=out_shape,...  9.57 us
    ppermute x5, starting transfers between devices, to_group(): lax.ppermute(x, 'group', [(g, (g + by) % group_count) for g in range(grou...  7.86 us
    pallas_call x2, Pallas kernels, target_operand(): pl.pallas_call(target_kernel, out_shape=pltpu.VMEM((blocks, width, 2 * ro...  5.09 us
    pallas_call x2, Pallas kernels, column_sums(): pl.pallas_call(functools.partial(column_kernel, counts), out_shape=(jax.S...  1.81 us
  transfers between devices with their start and end apart: 31, of which 22 were waited for; matrix products, arithmetic and copies ran while one was open for 0% of the time, Pallas kernels for 22%

profile of v8, /device:TPU:0, one launch (start us, length us, event | category | flops | bytes accessed | tf_op | source)
XLA Modules:
  0.0 84.1 jit_solution(805714390478101001)
XLA Ops:
  0.6 0.5 collective-permute-start.2
  1.1 1.2 %pack.1 = (f32[520,128]{1,0:T(8,128)S(1)}, f32[520,128]{1,0:T(8,128)S(1)}, f32[1040,128]{1,0:T(8,128)S(1)}) custom-call(s32[1]{0:T(128)} %bitcast.device.refs_0_, f32[8,128,128]{2,1,0:T(8,128)} %emb.1, f32[8,128]{1,0:T(8,128)} %refs_9_.1, s32[8,7]{1,0:T(8,128)} %cand_device.1, s32[8,8]{1,0:T(8,128)} %cand_block.1), custom_call_target="tpu_custom_call" | custom-call | tf_op jit(solution)/shard_map/pack/pallas_call | solution.py:133
  2.4 2.6 %collective-permute-start = (f32[520,128]{1,0:T(8,128)S(1)}, f32[520,128]{1,0:T(8,128)S(1)}, u32[]{:S(2)}, u32[]{:S(2)}) collective-permute-start(f32[520,128]{1,0:T(8,128)S(1)} %get-tuple-element.58.refs_1_), channel_id=1, source_target_pairs={{0,4},{1,5},{4,8},{5,9},{8,12},{9,13},{12,14},{13,15},{14,10},{15,... | collective-permute-start | bytes 798728 | tf_op jit(solution)/shard_map/ppermute | solution.py:503
  5.0 2.9 %target_operand.2.refs_2_.refs_3_.refs_5_ = bf16[32,128,256]{2,1,0:T(8,128)(2,1)S(1)} custom-call(f32[32,128,128]{2,1,0:T(8,128)} %emb_ref.1), custom_call_target="tpu_custom_call" | custom-call | tf_op jit(solution)/shard_map/target_operand/pallas_call | solution.py:90
  8.0 2.1 %collective-permute-start.3 = (f32[520,128]{1,0:T(8,128)S(1)}, f32[520,128]{1,0:T(8,128)S(1)}, u32[]{:S(2)}, u32[]{:S(2)}) collective-permute-start(f32[520,128]{1,0:T(8,128)S(1)} %get-tuple-element.57.refs_2_), channel_id=1, source_target_pairs={{0,4},{1,5},{4,8},{5,9},{8,12},{9,13},{12,14},{13,15},{14,10},{15,... | collective-permute-start | bytes 798728 | tf_op jit(solution)/shard_map/ppermute | solution.py:503
  10.1 2.1 %target_operand.3.refs_4_.refs_6_ = bf16[32,128,256]{2,1,0:T(8,128)(2,1)S(1)} custom-call(f32[32,128,128]{2,1,0:T(8,128)S(1)} %collective-permute-done.2.emb_ref), custom_call_target="tpu_custom_call" | custom-call | tf_op jit(solution)/shard_map/target_operand/pallas_call | solution.py:90
  12.2 2.0 %collective-permute-done.5.refs_4_ = f32[520,128]{1,0:T(8,128)S(1)} collective-permute-done((f32[520,128]{1,0:T(8,128)S(1)}, f32[520,128]{1,0:T(8,128)S(1)}, u32[]{:S(2)}, u32[]{:S(2)}) %collective-permute-start.5) | collective-permute-done | bytes 266272 | tf_op jit(solution)/shard_map/ppermute | solution.py:503
  14.3 1.6 %collective-permute-start.6 = (f32[520,128]{1,0:T(8,128)S(1)}, f32[520,128]{1,0:T(8,128)S(1)}, u32[]{:S(2)}, u32[]{:S(2)}) collective-permute-start(f32[520,128]{1,0:T(8,128)S(1)} %collective-permute-done.refs_1_), channel_id=1, source_target_pairs={{0,4},{1,5},{4,8},{5,9},{8,12},{9,13},{12,14},{13,15},{14,10},{15,... | collective-permute-start | bytes 798728 | tf_op jit(solution)/shard_map/ppermute | solution.py:503
  15.9 0.4 collective-permute-start.9
  16.3 1.5 %collective-permute-start.1 = (f32[1040,128]{1,0:T(8,128)S(1)}, f32[1040,128]{1,0:T(8,128)S(1)}, u32[]{:S(2)}, u32[]{:S(2)}) collective-permute-start(f32[1040,128]{1,0:T(8,128)S(1)} %get-tuple-element.53), channel_id=1, source_target_pairs={{0,16},{16,0},{1,17},{17,1},{2,18},{18,2},{3,19},{19,3},{4,20},{20... | collective-permute-start | bytes 1597448 | tf_op jit(solution)/shard_map/ppermute | solution.py:509
  17.8 1.5 %build_tiles.7 = (bf16[10,128,256]{2,1,0:T(8,128)(2,1)S(1)}, s32[21]{0:T(128)S(4)}, f32[64,128]{1,0:T(8,128)S(1)}, f32[64,128]{1,0:T(8,128)S(1)}, bf16[10,128,256]{2,1,0:T(8,128)(2,1)S(1)}) custom-call(s32[1]{0:T(128)} %bitcast.device.refs_0_, f32[520,128]{1,0:T(8,128)S(1)} %get-tuple-element.58.refs_1_, f32[520,128]{1,0:T(8,128)S(1)} %get-tuple-element.57.refs_2_, ...), custom_call_target="tpu_custom_call" | custom-call | tf_op jit(solution)/shard_map/build_tiles/pallas_call | solution.py:327
  19.3 0.7 collective-permute-done.4.refs_3_
  20.0 1.6 %collective-permute-start.7 = (f32[520,128]{1,0:T(8,128)S(1)}, f32[520,128]{1,0:T(8,128)S(1)}, u32[]{:S(2)}, u32[]{:S(2)}) collective-permute-start(f32[520,128]{1,0:T(8,128)S(1)} %collective-permute-done.3.refs_2_), channel_id=1, source_target_pairs={{0,4},{1,5},{4,8},{5,9},{8,12},{9,13},{12,14},{13,15},{14,10},{15,... | collective-permute-start | bytes 798728 | tf_op jit(solution)/shard_map/ppermute | solution.py:503
  21.6 0.4 collective-permute-start.8
  22.0 1.6 %collective-permute-done.6.refs_1_ = f32[520,128]{1,0:T(8,128)S(1)} collective-permute-done((f32[520,128]{1,0:T(8,128)S(1)}, f32[520,128]{1,0:T(8,128)S(1)}, u32[]{:S(2)}, u32[]{:S(2)}) %collective-permute-start.6) | collective-permute-done | bytes 266272 | tf_op jit(solution)/shard_map/ppermute | solution.py:503
  23.6 2.0 %collective-permute-start.10 = (f32[520,128]{1,0:T(8,128)S(1)}, f32[520,128]{1,0:T(8,128)S(1)}, u32[]{:S(2)}, u32[]{:S(2)}) collective-permute-start(f32[520,128]{1,0:T(8,128)S(1)} %collective-permute-done.6.refs_1_), channel_id=1, source_target_pairs={{0,4},{1,5},{4,8},{5,9},{8,12},{9,13},{12,14},{13,15},{14,10},{15,... | collective-permute-start | bytes 798728 | tf_op jit(solution)/shard_map/ppermute | solution.py:503
  25.7 2.0 %build_tiles.8 = (bf16[20,128,256]{2,1,0:T(8,128)(2,1)S(1)}, s32[41]{0:T(128)S(4)}, f32[64,128]{1,0:T(8,128)S(1)}, f32[64,128]{1,0:T(8,128)S(1)}, bf16[20,128,256]{2,1,0:T(8,128)(2,1)S(1)}) custom-call(s32[1]{0:T(128)} %bitcast.device.refs_0_, f32[520,128]{1,0:T(8,128)S(1)} %collective-permute-done.refs_1_, f32[520,128]{1,0:T(8,128)S(1)} %collective-permute-done.3.refs_2_, ...), custom_call_target="tpu_custom_call" | custom-call | tf_op jit(solution)/shard_map/build_tiles/pallas_call | solution.py:327
  27.7 1.6 %collective-permute-done.7.refs_2_ = f32[520,128]{1,0:T(8,128)S(1)} collective-permute-done((f32[520,128]{1,0:T(8,128)S(1)}, f32[520,128]{1,0:T(8,128)S(1)}, u32[]{:S(2)}, u32[]{:S(2)}) %collective-permute-start.7) | collective-permute-done | bytes 266272 | tf_op jit(solution)/shard_map/ppermute | solution.py:503
  29.3 2.1 %collective-permute-done.8.refs_3_ = f32[520,128]{1,0:T(8,128)S(1)} collective-permute-done((f32[520,128]{1,0:T(8,128)S(1)}, f32[520,128]{1,0:T(8,128)S(1)}, u32[]{:S(2)}, u32[]{:S(2)}) %collective-permute-start.8) | collective-permute-done | bytes 266272 | tf_op jit(solution)/shard_map/ppermute | solution.py:503
  31.4 1.6 %collective-permute-start.11 = (f32[520,128]{1,0:T(8,128)S(1)}, f32[520,128]{1,0:T(8,128)S(1)}, u32[]{:S(2)}, u32[]{:S(2)}) collective-permute-start(f32[520,128]{1,0:T(8,128)S(1)} %collective-permute-done.7.refs_2_), channel_id=1, source_target_pairs={{0,4},{1,5},{4,8},{5,9},{8,12},{9,13},{12,14},{13,15},{14,10},{15,... | collective-permute-start | bytes 798728 | tf_op jit(solution)/shard_map/ppermute | solution.py:503
  33.0 0.4 collective-permute-start.12
  33.4 2.0 %build_tiles.9 = (bf16[20,128,256]{2,1,0:T(8,128)(2,1)S(1)}, s32[41]{0:T(128)S(4)}, f32[64,128]{1,0:T(8,128)S(1)}, f32[64,128]{1,0:T(8,128)S(1)}, bf16[20,128,256]{2,1,0:T(8,128)(2,1)S(1)}) custom-call(s32[1]{0:T(128)} %bitcast.device.refs_0_, f32[520,128]{1,0:T(8,128)S(1)} %collective-permute-done.6.refs_1_, f32[520,128]{1,0:T(8,128)S(1)} %collective-permute-done.7.refs_2_, ...), custom_call_target="tpu_custom_call" | custom-call | tf_op jit(solution)/shard_map/build_tiles/pallas_call | solution.py:327
  35.4 1.7 %collective-permute-done.13.refs_4_ = f32[520,128]{1,0:T(8,128)S(1)} collective-permute-done((f32[520,128]{1,0:T(8,128)S(1)}, f32[520,128]{1,0:T(8,128)S(1)}, u32[]{:S(2)}, u32[]{:S(2)}) %collective-permute-start.13) | collective-permute-done | bytes 266272 | tf_op jit(solution)/shard_map/ppermute | solution.py:503
  37.1 1.6 %collective-permute-start.14 = (f32[520,128]{1,0:T(8,128)S(1)}, f32[520,128]{1,0:T(8,128)S(1)}, u32[]{:S(2)}, u32[]{:S(2)}) collective-permute-start(f32[520,128]{1,0:T(8,128)S(1)} %collective-permute-done.10.refs_1_), channel_id=1, source_target_pairs={{0,4},{1,5},{4,8},{5,9},{8,12},{9,13},{12,14},{13,15},{14,10},{15,... | collective-permute-start | bytes 798728 | tf_op jit(solution)/shard_map/ppermute | solution.py:503
  38.7 0.4 collective-permute-start.15
  39.1 1.3 %build_tiles.6 = (bf16[8,128,256]{2,1,0:T(8,128)(2,1)S(1)}, s32[8]{0:T(128)S(4)}, f32[8,128]{1,0:T(8,128)S(1)}, f32[8,128]{1,0:T(8,128)S(1)}) custom-call(s32[1]{0:T(128)} %bitcast.device.refs_0_, f32[1040,128]{1,0:T(8,128)S(1)} %collective-permute-done.1.refs_1_, bf16[32,128,256]{2,1,0:T(8,128)(2,1)S(1)} %target_operand.2.refs_2_.refs_3_.refs_5_), custom_call_target="tpu_custom_call" | custom-call | tf_op jit(solution)/shard_map/build_tiles/pallas_call | solution.py:327
  40.5 1.6 %collective-permute-start.16 = (f32[8,128]{1,0:T(8,128)S(1)}, f32[8,128]{1,0:T(8,128)S(1)}, u32[]{:S(2)}, u32[]{:S(2)}) collective-permute-start(f32[8,128]{1,0:T(8,128)S(1)} %get-tuple-element.79), channel_id=1, source_target_pairs={{0,16},{16,0},{1,17},{17,1},{2,18},{18,2},{3,19},{19,3},{4,20},{20... | collective-permute-start | bytes 12296 | tf_op jit(solution)/shard_map/ppermute | solution.py:509
  42.0 0.8 collective-permute-done.12.refs_3_
  42.8 2.0 %build_tiles.10 = (bf16[20,128,256]{2,1,0:T(8,128)(2,1)S(1)}, s32[41]{0:T(128)S(4)}, f32[64,128]{1,0:T(8,128)S(1)}, f32[64,128]{1,0:T(8,128)S(1)}, bf16[20,128,256]{2,1,0:T(8,128)(2,1)S(1)}) custom-call(s32[1]{0:T(128)} %bitcast.device.refs_0_, f32[520,128]{1,0:T(8,128)S(1)} %collective-permute-done.10.refs_1_, ...), custom_call_target="tpu_custom_call" | custom-call | tf_op jit(solution)/shard_map/build_tiles/pallas_call | solution.py:327
  44.8 1.4 %collective-permute-done.14.upper.refs_1_ = f32[520,128]{1,0:T(8,128)S(1)} collective-permute-done((f32[520,128]{1,0:T(8,128)S(1)}, f32[520,128]{1,0:T(8,128)S(1)}, u32[]{:S(2)}, u32[]{:S(2)}) %collective-permute-start.14) | collective-permute-done | bytes 266272 | tf_op jit(solution)/shard_map/ppermute | solution.py:503
  46.2 0.9 %plan_tiles.1 = (s32[21]{0:T(128)S(4)}, s32[11]{0:T(128)S(4)}) custom-call(s32[1]{0:T(128)} %bitcast.device.refs_0_, f32[520,128]{1,0:T(8,128)S(1)} %collective-permute-done.14.upper.refs_1_), custom_call_target="tpu_custom_call" | custom-call | tf_op jit(solution)/shard_map/plan_tiles/pallas_call | solution.py:279
  47.1 0.7 collective-permute-done.15.refs_2_
  47.8 0.8 build_tiles.11
  48.6 2.6 %collective-permute-start.17 = (f32[64,128]{1,0:T(8,128)S(1)}, f32[64,128]{1,0:T(8,128)S(1)}, u32[]{:S(2)}, u32[]{:S(2)}) collective-permute-start(f32[64,128]{1,0:T(8,128)S(1)} %get-tuple-element.81), channel_id=1, source_target_pairs={{0,8},{1,9},{2,10},{3,11},{4,12},{5,13},{6,14},{7,15},{8,0},{9,1},... | collective-permute-start | bytes 98312 | tf_op jit(solution)/shard_map/ppermute | solution.py:506
  51.2 2.2 %collective-permute-done.17 = f32[64,128]{1,0:T(8,128)S(1)} collective-permute-done((f32[64,128]{1,0:T(8,128)S(1)}, f32[64,128]{1,0:T(8,128)S(1)}, u32[]{:S(2)}, u32[]{:S(2)}) %collective-permute-start.17) | collective-permute-done | bytes 32800 | tf_op jit(solution)/shard_map/ppermute | solution.py:506
  53.4 2.1 %collective-permute-start.18 = (f32[64,128]{1,0:T(8,128)S(1)}, f32[64,128]{1,0:T(8,128)S(1)}, u32[]{:S(2)}, u32[]{:S(2)}) collective-permute-start(f32[64,128]{1,0:T(8,128)S(1)} %add.6.refs_0_), channel_id=1, source_target_pairs={{0,6},{1,7},{2,4},{3,5},{4,2},{5,3},{6,0},{7,1},{8,14},{9,15},{10,... | collective-permute-start | bytes 98312 | tf_op jit(solution)/shard_map/ppermute | solution.py:506
  55.5 0.6 collective-permute-start.19
  56.1 0.8 %collective-permute-start.20 = (f32[64,128]{1,0:T(8,128)S(1)}, f32[64,128]{1,0:T(8,128)S(1)}, u32[]{:S(2)}, u32[]{:S(2)}) collective-permute-start(f32[64,128]{1,0:T(8,128)S(1)} %add.6.refs_0_), channel_id=1, source_target_pairs={{0,2},{1,3},{2,0},{3,1},{4,6},{5,7},{6,4},{7,5},{8,10},{9,11},{10,... | collective-permute-start | bytes 98312 | tf_op jit(solution)/shard_map/ppermute | solution.py:506
  56.9 1.3 %collective-permute-done.18.refs_1_ = f32[64,128]{1,0:T(8,128)S(1)} collective-permute-done((f32[64,128]{1,0:T(8,128)S(1)}, f32[64,128]{1,0:T(8,128)S(1)}, u32[]{:S(2)}, u32[]{:S(2)}) %collective-permute-start.18) | collective-permute-done | bytes 32800 | tf_op jit(solution)/shard_map/ppermute | solution.py:506
  58.3 1.2 %collective-permute-done.19.refs_2_ = f32[64,128]{1,0:T(8,128)S(1)} collective-permute-done((f32[64,128]{1,0:T(8,128)S(1)}, f32[64,128]{1,0:T(8,128)S(1)}, u32[]{:S(2)}, u32[]{:S(2)}) %collective-permute-start.19) | collective-permute-done | bytes 32800 | tf_op jit(solution)/shard_map/ppermute | solution.py:506
  59.5 0.6 collective-permute-done.20.refs_3_
  60.0 1.6 %collective-permute-start.21 = (f32[64,128]{1,0:T(8,128)S(1)}, f32[64,128]{1,0:T(8,128)S(1)}, u32[]{:S(2)}, u32[]{:S(2)}) collective-permute-start(f32[64,128]{1,0:T(8,128)S(1)} %add_all.2.refs_5_), channel_id=1, source_target_pairs={{0,16},{16,0},{1,17},{17,1},{2,18},{18,2},{3,19},{19,3},{4,20},{20... | collective-permute-start | bytes 98312 | tf_op jit(solution)/shard_map/ppermute | solution.py:509
  61.6 0.9 %column_sums.2 = (f32[32,128]{1,0:T(8,128)S(1)}, f32[32,128]{1,0:T(8,128)S(1)}) custom-call(s32[21]{0:T(128)S(4)} %get-tuple-element.56.refs_0_, s32[41]{0:T(128)S(4)} %get-tuple-element.61.refs_1_, s32[41]{0:T(128)S(4)} %get-tuple-element.68.refs_2_, s32[41]{0:T(128)S(4)} %get-tuple-element.73.refs_3_, s32[21]{0:T(128)S(4)} %get-tuple-element.75.refs_8_.refs_4_, ...), custom_call_target="tpu_custom_call" | custom-call | tf_op jit(solution)/shard_map/column_sums/pallas_call | solution.py:396
  62.5 0.1 collective-permute-start.22
  62.6 1.2 %collective-permute-done.22.refs_5_ = f32[32,128]{1,0:T(8,128)S(1)} collective-permute-done((f32[32,128]{1,0:T(8,128)S(1)}, f32[32,128]{1,0:T(8,128)S(1)}, u32[]{:S(2)}, u32[]{:S(2)}) %collective-permute-start.22) | collective-permute-done | bytes 16416 | tf_op jit(solution)/shard_map/ppermute | solution.py:506
  63.8 0.2 collective-permute-done.21.refs_2_
  64.0 0.4 closing.2
  64.4 0.1 collective-permute-start.23
  64.5 1.6 %collective-permute-start.24 = (f32[8,128]{1,0:T(8,128)S(1)}, f32[8,128]{1,0:T(8,128)S(1)}, u32[]{:S(2)}, u32[]{:S(2)}) collective-permute-start(f32[8,128]{1,0:T(8,128)S(1)} %get-tuple-element.97), channel_id=1, source_target_pairs={{0,16},{16,0},{1,17},{17,1},{2,18},{18,2},{3,19},{19,3},{4,20},{20... | collective-permute-start | bytes 12296 | tf_op jit(solution)/shard_map/ppermute | solution.py:509
  66.1 1.0 %row_sums.1.rows = f32[64,128]{1,0:T(8,128)S(1)} custom-call(s32[21]{0:T(128)S(4)} %get-tuple-element.56.refs_0_, s32[41]{0:T(128)S(4)} %get-tuple-element.61.refs_1_, s32[41]{0:T(128)S(4)} %get-tuple-element.68.refs_2_, s32[41]{0:T(128)S(4)} %get-tuple-element.73.refs_3_, s32[21]{0:T(128)S(4)} %get-tuple-element.75.refs_8_.refs_4_, ...), custom_call_target="tpu_custom_call" | custom-call | tf_op jit(solution)/shard_map/row_sums/pallas_call | solution.py:475
  67.1 1.1 %collective-permute-done.24.part = f32[8,128]{1,0:T(8,128)S(1)} collective-permute-done((f32[8,128]{1,0:T(8,128)S(1)}, f32[8,128]{1,0:T(8,128)S(1)}, u32[]{:S(2)}, u32[]{:S(2)}) %collective-permute-start.24) | collective-permute-done | bytes 4128 | tf_op jit(solution)/shard_map/ppermute | solution.py:509
  68.2 2.5 %collective-permute-start.25 = (f32[64,128]{1,0:T(8,128)S(1)}, f32[64,128]{1,0:T(8,128)S(1)}, u32[]{:S(2)}, u32[]{:S(2)}) collective-permute-start(f32[64,128]{1,0:T(8,128)S(1)} %add_own.1), channel_id=1, source_target_pairs={{0,8},{1,9},{2,10},{3,11},{4,12},{5,13},{6,14},{7,15},{8,0},{9,1},... | collective-permute-start | bytes 98312 | tf_op jit(solution)/shard_map/ppermute | solution.py:506
  70.7 2.3 %collective-permute-done.25 = f32[64,128]{1,0:T(8,128)S(1)} collective-permute-done((f32[64,128]{1,0:T(8,128)S(1)}, f32[64,128]{1,0:T(8,128)S(1)}, u32[]{:S(2)}, u32[]{:S(2)}) %collective-permute-start.25) | collective-permute-done | bytes 32800 | tf_op jit(solution)/shard_map/ppermute | solution.py:506
  73.0 1.9 %collective-permute-start.26 = (f32[64,128]{1,0:T(8,128)S(1)}, f32[64,128]{1,0:T(8,128)S(1)}, u32[]{:S(2)}, u32[]{:S(2)}) collective-permute-start(f32[64,128]{1,0:T(8,128)S(1)} %add.7.refs_0_), channel_id=1, source_target_pairs={{0,6},{1,7},{2,4},{3,5},{4,2},{5,3},{6,0},{7,1},{8,14},{9,15},{10,... | collective-permute-start | bytes 98312 | tf_op jit(solution)/shard_map/ppermute | solution.py:506
  74.9 0.5 collective-permute-start.27
  75.3 1.2 %collective-permute-start.28 = (f32[64,128]{1,0:T(8,128)S(1)}, f32[64,128]{1,0:T(8,128)S(1)}, u32[]{:S(2)}, u32[]{:S(2)}) collective-permute-start(f32[64,128]{1,0:T(8,128)S(1)} %add.7.refs_0_), channel_id=1, source_target_pairs={{0,2},{1,3},{2,0},{3,1},{4,6},{5,7},{6,4},{7,5},{8,10},{9,11},{10,... | collective-permute-start | bytes 98312 | tf_op jit(solution)/shard_map/ppermute | solution.py:506
  76.5 1.3 %collective-permute-done.26.refs_1_ = f32[64,128]{1,0:T(8,128)S(1)} collective-permute-done((f32[64,128]{1,0:T(8,128)S(1)}, f32[64,128]{1,0:T(8,128)S(1)}, u32[]{:S(2)}, u32[]{:S(2)}) %collective-permute-start.26) | collective-permute-done | bytes 32800 | tf_op jit(solution)/shard_map/ppermute | solution.py:506
  77.8 1.0 %collective-permute-done.27.refs_2_ = f32[64,128]{1,0:T(8,128)S(1)} collective-permute-done((f32[64,128]{1,0:T(8,128)S(1)}, f32[64,128]{1,0:T(8,128)S(1)}, u32[]{:S(2)}, u32[]{:S(2)}) %collective-permute-start.27) | collective-permute-done | bytes 32800 | tf_op jit(solution)/shard_map/ppermute | solution.py:506
  78.8 0.5 collective-permute-done.28.refs_3_
  79.3 1.6 %collective-permute-start.29 = (f32[64,128]{1,0:T(8,128)S(1)}, f32[64,128]{1,0:T(8,128)S(1)}, u32[]{:S(2)}, u32[]{:S(2)}) collective-permute-start(f32[64,128]{1,0:T(8,128)S(1)} %add_all.3.refs_5_.refs_8_), channel_id=1, source_target_pairs={{0,16},{16,0},{1,17},{17,1},{2,18},{18,2},{3,19},{19,3},{4,20},{20... | collective-permute-start | bytes 98312 | tf_op jit(solution)/shard_map/ppermute | solution.py:509
  80.9 0.9 %column_sums.3 = (f32[32,128]{1,0:T(8,128)S(1)}, f32[32,128]{1,0:T(8,128)S(1)}) custom-call(s32[21]{0:T(128)S(4)} %get-tuple-element.56.refs_0_, s32[41]{0:T(128)S(4)} %get-tuple-element.61.refs_1_, s32[41]{0:T(128)S(4)} %get-tuple-element.68.refs_2_, s32[41]{0:T(128)S(4)} %get-tuple-element.73.refs_3_, s32[21]{0:T(128)S(4)} %get-tuple-element.75.refs_8_.refs_4_, ...), custom_call_target="tpu_custom_call" | custom-call | tf_op jit(solution)/shard_map/column_sums/pallas_call | solution.py:396
  81.9 1.2 %collective-permute-done.30.refs_5_ = f32[32,128]{1,0:T(8,128)S(1)} collective-permute-done((f32[32,128]{1,0:T(8,128)S(1)}, f32[32,128]{1,0:T(8,128)S(1)}, u32[]{:S(2)}, u32[]{:S(2)}) %collective-permute-start.30) | collective-permute-done | bytes 16416 | tf_op jit(solution)/shard_map/ppermute | solution.py:506
  83.0 0.2 collective-permute-done.29.refs_2_
  83.3 0.8 closing.3
  (22 shorter events, 0.2 us)
Async XLA Ops:
  0.6 9.5 %collective-permute-start.2 = (f32[32,128,128]{2,1,0:T(8,128)}, f32[32,128,128]{2,1,0:T(8,128)S(1)}, u32[]{:S(2)}, u32[]{:S(2)}) collective-permute-start(f32[32,128,128]{2,1,0:T(8,128)} %emb_ref.1), channel_id=1, source_target_pairs={{0,1},{1,0},{2,3},{3,2},{4,5},{5,4},{6,7},{7,6},{8,9},{9,8},{10,11... | collective-permute-start | bytes 6291464 | tf_op jit(solution)/shard_map/ppermute | solution.py:506
  2.4 9.8 %collective-permute-start = (f32[520,128]{1,0:T(8,128)S(1)}, f32[520,128]{1,0:T(8,128)S(1)}, u32[]{:S(2)}, u32[]{:S(2)}) collective-permute-start(f32[520,128]{1,0:T(8,128)S(1)} %get-tuple-element.58.refs_1_), channel_id=1, source_target_pairs={{0,4},{1,5},{4,8},{5,9},{8,12},{9,13},{12,14},{13,15},{14,10},{15,... | collective-permute-start | bytes 798728 | tf_op jit(solution)/shard_map/ppermute | solution.py:503
  5.0 9.2 %collective-permute-start.5 = (f32[520,128]{1,0:T(8,128)S(1)}, f32[520,128]{1,0:T(8,128)S(1)}, u32[]{:S(2)}, u32[]{:S(2)}) collective-permute-start(f32[520,128]{1,0:T(8,128)S(1)} %get-tuple-element.57.refs_2_), channel_id=1, source_target_pairs={{0,2},{1,3},{4,0},{5,1},{8,4},{9,5},{12,8},{13,9},{14,12},{15,13},... | collective-permute-start | bytes 798728 | tf_op jit(solution)/shard_map/ppermute | solution.py:503
  8.0 11.3 %collective-permute-start.3 = (f32[520,128]{1,0:T(8,128)S(1)}, f32[520,128]{1,0:T(8,128)S(1)}, u32[]{:S(2)}, u32[]{:S(2)}) collective-permute-start(f32[520,128]{1,0:T(8,128)S(1)} %get-tuple-element.57.refs_2_), channel_id=1, source_target_pairs={{0,4},{1,5},{4,8},{5,9},{8,12},{9,13},{12,14},{13,15},{14,10},{15,... | collective-permute-start | bytes 798728 | tf_op jit(solution)/shard_map/ppermute | solution.py:503
  10.1 9.9 %collective-permute-start.4 = (f32[520,128]{1,0:T(8,128)S(1)}, f32[520,128]{1,0:T(8,128)S(1)}, u32[]{:S(2)}, u32[]{:S(2)}) collective-permute-start(f32[520,128]{1,0:T(8,128)S(1)} %get-tuple-element.58.refs_1_), channel_id=1, source_target_pairs={{0,2},{1,3},{4,0},{5,1},{8,4},{9,5},{12,8},{13,9},{14,12},{15,13},... | collective-permute-start | bytes 798728 | tf_op jit(solution)/shard_map/ppermute | solution.py:503
  14.3 9.3 %collective-permute-start.6 = (f32[520,128]{1,0:T(8,128)S(1)}, f32[520,128]{1,0:T(8,128)S(1)}, u32[]{:S(2)}, u32[]{:S(2)}) collective-permute-start(f32[520,128]{1,0:T(8,128)S(1)} %collective-permute-done.refs_1_), channel_id=1, source_target_pairs={{0,4},{1,5},{4,8},{5,9},{8,12},{9,13},{12,14},{13,15},{14,10},{15,... | collective-permute-start | bytes 798728 | tf_op jit(solution)/shard_map/ppermute | solution.py:503
  15.9 9.8 %collective-permute-start.9 = (f32[520,128]{1,0:T(8,128)S(1)}, f32[520,128]{1,0:T(8,128)S(1)}, u32[]{:S(2)}, u32[]{:S(2)}) collective-permute-start(f32[520,128]{1,0:T(8,128)S(1)} %collective-permute-done.5.refs_4_), channel_id=1, source_target_pairs={{0,2},{1,3},{4,0},{5,1},{8,4},{9,5},{12,8},{13,9},{14,12},{15,13},... | collective-permute-start | bytes 798728 | tf_op jit(solution)/shard_map/ppermute | solution.py:503
  16.3 22.8 %collective-permute-start.1 = (f32[1040,128]{1,0:T(8,128)S(1)}, f32[1040,128]{1,0:T(8,128)S(1)}, u32[]{:S(2)}, u32[]{:S(2)}) collective-permute-start(f32[1040,128]{1,0:T(8,128)S(1)} %get-tuple-element.53), channel_id=1, source_target_pairs={{0,16},{16,0},{1,17},{17,1},{2,18},{18,2},{3,19},{19,3},{4,20},{20... | collective-permute-start | bytes 1597448 | tf_op jit(solution)/shard_map/ppermute | solution.py:509
  20.0 9.3 %collective-permute-start.7 = (f32[520,128]{1,0:T(8,128)S(1)}, f32[520,128]{1,0:T(8,128)S(1)}, u32[]{:S(2)}, u32[]{:S(2)}) collective-permute-start(f32[520,128]{1,0:T(8,128)S(1)} %collective-permute-done.3.refs_2_), channel_id=1, source_target_pairs={{0,4},{1,5},{4,8},{5,9},{8,12},{9,13},{12,14},{13,15},{14,10},{15,... | collective-permute-start | bytes 798728 | tf_op jit(solution)/shard_map/ppermute | solution.py:503
  21.6 9.8 %collective-permute-start.8 = (f32[520,128]{1,0:T(8,128)S(1)}, f32[520,128]{1,0:T(8,128)S(1)}, u32[]{:S(2)}, u32[]{:S(2)}) collective-permute-start(f32[520,128]{1,0:T(8,128)S(1)} %collective-permute-done.4.refs_3_), channel_id=1, source_target_pairs={{0,2},{1,3},{4,0},{5,1},{8,4},{9,5},{12,8},{13,9},{14,12},{15,13},... | collective-permute-start | bytes 798728 | tf_op jit(solution)/shard_map/ppermute | solution.py:503
  23.6 11.8 %collective-permute-start.10 = (f32[520,128]{1,0:T(8,128)S(1)}, f32[520,128]{1,0:T(8,128)S(1)}, u32[]{:S(2)}, u32[]{:S(2)}) collective-permute-start(f32[520,128]{1,0:T(8,128)S(1)} %collective-permute-done.6.refs_1_), channel_id=1, source_target_pairs={{0,4},{1,5},{4,8},{5,9},{8,12},{9,13},{12,14},{13,15},{14,10},{15,... | collective-permute-start | bytes 798728 | tf_op jit(solution)/shard_map/ppermute | solution.py:503
  25.7 11.4 %collective-permute-start.13 = (f32[520,128]{1,0:T(8,128)S(1)}, f32[520,128]{1,0:T(8,128)S(1)}, u32[]{:S(2)}, u32[]{:S(2)}) collective-permute-start(f32[520,128]{1,0:T(8,128)S(1)} %collective-permute-done.9.refs_4_), channel_id=1, source_target_pairs={{0,2},{1,3},{4,0},{5,1},{8,4},{9,5},{12,8},{13,9},{14,12},{15,13},... | collective-permute-start | bytes 798728 | tf_op jit(solution)/shard_map/ppermute | solution.py:503
  31.4 10.6 %collective-permute-start.11 = (f32[520,128]{1,0:T(8,128)S(1)}, f32[520,128]{1,0:T(8,128)S(1)}, u32[]{:S(2)}, u32[]{:S(2)}) collective-permute-start(f32[520,128]{1,0:T(8,128)S(1)} %collective-permute-done.7.refs_2_), channel_id=1, source_target_pairs={{0,4},{1,5},{4,8},{5,9},{8,12},{9,13},{12,14},{13,15},{14,10},{15,... | collective-permute-start | bytes 798728 | tf_op jit(solution)/shard_map/ppermute | solution.py:503
  33.0 9.8 %collective-permute-start.12 = (f32[520,128]{1,0:T(8,128)S(1)}, f32[520,128]{1,0:T(8,128)S(1)}, u32[]{:S(2)}, u32[]{:S(2)}) collective-permute-start(f32[520,128]{1,0:T(8,128)S(1)} %collective-permute-done.8.refs_3_), channel_id=1, source_target_pairs={{0,2},{1,3},{4,0},{5,1},{8,4},{9,5},{12,8},{13,9},{14,12},{15,13},... | collective-permute-start | bytes 798728 | tf_op jit(solution)/shard_map/ppermute | solution.py:503
  37.1 9.1 %collective-permute-start.14 = (f32[520,128]{1,0:T(8,128)S(1)}, f32[520,128]{1,0:T(8,128)S(1)}, u32[]{:S(2)}, u32[]{:S(2)}) collective-permute-start(f32[520,128]{1,0:T(8,128)S(1)} %collective-permute-done.10.refs_1_), channel_id=1, source_target_pairs={{0,4},{1,5},{4,8},{5,9},{8,12},{9,13},{12,14},{13,15},{14,10},{15,... | collective-permute-start | bytes 798728 | tf_op jit(solution)/shard_map/ppermute | solution.py:503
  38.7 9.1 %collective-permute-start.15 = (f32[520,128]{1,0:T(8,128)S(1)}, f32[520,128]{1,0:T(8,128)S(1)}, u32[]{:S(2)}, u32[]{:S(2)}) collective-permute-start(f32[520,128]{1,0:T(8,128)S(1)} %collective-permute-done.13.refs_4_), channel_id=1, source_target_pairs={{0,2},{1,3},{4,0},{5,1},{8,4},{9,5},{12,8},{13,9},{14,12},{15,13},... | collective-permute-start | bytes 798728 | tf_op jit(solution)/shard_map/ppermute | solution.py:503
  40.5 6.6 %collective-permute-start.16 = (f32[8,128]{1,0:T(8,128)S(1)}, f32[8,128]{1,0:T(8,128)S(1)}, u32[]{:S(2)}, u32[]{:S(2)}) collective-permute-start(f32[8,128]{1,0:T(8,128)S(1)} %get-tuple-element.79), channel_id=1, source_target_pairs={{0,16},{16,0},{1,17},{17,1},{2,18},{18,2},{3,19},{19,3},{4,20},{20... | collective-permute-start | bytes 12296 | tf_op jit(solution)/shard_map/ppermute | solution.py:509
  48.6 4.8 %collective-permute-start.17 = (f32[64,128]{1,0:T(8,128)S(1)}, f32[64,128]{1,0:T(8,128)S(1)}, u32[]{:S(2)}, u32[]{:S(2)}) collective-permute-start(f32[64,128]{1,0:T(8,128)S(1)} %get-tuple-element.81), channel_id=1, source_target_pairs={{0,8},{1,9},{2,10},{3,11},{4,12},{5,13},{6,14},{7,15},{8,0},{9,1},... | collective-permute-start | bytes 98312 | tf_op jit(solution)/shard_map/ppermute | solution.py:506
  53.4 4.8 %collective-permute-start.18 = (f32[64,128]{1,0:T(8,128)S(1)}, f32[64,128]{1,0:T(8,128)S(1)}, u32[]{:S(2)}, u32[]{:S(2)}) collective-permute-start(f32[64,128]{1,0:T(8,128)S(1)} %add.6.refs_0_), channel_id=1, source_target_pairs={{0,6},{1,7},{2,4},{3,5},{4,2},{5,3},{6,0},{7,1},{8,14},{9,15},{10,... | collective-permute-start | bytes 98312 | tf_op jit(solution)/shard_map/ppermute | solution.py:506
  55.5 3.9 %collective-permute-start.19 = (f32[64,128]{1,0:T(8,128)S(1)}, f32[64,128]{1,0:T(8,128)S(1)}, u32[]{:S(2)}, u32[]{:S(2)}) collective-permute-start(f32[64,128]{1,0:T(8,128)S(1)} %add.6.refs_0_), channel_id=1, source_target_pairs={{0,4},{1,5},{2,6},{3,7},{4,0},{5,1},{6,2},{7,3},{8,12},{9,13},{10,... | collective-permute-start | bytes 98312 | tf_op jit(solution)/shard_map/ppermute | solution.py:506
  56.1 3.9 %collective-permute-start.20 = (f32[64,128]{1,0:T(8,128)S(1)}, f32[64,128]{1,0:T(8,128)S(1)}, u32[]{:S(2)}, u32[]{:S(2)}) collective-permute-start(f32[64,128]{1,0:T(8,128)S(1)} %add.6.refs_0_), channel_id=1, source_target_pairs={{0,2},{1,3},{2,0},{3,1},{4,6},{5,7},{6,4},{7,5},{8,10},{9,11},{10,... | collective-permute-start | bytes 98312 | tf_op jit(solution)/shard_map/ppermute | solution.py:506
  60.0 4.0 %collective-permute-start.21 = (f32[64,128]{1,0:T(8,128)S(1)}, f32[64,128]{1,0:T(8,128)S(1)}, u32[]{:S(2)}, u32[]{:S(2)}) collective-permute-start(f32[64,128]{1,0:T(8,128)S(1)} %add_all.2.refs_5_), channel_id=1, source_target_pairs={{0,16},{16,0},{1,17},{17,1},{2,18},{18,2},{3,19},{19,3},{4,20},{20... | collective-permute-start | bytes 98312 | tf_op jit(solution)/shard_map/ppermute | solution.py:509
  61.6 2.4 %copy-start = (f32[32,128]{1,0:T(8,128)S(1)}, f32[32,128]{1,0:T(8,128)}, u32[]{:S(2)}) copy-start(f32[32,128]{1,0:T(8,128)} %refs_6_.3) | copy-start | bytes 49156
  62.5 1.2 %collective-permute-start.22 = (f32[32,128]{1,0:T(8,128)S(1)}, f32[32,128]{1,0:T(8,128)S(1)}, u32[]{:S(2)}, u32[]{:S(2)}) collective-permute-start(f32[32,128]{1,0:T(8,128)S(1)} %get-tuple-element.90), channel_id=1, source_target_pairs={{0,1},{1,0},{2,3},{3,2},{4,5},{5,4},{6,7},{7,6},{8,9},{9,8},{10,11... | collective-permute-start | bytes 49160 | tf_op jit(solution)/shard_map/ppermute | solution.py:506
  64.4 1.7 %collective-permute-start.23 = (f32[32,128]{1,0:T(8,128)S(1)}, f32[32,128]{1,0:T(8,128)S(1)}, u32[]{:S(2)}, u32[]{:S(2)}) collective-permute-start(f32[32,128]{1,0:T(8,128)S(1)} %get-tuple-element.92.refs_5_), channel_id=1, source_target_pairs={{0,1},{1,0},{2,3},{3,2},{4,5},{5,4},{6,7},{7,6},{8,9},{9,8},{10,11... | collective-permute-start | bytes 49160 | tf_op jit(solution)/shard_map/ppermute | solution.py:506
  64.5 3.7 %collective-permute-start.24 = (f32[8,128]{1,0:T(8,128)S(1)}, f32[8,128]{1,0:T(8,128)S(1)}, u32[]{:S(2)}, u32[]{:S(2)}) collective-permute-start(f32[8,128]{1,0:T(8,128)S(1)} %get-tuple-element.97), channel_id=1, source_target_pairs={{0,16},{16,0},{1,17},{17,1},{2,18},{18,2},{3,19},{19,3},{4,20},{20... | collective-permute-start | bytes 12296 | tf_op jit(solution)/shard_map/ppermute | solution.py:509
  68.2 4.8 %collective-permute-start.25 = (f32[64,128]{1,0:T(8,128)S(1)}, f32[64,128]{1,0:T(8,128)S(1)}, u32[]{:S(2)}, u32[]{:S(2)}) collective-permute-start(f32[64,128]{1,0:T(8,128)S(1)} %add_own.1), channel_id=1, source_target_pairs={{0,8},{1,9},{2,10},{3,11},{4,12},{5,13},{6,14},{7,15},{8,0},{9,1},... | collective-permute-start | bytes 98312 | tf_op jit(solution)/shard_map/ppermute | solution.py:506
  73.0 4.8 %collective-permute-start.26 = (f32[64,128]{1,0:T(8,128)S(1)}, f32[64,128]{1,0:T(8,128)S(1)}, u32[]{:S(2)}, u32[]{:S(2)}) collective-permute-start(f32[64,128]{1,0:T(8,128)S(1)} %add.7.refs_0_), channel_id=1, source_target_pairs={{0,6},{1,7},{2,4},{3,5},{4,2},{5,3},{6,0},{7,1},{8,14},{9,15},{10,... | collective-permute-start | bytes 98312 | tf_op jit(solution)/shard_map/ppermute | solution.py:506
  74.9 3.9 %collective-permute-start.27 = (f32[64,128]{1,0:T(8,128)S(1)}, f32[64,128]{1,0:T(8,128)S(1)}, u32[]{:S(2)}, u32[]{:S(2)}) collective-permute-start(f32[64,128]{1,0:T(8,128)S(1)} %add.7.refs_0_), channel_id=1, source_target_pairs={{0,4},{1,5},{2,6},{3,7},{4,0},{5,1},{6,2},{7,3},{8,12},{9,13},{10,... | collective-permute-start | bytes 98312 | tf_op jit(solution)/shard_map/ppermute | solution.py:506
  75.3 3.9 %collective-permute-start.28 = (f32[64,128]{1,0:T(8,128)S(1)}, f32[64,128]{1,0:T(8,128)S(1)}, u32[]{:S(2)}, u32[]{:S(2)}) collective-permute-start(f32[64,128]{1,0:T(8,128)S(1)} %add.7.refs_0_), channel_id=1, source_target_pairs={{0,2},{1,3},{2,0},{3,1},{4,6},{5,7},{6,4},{7,5},{8,10},{9,11},{10,... | collective-permute-start | bytes 98312 | tf_op jit(solution)/shard_map/ppermute | solution.py:506
  79.3 4.0 %copy-start.1 = (f32[8,128]{1,0:T(8,128)S(1)}, f32[8,128]{1,0:T(8,128)}, u32[]{:S(2)}) copy-start(f32[8,128]{1,0:T(8,128)} %refs_9_.1) | copy-start | bytes 12292
  79.3 4.0 %collective-permute-start.29 = (f32[64,128]{1,0:T(8,128)S(1)}, f32[64,128]{1,0:T(8,128)S(1)}, u32[]{:S(2)}, u32[]{:S(2)}) collective-permute-start(f32[64,128]{1,0:T(8,128)S(1)} %add_all.3.refs_5_.refs_8_), channel_id=1, source_target_pairs={{0,16},{16,0},{1,17},{17,1},{2,18},{18,2},{3,19},{19,3},{4,20},{20... | collective-permute-start | bytes 98312 | tf_op jit(solution)/shard_map/ppermute | solution.py:509
  81.8 1.2 %collective-permute-start.30 = (f32[32,128]{1,0:T(8,128)S(1)}, f32[32,128]{1,0:T(8,128)S(1)}, u32[]{:S(2)}, u32[]{:S(2)}) collective-permute-start(f32[32,128]{1,0:T(8,128)S(1)} %get-tuple-element.99), channel_id=1, source_target_pairs={{0,1},{1,0},{2,3},{3,2},{4,5},{5,4},{6,7},{7,6},{8,9},{9,8},{10,11... | collective-permute-start | bytes 49160 | tf_op jit(solution)/shard_map/ppermute | solution.py:506
